TPU v7x, 32 devices: a whole 2x2x4 slice. The times are simulated.
32 devices in a mesh: wide: 8 (over z, y), narrow: 4 (over x, core).
Axes of the slice: x: 2, y: 2, z: 4, core: 2. Of those that a mesh axis runs over, the one named last changes fastest.
Arguments:
- tokens: bfloat16 [8, 1024, 1024], P('wide'), may hold values from -6 to 6
- conditions: float32 [8, 6, 1024], P('wide'), may hold values from -3 to 3
- item_live: int32 [8], P('wide'), may hold values from 0 to 1, as said below
- cotangent: bfloat16 [8, 1024, 1024], P('wide'), may hold values from -6 to 6
- modulation_table: float32 [6, 1024], replicated, may hold values from -3 to 3
- mixer_kernel: float32 [9, 1024], replicated, may hold values from -2 to 2
- hidden_kernel: float32 [9, 4096], P(None, 'narrow'), may hold values from -2 to 2
- attend_weight: float32 [1024, 3, 1024], P(None, None, 'narrow'), may hold values from -0.1875 to 0.1875
- output_weight: float32 [1024, 1024], P('narrow'), may hold values from -3 to 3
- expand_weight: float32 [1024, 4096], P(None, 'narrow'), may hold values from -0.1875 to 0.1875
- reduce_weight: float32 [4096, 1024], P('narrow'), may hold values from -0.15234375 to 0.15234375
- attend_moment: float32 [1024, 3, 1024], P(None, None, 'narrow'), may hold values from -0.0014095466 to 0.0014095466
- output_moment: float32 [1024, 1024], P('narrow'), may hold values from -0.0014095466 to 0.0014095466
- expand_moment: float32 [1024, 4096], P(None, 'narrow'), may hold values from -0.0014095466 to 0.0014095466
- reduce_moment: float32 [4096, 1024], P('narrow'), may hold values from -0.0014095466 to 0.0014095466
- table_first: float32 [6, 1024], replicated, may hold values from -0.00014095465 to 0.00014095465
- table_second: float32 [6, 1024], replicated, may hold values from 7.947286e-11 to 3.1789144e-10
- mixer_first: float32 [9, 1024], replicated, may hold values from -0.00014095465 to 0.00014095465
- mixer_second: float32 [9, 1024], replicated, may hold values from 7.947286e-11 to 3.1789144e-10
- hidden_first: float32 [9, 4096], P(None, 'narrow'), may hold values from -0.00014095465 to 0.00014095465
- hidden_second: float32 [9, 4096], P(None, 'narrow'), may hold values from 7.947286e-11 to 3.1789144e-10
Outputs:
- block_out: bfloat16 [8, 1024, 1024], P('wide')
- tokens_gradient: bfloat16 [8, 1024, 1024], P('wide')
- gradient_norm: float32 [], replicated
- attend_carried: float32 [1024, 3, 1024], P(None, None, 'narrow')
- output_carried: float32 [1024, 1024], P('narrow')
- expand_carried: float32 [1024, 4096], P(None, 'narrow')
- reduce_carried: float32 [4096, 1024], P('narrow')
- attend_result: float32 [1024, 3, 1024], P(None, None, 'narrow')
- output_result: float32 [1024, 1024], P('narrow')
- expand_result: float32 [1024, 4096], P(None, 'narrow')
- reduce_result: float32 [4096, 1024], P('narrow')
- table_moment: float32 [6, 1024], replicated
- table_square: float32 [6, 1024], replicated
- table_result: float32 [6, 1024], replicated
- mixer_moment: float32 [9, 1024], replicated
- mixer_square: float32 [9, 1024], replicated
- mixer_result: float32 [9, 1024], replicated
- hidden_moment: float32 [9, 4096], P(None, 'narrow')
- hidden_square: float32 [9, 4096], P(None, 'narrow')
- hidden_result: float32 [9, 4096], P(None, 'narrow')
Inputs may be any that keep to these rules, and one draw needn't show every extreme that they name: `item_live`: in each aligned block of 1 items (the slots of one index of wide) the live items come first, and at least one block is wholly live.
All inputs are finite; a program needn't handle non-finite values.
Results may differ from a plain program's by a relative error of at most 0.014.
The roundings to bfloat16 on the way count: a program that leaves them out, or rounds other values in their place, can miss the bound.
Values sent between devices are 32-bit elements; how exact they have to be, the bound alone decides.
A program may use at most 320 MiB of HBM per device.

v0:
```python
import math

import jax
import jax.numpy as jnp
from jax import lax
from jax.sharding import PartitionSpec as P

D = 1024
HEAD = 64
FF = 4096
GRID = 32
NEWTON = 5
STEP = 10


first_decay = 0.9
second_decay = 0.999
adam_rate = 0.3
muon_rate = 0.15
muon_momentum = 0.5
weight_decay = 0.01
newton_terms = (3.4445, -4.775, 2.0315)
gelu_slope = 0.7978845608
gelu_cubic = 0.044715


def layer_norm(values):
    average = jnp.mean(values, axis=-1, keepdims=True)
    centred = values - average
    spread = jnp.mean(centred * centred, axis=-1, keepdims=True)
    return centred * lax.rsqrt(spread + 1e-06)


def gelu_tanh(values):
    return (
        0.5
        * values
        * (1.0 + jnp.tanh(gelu_slope * (values + gelu_cubic * values * values * values)))
    )


def depthwise(values, kernel):
    grid_side = GRID
    shaped = values.reshape(values.shape[0], grid_side, grid_side, values.shape[-1])
    padded = jnp.pad(shaped, ((0, 0), (1, 1), (1, 1), (0, 0)))
    summed = jnp.zeros_like(shaped)
    for tap_row in range(3):
        for tap_col in range(3):
            summed = (
                summed
                + kernel[tap_row * 3 + tap_col]
                * padded[:, tap_row : tap_row + grid_side, tap_col : tap_col + grid_side]
            )
    return summed.reshape(values.shape)


def mixer_piece(token_rows, offset, stretch, kernel):
    return depthwise(layer_norm(token_rows) * (1.0 + stretch) + offset, kernel)


def entry_piece(hidden, offset, stretch):
    return layer_norm(hidden) * (1.0 + stretch) + offset


def middle_piece(upward, kernel):
    return gelu_tanh(depthwise(upward, kernel))


def attend_forward(queries, key_rows, value_rows):
    seq_len = queries.shape[0]
    block_rows = min(512, seq_len)
    blocks = queries.reshape(seq_len // block_rows, block_rows, queries.shape[1], queries.shape[2])
    scale_factor = HEAD ** (-0.5)

    def one_block(query_block):
        scores = (
            jnp.einsum("qhe,khe->hqk", query_block, key_rows, preferred_element_type=jnp.float32)
            * scale_factor
        )
        row_peak = jnp.max(scores, axis=-1, keepdims=True)
        weights = jnp.exp(scores - row_peak)
        summed = jnp.sum(weights, axis=-1, keepdims=True)
        soft_low = (weights / summed).astype(jnp.bfloat16)
        context = jnp.einsum(
            "hqk,khe->qhe", soft_low, value_rows, preferred_element_type=jnp.float32
        )
        return (context.astype(jnp.bfloat16), (row_peak + jnp.log(summed))[:, :, 0])

    context, logsum = lax.map(one_block, blocks)
    return (context.reshape(seq_len, -1), logsum)


def attend_backward(queries, key_rows, value_rows, logsum, grad_context):
    seq_len = queries.shape[0]
    block_rows = min(512, seq_len)
    block_count = seq_len // block_rows
    query_blocks = queries.reshape(block_count, block_rows, queries.shape[1], queries.shape[2])
    grad_blocks = grad_context.reshape(block_count, block_rows, queries.shape[1], queries.shape[2])
    scale_factor = HEAD ** (-0.5)

    def one_block(running, pieces):
        grad_keys, grad_values = running
        query_block, grad_block, logsum_block = pieces
        scores = (
            jnp.einsum("qhe,khe->hqk", query_block, key_rows, preferred_element_type=jnp.float32)
            * scale_factor
        )
        weights = jnp.exp(scores - logsum_block[:, :, None])
        soft_low = weights.astype(jnp.bfloat16)
        grad_values = grad_values + jnp.einsum(
            "hqk,qhe->khe", soft_low, grad_block, preferred_element_type=jnp.float32
        )
        grad_weights = jnp.einsum(
            "qhe,khe->hqk", grad_block, value_rows, preferred_element_type=jnp.float32
        )
        grad_scores = weights * (
            grad_weights - jnp.sum(weights * grad_weights, axis=-1, keepdims=True)
        )
        grad_low = grad_scores.astype(jnp.bfloat16)
        grad_query = (
            jnp.einsum("hqk,khe->qhe", grad_low, key_rows, preferred_element_type=jnp.float32)
            * scale_factor
        )
        grad_keys = (
            grad_keys
            + jnp.einsum("hqk,qhe->khe", grad_low, query_block, preferred_element_type=jnp.float32)
            * scale_factor
        )
        return ((grad_keys, grad_values), grad_query)

    start_sums = jnp.zeros(key_rows.shape, jnp.float32)
    finals, grad_queries = lax.scan(
        one_block, (start_sums, start_sums), (query_blocks, grad_blocks, logsum)
    )
    grad_queries = grad_queries.reshape(key_rows.shape)
    return jnp.stack([grad_queries, finals[0], finals[1]], axis=1)


def partial_gram(matrix, layout):
    contract = 1 if layout == "columns" else 0
    return lax.dot_general(
        matrix,
        matrix,
        (((contract,), (contract,)), ((), ())),
        precision=lax.Precision.HIGHEST,
        preferred_element_type=jnp.float32,
    )


def apply_gram(gramian, matrix, layout):
    if layout == "columns":
        return jnp.dot(
            gramian, matrix, precision=lax.Precision.HIGHEST, preferred_element_type=jnp.float32
        )
    return jnp.dot(
        matrix, gramian, precision=lax.Precision.HIGHEST, preferred_element_type=jnp.float32
    )


def orthogonalize(matrices, layouts, viewer, combine):
    gramians = combine(
        [partial_gram(viewer(matrix, layout), layout) for matrix, layout in zip(matrices, layouts)]
    )
    current = []
    squared = []
    for position in range(len(matrices)):
        factor = 1.0 / (jnp.sqrt(jnp.trace(gramians[position])) + 1e-07)
        current.append(matrices[position] * factor)
        squared.append(gramians[position] * (factor * factor))
    for iteration in range(NEWTON):
        if iteration > 0:
            stacked = combine(
                [
                    partial_gram(viewer(matrix, layout), layout)
                    for matrix, layout in zip(current, layouts)
                ]
            )
            squared = [stacked[position] for position in range(len(current))]
        updated = []
        for matrix, layout, gramian in zip(current, layouts, squared):
            applied = apply_gram(gramian, matrix, layout)
            twice_applied = apply_gram(gramian, applied, layout)
            updated.append(
                newton_terms[0] * matrix
                + newton_terms[1] * applied
                + newton_terms[2] * twice_applied
            )
        current = updated
    return current


def adam_update(weight, moment, square, gradient):
    moment_new = first_decay * moment + (1.0 - first_decay) * gradient
    square_new = second_decay * square + (1.0 - second_decay) * gradient * gradient
    moment_hat = moment_new / (1.0 - first_decay**STEP)
    square_hat = square_new / (1.0 - second_decay**STEP)
    weight_new = weight * (1.0 - adam_rate * weight_decay) - adam_rate * moment_hat / (
        jnp.sqrt(square_hat) + 1e-08
    )
    return (moment_new, square_new, weight_new)


def muon_finish(weight, polar_part, longest):
    return (
        weight * (1.0 - muon_rate * weight_decay)
        - muon_rate * 0.2 * math.sqrt(longest) * polar_part
    )


def whole_view(matrix, layout):
    return matrix


def local(
    tokens,
    conditions,
    item_live,
    cotangent,
    modulation_table,
    mixer_kernel,
    hidden_kernel,
    attend_weight,
    output_weight,
    expand_weight,
    reduce_weight,
    attend_moment,
    output_moment,
    expand_moment,
    reduce_moment,
    table_first,
    table_second,
    mixer_first,
    mixer_second,
    hidden_first,
    hidden_second,
):
    item_count = tokens.shape[0]
    seq_len = tokens.shape[1]
    local_heads = attend_weight.shape[2] // HEAD
    live_mask = item_live.astype(jnp.float32)[:, None, None]
    token_rows = tokens.astype(jnp.float32)
    modulation = modulation_table[None] + conditions
    shift_one = modulation[:, 0:1]
    scale_one = modulation[:, 1:2]
    gate_one = modulation[:, 2:3]
    shift_two = modulation[:, 3:4]
    scale_two = modulation[:, 4:5]
    gate_two = modulation[:, 5:6]
    mixed_rows, mixer_pull = jax.vjp(mixer_piece, token_rows, shift_one, scale_one, mixer_kernel)
    mixed_low = mixed_rows.astype(jnp.bfloat16)
    attend_low = attend_weight.astype(jnp.bfloat16)
    triple = jnp.einsum(
        "isd,dkc->iskc", mixed_low, attend_low, preferred_element_type=jnp.float32
    ).astype(jnp.bfloat16)
    heads_split = triple.reshape(item_count, seq_len, 3, local_heads, HEAD)

    def attend_item(member):
        return attend_forward(member[:, 0], member[:, 1], member[:, 2])

    context, logsum = lax.map(attend_item, heads_split)
    output_low = output_weight.astype(jnp.bfloat16)
    branch = lax.psum(
        jnp.einsum("isc,cd->isd", context, output_low, preferred_element_type=jnp.float32), "narrow"
    )
    hidden = token_rows + gate_one * branch
    expand_entry, entry_pull = jax.vjp(entry_piece, hidden, shift_two, scale_two)
    entry_low = expand_entry.astype(jnp.bfloat16)
    expand_low = expand_weight.astype(jnp.bfloat16)
    upward = jnp.einsum("isd,df->isf", entry_low, expand_low, preferred_element_type=jnp.float32)
    activated, middle_pull = jax.vjp(middle_piece, upward, hidden_kernel)
    activated_low = activated.astype(jnp.bfloat16)
    reduce_low = reduce_weight.astype(jnp.bfloat16)
    ffn_branch = lax.psum(
        jnp.einsum("isf,fd->isd", activated_low, reduce_low, preferred_element_type=jnp.float32),
        "narrow",
    )
    block_out = (live_mask * (hidden + gate_two * ffn_branch)).astype(jnp.bfloat16)
    grad_result = cotangent.astype(jnp.float32) * live_mask
    grad_gate_two = jnp.sum(ffn_branch * grad_result, axis=1)
    grad_ffn_low = (gate_two * grad_result).astype(jnp.bfloat16)
    grad_reduce = jnp.einsum(
        "isf,isd->fd", activated_low, grad_ffn_low, preferred_element_type=jnp.float32
    )
    grad_activated = jnp.einsum(
        "isd,fd->isf", grad_ffn_low, reduce_low, preferred_element_type=jnp.float32
    )
    grad_upward, grad_hidden_kernel = middle_pull(grad_activated)
    grad_up_low = grad_upward.astype(jnp.bfloat16)
    grad_expand = jnp.einsum(
        "isd,isf->df", entry_low, grad_up_low, preferred_element_type=jnp.float32
    )
    grad_entry = lax.psum(
        jnp.einsum("isf,df->isd", grad_up_low, expand_low, preferred_element_type=jnp.float32),
        "narrow",
    )
    grad_hidden, grad_shift_two, grad_scale_two = entry_pull(grad_entry)
    grad_hidden = grad_hidden + grad_result
    grad_gate_one = jnp.sum(branch * grad_hidden, axis=1)
    grad_branch_low = (gate_one * grad_hidden).astype(jnp.bfloat16)
    grad_output = jnp.einsum(
        "isc,isd->cd", context, grad_branch_low, preferred_element_type=jnp.float32
    )
    grad_context = jnp.einsum(
        "isd,cd->isc", grad_branch_low, output_low, preferred_element_type=jnp.float32
    ).astype(jnp.bfloat16)

    def attend_item_back(pieces):
        member, logsum_item, grad_item = pieces
        return attend_backward(
            member[:, 0],
            member[:, 1],
            member[:, 2],
            logsum_item,
            grad_item.reshape(seq_len, local_heads, HEAD),
        )

    grad_split = lax.map(attend_item_back, (heads_split, logsum, grad_context))
    grad_triple = grad_split.reshape(item_count, seq_len, 3, local_heads * HEAD).astype(
        jnp.bfloat16
    )
    grad_attend = jnp.einsum(
        "isd,iskc->dkc", mixed_low, grad_triple, preferred_element_type=jnp.float32
    )
    grad_mixed = lax.psum(
        jnp.einsum("iskc,dkc->isd", grad_triple, attend_low, preferred_element_type=jnp.float32),
        "narrow",
    )
    grad_tokens, grad_shift_one, grad_scale_one, grad_mixer_kernel = mixer_pull(grad_mixed)
    tokens_gradient = (grad_tokens + grad_hidden).astype(jnp.bfloat16)
    grad_table = jnp.sum(
        jnp.stack(
            [
                grad_shift_one[:, 0],
                grad_scale_one[:, 0],
                grad_gate_one,
                grad_shift_two[:, 0],
                grad_scale_two[:, 0],
                grad_gate_two,
            ],
            axis=1,
        ),
        axis=0,
    )
    summed = lax.psum(
        (
            grad_table,
            grad_mixer_kernel,
            grad_hidden_kernel,
            grad_attend,
            grad_output,
            grad_expand,
            grad_reduce,
        ),
        "wide",
    )
    shared_squares = jnp.sum(summed[0] * summed[0]) + jnp.sum(summed[1] * summed[1])
    split_squares = sum((jnp.sum(gradient * gradient) for gradient in summed[2:]))
    gradient_norm = jnp.sqrt(lax.psum(split_squares, "narrow") + shared_squares)
    clip_factor = jnp.minimum(1.0, 1.0 / (gradient_norm + 1e-06))
    table_moment, table_square, table_result = adam_update(
        modulation_table, table_first, table_second, clip_factor * summed[0]
    )
    mixer_moment, mixer_square, mixer_result = adam_update(
        mixer_kernel, mixer_first, mixer_second, clip_factor * summed[1]
    )
    hidden_moment, hidden_square, hidden_result = adam_update(
        hidden_kernel, hidden_first, hidden_second, clip_factor * summed[2]
    )
    moments = (attend_moment, output_moment, expand_moment, reduce_moment)
    carried = [
        muon_momentum * moment + clip_factor * gradient
        for moment, gradient in zip(moments, summed[3:])
    ]
    matrices = [carried[0].reshape(carried[0].shape[0], -1), carried[1], carried[2], carried[3]]
    layouts = ("columns", "rows", "columns", "rows")
    wide_index = lax.axis_index("wide")
    wide_count = lax.axis_size("wide")

    def wide_view(matrix, layout):
        axis_pos = 1 if layout == "columns" else 0
        piece_size = matrix.shape[axis_pos] // wide_count
        return lax.dynamic_slice_in_dim(matrix, wide_index * piece_size, piece_size, axis_pos)

    def combine(partials):
        shares = lax.psum_scatter(
            jnp.stack(partials), ("wide", "narrow"), scatter_dimension=1, tiled=True
        )
        return lax.all_gather(shares, ("wide", "narrow"), axis=1, tiled=True)

    owned_parts = orthogonalize(
        [wide_view(matrix, layout) for matrix, layout in zip(matrices, layouts)],
        layouts,
        whole_view,
        combine,
    )
    polar_parts = list(
        (
            lax.all_gather(owned_parts[0], "wide", axis=1, tiled=True),
            lax.all_gather(owned_parts[1], "wide", axis=0, tiled=True),
            lax.all_gather(owned_parts[2], "wide", axis=1, tiled=True),
            lax.all_gather(owned_parts[3], "wide", axis=0, tiled=True),
        )
    )
    attend_result = muon_finish(attend_weight, polar_parts[0].reshape(attend_weight.shape), 3 * D)
    output_result = muon_finish(output_weight, polar_parts[1], D)
    expand_result = muon_finish(expand_weight, polar_parts[2], FF)
    reduce_result = muon_finish(reduce_weight, polar_parts[3], FF)
    return (
        block_out,
        tokens_gradient,
        gradient_norm,
        carried[0],
        carried[1],
        carried[2],
        carried[3],
        attend_result,
        output_result,
        expand_result,
        reduce_result,
        table_moment,
        table_square,
        table_result,
        mixer_moment,
        mixer_square,
        mixer_result,
        hidden_moment,
        hidden_square,
        hidden_result,
    )


def solution(mesh):
    placed = (
        P("wide", None, None),
        P("wide", None, None),
        P("wide"),
        P("wide", None, None),
        P(),
        P(),
        P(None, "narrow"),
        P(None, None, "narrow"),
        P("narrow", None),
        P(None, "narrow"),
        P("narrow", None),
        P(None, None, "narrow"),
        P("narrow", None),
        P(None, "narrow"),
        P("narrow", None),
        P(),
        P(),
        P(),
        P(),
        P(None, "narrow"),
        P(None, "narrow"),
    )
    return jax.shard_map(
        local,
        mesh=mesh,
        in_specs=placed,
        out_specs=(
            P("wide", None, None),
            P("wide", None, None),
            P(),
            P(None, None, "narrow"),
            P("narrow", None),
            P(None, "narrow"),
            P("narrow", None),
            P(None, None, "narrow"),
            P("narrow", None),
            P(None, "narrow"),
            P("narrow", None),
            P(),
            P(),
            P(),
            P(),
            P(),
            P(),
            P(None, "narrow"),
            P(None, "narrow"),
            P(None, "narrow"),
        ),
        check_vma=False,
    )
```

profile of v0, /device:TPU:13, one launch (start us, length us, event | category | flops | bytes accessed | tf_op | source)
XLA Modules:
  0.0 3129.1 jit_solution(18133927110120135257)
XLA Ops:
  15.3 18.4 add_convert_fusion.2
  40.5 12.4 while.45
  60.3 85.7 %all-reduce.47.cloned.1.call-done = f32[1,1024,1024]{2,1,0:T(8,128)} async-done(((f32[1,1024,1024]{2,1,0:T(8,128)}), f32[1,1024,1024]{2,1,0:T(8,128)}) %all-reduce.47.cloned.1.call-update) | async-done | bytes 4194320 | tf_op jit(solution)/shard_map/psum | solution.py:262
  157.0 18.9 fusion.59
  175.9 25.3 multiply_reduce_fusion.24
  201.2 13.5 broadcast_multiply_fusion
  214.7 6.5 pad_add_fusion.1
  221.2 10.5 fusion.60
  244.2 77.7 %all-reduce.49.cloned.1.call-done = f32[1,1024,1024]{2,1,0:T(8,128)} async-done(((f32[1,1024,1024]{2,1,0:T(8,128)}), f32[1,1024,1024]{2,1,0:T(8,128)}) %all-reduce.49.cloned.1.call-update) | async-done | bytes 4194320 | tf_op jit(solution)/shard_map/psum | solution.py:292
  338.4 21.3 while.46
  387.4 136.9 %all-reduce.55.cloned.1.call-done = (f32[1,1024,1024]{2,1,0:T(8,128)}, f32[1,1024,1024]{2,1,0:T(8,128)}) async-done(((f32[1,1024,1024]{2,1,0:T(8,128)}, f32[1,1024,1024]{2,1,0:T(8,128)}), (f32[1,1024,1024]{2,1,0:T(8,128)}, f32[1,1024,1024]{2,1,0:T(8,128)})) %all-reduce.55.cloned.1.call-update) | async-done | bytes 8388624 | tf_op jit(solution)/shard_map/psum | solution.py:273
  524.4 15.5 broadcast_multiply_fusion.9
  539.8 7.6 multiply_reduce_fusion.10
  547.4 9.4 pad_add_fusion
  556.8 12.8 fusion.238
  574.1 7.4 multiply_reduce_fusion.11
  588.3 63.4 %all-reduce.51.cloned.1.call-done = (f32[9,1024]{1,0:T(8,128)}, f32[6,1024]{1,0:T(8,128)}, f32[9,1024]{1,0:T(8,128)}) async-done(((f32[9,1024]{1,0:T(8,128)}, f32[6,1024]{1,0:T(8,128)}, f32[9,1024]{1,0:T(8,128)}), (f32[9,1024]{1,0:T(8,128)}, f32[6,1024]{1,0:T(8,128)}, f32[9,1024]{1,0:T(8,128)})) %all-reduce.51.cloned.1.call-update) | async-done | bytes 98320 | tf_op jit(solution)/shard_map/psum | solution.py:344
  656.0 402.3 %all-reduce.53.cloned.1.call-done = (f32[1024,3,256]{2,0,1:T(8,128)}, f32[256,1024]{1,0:T(8,128)}, f32[1024,1024]{1,0:T(8,128)}, f32[1024,1024]{1,0:T(8,128)}) async-done(((f32[1024,3,256]{2,0,1:T(8,128)}, f32[256,1024]{1,0:T(8,128)}, f32[1024,1024]{1,0:T(8,128)}, f32[1024,1024]{1,0:T(8,128)}), (f32[1024,3,256]{2,0,1:T(8,128)}, f32[256,1024]{1,0:T(8,128)}, f32[1024,1024]{1,0:T(8,128)}, ...) | async-done | bytes 12582928 | tf_op jit(solution)/shard_map/psum | solution.py:344
  1070.8 6.3 psum.93
  1085.3 12.3 multiply_add_fusion.3
  1116.2 6.1 pad_maximum_fusion
  1122.4 185.9 %reduce-scatter.6.cloned.1.call-done = f32[4,32,1024]{2,1,0:T(8,128)} async-done(((f32[4,1024,1024]{2,1,0:T(8,128)}), f32[4,32,1024]{2,1,0:T(8,128)}) %reduce-scatter.6.cloned.1.call-update) | async-done | bytes 524304 | tf_op jit(solution)/shard_map/reduce_scatter | solution.py:385
  1308.4 117.0 %all-gather.10.cloned.1.call-done = f32[4,1024,1024]{2,1,0:T(8,128)} async-done(((f32[4,32,1024]{2,1,0:T(8,128)}), f32[4,1024,1024]{2,1,0:T(8,128)}) %all-gather.10.cloned.1.call-update) | async-done | bytes 16777232 | tf_op jit(solution)/shard_map/all_gather | solution.py:388
  1425.4 7.5 select_reduce_fusion.2
  1441.8 6.0 fusion.156
  1488.7 6.1 pad_maximum_fusion.1
  1494.9 183.5 %reduce-scatter.8.cloned.1.call-done = f32[4,32,1024]{2,1,0:T(8,128)} async-done(((f32[4,1024,1024]{2,1,0:T(8,128)}), f32[4,32,1024]{2,1,0:T(8,128)}) %reduce-scatter.8.cloned.1.call-update) | async-done | bytes 524304 | tf_op jit(solution)/shard_map/reduce_scatter | solution.py:385
  1678.5 117.1 %all-gather.12.cloned.1.call-done = f32[4,1024,1024]{2,1,0:T(8,128)} async-done(((f32[4,32,1024]{2,1,0:T(8,128)}), f32[4,1024,1024]{2,1,0:T(8,128)}) %all-gather.12.cloned.1.call-update) | async-done | bytes 16777232 | tf_op jit(solution)/shard_map/all_gather | solution.py:388
  1800.9 6.1 fusion.145
  1842.2 6.1 pad_maximum_fusion.2
  1848.3 183.5 %reduce-scatter.10.cloned.1.call-done = f32[4,32,1024]{2,1,0:T(8,128)} async-done(((f32[4,1024,1024]{2,1,0:T(8,128)}), f32[4,32,1024]{2,1,0:T(8,128)}) %reduce-scatter.10.cloned.1.call-update) | async-done | bytes 524304 | tf_op jit(solution)/shard_map/reduce_scatter | solution.py:385
  2031.9 117.1 %all-gather.14.cloned.1.call-done = f32[4,1024,1024]{2,1,0:T(8,128)} async-done(((f32[4,32,1024]{2,1,0:T(8,128)}), f32[4,1024,1024]{2,1,0:T(8,128)}) %all-gather.14.cloned.1.call-update) | async-done | bytes 16777232 | tf_op jit(solution)/shard_map/all_gather | solution.py:388
  2154.4 6.1 fusion.147
  2195.7 6.1 pad_maximum_fusion.3
  2201.8 183.5 %reduce-scatter.12.cloned.1.call-done = f32[4,32,1024]{2,1,0:T(8,128)} async-done(((f32[4,1024,1024]{2,1,0:T(8,128)}), f32[4,32,1024]{2,1,0:T(8,128)}) %reduce-scatter.12.cloned.1.call-update) | async-done | bytes 524304 | tf_op jit(solution)/shard_map/reduce_scatter | solution.py:385
  2385.4 117.1 %all-gather.16.cloned.1.call-done = f32[4,1024,1024]{2,1,0:T(8,128)} async-done(((f32[4,32,1024]{2,1,0:T(8,128)}), f32[4,1024,1024]{2,1,0:T(8,128)}) %all-gather.16.cloned.1.call-update) | async-done | bytes 16777232 | tf_op jit(solution)/shard_map/all_gather | solution.py:388
  2507.9 6.1 fusion.149
  2549.1 6.1 pad_maximum_fusion.4
  2555.3 183.5 %reduce-scatter.14.cloned.1.call-done = f32[4,32,1024]{2,1,0:T(8,128)} async-done(((f32[4,1024,1024]{2,1,0:T(8,128)}), f32[4,32,1024]{2,1,0:T(8,128)}) %reduce-scatter.14.cloned.1.call-update) | async-done | bytes 524304 | tf_op jit(solution)/shard_map/reduce_scatter | solution.py:385
  2738.8 117.0 %all-gather.18.cloned.1.call-done = f32[4,1024,1024]{2,1,0:T(8,128)} async-done(((f32[4,32,1024]{2,1,0:T(8,128)}), f32[4,1024,1024]{2,1,0:T(8,128)}) %all-gather.18.cloned.1.call-update) | async-done | bytes 16777232 | tf_op jit(solution)/shard_map/all_gather | solution.py:388
  2866.1 6.4 fusion.91
  2872.4 7.2 fusion.169
  2895.4 6.6 fusion.151
  2905.9 58.7 %all-gather.20.cloned.1.call-done = f32[1024,768]{0,1:T(8,128)} async-done(((f32[1024,96]{0,1:T(8,128)}), f32[1024,768]{0,1:T(8,128)}) %all-gather.20.cloned.1.call-update) | async-done | bytes 3145744 | tf_op jit(solution)/shard_map/all_gather | solution.py:398
  2974.1 64.7 %all-gather.26.cloned.1.call-done = f32[1024,1024]{1,0:T(8,128)} async-done(((f32[128,1024]{1,0:T(8,128)}), f32[1024,1024]{1,0:T(8,128)}) %all-gather.26.cloned.1.call-update) | async-done | bytes 4194320 | tf_op jit(solution)/shard_map/all_gather | solution.py:401
  3038.8 7.0 multiply_subtract_fusion
  3045.8 68.5 %all-gather.24.cloned.1.call-done = f32[1024,1024]{1,0:T(8,128)} async-done(((f32[1024,128]{1,0:T(8,128)}), f32[1024,1024]{1,0:T(8,128)}) %all-gather.24.cloned.1.call-update) | async-done | bytes 4194320 | tf_op jit(solution)/shard_map/all_gather | solution.py:400
  3114.2 7.0 multiply_subtract_fusion.1
  (419 shorter events, 379.3 us)
Async XLA Ops:
  7.2 138.8 %all-reduce.47.cloned.1.call-start = ((), (), s32[]{:S(2)}) async-start(), calls=%async_computation.5 | async-start | bytes 8388608 | tf_op jit(solution)/shard_map/psum | solution.py:262
  12.3 21.4 copy-start.61
  12.3 21.3 copy-start.59
  12.4 21.3 copy-start.67
  12.4 137.1 %copy-start.100 = (f32[1,1,1024]{2,1,0:T(1,128)}, f32[1,1,1024]{2,1,0:T(1,128)S(1)}, u32[]{:S(2)}) copy-start(f32[1,1,1024]{2,1,0:T(1,128)S(1)} %get-tuple-element.318) | copy-start | bytes 12292
  12.4 163.5 %copy-start.93 = (f32[1,1,1024]{2,1,0:T(1,128)}, f32[1,1,1024]{2,1,0:T(1,128)S(1)}, u32[]{:S(2)}) copy-start(f32[1,1,1024]{2,1,0:T(1,128)S(1)} %get-tuple-element.317) | copy-start | bytes 12292
  12.4 21.3 copy-start.71
  12.4 21.3 copy-start.73
  12.4 21.3 copy-start.75
  12.5 21.3 copy-start.77
  12.5 21.3 copy-start.79
  12.5 21.3 copy-start.81
  12.5 21.3 copy-start.83
  12.5 21.3 copy-start.85
  12.5 21.3 copy-start.87
  15.3 18.5 copy-start.34
  59.4 262.5 %all-reduce.49.cloned.1.call-start = ((), (), s32[]{:S(2)}) async-start(), calls=%async_computation.6 | async-start | bytes 8388608 | tf_op jit(solution)/shard_map/psum | solution.py:292
  157.0 18.9 copy-start.16
  236.1 288.2 %all-reduce.55.cloned.1.call-start = ((), (), s32[]{:S(2)}) async-start(), calls=%async_computation.23 | async-start | bytes 16777216 | tf_op jit(solution)/shard_map/psum | solution.py:273
  370.9 280.8 %all-reduce.51.cloned.1.call-start = ((), (), s32[]{:S(2)}) async-start(), calls=%async_computation.21 | async-start | bytes 327680 | tf_op jit(solution)/shard_map/psum | solution.py:344
  385.2 139.1 %copy-start.72 = (f32[1,1024]{1,0:T(1,128)S(1)}, f32[1,1024]{1,0:T(1,128)}, u32[]{:S(2)}) copy-start(f32[1,1024]{1,0:T(1,128)} %copy-done.71) | copy-start | bytes 12292
  385.2 139.1 %copy-start.74 = (f32[1,1024]{1,0:T(1,128)S(1)}, f32[1,1024]{1,0:T(1,128)}, u32[]{:S(2)}) copy-start(f32[1,1024]{1,0:T(1,128)} %copy-done.73) | copy-start | bytes 12292
  385.2 139.1 %copy-start.76 = (f32[1,1024]{1,0:T(1,128)S(1)}, f32[1,1024]{1,0:T(1,128)}, u32[]{:S(2)}) copy-start(f32[1,1024]{1,0:T(1,128)} %copy-done.75) | copy-start | bytes 12292
  385.2 139.1 %copy-start.78 = (f32[1,1024]{1,0:T(1,128)S(1)}, f32[1,1024]{1,0:T(1,128)}, u32[]{:S(2)}) copy-start(f32[1,1024]{1,0:T(1,128)} %copy-done.77) | copy-start | bytes 12292
  385.2 139.1 %copy-start.80 = (f32[1,1024]{1,0:T(1,128)S(1)}, f32[1,1024]{1,0:T(1,128)}, u32[]{:S(2)}) copy-start(f32[1,1024]{1,0:T(1,128)} %copy-done.79) | copy-start | bytes 12292
  385.2 139.1 %copy-start.82 = (f32[1,1024]{1,0:T(1,128)S(1)}, f32[1,1024]{1,0:T(1,128)}, u32[]{:S(2)}) copy-start(f32[1,1024]{1,0:T(1,128)} %copy-done.81) | copy-start | bytes 12292
  385.2 139.1 %copy-start.84 = (f32[1,1024]{1,0:T(1,128)S(1)}, f32[1,1024]{1,0:T(1,128)}, u32[]{:S(2)}) copy-start(f32[1,1024]{1,0:T(1,128)} %copy-done.83) | copy-start | bytes 12292
  385.3 139.1 %copy-start.86 = (f32[1,1024]{1,0:T(1,128)S(1)}, f32[1,1024]{1,0:T(1,128)}, u32[]{:S(2)}) copy-start(f32[1,1024]{1,0:T(1,128)} %copy-done.85) | copy-start | bytes 12292
  582.9 475.3 %all-reduce.53.cloned.1.call-start = ((), (), s32[]{:S(2)}) async-start(), calls=%async_computation.22 | async-start | bytes 25165824 | tf_op jit(solution)/shard_map/psum | solution.py:344
  588.2 720.1 %reduce-scatter.6.cloned.1.call-start = ((), (), s32[]{:S(2)}) async-start(), calls=%async_computation.7 | async-start | bytes 17301504 | tf_op jit(solution)/shard_map/reduce_scatter | solution.py:385
  1062.3 15.6 copy-start.38
  1122.3 303.1 %all-gather.10.cloned.1.call-start = ((), (), s32[]{:S(2)}) async-start(), calls=%async_computation.8 | async-start | bytes 17301504 | tf_op jit(solution)/shard_map/all_gather | solution.py:388
  1308.3 370.0 %reduce-scatter.8.cloned.1.call-start = ((), (), s32[]{:S(2)}) async-start(), calls=%async_computation.9 | async-start | bytes 17301504 | tf_op jit(solution)/shard_map/reduce_scatter | solution.py:385
  1435.9 20.4 copy-start
  1494.8 300.7 %all-gather.12.cloned.1.call-start = ((), (), s32[]{:S(2)}) async-start(), calls=%async_computation.10 | async-start | bytes 17301504 | tf_op jit(solution)/shard_map/all_gather | solution.py:388
  1678.4 353.5 %reduce-scatter.10.cloned.1.call-start = ((), (), s32[]{:S(2)}) async-start(), calls=%async_computation.11 | async-start | bytes 17301504 | tf_op jit(solution)/shard_map/reduce_scatter | solution.py:385
  1795.6 19.5 copy-start.10
  1848.3 300.7 %all-gather.14.cloned.1.call-start = ((), (), s32[]{:S(2)}) async-start(), calls=%async_computation.12 | async-start | bytes 17301504 | tf_op jit(solution)/shard_map/all_gather | solution.py:388
  2031.9 353.4 %reduce-scatter.12.cloned.1.call-start = ((), (), s32[]{:S(2)}) async-start(), calls=%async_computation.13 | async-start | bytes 17301504 | tf_op jit(solution)/shard_map/reduce_scatter | solution.py:385
  2149.0 19.5 copy-start.11
  2201.8 300.7 %all-gather.16.cloned.1.call-start = ((), (), s32[]{:S(2)}) async-start(), calls=%async_computation.14 | async-start | bytes 17301504 | tf_op jit(solution)/shard_map/all_gather | solution.py:388
  2385.4 353.4 %reduce-scatter.14.cloned.1.call-start = ((), (), s32[]{:S(2)}) async-start(), calls=%async_computation.15 | async-start | bytes 17301504 | tf_op jit(solution)/shard_map/reduce_scatter | solution.py:385
  2502.5 19.5 copy-start.12
  2555.2 300.6 %all-gather.18.cloned.1.call-start = ((), (), s32[]{:S(2)}) async-start(), calls=%async_computation.16 | async-start | bytes 17301504 | tf_op jit(solution)/shard_map/all_gather | solution.py:388
  2738.8 164.7 %all-gather.22.cloned.1.call-start = ((), (), s32[]{:S(2)}) async-start(), calls=%async_computation.18 | async-start | bytes 1179648 | tf_op jit(solution)/shard_map/all_gather | solution.py:399
  2865.8 98.8 %all-gather.20.cloned.1.call-start = ((), (), s32[]{:S(2)}) async-start(), calls=%async_computation.17 | async-start | bytes 3538944 | tf_op jit(solution)/shard_map/all_gather | solution.py:398
  2879.7 159.1 %all-gather.26.cloned.1.call-start = ((), (), s32[]{:S(2)}) async-start(), calls=%async_computation.20 | async-start | bytes 4718592 | tf_op jit(solution)/shard_map/all_gather | solution.py:401
  2889.8 224.5 %all-gather.24.cloned.1.call-start = ((), (), s32[]{:S(2)}) async-start(), calls=%async_computation.19 | async-start | bytes 4718592 | tf_op jit(solution)/shard_map/all_gather | solution.py:400
  (88 other events, 472.4 us)
Sparse Core Ops, SparseCore 0:
  59.5 86.4 all-reduce.46
  236.2 85.6 all-reduce.48
  370.9 153.3 all-reduce.54
  583.0 68.5 all-reduce.50
  658.1 400.0 all-reduce.52
  1122.5 185.8 reduce-scatter.5
  1311.2 114.1 all-gather.9
  1495.0 183.3 reduce-scatter.7
  1681.3 114.2 all-gather.11
  1848.4 183.4 reduce-scatter.9
  2034.8 114.1 all-gather.13
  2201.9 183.4 reduce-scatter.11
  2388.3 114.1 all-gather.15
  2555.3 183.3 reduce-scatter.13
  2741.5 114.2 all-gather.17
  2866.0 36.3 all-gather.21
  2905.0 59.5 all-gather.19
  2967.2 71.5 all-gather.25
  3041.4 72.7 all-gather.23
where the time goes:
time: 3140 us; the launch traced here: 3130 us
  waiting for transfers between devices  2460 us (78%)
  matrix products  351 us (11%)
  other arithmetic  250 us (8%)
    reduce_scatter x5, waiting for transfers between devices, combine(): lax.psum_scatter(jnp.stack(partials), ('wide', 'narrow'), scatter_dimensi...  920 us
    all_gather x5, waiting for transfers between devices, combine(): return lax.all_gather(shares, ('wide', 'narrow'), axis=1, tiled=True)  585 us
    psum x2, waiting for transfers between devices, local(): lax.psum((grad_table, grad_mixer_kernel, grad_hidden_kernel, grad_attend,...  466 us
    psum x1, waiting for transfers between devices, local(): lax.psum(jnp.einsum('isf,fd->isd', activated_low, reduce_low, preferred_e...  137 us
    dot_general x20, matrix products, apply_gram(): jnp.dot(gramian, matrix, precision=lax.Precision.HIGHEST, preferred_eleme...  108 us
    psum x1, waiting for transfers between devices, local(): lax.psum(jnp.einsum('isc,cd->isd', context, output_low, preferred_element...  85.7 us
    psum x1, waiting for transfers between devices, local(): lax.psum(jnp.einsum('isf,df->isd', grad_up_low, expand_low, preferred_ele...  77.7 us
    dot_general x20, matrix products, partial_gram(): lax.dot_general(matrix, matrix, (((contract,), (contract,)), ((), ())), p...  75.2 us
  transfers between devices with their start and end apart: 19, of which 18 were waited for; matrix products, arithmetic and copies ran while one was open for 3% of the time, Pallas kernels for 0%

commit v1 on v0

--- a/solution.py
+++ b/solution.py
@@ -1,8 +1,11 @@
+import functools
 import math
 
 import jax
 import jax.numpy as jnp
 from jax import lax
+from jax.experimental import pallas as pl
+from jax.experimental.pallas import tpu as pltpu
 from jax.sharding import PartitionSpec as P
 
 D = 1024
@@ -136,57 +139,497 @@
     return jnp.stack([grad_queries, finals[0], finals[1]], axis=1)
 
 
-def partial_gram(matrix, layout):
-    contract = 1 if layout == "columns" else 0
-    return lax.dot_general(
-        matrix,
-        matrix,
-        (((contract,), (contract,)), ((), ())),
-        precision=lax.Precision.HIGHEST,
-        preferred_element_type=jnp.float32,
-    )
-
-
-def apply_gram(gramian, matrix, layout):
-    if layout == "columns":
-        return jnp.dot(
-            gramian, matrix, precision=lax.Precision.HIGHEST, preferred_element_type=jnp.float32
-        )
-    return jnp.dot(
-        matrix, gramian, precision=lax.Precision.HIGHEST, preferred_element_type=jnp.float32
-    )
-
-
-def orthogonalize(matrices, layouts, viewer, combine):
-    gramians = combine(
-        [partial_gram(viewer(matrix, layout), layout) for matrix, layout in zip(matrices, layouts)]
-    )
-    current = []
-    squared = []
-    for position in range(len(matrices)):
-        factor = 1.0 / (jnp.sqrt(jnp.trace(gramians[position])) + 1e-07)
-        current.append(matrices[position] * factor)
-        squared.append(gramians[position] * (factor * factor))
-    for iteration in range(NEWTON):
-        if iteration > 0:
-            stacked = combine(
-                [
-                    partial_gram(viewer(matrix, layout), layout)
-                    for matrix, layout in zip(current, layouts)
-                ]
+MESH = pl.DeviceIdType.MESH
+BLK = 256
+LANES = 128
+MATRICES = 4
+
+
+def partner(index, bit):
+    return index + (1 - 2 * ((index // bit) % 2)) * bit
+
+
+def bits_of(count):
+    found = []
+    bit = 1
+    while bit < count:
+        found.append(bit)
+        bit *= 2
+    return found
+
+
+def place_at(axis, bit):
+    place = {"wide": lax.axis_index("wide"), "narrow": lax.axis_index("narrow")}
+    place[axis] = partner(place[axis], bit)
+    return (place["wide"], place["narrow"])
+
+
+def greet(places):
+    barrier = pltpu.get_barrier_semaphore()
+    for place in places:
+        pl.semaphore_signal(barrier, inc=1, device_id=place, device_id_type=MESH)
+    pl.semaphore_wait(barrier, len(places))
+
+
+def send(src, dst, sends, arrivals, slot, place):
+    copy = pltpu.make_async_remote_copy(
+        src_ref=src,
+        dst_ref=dst,
+        send_sem=sends.at[slot],
+        recv_sem=arrivals.at[slot],
+        device_id=place,
+        device_id_type=MESH,
+    )
+    copy.start()
+    return copy
+
+
+def narrow_sum_kernel(far_bits, pieces, x_ref, o_ref, near, far, held, sends, arrivals, local):
+    rows = x_ref.shape[0] // 2
+    step = rows // pieces
+    core = lax.axis_index("narrow") % 2
+    mine, theirs = core * rows, (1 - core) * rows
+    near_place = place_at("narrow", 1)
+    far_places = [place_at("narrow", bit) for bit in far_bits]
+    greet([near_place] + far_places)
+    block = lambda base, p: pl.ds(pl.multiple_of(base + p * step, 8), step)
+    count = len(far_bits)
+    first = [
+        send(x_ref.at[block(theirs, p)], near.at[p], sends, arrivals, p, near_place)
+        for p in range(pieces)
+    ]
+    loads = [
+        pltpu.make_async_copy(x_ref.at[block(mine, p)], held.at[0, p], local.at[p])
+        for p in range(pieces)
+    ]
+    for load in loads:
+        load.start()
+    crossings = [[None] * pieces for _ in range(count)]
+    last = []
+    for p in range(pieces):
+        loads[p].wait()
+        first[p].wait_recv()
+        held[0, p] = held[0, p] + near[p]
+        crossings[0][p] = send(
+            held.at[0, p], far.at[0, p], sends, arrivals, pieces + p, far_places[0]
+        )
+    for b in range(count):
+        for p in range(pieces):
+            crossings[b][p].wait_recv()
+            held[b + 1, p] = held[b, p] + far[b, p]
+            if b + 1 < count:
+                crossings[b + 1][p] = send(
+                    held.at[b + 1, p],
+                    far.at[b + 1, p],
+                    sends,
+                    arrivals,
+                    (b + 2) * pieces + p,
+                    far_places[b + 1],
+                )
+            else:
+                last.append(
+                    send(
+                        held.at[count, p],
+                        o_ref.at[block(mine, p)],
+                        sends,
+                        arrivals,
+                        (count + 1) * pieces + p,
+                        near_place,
+                    )
+                )
+    keeps = [
+        pltpu.make_async_copy(held.at[count, p], o_ref.at[block(mine, p)], local.at[p])
+        for p in range(pieces)
+    ]
+    for keep in keeps:
+        keep.start()
+    for copy in first:
+        copy.wait_send()
+    for row in crossings:
+        for copy in row:
+            copy.wait_send()
+    for copy in last:
+        copy.wait()
+    for keep in keeps:
+        keep.wait()
+
+
+def narrow_sum(values, number):
+    far_bits = bits_of(lax.axis_size("narrow"))[1:]
+    count = len(far_bits)
+    pieces = 4
+    shape = values.shape
+    flat = values.reshape(-1, shape[-1])
+    step = flat.shape[0] // (2 * pieces)
+    slots = (count + 2) * pieces
+    total = pl.pallas_call(
+        functools.partial(narrow_sum_kernel, far_bits, pieces),
+        out_shape=jax.ShapeDtypeStruct(flat.shape, jnp.float32),
+        in_specs=[pl.BlockSpec(memory_space=pl.ANY)],
+        out_specs=pl.BlockSpec(memory_space=pl.ANY),
+        scratch_shapes=[
+            pltpu.VMEM((pieces, step, flat.shape[1]), jnp.float32),
+            pltpu.VMEM((count, pieces, step, flat.shape[1]), jnp.float32),
+            pltpu.VMEM((count + 1, pieces, step, flat.shape[1]), jnp.float32),
+            pltpu.SemaphoreType.DMA((slots,)),
+            pltpu.SemaphoreType.DMA((slots,)),
+            pltpu.SemaphoreType.DMA((pieces,)),
+        ],
+        compiler_params=pltpu.CompilerParams(
+            collective_id=number, has_side_effects=True, vmem_limit_bytes=32 * 2**20
+        ),
+        cost_estimate=pl.CostEstimate(
+            flops=flat.size, bytes_accessed=flat.size * 32, transcendentals=0
+        ),
+    )(flat)
+    return total.reshape(shape)
+
+
+def narrow_sum_steps(values):
+    shape = values.shape
+    values = values.reshape(-1, shape[-1])
+    rows = values.shape[0] // 2
+    side = lax.axis_index("narrow") % 2
+    give = lax.dynamic_slice_in_dim(values, (1 - side) * rows, rows, 0)
+    keep = lax.dynamic_slice_in_dim(values, side * rows, rows, 0)
+    values = keep + permute(give, "narrow", 1)
+    for bit in bits_of(lax.axis_size("narrow"))[1:]:
+        values = values + permute(values, "narrow", bit)
+    other = permute(values, "narrow", 1)
+    return jnp.where(
+        side == 0,
+        jnp.concatenate([values, other], axis=0),
+        jnp.concatenate([other, values], axis=0),
+    ).reshape(shape)
+
+
+def small_kernel(
+    wide_bits,
+    narrow_bits,
+    shared_rows,
+    split_rows,
+    x_ref,
+    o_ref,
+    norm_ref,
+    slots,
+    sends,
+    arrivals,
+    spare,
+    spare_in,
+):
+    wide_places = [place_at("wide", bit) for bit in wide_bits]
+    narrow_places = [place_at("narrow", bit) for bit in narrow_bits]
+    greet(wide_places + narrow_places)
+    count = len(wide_bits)
+    copies = []
+    slots[0] = x_ref[...]
+    for b in range(count):
+        copy = send(slots.at[b], slots.at[count + 1 + b], sends, arrivals, b, wide_places[b])
+        copies.append(copy)
+        copy.wait_recv()
+        slots[b + 1] = slots[b] + slots[count + 1 + b]
+    total = slots[count]
+    o_ref[...] = total
+    shared_part = total[:shared_rows]
+    split_part = total[shared_rows : shared_rows + split_rows]
+    shared = jnp.sum(shared_part * shared_part)
+    split_sum = jnp.sum(split_part * split_part) + jnp.sum(
+        total[shared_rows + split_rows : shared_rows + split_rows + 1]
+    )
+    spare[0] = jnp.full(spare.shape[1:], split_sum, jnp.float32)
+    for b in range(len(narrow_bits)):
+        copy = send(spare.at[b], spare_in.at[b], sends, arrivals, count + b, narrow_places[b])
+        copies.append(copy)
+        copy.wait_recv()
+        spare[b + 1] = spare[b] + spare_in[b]
+    norm_ref[...] = jnp.sqrt(spare[len(narrow_bits)] + shared)
+    for copy in copies:
+        copy.wait_send()
+
+
+def small_sums(stacked, shared_rows, split_rows, number):
+    wide_bits = bits_of(lax.axis_size("wide"))
+    narrow_bits = bits_of(lax.axis_size("narrow"))
+    vmem = pl.BlockSpec(memory_space=pltpu.VMEM)
+    count = len(wide_bits)
+    total = count + len(narrow_bits)
+    return pl.pallas_call(
+        functools.partial(small_kernel, wide_bits, narrow_bits, shared_rows, split_rows),
+        out_shape=(
+            jax.ShapeDtypeStruct(stacked.shape, jnp.float32),
+            jax.ShapeDtypeStruct((8, LANES), jnp.float32),
+        ),
+        in_specs=[vmem],
+        out_specs=(vmem, vmem),
+        scratch_shapes=[
+            pltpu.VMEM((2 * count + 1,) + stacked.shape, jnp.float32),
+            pltpu.SemaphoreType.DMA((total,)),
+            pltpu.SemaphoreType.DMA((total,)),
+            pltpu.VMEM((len(narrow_bits) + 1, 8, LANES), jnp.float32),
+            pltpu.VMEM((len(narrow_bits), 8, LANES), jnp.float32),
+        ],
+        compiler_params=pltpu.CompilerParams(
+            collective_id=number, has_side_effects=True, vmem_limit_bytes=16 * 2**20
+        ),
+    )(stacked)
+
+
+def permute(values, axis, bit):
+    size = lax.axis_size(axis)
+    return lax.ppermute(values, axis, [(index, index ^ bit) for index in range(size)])
+
+
+def wide_scatter(values):
+    for bit in bits_of(lax.axis_size("wide")):
+        rows = values.shape[0] // 2
+        side = (lax.axis_index("wide") // bit) % 2
+        give = lax.dynamic_slice_in_dim(values, (1 - side) * rows, rows, 0)
+        keep = lax.dynamic_slice_in_dim(values, side * rows, rows, 0)
+        values = keep + permute(give, "wide", bit)
+    return values
+
+
+def wide_gather(values):
+    for bit in reversed(bits_of(lax.axis_size("wide"))):
+        side = (lax.axis_index("wide") // bit) % 2
+        other = permute(values, "wide", bit)
+        values = jnp.where(
+            side == 0,
+            jnp.concatenate([values, other], axis=0),
+            jnp.concatenate([other, values], axis=0),
+        )
+    return values
+
+
+def gram_kernel(narrow_bits, gathers, x_ref, o_ref, halves, inbox, sends, arrivals, local):
+    parts, rows = x_ref.shape[0], x_ref.shape[1]
+    sub = parts // MATRICES
+    w, n = lax.axis_index("wide"), lax.axis_index("narrow")
+    places = {}
+    for axis, bit in [("narrow", bit) for bit in narrow_bits] + gathers:
+        places[(axis, bit)] = place_at(axis, bit)
+    greet(list(places.values()))
+    load = pltpu.make_async_copy(x_ref, halves, local.at[0])
+    load.start()
+    load.wait()
+    base = 0 * n
+    size, at, slot = parts, 0, 0
+    for bit in reversed(narrow_bits):
+        size //= 2
+        side = (n // bit) % 2
+        copy = send(
+            halves.at[pl.ds(base + (1 - side) * size, size)],
+            inbox.at[pl.ds(at, size)],
+            sends,
+            arrivals,
+            slot,
+            places[("narrow", bit)],
+        )
+        base = base + side * size
+        copy.wait()
+        for s in range(size):
+            halves[base + s] = halves[base + s] + inbox[at + s]
+        at += size
+        slot += 1
+
+    def rows_of(item):
+        big, small = w, n % sub
+        for index, (axis, bit) in enumerate(gathers):
+            if (item >> index) % 2:
+                if axis == "wide":
+                    big = partner(big, bit)
+                else:
+                    small = partner(small, bit)
+        return pl.ds(pl.multiple_of((big * sub + small) * rows, 8), rows)
+
+    keep = pltpu.make_async_copy(halves.at[n], o_ref.at[rows_of(0)], local.at[0])
+    keep.start()
+    copies = {}
+    order = sorted(range(2 ** len(gathers)), key=lambda item: (bin(item).count("1"), item))
+    for item in order:
+        if item:
+            copies[item].wait_recv()
+        for index in reversed(range(item.bit_length(), len(gathers))):
+            later = item + 2**index
+            src = o_ref.at[rows_of(item)] if item else halves.at[n]
+            copies[later] = send(
+                src, o_ref.at[rows_of(item)], sends, arrivals, slot + later - 1, places[gathers[index]]
             )
-            squared = [stacked[position] for position in range(len(current))]
-        updated = []
-        for matrix, layout, gramian in zip(current, layouts, squared):
-            applied = apply_gram(gramian, matrix, layout)
-            twice_applied = apply_gram(gramian, applied, layout)
-            updated.append(
-                newton_terms[0] * matrix
-                + newton_terms[1] * applied
-                + newton_terms[2] * twice_applied
+    keep.wait()
+    for copy in copies.values():
+        copy.wait_send()
+
+
+def gram_whole(partial, number):
+    narrow_bits = bits_of(lax.axis_size("narrow"))
+    wide_bits = bits_of(lax.axis_size("wide"))
+    parts, rows, width = partial.shape
+    sub = parts // MATRICES
+    gathers = [("narrow", bit) for bit in bits_of(sub)]
+    gathers += [("wide", bit) for bit in reversed(wide_bits)]
+    slots = len(narrow_bits) + 2 ** len(gathers) - 1
+    return pl.pallas_call(
+        functools.partial(gram_kernel, narrow_bits, gathers),
+        out_shape=jax.ShapeDtypeStruct((width, width), jnp.float32),
+        in_specs=[pl.BlockSpec(memory_space=pl.ANY)],
+        out_specs=pl.BlockSpec(memory_space=pl.ANY),
+        scratch_shapes=[
+            pltpu.VMEM(partial.shape, jnp.float32),
+            pltpu.VMEM(partial.shape, jnp.float32),
+            pltpu.SemaphoreType.DMA((slots,)),
+            pltpu.SemaphoreType.DMA((slots,)),
+            pltpu.SemaphoreType.DMA((1,)),
+        ],
+        compiler_params=pltpu.CompilerParams(
+            collective_id=number, has_side_effects=True, vmem_limit_bytes=16 * 2**20
+        ),
+    )(partial)
+
+
+def split(values):
+    high = values.astype(jnp.bfloat16)
+    return high, (values - high.astype(jnp.float32)).astype(jnp.bfloat16)
+
+
+def product(left_high, left_low, right_high, right_low):
+    dot = functools.partial(jnp.dot, preferred_element_type=jnp.float32)
+    return dot(left_high, right_high) + (dot(left_high, right_low) + dot(left_low, right_high))
+
+
+def polar_kernel(g_ref, q_ref, gh, gl, ph, pw, th, tl):
+    size = g_ref.shape[0]
+    blocks = size // BLK
+    first, second, third = newton_terms
+    rows = lambda block: pl.ds(block * BLK, BLK)
+    square = (BLK, BLK)
+    unit = (
+        lax.broadcasted_iota(jnp.int32, square, 0) == lax.broadcasted_iota(jnp.int32, square, 1)
+    ).astype(jnp.float32)
+    trace = jnp.zeros((), jnp.float32)
+    for i in range(blocks):
+        trace = trace + jnp.sum(g_ref[rows(i), rows(i)] * unit)
+    factor = 1.0 / (jnp.sqrt(trace) + 1e-07)
+    for i in range(blocks):
+        gh[rows(i), :], gl[rows(i), :] = split(g_ref[rows(i), :] * (factor * factor))
+
+    def put(high, low, i, j, values):
+        high[rows(i), rows(j)], low[rows(i), rows(j)] = split(values)
+        if i != j:
+            high[rows(j), rows(i)], low[rows(j), rows(i)] = split(values.T)
+
+    def symmetric(left, right, emit):
+        for i in range(blocks):
+            columns = pl.ds(i * BLK, size - i * BLK)
+            values = product(
+                left[0][rows(i), :], left[1][rows(i), :], right[0][:, columns], right[1][:, columns]
             )
-        current = updated
-    return current
+            for j in range(i, blocks):
+                emit(i, j, values[:, (j - i) * BLK : (j - i + 1) * BLK])
+
+    def emit_terms(i, j, values):
+        gram = gh[rows(i), rows(j)].astype(jnp.float32) + gl[rows(i), rows(j)].astype(jnp.float32)
+        terms = second * gram + third * values
+        if i == j:
+            terms = terms + first * unit
+        put(ph, pw, i, j, terms)
+
+    def emit_total(i, j, values):
+        q_ref[rows(i), rows(j)] = values
+        if i != j:
+            q_ref[rows(j), rows(i)] = values.T
+
+    symmetric((gh, gl), (gh, gl), emit_terms)
+    for i in range(blocks):
+        q_ref[rows(i), :] = (
+            ph[rows(i), :].astype(jnp.float32) + pw[rows(i), :].astype(jnp.float32)
+        ) * factor
+
+    def one_step(step, carry):
+        symmetric((ph, pw), (gh, gl), functools.partial(put, th, tl))
+        symmetric((th, tl), (ph, pw), functools.partial(put, gh, gl))
+        symmetric((gh, gl), (gh, gl), emit_terms)
+        for i in range(blocks):
+            th[rows(i), :], tl[rows(i), :] = split(q_ref[rows(i), :])
+        symmetric((ph, pw), (th, tl), emit_total)
+        return carry
+
+    lax.fori_loop(0, NEWTON - 1, one_step, 0)
+
+
+def polar_factor(gramian):
+    size = gramian.shape[0]
+    vmem = pl.BlockSpec(memory_space=pltpu.VMEM)
+    return pl.pallas_call(
+        polar_kernel,
+        out_shape=jax.ShapeDtypeStruct((size, size), jnp.float32),
+        in_specs=[vmem],
+        out_specs=vmem,
+        scratch_shapes=[pltpu.VMEM((size, size), jnp.bfloat16)] * 6,
+        compiler_params=pltpu.CompilerParams(vmem_limit_bytes=48 * 2**20),
+        cost_estimate=pl.CostEstimate(
+            flops=17 * 6 * size**3, bytes_accessed=8 * size * size, transcendentals=0
+        ),
+    )(gramian)
+
+
+def spread_kernel(sub, pieces, q_ref, o_ref, sends, arrivals, local):
+    size = q_ref.shape[0]
+    half = size // 2
+    step = half // pieces
+    w, n = lax.axis_index("wide"), lax.axis_index("narrow")
+    own = n // sub
+    across = partner(own, 2)
+    near_place, far_place = place_at("narrow", sub), place_at("narrow", 2 * sub)
+    side_place = place_at("wide", 1)
+    greet([near_place, far_place, side_place])
+    top = w % 2
+    rows = lambda side, p: pl.ds(pl.multiple_of(side * half + p * step, 8), step)
+    keep = pltpu.make_async_copy(q_ref, o_ref.at[own], local.at[0])
+    keep.start()
+    copies = []
+
+    def push(src, dst, place):
+        copies.append(send(src, dst, sends, arrivals, len(copies), place))
+        return copies[-1]
+
+    crossing = [
+        push(q_ref.at[rows(top, p)], o_ref.at[own, rows(top, p)], far_place) for p in range(pieces)
+    ]
+    landing = [push(q_ref, o_ref.at[own], near_place)]
+    aside = []
+    for p in range(pieces):
+        crossing[p].wait_recv()
+        spot = o_ref.at[across, rows(top, p)]
+        aside.append(push(spot, spot, side_place))
+        landing.append(push(spot, spot, near_place))
+    for p in range(pieces):
+        aside[p].wait_recv()
+        spot = o_ref.at[across, rows(1 - top, p)]
+        landing.append(push(spot, spot, near_place))
+    keep.wait()
+    for copy in copies:
+        copy.wait_send()
+    for copy in landing:
+        copy.wait_recv()
+
+
+def spread(factor, number):
+    size = factor.shape[0]
+    pieces = 4
+    slots = 1 + 4 * pieces
+    sub = lax.axis_size("narrow") // MATRICES
+    return pl.pallas_call(
+        functools.partial(spread_kernel, sub, pieces),
+        out_shape=jax.ShapeDtypeStruct((MATRICES, size, size), jnp.float32),
+        in_specs=[pl.BlockSpec(memory_space=pl.ANY)],
+        out_specs=pl.BlockSpec(memory_space=pl.ANY),
+        scratch_shapes=[
+            pltpu.SemaphoreType.DMA((slots,)),
+            pltpu.SemaphoreType.DMA((slots,)),
+            pltpu.SemaphoreType.DMA((1,)),
+        ],
+        compiler_params=pltpu.CompilerParams(collective_id=number, has_side_effects=True),
+    )(factor)
 
 
 def adam_update(weight, moment, square, gradient):
@@ -207,8 +650,23 @@
     )
 
 
-def whole_view(matrix, layout):
-    return matrix
+def row_block_gram(matrix, layout, start, count):
+    axis = 0 if layout == "columns" else 1
+    block = lax.dynamic_slice_in_dim(matrix, start, count, axis)
+    return lax.dot_general(
+        block,
+        matrix,
+        (((1 - axis,), (1 - axis,)), ((), ())),
+        precision=lax.Precision.HIGH,
+        preferred_element_type=jnp.float32,
+    )
+
+
+def apply_factor(factor, matrix, layout):
+    left, right = (factor, matrix) if layout == "columns" else (matrix, factor)
+    return jnp.dot(
+        left, right, precision=lax.Precision.HIGH, preferred_element_type=jnp.float32
+    )
 
 
 def local(
@@ -259,8 +717,8 @@
 
     context, logsum = lax.map(attend_item, heads_split)
     output_low = output_weight.astype(jnp.bfloat16)
-    branch = lax.psum(
-        jnp.einsum("isc,cd->isd", context, output_low, preferred_element_type=jnp.float32), "narrow"
+    branch = narrow_sum(
+        jnp.einsum("isc,cd->isd", context, output_low, preferred_element_type=jnp.float32), 1
     )
     hidden = token_rows + gate_one * branch
     expand_entry, entry_pull = jax.vjp(entry_piece, hidden, shift_two, scale_two)
@@ -270,9 +728,8 @@
     activated, middle_pull = jax.vjp(middle_piece, upward, hidden_kernel)
     activated_low = activated.astype(jnp.bfloat16)
     reduce_low = reduce_weight.astype(jnp.bfloat16)
-    ffn_branch = lax.psum(
-        jnp.einsum("isf,fd->isd", activated_low, reduce_low, preferred_element_type=jnp.float32),
-        "narrow",
+    ffn_branch = narrow_sum_steps(
+        jnp.einsum("isf,fd->isd", activated_low, reduce_low, preferred_element_type=jnp.float32)
     )
     block_out = (live_mask * (hidden + gate_two * ffn_branch)).astype(jnp.bfloat16)
     grad_result = cotangent.astype(jnp.float32) * live_mask
@@ -289,9 +746,8 @@
     grad_expand = jnp.einsum(
         "isd,isf->df", entry_low, grad_up_low, preferred_element_type=jnp.float32
     )
-    grad_entry = lax.psum(
-        jnp.einsum("isf,df->isd", grad_up_low, expand_low, preferred_element_type=jnp.float32),
-        "narrow",
+    grad_entry = narrow_sum(
+        jnp.einsum("isf,df->isd", grad_up_low, expand_low, preferred_element_type=jnp.float32), 2
     )
     grad_hidden, grad_shift_two, grad_scale_two = entry_pull(grad_entry)
     grad_hidden = grad_hidden + grad_result
@@ -321,9 +777,8 @@
     grad_attend = jnp.einsum(
         "isd,iskc->dkc", mixed_low, grad_triple, preferred_element_type=jnp.float32
     )
-    grad_mixed = lax.psum(
-        jnp.einsum("iskc,dkc->isd", grad_triple, attend_low, preferred_element_type=jnp.float32),
-        "narrow",
+    grad_mixed = narrow_sum(
+        jnp.einsum("iskc,dkc->isd", grad_triple, attend_low, preferred_element_type=jnp.float32), 3
     )
     grad_tokens, grad_shift_one, grad_scale_one, grad_mixer_kernel = mixer_pull(grad_mixed)
     tokens_gradient = (grad_tokens + grad_hidden).astype(jnp.bfloat16)
@@ -341,66 +796,58 @@
         ),
         axis=0,
     )
-    summed = lax.psum(
-        (
-            grad_table,
-            grad_mixer_kernel,
-            grad_hidden_kernel,
-            grad_attend,
-            grad_output,
-            grad_expand,
-            grad_reduce,
-        ),
-        "wide",
-    )
-    shared_squares = jnp.sum(summed[0] * summed[0]) + jnp.sum(summed[1] * summed[1])
-    split_squares = sum((jnp.sum(gradient * gradient) for gradient in summed[2:]))
-    gradient_norm = jnp.sqrt(lax.psum(split_squares, "narrow") + shared_squares)
+    width = tokens.shape[2]
+    gradients = [grad_attend.reshape(width, -1), grad_output, grad_expand, grad_reduce]
+    shares = [wide_scatter(gradient) for gradient in gradients]
+    squares = sum(
+        jnp.sum((share * share).reshape(-1, width), axis=0) for share in shares
+    )
+    shared_rows = grad_table.shape[0] + grad_mixer_kernel.shape[0]
+    hidden_rows = -(-grad_hidden_kernel.size // width)
+    padding = hidden_rows * width - grad_hidden_kernel.size
+    hidden_flat = jnp.pad(grad_hidden_kernel.reshape(-1), (0, padding))
+    stacked = jnp.concatenate(
+        [grad_table, grad_mixer_kernel, hidden_flat.reshape(hidden_rows, width), squares[None]],
+        axis=0,
+    )
+    stacked = jnp.pad(stacked, ((0, -stacked.shape[0] % 8), (0, 0)))
+    small, norm = small_sums(stacked, shared_rows, hidden_rows, 4)
+    gradient_norm = norm[0, 0]
     clip_factor = jnp.minimum(1.0, 1.0 / (gradient_norm + 1e-06))
+    summed_table = small[: grad_table.shape[0]]
+    summed_mixer = small[grad_table.shape[0] : shared_rows]
+    summed_hidden = small[shared_rows : shared_rows + hidden_rows].reshape(-1)
+    summed_hidden = summed_hidden[: hidden_kernel.size].reshape(hidden_kernel.shape)
     table_moment, table_square, table_result = adam_update(
-        modulation_table, table_first, table_second, clip_factor * summed[0]
+        modulation_table, table_first, table_second, clip_factor * summed_table
     )
     mixer_moment, mixer_square, mixer_result = adam_update(
-        mixer_kernel, mixer_first, mixer_second, clip_factor * summed[1]
+        mixer_kernel, mixer_first, mixer_second, clip_factor * summed_mixer
     )
     hidden_moment, hidden_square, hidden_result = adam_update(
-        hidden_kernel, hidden_first, hidden_second, clip_factor * summed[2]
+        hidden_kernel, hidden_first, hidden_second, clip_factor * summed_hidden
     )
     moments = (attend_moment, output_moment, expand_moment, reduce_moment)
     carried = [
-        muon_momentum * moment + clip_factor * gradient
-        for moment, gradient in zip(moments, summed[3:])
+        muon_momentum * moment + clip_factor * wide_gather(share).reshape(moment.shape)
+        for moment, share in zip(moments, shares)
     ]
-    matrices = [carried[0].reshape(carried[0].shape[0], -1), carried[1], carried[2], carried[3]]
+    matrices = [carried[0].reshape(width, -1), carried[1], carried[2], carried[3]]
     layouts = ("columns", "rows", "columns", "rows")
-    wide_index = lax.axis_index("wide")
-    wide_count = lax.axis_size("wide")
-
-    def wide_view(matrix, layout):
-        axis_pos = 1 if layout == "columns" else 0
-        piece_size = matrix.shape[axis_pos] // wide_count
-        return lax.dynamic_slice_in_dim(matrix, wide_index * piece_size, piece_size, axis_pos)
-
-    def combine(partials):
-        shares = lax.psum_scatter(
-            jnp.stack(partials), ("wide", "narrow"), scatter_dimension=1, tiled=True
-        )
-        return lax.all_gather(shares, ("wide", "narrow"), axis=1, tiled=True)
-
-    owned_parts = orthogonalize(
-        [wide_view(matrix, layout) for matrix, layout in zip(matrices, layouts)],
-        layouts,
-        whole_view,
-        combine,
-    )
-    polar_parts = list(
-        (
-            lax.all_gather(owned_parts[0], "wide", axis=1, tiled=True),
-            lax.all_gather(owned_parts[1], "wide", axis=0, tiled=True),
-            lax.all_gather(owned_parts[2], "wide", axis=1, tiled=True),
-            lax.all_gather(owned_parts[3], "wide", axis=0, tiled=True),
-        )
-    )
+    block_rows = width // lax.axis_size("wide")
+    start = lax.axis_index("wide") * block_rows
+    sub = lax.axis_size("narrow") // MATRICES
+    partial = jnp.stack(
+        [
+            row_block_gram(matrix, layout, start, block_rows)
+            for matrix, layout in zip(matrices, layouts)
+        ]
+    ).reshape(MATRICES * sub, block_rows // sub, width)
+    factors = spread(polar_factor(gram_whole(partial, 5)), 6)
+    polar_parts = [
+        apply_factor(factors[position], matrix, layout)
+        for position, (matrix, layout) in enumerate(zip(matrices, layouts))
+    ]
     attend_result = muon_finish(attend_weight, polar_parts[0].reshape(attend_weight.shape), 3 * D)
     output_result = muon_finish(output_weight, polar_parts[1], D)
     expand_result = muon_finish(expand_weight, polar_parts[2], FF)

time: 3140 us -> 1100 us (0.35)
  waiting for transfers between devices: 2460 us -> 157 us
  Pallas kernels: 0 us -> 480 us
  matrix products: 351 us -> 132 us
  starting transfers between devices: 1.33 us -> 39 us
  other arithmetic: 250 us -> 214 us
    reduce_scatter x5 -> x0, waiting for transfers between devices: 920 us -> none  [combine(): lax.psum_scatter(jnp.stack(partials), ('wide', 'narrow'), scatter_dimensi...]
    all_gather x9 -> x0, waiting for transfers between devices: 777 us -> none  [the longest x5 585 us: combine(): return lax.all_gather(shares, ('wide', 'narrow'), axis=1, tiled=True)]
    psum x5 -> x0, waiting for transfers between devices: 766 us -> none  [the longest x2 466 us: local(): lax.psum((grad_table, grad_mixer_kernel, grad_hidden_kernel, grad_attend,...]
    pallas_call x0 -> x7, Pallas kernels: none -> 480 us  [the longest x3 156 us: narrow_sum(): pl.pallas_call(functools.partial(narrow_sum_kernel, far_bits, pieces), ou...]
    dot_general x60 -> x8, matrix products: 256 us -> 39.3 us  [the longest x4 32 us: apply_factor(): jnp.dot(left, right, precision=lax.Precision.HIGH, preferred_element_type...]
    ppermute x0 -> x27, waiting for transfers between devices: none -> 157 us  [permute(): lax.ppermute(values, axis, [(index, index ^ bit) for index in range(size)])]
    ppermute x0 -> x27, starting transfers between devices: none -> 39 us  [permute(): lax.ppermute(values, axis, [(index, index ^ bit) for index in range(size)])]
  transfers between devices with their start and end apart: 19 -> 27, of which waited for: 18 -> 10; matrix products, arithmetic and copies ran while one was open for 3% -> 24% of each run, Pallas kernels for 0% -> 12%
where the time goes in v1:
time: 1100 us; the launch traced here: 1080 us
  Pallas kernels  480 us (44%)
  other arithmetic  214 us (19%)
  waiting for transfers between devices  157 us (14%)
  matrix products  132 us (12%)
  local copies, waits for them, and re-layouts  57.6 us (5%)
  starting transfers between devices  39 us (4%)
    ppermute x27, waiting for transfers between devices, permute(): lax.ppermute(values, axis, [(index, index ^ bit) for index in range(size)])  157 us
    pallas_call x3, Pallas kernels, narrow_sum(): pl.pallas_call(functools.partial(narrow_sum_kernel, far_bits, pieces), ou...  156 us
    pallas_call x1, Pallas kernels, spread(): pl.pallas_call(functools.partial(spread_kernel, sub, pieces), out_shape=j...  130 us
    pallas_call x1, Pallas kernels, gram_whole(): pl.pallas_call(functools.partial(gram_kernel, narrow_bits, gathers), out_...  91.7 us
    pallas_call x1, Pallas kernels, polar_factor(): pl.pallas_call(polar_kernel, out_shape=jax.ShapeDtypeStruct((size, size),...  75.9 us
    ppermute x27, starting transfers between devices, permute(): lax.ppermute(values, axis, [(index, index ^ bit) for index in range(size)])  39 us
    dot_general x4, matrix products, apply_factor(): jnp.dot(left, right, precision=lax.Precision.HIGH, preferred_element_type...  32 us
    unnamed x226, local copies, waits for them, and re-layouts  28.5 us
  transfers between devices with their start and end apart: 27, of which 10 were waited for; matrix products, arithmetic and copies ran while one was open for 24% of the time, Pallas kernels for 12%

profile of v1, /device:TPU:13, one launch (start us, length us, event | category | flops | bytes accessed | tf_op | source)
XLA Modules:
  0.0 1085.0 jit_solution(17076174167209466573)
XLA Ops:
  9.4 18.3 %add_convert_fusion.2 = bf16[1,32,32,1024]{3,2,1,0:T(8,128)(2,1)} fusion(f32[1,32,32,1024]{3,2,1,0:T(8,128)} %bitcast.319, f32[1024]{0:T(1024)S(1)} %bitcast.389, f32[1024]{0:T(1024)S(1)} %bitcast.375, f32[1024]{0:T(1024)S(1)} %bitcast.377, f32[1024]{0:T(1024)S(1)} %bitcast.379, f32[1024]{0:T(1024)S(1)} %bitcast.381, f32[1024]{0:T(1024)S(1)} %bitcast.383, ...), kind=kLoop, calls=%fused_computation.168 | loop fusion | flops 18874368 | bytes 6328320 | tf_op jit(solution)/shard_map/convert_element_type | solution.py:708
  34.7 12.4 %while.45 = (s32[]{:T(128)}, bf16[2,512,4,64]{1,3,2,0:T(8,128)(2,1)}, f32[2,4,512]{2,1,0:T(4,128)S(1)}, bf16[2,512,4,64]{1,3,2,0:T(8,128)(2,1)S(1)}, bf16[1024,4...) while((s32[]{:T(128)}, bf16[2,512,4,64]{1,3,2,0:T(8,128)(2,1)}, ...), condition=%wide.region_5.6_spmd, body=%wide.region_2.5_spmd.sunk | while | flops 555874304 | bytes 33095860 | solution.py:92
  51.5 52.2 %shard_map.356 = f32[1024,1024]{1,0:T(8,128)S(1)} custom-call(f32[1024,1024]{1,0:T(8,128)S(1)} %fusion.127.x_ref), custom_call_target="tpu_custom_call" | custom-call | flops 1048576 | bytes 33554432 | tf_op jit(solution)/shard_map/pallas_call | solution.py:265
  108.3 7.9 fusion.115
  116.2 18.9 %fusion.59 = (bf16[1,32,32,1024]{3,2,1,0:T(8,128)(2,1)}, f32[1,32,32,1024]{3,2,1,0:T(8,128)}) fusion(f32[1024]{0:T(1024)S(1)} %bitcast.369, f32[1024]{0:T(1024)S(1)} %bitcast.355, f32[1024]{0:T(1024)S(1)} %bitcast.357, f32[1024]{0:T(1024)S(1)} %bitcast.359, f32[1,32,32,1024]{3,2,1,0:T(8,128)} %bitcast.321, f32[1024]{0:T(1024)S(1)} %bitcast.361, ...), kind=kLoop, calls=%fused_computation.92 | loop fusion | flops 27262976 | bytes 10522624 | tf_op jit(solution)/shard_map/convert_element_type | solution.py:729
  135.1 4.0 fusion.96
  142.9 25.6 %multiply_reduce_fusion.10 = (f32[1024]{0:T(1024)}, f32[1024]{0:T(1024)}, f32[1024]{0:T(1024)}, f32[1024]{0:T(1024)}, f32[1024]{0:T(1024)}, /*index=5*/f32[1024]...) fusion(f32[1,32,32,1024]{3,2,1,0:T(8,128)} %bitcast.322, f32[1024,1024]{1,0:T(8,128)} %param.35, ...), kind=kOutput, calls=%fused_computation.148 | convolution fusion | flops 2193612800 | bytes 18911236 | tf_op jit(solution)/shard_map/isd,fd->isf/dot_general | solution.py:741
  168.5 13.3 %broadcast_multiply_fusion = (f32[1,32,32,1024]{3,2,1,0:T(8,128)}, f32[1,32,32,1024]{3,2,1,0:T(8,128)S(1)}, f32[1,32,32,1024]{3,2,1,0:T(8,128)}, f32[1,32,32,102...) fusion(f32[1,32,32,1024]{3,2,1,0:T(8,128)} %bitcast.323, ...), kind=kLoop, calls=%fused_computation.184 | loop fusion | flops 9437184 | bytes 41979904 | tf_op jit(solution)/shard_map/transpose(jvp())/mul | solution.py:54
  181.8 6.5 pad_add_fusion.1
  188.3 10.5 fusion.60
  207.3 4.3 fusion.111
  219.2 30.9 %collective-permute-done.9 = f32[512,1024]{1,0:T(8,128)S(1)} collective-permute-done((f32[512,1024]{1,0:T(8,128)}, f32[512,1024]{1,0:T(8,128)S(1)}, u32[]{:S(2)}, u32[]{:S(2)}) %collective-permute-start.9) | collective-permute-done | bytes 2097184 | tf_op jit(solution)/shard_map/ppermute | solution.py:379
  259.6 25.4 %collective-permute-done.10 = f32[256,1024]{1,0:T(8,128)} collective-permute-done((f32[256,1024]{1,0:T(8,128)}, f32[256,1024]{1,0:T(8,128)}, u32[]{:S(2)}, u32[]{:S(2)}) %collective-permute-start.10) | collective-permute-done | bytes 1048608 | tf_op jit(solution)/shard_map/ppermute | solution.py:379
  288.2 3.9 collective-permute-start.11
  294.8 30.7 %collective-permute-done.11 = f32[128,1024]{1,0:T(8,128)} collective-permute-done((f32[128,1024]{1,0:T(8,128)}, f32[128,1024]{1,0:T(8,128)}, u32[]{:S(2)}, u32[]{:S(2)}) %collective-permute-start.11) | collective-permute-done | bytes 524320 | tf_op jit(solution)/shard_map/ppermute | solution.py:379
  335.5 4.4 fusion.113.x_ref
  342.0 51.5 %shard_map.357 = f32[1024,1024]{1,0:T(8,128)S(1)} custom-call(f32[1024,1024]{1,0:T(8,128)S(1)} %copy-done.7), custom_call_target="tpu_custom_call" | custom-call | flops 1048576 | bytes 33554432 | tf_op jit(solution)/shard_map/pallas_call | solution.py:265
  393.6 4.2 maximum_select_fusion.10
  404.4 3.5 copy.68
  411.0 4.6 multiply_reduce_fusion.6
  415.6 7.2 collective-permute-done.25
  422.7 4.1 maximum_select_fusion.5
  428.1 17.1 %collective-permute-done.22 = f32[256,1024]{1,0:T(8,128)} collective-permute-done((f32[256,1024]{1,0:T(8,128)}, f32[256,1024]{1,0:T(8,128)}, u32[]{:S(2)}, u32[]{:S(2)}) %collective-permute-start.22) | collective-permute-done | bytes 1048608 | tf_op jit(solution)/shard_map/ppermute | solution.py:379
  445.2 4.1 maximum_select_fusion.4
  450.6 5.5 fusion.149
  465.2 21.7 %while.46 = (s32[]{:T(128)}, f32[1024,4,64]{0,2,1:T(8,128)S(1)}, f32[1024,4,64]{0,2,1:T(8,128)S(1)}, bf16[2,512,4,64]{1,3,2,0:T(8,128)(2,1)}, bf16[2,512,4,64]{1...) while((s32[]{:T(128)}, f32[1024,4,64]{0,2,1:T(8,128)S(1)}, ...), condition=%wide.region_12.13_spmd.clone, body=%wide.region_10.12_spmd.clone.sunk | while | flops 1368782848 | bytes 78700808 | solution.py:135
  494.7 6.3 convolution_bitcast_fusion.x_ref
  503.1 4.0 fusion.154
  510.6 52.8 %shard_map.358 = f32[1024,1024]{1,0:T(8,128)S(1)} custom-call(f32[1024,1024]{1,0:T(8,128)S(1)} %copy-done.6), custom_call_target="tpu_custom_call" | custom-call | flops 1048576 | bytes 33554432 | tf_op jit(solution)/shard_map/pallas_call | solution.py:265
  563.5 12.7 %broadcast_multiply_fusion.9 = (f32[1,32,32,1024]{3,2,1,0:T(8,128)}, f32[1,32,32,1024]{3,2,1,0:T(8,128)}, f32[1,32,32,1024]{3,2,1,0:T(8,128)}, f32[1,32,32,1024]...) fusion(f32[1,32,32,1024]{3,2,1,0:T(8,128)S(1)} %bitcast.317, ...), kind=kLoop, calls=%fused_computation.193 | loop fusion | flops 9437184 | bytes 41979904 | tf_op jit(solution)/shard_map/transpose(jvp())/mul | solution.py:54
  576.2 6.5 pad_add_fusion
  582.7 11.3 %fusion.147 = (f32[1024]{0:T(1024)S(1)}, f32[1,32,32,1024]{3,2,1,0:T(8,128)S(1)}) fusion(f32[1,32,32,1024]{3,2,1,0:T(8,128)} %get-tuple-element.295, f32[1,32,32,1024]{3,2,1,0:T(8,128)} %get-tuple-element.296, f32[1,32,32,1024]{3,2,1,0:T(8,128)} %get-tuple-element.297, f32[1,32,32,1024]{3,2,1,0:T(8,128)} %get-tuple-element.298, ...), kind=kLoop, calls=%fused_computation.312 | loop fusion | flops 7339008 | bytes 33558528 | tf_op jit(solution)/shard_map/transpose(jvp())/reduce_sum | solution.py:61
  598.9 7.5 multiply_reduce_fusion.19
  611.9 16.3 %multiply_reduce_fusion.18 = (f32[1024]{0:T(1024)S(1)}, f32[1024]{0:T(1024)S(1)}, f32[1024]{0:T(1024)S(1)}, f32[1024]{0:T(1024)}, f32[1024]{0:T(1024)}, /*index=5*/f32[1024]{0:T(1024)}, f32[1024]{0:T(1024)}, f32[1024]{0:T(1024)}) fusion(f32[1,32,32,1024]{3,2,1,0:T(8,128)} %bitcast.320, f32[1024,1024]{1,0:T(8,128)S(1)} %shard_map.358), kind=kLoop, calls=%fused_computation.156 | loop fusion | flops 16769024 | bytes 8421376 | tf_op jit(solution)/shard_map/transpose(jvp())/reduce_sum | solution.py:54
  636.5 9.4 collective-permute-start.19
  646.2 6.5 collective-permute-done.5
  659.8 25.9 %shard_map.359 = (f32[32,1024]{1,0:T(8,128)S(1)}, f32[8,128]{1,0:T(8,128)S(1)}) custom-call(f32[32,1024]{1,0:T(8,128)S(1)} %select_maximum_fusion.x_ref), custom_call_target="tpu_custom_call" | custom-call | tf_op jit(solution)/shard_map/pallas_call | solution.py:356
  691.1 4.6 fusion.62
  695.7 10.3 collective-permute-done.16
  710.2 5.0 fusion.64
  717.4 23.8 %collective-permute-done.17 = f32[512,768]{0,1:T(8,128)S(1)} collective-permute-done((f32[512,768]{0,1:T(8,128)S(1)}, f32[512,768]{0,1:T(8,128)S(1)}, u32[]{:S(2)}, u32[]{:S(2)}) %collective-permute-start.17) | collective-permute-done | bytes 1572896 | tf_op jit(solution)/shard_map/ppermute | solution.py:379
  744.0 3.5 copy.69
  750.7 91.7 %shard_map.360.g_ref = f32[1024,1024]{1,0:T(8,128)S(1)} custom-call(f32[4,128,1024]{2,1,0:T(8,128)S(1)} %pad_maximum_fusion.x_ref), custom_call_target="tpu_custom_call" | custom-call | tf_op jit(solution)/shard_map/pallas_call | solution.py:471
  844.5 75.9 %shard_map.361.q_ref = f32[1024,1024]{1,0:T(8,128)S(1)} custom-call(f32[1024,1024]{1,0:T(8,128)} %copy-done.5), custom_call_target="tpu_custom_call" | custom-call | flops 109521666048 | bytes 8388608 | tf_op jit(solution)/shard_map/pallas_call | solution.py:562
  922.4 130.2 %shard_map.362 = f32[4,1024,1024]{2,1,0:T(8,128)} custom-call(f32[1024,1024]{1,0:T(8,128)} %copy-done.4), custom_call_target="tpu_custom_call" | custom-call | tf_op jit(solution)/shard_map/pallas_call | solution.py:621
  1052.6 9.8 multiply_subtract_fusion.2
  1065.7 10.2 multiply_subtract_fusion
  1076.0 8.6 multiply_subtract_fusion.1
  (416 shorter events, 188.3 us)
Async XLA Ops:
  142.7 72.6 %collective-permute-start.12 = (f32[512,1024]{1,0:T(8,128)}, f32[512,1024]{1,0:T(8,128)}, u32[]{:S(2)}, u32[]{:S(2)}) collective-permute-start(f32[512,1024]{1,0:T(8,128)} %constant_dynamic-slice_fusion.2), channel_id=1, source_target_pairs={{0,4},{4,0},{8,12},{12,8},{16,20},{20,16},{24,28},{28,24},{1,5},{5... | collective-permute-start | bytes 6291464 | tf_op jit(solution)/shard_map/ppermute | solution.py:379
  203.1 47.0 %collective-permute-start.9 = (f32[512,1024]{1,0:T(8,128)}, f32[512,1024]{1,0:T(8,128)S(1)}, u32[]{:S(2)}, u32[]{:S(2)}) collective-permute-start(f32[512,1024]{1,0:T(8,128)} %constant_dynamic-slice_fusion.5), channel_id=1, source_target_pairs={{0,4},{4,0},{8,12},{12,8},{16,20},{20,16},{24,28},{28,24},{1,5},{5... | collective-permute-start | bytes 6291464 | tf_op jit(solution)/shard_map/ppermute | solution.py:379
  214.9 37.1 %collective-permute-start = (f32[512,1024]{1,0:T(8,128)}, f32[512,1024]{1,0:T(8,128)}, u32[]{:S(2)}, u32[]{:S(2)}) collective-permute-start(f32[512,1024]{1,0:T(8,128)} %constant_dynamic-slice_fusion.12), channel_id=1, source_target_pairs={{0,1},{1,0},{2,3},{3,2},{4,5},{5,4},{6,7},{7,6},{8,9},{9,8},{10,11... | collective-permute-start | bytes 6291464 | tf_op jit(solution)/shard_map/ppermute | solution.py:379
  215.3 34.8 %copy-start.44 = (f32[1024,1024]{1,0:T(8,128)S(1)}, f32[1024,1024]{1,0:T(8,128)}, u32[]{:S(2)}) copy-start(f32[1024,1024]{1,0:T(8,128)} %copy-done.43) | copy-start | bytes 12582916
  218.1 32.5 %copy-start.32 = (f32[512,1024]{1,0:T(8,128)}, f32[512,1024]{1,0:T(8,128)S(1)}, u32[]{:S(2)}) copy-start(f32[512,1024]{1,0:T(8,128)S(1)} %dynamic-slice_add_fusion) | copy-start | bytes 6291460
  219.2 32.8 %copy-start.42 = (f32[1024,1024]{1,0:T(8,128)S(1)}, f32[1024,1024]{1,0:T(8,128)}, u32[]{:S(2)}) copy-start(f32[1024,1024]{1,0:T(8,128)} %fusion.111) | copy-start | bytes 12582916
  219.2 35.5 %collective-permute-start.13 = (f32[256,1024]{1,0:T(8,128)}, f32[256,1024]{1,0:T(8,128)}, u32[]{:S(2)}, u32[]{:S(2)}) collective-permute-start(f32[256,1024]{1,0:T(8,128)} %constant_dynamic-slice_fusion.1), channel_id=1, source_target_pairs={{0,8},{4,12},{8,0},{12,4},{16,24},{20,28},{24,16},{28,20},{1,9},{5... | collective-permute-start | bytes 3145736 | tf_op jit(solution)/shard_map/ppermute | solution.py:379
  251.7 33.3 %collective-permute-start.10 = (f32[256,1024]{1,0:T(8,128)}, f32[256,1024]{1,0:T(8,128)}, u32[]{:S(2)}, u32[]{:S(2)}) collective-permute-start(f32[256,1024]{1,0:T(8,128)} %constant_dynamic-slice_fusion.4), channel_id=1, source_target_pairs={{0,8},{4,12},{8,0},{12,4},{16,24},{20,28},{24,16},{28,20},{1,9},{5... | collective-permute-start | bytes 3145736 | tf_op jit(solution)/shard_map/ppermute | solution.py:379
  254.0 77.3 %collective-permute-start.1 = (f32[512,1024]{1,0:T(8,128)S(1)}, f32[512,1024]{1,0:T(8,128)}, u32[]{:S(2)}, u32[]{:S(2)}) collective-permute-start(f32[512,1024]{1,0:T(8,128)S(1)} %dynamic-slice_add_fusion.2), channel_id=1, source_target_pairs={{0,2},{1,3},{2,0},{3,1},{4,6},{5,7},{6,4},{7,5},{8,10},{9,11},{10,... | collective-permute-start | bytes 6291464 | tf_op jit(solution)/shard_map/ppermute | solution.py:379
  254.7 30.3 %copy-start.34 = (f32[512,1024]{1,0:T(8,128)S(1)}, f32[512,1024]{1,0:T(8,128)}, u32[]{:S(2)}) copy-start(f32[512,1024]{1,0:T(8,128)} %copy-done.33) | copy-start | bytes 6291460
  257.4 34.7 %collective-permute-start.14 = (f32[128,1024]{1,0:T(8,128)}, f32[128,1024]{1,0:T(8,128)}, u32[]{:S(2)}, u32[]{:S(2)}) collective-permute-start(f32[128,1024]{1,0:T(8,128)} %constant_dynamic-slice_fusion), channel_id=1, source_target_pairs={{0,16},{4,20},{8,24},{12,28},{16,0},{20,4},{24,8},{28,12},{1,17},{... | collective-permute-start | bytes 1572872 | tf_op jit(solution)/shard_map/ppermute | solution.py:379
  288.2 37.3 %collective-permute-start.11 = (f32[128,1024]{1,0:T(8,128)}, f32[128,1024]{1,0:T(8,128)}, u32[]{:S(2)}, u32[]{:S(2)}) collective-permute-start(f32[128,1024]{1,0:T(8,128)} %constant_dynamic-slice_fusion.3), channel_id=1, source_target_pairs={{0,16},{4,20},{8,24},{12,28},{16,0},{20,4},{24,8},{28,12},{1,17},{... | collective-permute-start | bytes 1572872 | tf_op jit(solution)/shard_map/ppermute | solution.py:379
  294.8 40.7 %copy-start.49 = (f32[1024,1024]{1,0:T(8,128)S(1)}, f32[1024,1024]{1,0:T(8,128)}, u32[]{:S(2)}) copy-start(f32[1024,1024]{1,0:T(8,128)} %param.34) | copy-start | bytes 12582916
  294.8 40.7 %copy-start.56 = (bf16[1,32,32,1024]{3,2,1,0:T(8,128)(2,1)S(1)}, bf16[1,32,32,1024]{3,2,1,0:T(8,128)(2,1)}, u32[]{:S(2)}) copy-start(bf16[1,32,32,1024]{3,2,1,0:T(8,128)(2,1)} %copy-done.55) | copy-start | bytes 6291460
  294.8 98.8 %collective-permute-start.24 = (f32[128,1024]{1,0:T(8,128)}, f32[128,1024]{1,0:T(8,128)}, u32[]{:S(2)}, u32[]{:S(2)}) collective-permute-start(f32[128,1024]{1,0:T(8,128)} %get-tuple-element.282), channel_id=1, source_target_pairs={{0,16},{4,20},{8,24},{12,28},{16,0},{20,4},{24,8},{28,12},{1,17},{... | collective-permute-start | bytes 1572872 | tf_op jit(solution)/shard_map/ppermute | solution.py:379
  328.2 69.6 %collective-permute-start.21 = (f32[128,1024]{1,0:T(8,128)}, f32[128,1024]{1,0:T(8,128)}, u32[]{:S(2)}, u32[]{:S(2)}) collective-permute-start(f32[128,1024]{1,0:T(8,128)} %get-tuple-element.280), channel_id=1, source_target_pairs={{0,16},{4,20},{8,24},{12,28},{16,0},{20,4},{24,8},{28,12},{1,17},{... | collective-permute-start | bytes 1572872 | tf_op jit(solution)/shard_map/ppermute | solution.py:379
  334.6 115.9 %collective-permute-start.2 = (f32[512,1024]{1,0:T(8,128)}, f32[512,1024]{1,0:T(8,128)}, u32[]{:S(2)}, u32[]{:S(2)}) collective-permute-start(f32[512,1024]{1,0:T(8,128)} %add.494), channel_id=1, source_target_pairs={{0,1},{1,0},{2,3},{3,2},{4,5},{5,4},{6,7},{7,6},{8,9},{9,8},{10,11... | collective-permute-start | bytes 6291464 | tf_op jit(solution)/shard_map/ppermute | solution.py:379
  397.8 24.9 %collective-permute-start.25 = (f32[256,1024]{1,0:T(8,128)}, f32[256,1024]{1,0:T(8,128)}, u32[]{:S(2)}, u32[]{:S(2)}) collective-permute-start(f32[256,1024]{1,0:T(8,128)} %maximum_select_fusion.10), channel_id=1, source_target_pairs={{0,8},{4,12},{8,0},{12,4},{16,24},{20,28},{24,16},{28,20},{1,9},{5... | collective-permute-start | bytes 3145736 | tf_op jit(solution)/shard_map/ppermute | solution.py:379
  400.5 44.7 %collective-permute-start.22 = (f32[256,1024]{1,0:T(8,128)}, f32[256,1024]{1,0:T(8,128)}, u32[]{:S(2)}, u32[]{:S(2)}) collective-permute-start(f32[256,1024]{1,0:T(8,128)} %maximum_select_fusion.9), channel_id=1, source_target_pairs={{0,8},{4,12},{8,0},{12,4},{16,24},{20,28},{24,16},{28,20},{1,9},{5... | collective-permute-start | bytes 3145736 | tf_op jit(solution)/shard_map/ppermute | solution.py:379
  415.5 35.0 %copy-start.1 = (f32[1024,1024]{1,0:T(8,128)S(1)}, f32[1024,1024]{1,0:T(8,128)}, u32[]{:S(2)}) copy-start(f32[1024,1024]{1,0:T(8,128)} %copy-done) | copy-start | bytes 12582916
  415.6 35.0 %copy-start.16 = (f32[1,1024,1024]{2,1,0:T(8,128)S(1)}, f32[1,1024,1024]{2,1,0:T(8,128)}, u32[]{:S(2)}) copy-start(f32[1,1024,1024]{2,1,0:T(8,128)} %copy-done.13) | copy-start | bytes 12582916
  426.8 283.4 %collective-permute-start.26 = (f32[512,1024]{1,0:T(8,128)}, f32[512,1024]{1,0:T(8,128)}, u32[]{:S(2)}, u32[]{:S(2)}) collective-permute-start(f32[512,1024]{1,0:T(8,128)} %maximum_select_fusion.5), channel_id=1, source_target_pairs={{0,4},{4,0},{8,12},{12,8},{16,20},{20,16},{24,28},{28,24},{1,5},{5... | collective-permute-start | bytes 6291464 | tf_op jit(solution)/shard_map/ppermute | solution.py:379
  449.3 241.8 %collective-permute-start.23 = (f32[512,1024]{1,0:T(8,128)}, f32[512,1024]{1,0:T(8,128)}, u32[]{:S(2)}, u32[]{:S(2)}) collective-permute-start(f32[512,1024]{1,0:T(8,128)} %maximum_select_fusion.4), channel_id=1, source_target_pairs={{0,4},{4,0},{8,12},{12,8},{16,20},{20,16},{24,28},{28,24},{1,5},{5... | collective-permute-start | bytes 6291464 | tf_op jit(solution)/shard_map/ppermute | solution.py:379
  501.0 96.6 %collective-permute-start.6 = (f32[128,1024]{1,0:T(8,128)S(1)}, f32[128,1024]{1,0:T(8,128)}, u32[]{:S(2)}, u32[]{:S(2)}) collective-permute-start(f32[128,1024]{1,0:T(8,128)S(1)} %constant_dynamic-slice_fusion.8), channel_id=1, source_target_pairs={{0,4},{4,0},{8,12},{12,8},{16,20},{20,16},{24,28},{28,24},{1,5},{5... | collective-permute-start | bytes 1572872 | tf_op jit(solution)/shard_map/ppermute | solution.py:379
  509.3 54.1 %copy-start.82 = (f32[1,1024]{1,0:T(1,128)S(1)}, f32[1,1024]{1,0:T(1,128)}, u32[]{:S(2)}) copy-start(f32[1,1024]{1,0:T(1,128)} %copy-done.81) | copy-start | bytes 12292
  509.3 54.1 %copy-start.84 = (f32[1,1024]{1,0:T(1,128)S(1)}, f32[1,1024]{1,0:T(1,128)}, u32[]{:S(2)}) copy-start(f32[1,1024]{1,0:T(1,128)} %copy-done.83) | copy-start | bytes 12292
  509.3 54.1 %copy-start.86 = (f32[1,1024]{1,0:T(1,128)S(1)}, f32[1,1024]{1,0:T(1,128)}, u32[]{:S(2)}) copy-start(f32[1,1024]{1,0:T(1,128)} %copy-done.85) | copy-start | bytes 12292
  509.3 54.2 %copy-start.88 = (f32[1,1024]{1,0:T(1,128)S(1)}, f32[1,1024]{1,0:T(1,128)}, u32[]{:S(2)}) copy-start(f32[1,1024]{1,0:T(1,128)} %copy-done.87) | copy-start | bytes 12292
  509.3 54.2 %copy-start.90 = (f32[1,1024]{1,0:T(1,128)S(1)}, f32[1,1024]{1,0:T(1,128)}, u32[]{:S(2)}) copy-start(f32[1,1024]{1,0:T(1,128)} %copy-done.89) | copy-start | bytes 12292
  509.3 54.2 %copy-start.92 = (f32[1,1024]{1,0:T(1,128)S(1)}, f32[1,1024]{1,0:T(1,128)}, u32[]{:S(2)}) copy-start(f32[1,1024]{1,0:T(1,128)} %copy-done.91) | copy-start | bytes 12292
  509.3 54.2 %copy-start.94 = (f32[1,1024]{1,0:T(1,128)S(1)}, f32[1,1024]{1,0:T(1,128)}, u32[]{:S(2)}) copy-start(f32[1,1024]{1,0:T(1,128)} %copy-done.93) | copy-start | bytes 12292
  509.3 54.2 %copy-start.96 = (f32[1,1024]{1,0:T(1,128)S(1)}, f32[1,1024]{1,0:T(1,128)}, u32[]{:S(2)}) copy-start(f32[1,1024]{1,0:T(1,128)} %copy-done.95) | copy-start | bytes 12292
  509.3 54.2 %copy-start.98 = (f32[1,1024]{1,0:T(1,128)S(1)}, f32[1,1024]{1,0:T(1,128)}, u32[]{:S(2)}) copy-start(f32[1,1024]{1,0:T(1,128)} %copy-done.97) | copy-start | bytes 12292
  509.3 99.3 %collective-permute-start.3 = (f32[512,768]{0,1:T(8,128)}, f32[512,768]{0,1:T(8,128)}, u32[]{:S(2)}, u32[]{:S(2)}) collective-permute-start(f32[512,768]{0,1:T(8,128)} %constant_dynamic-slice_fusion.11), channel_id=1, source_target_pairs={{0,4},{4,0},{8,12},{12,8},{16,20},{20,16},{24,28},{28,24},{1,5},{5... | collective-permute-start | bytes 4718600 | tf_op jit(solution)/shard_map/ppermute | solution.py:379
  598.8 7.6 collective-permute-start.7
  606.5 21.7 %collective-permute-start.8 = (f32[32,1024]{1,0:T(8,128)S(1)}, f32[32,1024]{1,0:T(8,128)S(1)}, u32[]{:S(2)}, u32[]{:S(2)}) collective-permute-start(f32[32,1024]{1,0:T(8,128)S(1)} %constant_dynamic-slice_fusion.6), channel_id=1, source_target_pairs={{0,16},{4,20},{8,24},{12,28},{16,0},{20,4},{24,8},{28,12},{1,17},{... | collective-permute-start | bytes 393224 | tf_op jit(solution)/shard_map/ppermute | solution.py:379
  611.6 19.8 %collective-permute-start.4 = (f32[256,768]{0,1:T(8,128)S(1)}, f32[256,768]{0,1:T(8,128)}, u32[]{:S(2)}, u32[]{:S(2)}) collective-permute-start(f32[256,768]{0,1:T(8,128)S(1)} %constant_dynamic-slice_fusion.10), channel_id=1, source_target_pairs={{0,8},{4,12},{8,0},{12,4},{16,24},{20,28},{24,16},{28,20},{1,9},{5... | collective-permute-start | bytes 2359304 | tf_op jit(solution)/shard_map/ppermute | solution.py:379
  628.2 8.2 collective-permute-start.18
  633.1 19.6 %collective-permute-start.5 = (f32[128,768]{0,1:T(8,128)S(1)}, f32[128,768]{0,1:T(8,128)S(1)}, u32[]{:S(2)}, u32[]{:S(2)}) collective-permute-start(f32[128,768]{0,1:T(8,128)S(1)} %constant_dynamic-slice_fusion.9), channel_id=1, source_target_pairs={{0,16},{4,20},{8,24},{12,28},{16,0},{20,4},{24,8},{28,12},{1,17},{... | collective-permute-start | bytes 1179656 | tf_op jit(solution)/shard_map/ppermute | solution.py:379
  636.5 51.5 %copy-start.70 = (f32[6,1024]{1,0:T(8,128)S(1)}, f32[6,1024]{1,0:T(8,128)}, u32[]{:S(2)}) copy-start(f32[6,1024]{1,0:T(8,128)} %param.29) | copy-start | bytes 73732
  636.5 22.5 %collective-permute-start.19 = (f32[64,1024]{1,0:T(8,128)S(1)}, f32[64,1024]{1,0:T(8,128)S(1)}, u32[]{:S(2)}, u32[]{:S(2)}) collective-permute-start(f32[64,1024]{1,0:T(8,128)S(1)} %maximum_select_fusion.14), channel_id=1, source_target_pairs={{0,8},{4,12},{8,0},{12,4},{16,24},{20,28},{24,16},{28,20},{1,9},{5... | collective-permute-start | bytes 786440 | tf_op jit(solution)/shard_map/ppermute | solution.py:379
  652.7 34.2 %collective-permute-start.15 = (f32[128,768]{0,1:T(8,128)S(1)}, f32[128,768]{0,1:T(8,128)S(1)}, u32[]{:S(2)}, u32[]{:S(2)}) collective-permute-start(f32[128,768]{0,1:T(8,128)S(1)} %get-tuple-element.278), channel_id=1, source_target_pairs={{0,16},{4,20},{8,24},{12,28},{16,0},{20,4},{24,8},{28,12},{1,17},{... | collective-permute-start | bytes 1179656 | tf_op jit(solution)/shard_map/ppermute | solution.py:379
  659.0 30.5 %collective-permute-start.20 = (f32[128,1024]{1,0:T(8,128)S(1)}, f32[128,1024]{1,0:T(8,128)S(1)}, u32[]{:S(2)}, u32[]{:S(2)}) collective-permute-start(f32[128,1024]{1,0:T(8,128)S(1)} %maximum_select_fusion.13), channel_id=1, source_target_pairs={{0,4},{4,0},{8,12},{12,8},{16,20},{20,16},{24,28},{28,24},{1,5},{5... | collective-permute-start | bytes 1572872 | tf_op jit(solution)/shard_map/ppermute | solution.py:379
  687.0 19.0 %collective-permute-start.16 = (f32[256,768]{0,1:T(8,128)S(1)}, f32[256,768]{0,1:T(8,128)S(1)}, u32[]{:S(2)}, u32[]{:S(2)}) collective-permute-start(f32[256,768]{0,1:T(8,128)S(1)} %maximum_select_fusion.12), channel_id=1, source_target_pairs={{0,8},{4,12},{8,0},{12,4},{16,24},{20,28},{24,16},{28,20},{1,9},{5... | collective-permute-start | bytes 2359304 | tf_op jit(solution)/shard_map/ppermute | solution.py:379
  691.0 371.4 %copy-start.31 = (f32[256,1024]{1,0:T(8,128)}, f32[256,1024]{1,0:T(8,128)S(1)}, u32[]{:S(2)}) copy-start(f32[256,1024]{1,0:T(8,128)S(1)} %fusion.109) | copy-start | bytes 3145732
  706.2 34.9 %collective-permute-start.17 = (f32[512,768]{0,1:T(8,128)S(1)}, f32[512,768]{0,1:T(8,128)S(1)}, u32[]{:S(2)}, u32[]{:S(2)}) collective-permute-start(f32[512,768]{0,1:T(8,128)S(1)} %maximum_select_fusion.7), channel_id=1, source_target_pairs={{0,4},{4,0},{8,12},{12,8},{16,20},{20,16},{24,28},{28,24},{1,5},{5... | collective-permute-start | bytes 4718600 | tf_op jit(solution)/shard_map/ppermute | solution.py:379
  715.3 25.9 %copy-start.28 = (f32[1024,3,256]{0,2,1:T(8,128)S(1)}, f32[1024,3,256]{0,2,1:T(8,128)}, u32[]{:S(2)}) copy-start(f32[1024,3,256]{0,2,1:T(8,128)} %copy.68) | copy-start | bytes 9437188
  922.4 140.0 %copy-start.30 = (f32[256,1024]{1,0:T(8,128)S(1)}, f32[256,1024]{1,0:T(8,128)}, u32[]{:S(2)}) copy-start(f32[256,1024]{1,0:T(8,128)} %param.33) | copy-start | bytes 3145732
  (104 other events, 913.8 us)

commit v2 on v1

--- a/solution.py
+++ b/solution.py
@@ -285,22 +285,21 @@
     return total.reshape(shape)
 
 
-def narrow_sum_steps(values):
-    shape = values.shape
-    values = values.reshape(-1, shape[-1])
+def core_scatter(values):
     rows = values.shape[0] // 2
     side = lax.axis_index("narrow") % 2
     give = lax.dynamic_slice_in_dim(values, (1 - side) * rows, rows, 0)
     keep = lax.dynamic_slice_in_dim(values, side * rows, rows, 0)
-    values = keep + permute(give, "narrow", 1)
-    for bit in bits_of(lax.axis_size("narrow"))[1:]:
-        values = values + permute(values, "narrow", bit)
-    other = permute(values, "narrow", 1)
+    return keep, permute(give, "narrow", 1)
+
+
+def core_place(half, other):
+    side = lax.axis_index("narrow") % 2
     return jnp.where(
         side == 0,
-        jnp.concatenate([values, other], axis=0),
-        jnp.concatenate([other, values], axis=0),
-    ).reshape(shape)
+        jnp.concatenate([half, other], axis=0),
+        jnp.concatenate([other, half], axis=0),
+    )
 
 
 def small_kernel(
@@ -379,26 +378,53 @@
     return lax.ppermute(values, axis, [(index, index ^ bit) for index in range(size)])
 
 
-def wide_scatter(values):
-    for bit in bits_of(lax.axis_size("wide")):
-        rows = values.shape[0] // 2
-        side = (lax.axis_index("wide") // bit) % 2
-        give = lax.dynamic_slice_in_dim(values, (1 - side) * rows, rows, 0)
-        keep = lax.dynamic_slice_in_dim(values, side * rows, rows, 0)
-        values = keep + permute(give, "wide", bit)
-    return values
-
-
-def wide_gather(values):
-    for bit in reversed(bits_of(lax.axis_size("wide"))):
-        side = (lax.axis_index("wide") // bit) % 2
-        other = permute(values, "wide", bit)
-        values = jnp.where(
-            side == 0,
-            jnp.concatenate([values, other], axis=0),
-            jnp.concatenate([other, values], axis=0),
-        )
-    return values
+def together(*values):
+    return lax.optimization_barrier(values)
+
+
+def pair_scatter(values):
+    rows = values.shape[0] // 2
+    side = lax.axis_index("wide") % 2
+    give = lax.dynamic_slice_in_dim(values, (1 - side) * rows, rows, 0)
+    keep = lax.dynamic_slice_in_dim(values, side * rows, rows, 0)
+    return keep, permute(give, "wide", 1)
+
+
+def line_scatter(values):
+    count = lax.axis_size("wide") // 2
+    rows = values.shape[0] // count
+    place = lax.axis_index("wide") // 2
+    keep = lax.dynamic_slice_in_dim(values, place * rows, rows, 0)
+    arrived = []
+    for offset in range(1, count):
+        give = lax.dynamic_slice_in_dim(values, (place ^ offset) * rows, rows, 0)
+        arrived.append(permute(give, "wide", 2 * offset))
+    return keep, arrived
+
+
+def line_gather(share):
+    count = lax.axis_size("wide") // 2
+    return [permute(share, "wide", 2 * offset) for offset in range(1, count)]
+
+
+def line_place(share, arrived):
+    count = lax.axis_size("wide") // 2
+    rows = share.shape[0]
+    place = lax.axis_index("wide") // 2
+    whole = jnp.zeros((count * rows,) + share.shape[1:], share.dtype)
+    whole = lax.dynamic_update_slice_in_dim(whole, share, place * rows, 0)
+    for offset, piece in zip(range(1, count), arrived):
+        whole = lax.dynamic_update_slice_in_dim(whole, piece, (place ^ offset) * rows, 0)
+    return whole
+
+
+def pair_place(half, other):
+    side = lax.axis_index("wide") % 2
+    return jnp.where(
+        side == 0,
+        jnp.concatenate([half, other], axis=0),
+        jnp.concatenate([other, half], axis=0),
+    )
 
 
 def gram_kernel(narrow_bits, gathers, x_ref, o_ref, halves, inbox, sends, arrivals, local):
@@ -592,22 +618,28 @@
         copies.append(send(src, dst, sends, arrivals, len(copies), place))
         return copies[-1]
 
-    crossing = [
-        push(q_ref.at[rows(top, p)], o_ref.at[own, rows(top, p)], far_place) for p in range(pieces)
-    ]
+    cross = lambda p: push(q_ref.at[rows(top, p)], o_ref.at[own, rows(top, p)], far_place)
+    crossing = [cross(p) for p in range(2)]
     landing = [push(q_ref, o_ref.at[own], near_place)]
     aside = []
     for p in range(pieces):
-        crossing[p].wait_recv()
+        crossing[p].wait()
+        if p + 2 < pieces:
+            crossing.append(cross(p + 2))
+        if p >= 2:
+            aside[p - 2].wait()
         spot = o_ref.at[across, rows(top, p)]
         aside.append(push(spot, spot, side_place))
         landing.append(push(spot, spot, near_place))
-    for p in range(pieces):
-        aside[p].wait_recv()
+        if p >= 2:
+            spot = o_ref.at[across, rows(1 - top, p - 2)]
+            landing.append(push(spot, spot, near_place))
+    for p in range(pieces - 2, pieces):
+        aside[p].wait()
         spot = o_ref.at[across, rows(1 - top, p)]
         landing.append(push(spot, spot, near_place))
     keep.wait()
-    for copy in copies:
+    for copy in landing:
         copy.wait_send()
     for copy in landing:
         copy.wait_recv()
@@ -615,13 +647,13 @@
 
 def spread(factor, number):
     size = factor.shape[0]
-    pieces = 4
+    pieces = 8
     slots = 1 + 4 * pieces
     sub = lax.axis_size("narrow") // MATRICES
     return pl.pallas_call(
         functools.partial(spread_kernel, sub, pieces),
         out_shape=jax.ShapeDtypeStruct((MATRICES, size, size), jnp.float32),
-        in_specs=[pl.BlockSpec(memory_space=pl.ANY)],
+        in_specs=[pl.BlockSpec(memory_space=pltpu.VMEM)],
         out_specs=pl.BlockSpec(memory_space=pl.ANY),
         scratch_shapes=[
             pltpu.SemaphoreType.DMA((slots,)),
@@ -728,16 +760,16 @@
     activated, middle_pull = jax.vjp(middle_piece, upward, hidden_kernel)
     activated_low = activated.astype(jnp.bfloat16)
     reduce_low = reduce_weight.astype(jnp.bfloat16)
-    ffn_branch = narrow_sum_steps(
-        jnp.einsum("isf,fd->isd", activated_low, reduce_low, preferred_element_type=jnp.float32)
-    )
-    block_out = (live_mask * (hidden + gate_two * ffn_branch)).astype(jnp.bfloat16)
+    ffn_partial = jnp.einsum(
+        "isf,fd->isd", activated_low, reduce_low, preferred_element_type=jnp.float32
+    )
+    ffn_keep, ffn_other = core_scatter(ffn_partial.reshape(-1, ffn_partial.shape[-1]))
     grad_result = cotangent.astype(jnp.float32) * live_mask
-    grad_gate_two = jnp.sum(ffn_branch * grad_result, axis=1)
     grad_ffn_low = (gate_two * grad_result).astype(jnp.bfloat16)
     grad_reduce = jnp.einsum(
         "isf,isd->fd", activated_low, grad_ffn_low, preferred_element_type=jnp.float32
     )
+    reduce_keep, reduce_other = pair_scatter(grad_reduce)
     grad_activated = jnp.einsum(
         "isd,fd->isf", grad_ffn_low, reduce_low, preferred_element_type=jnp.float32
     )
@@ -746,9 +778,24 @@
     grad_expand = jnp.einsum(
         "isd,isf->df", entry_low, grad_up_low, preferred_element_type=jnp.float32
     )
+    reduce_other, ffn_other, grad_up_low = together(reduce_other, ffn_other, grad_up_low)
+    reduce_half = reduce_keep + reduce_other
+    ffn_half = ffn_keep + ffn_other
+    reduce_half, ffn_half, grad_up_low = together(reduce_half, ffn_half, grad_up_low)
+    reduce_keep, reduce_pieces = line_scatter(reduce_half)
+    expand_keep, expand_other = pair_scatter(grad_expand)
     grad_entry = narrow_sum(
         jnp.einsum("isf,df->isd", grad_up_low, expand_low, preferred_element_type=jnp.float32), 2
     )
+    *reduce_pieces, expand_other, ffn_half, grad_entry = together(
+        *reduce_pieces, expand_other, ffn_half, grad_entry
+    )
+    reduce_share = reduce_keep + sum(reduce_pieces)
+    expand_half = expand_keep + expand_other
+    reduce_share, expand_half, grad_entry = together(reduce_share, expand_half, grad_entry)
+    reduce_pieces = line_gather(reduce_share)
+    expand_keep, expand_pieces = line_scatter(expand_half)
+    ffn_across = [permute(ffn_half, "narrow", bit) for bit in bits_of(lax.axis_size("narrow"))[1:2]]
     grad_hidden, grad_shift_two, grad_scale_two = entry_pull(grad_entry)
     grad_hidden = grad_hidden + grad_result
     grad_gate_one = jnp.sum(branch * grad_hidden, axis=1)
@@ -774,12 +821,43 @@
     grad_triple = grad_split.reshape(item_count, seq_len, 3, local_heads * HEAD).astype(
         jnp.bfloat16
     )
+    output_keep, output_other = pair_scatter(grad_output)
+    *pieces, ffn_crossed, output_other, grad_triple = together(
+        *reduce_pieces, *expand_pieces, ffn_across[0], output_other, grad_triple
+    )
+    reduce_pieces, expand_pieces = pieces[: len(reduce_pieces)], pieces[len(reduce_pieces) :]
+    ffn_half = ffn_half + ffn_crossed
+    for bit in bits_of(lax.axis_size("narrow"))[2:]:
+        ffn_half = ffn_half + permute(ffn_half, "narrow", bit)
+    reduce_line = line_place(reduce_share, reduce_pieces)
+    expand_share = expand_keep + sum(expand_pieces)
+    output_half = output_keep + output_other
+    ffn_half, reduce_line, expand_share, output_half, grad_triple = together(
+        ffn_half, reduce_line, expand_share, output_half, grad_triple
+    )
+    ffn_other = permute(ffn_half, "narrow", 1)
+    reduce_other = permute(reduce_line, "wide", 1)
+    expand_pieces = line_gather(expand_share)
+    output_keep, output_pieces = line_scatter(output_half)
     grad_attend = jnp.einsum(
         "isd,iskc->dkc", mixed_low, grad_triple, preferred_element_type=jnp.float32
     )
+    width = tokens.shape[2]
+    attend_keep, attend_other = pair_scatter(grad_attend.reshape(width, -1))
     grad_mixed = narrow_sum(
         jnp.einsum("iskc,dkc->isd", grad_triple, attend_low, preferred_element_type=jnp.float32), 3
     )
+    *expand_pieces, ffn_other, attend_other, grad_mixed = together(
+        *expand_pieces, ffn_other, attend_other, grad_mixed
+    )
+    expand_line = line_place(expand_share, expand_pieces)
+    attend_half = attend_keep + attend_other
+    expand_line, attend_half, grad_mixed = together(expand_line, attend_half, grad_mixed)
+    expand_other = permute(expand_line, "wide", 1)
+    attend_keep, attend_pieces = line_scatter(attend_half)
+    ffn_branch = core_place(ffn_half, ffn_other).reshape(ffn_partial.shape)
+    block_out = (live_mask * (hidden + gate_two * ffn_branch)).astype(jnp.bfloat16)
+    grad_gate_two = jnp.sum(ffn_branch * grad_result, axis=1)
     grad_tokens, grad_shift_one, grad_scale_one, grad_mixer_kernel = mixer_pull(grad_mixed)
     tokens_gradient = (grad_tokens + grad_hidden).astype(jnp.bfloat16)
     grad_table = jnp.sum(
@@ -796,9 +874,13 @@
         ),
         axis=0,
     )
-    width = tokens.shape[2]
-    gradients = [grad_attend.reshape(width, -1), grad_output, grad_expand, grad_reduce]
-    shares = [wide_scatter(gradient) for gradient in gradients]
+    *pieces, grad_table = together(*attend_pieces, *output_pieces, grad_table)
+    attend_pieces, output_pieces = pieces[: len(attend_pieces)], pieces[len(attend_pieces) :]
+    attend_share = attend_keep + sum(attend_pieces)
+    output_share = output_keep + sum(output_pieces)
+    attend_pieces = line_gather(attend_share)
+    output_pieces = line_gather(output_share)
+    shares = [attend_share, output_share, expand_share, reduce_share]
     squares = sum(
         jnp.sum((share * share).reshape(-1, width), axis=0) for share in shares
     )
@@ -812,12 +894,29 @@
     )
     stacked = jnp.pad(stacked, ((0, -stacked.shape[0] % 8), (0, 0)))
     small, norm = small_sums(stacked, shared_rows, hidden_rows, 4)
-    gradient_norm = norm[0, 0]
-    clip_factor = jnp.minimum(1.0, 1.0 / (gradient_norm + 1e-06))
     summed_table = small[: grad_table.shape[0]]
     summed_mixer = small[grad_table.shape[0] : shared_rows]
     summed_hidden = small[shared_rows : shared_rows + hidden_rows].reshape(-1)
     summed_hidden = summed_hidden[: hidden_kernel.size].reshape(hidden_kernel.shape)
+    moments = (attend_moment, output_moment, expand_moment, reduce_moment)
+    *pieces, reduce_other, expand_other, norm = together(
+        *attend_pieces, *output_pieces, reduce_other, expand_other, norm
+    )
+    gradient_norm = norm[0, 0]
+    clip_factor = jnp.minimum(1.0, 1.0 / (gradient_norm + 1e-06))
+    attend_pieces, output_pieces = pieces[: len(attend_pieces)], pieces[len(attend_pieces) :]
+    attend_line = line_place(attend_share, attend_pieces)
+    output_line = line_place(output_share, output_pieces)
+    gathered = [
+        pair_place(attend_line, permute(attend_line, "wide", 1)),
+        pair_place(output_line, permute(output_line, "wide", 1)),
+        pair_place(expand_line, expand_other),
+        pair_place(reduce_line, reduce_other),
+    ]
+    carried = [
+        muon_momentum * moment + clip_factor * gradient.reshape(moment.shape)
+        for moment, gradient in zip(moments, gathered)
+    ]
     table_moment, table_square, table_result = adam_update(
         modulation_table, table_first, table_second, clip_factor * summed_table
     )
@@ -827,11 +926,6 @@
     hidden_moment, hidden_square, hidden_result = adam_update(
         hidden_kernel, hidden_first, hidden_second, clip_factor * summed_hidden
     )
-    moments = (attend_moment, output_moment, expand_moment, reduce_moment)
-    carried = [
-        muon_momentum * moment + clip_factor * wide_gather(share).reshape(moment.shape)
-        for moment, share in zip(moments, shares)
-    ]
     matrices = [carried[0].reshape(width, -1), carried[1], carried[2], carried[3]]
     layouts = ("columns", "rows", "columns", "rows")
     block_rows = width // lax.axis_size("wide")

time: 1100 us -> 985 us (0.90)
  Pallas kernels: 480 us -> 408 us
  waiting for transfers between devices: 157 us -> 127 us
  other arithmetic: 214 us -> 194 us
  local copies, waits for them, and re-layouts: 57.6 us -> 74.5 us
    pallas_call x1, Pallas kernels: 130 us -> 60.4 us  [spread(): pl.pallas_call(functools.partial(spread_kernel, sub, pieces), out_shape=j...]
    ppermute x27 -> x35, waiting for transfers between devices: 157 us -> 127 us  [permute(): lax.ppermute(values, axis, [(index, index ^ bit) for index in range(size)])]
    select_n x10 -> x0, other arithmetic: 15.8 us -> none  [wide_gather(): jnp.where(side == 0, jnp.concatenate([values, other], axis=0), jnp.concat...]
    ppermute x27 -> x35, starting transfers between devices: 39 us -> 34.6 us  [permute(): lax.ppermute(values, axis, [(index, index ^ bit) for index in range(size)])]
    unnamed x226 -> x208, local copies, waits for them, and re-layouts: 28.5 us -> 27.3 us
    add x14 -> x11, other arithmetic: 29.8 us -> 30.8 us  [the longest x4 13.3 us: local(): muon_momentum * moment + clip_factor * gradient.reshape(moment.shape)]
  transfers between devices with their start and end apart: 27 -> 35, of which waited for: 10 -> 7; matrix products, arithmetic and copies ran while one was open for 24% -> 24% of each run, Pallas kernels for 12% -> 13%
where the time goes in v2:
time: 985 us; the launch traced here: 974 us
  Pallas kernels  408 us (41%)
  other arithmetic  194 us (20%)
  matrix products  131 us (13%)
  waiting for transfers between devices  127 us (13%)
  local copies, waits for them, and re-layouts  74.5 us (8%)
  starting transfers between devices  34.6 us (4%)
    pallas_call x3, Pallas kernels, narrow_sum(): pl.pallas_call(functools.partial(narrow_sum_kernel, far_bits, pieces), ou...  156 us
    ppermute x35, waiting for transfers between devices, permute(): lax.ppermute(values, axis, [(index, index ^ bit) for index in range(size)])  127 us
    pallas_call x1, Pallas kernels, gram_whole(): pl.pallas_call(functools.partial(gram_kernel, narrow_bits, gathers), out_...  88.9 us
    pallas_call x1, Pallas kernels, polar_factor(): pl.pallas_call(polar_kernel, out_shape=jax.ShapeDtypeStruct((size, size),...  75.9 us
    pallas_call x1, Pallas kernels, spread(): pl.pallas_call(functools.partial(spread_kernel, sub, pieces), out_shape=j...  60.4 us
    ppermute x35, starting transfers between devices, permute(): lax.ppermute(values, axis, [(index, index ^ bit) for index in range(size)])  34.6 us
    dot_general x4, matrix products, apply_factor(): jnp.dot(left, right, precision=lax.Precision.HIGH, preferred_element_type...  33.5 us
    unnamed x208, local copies, waits for them, and re-layouts  27.3 us
  transfers between devices with their start and end apart: 35, of which 7 were waited for; matrix products, arithmetic and copies ran while one was open for 24% of the time, Pallas kernels for 13%

profile of v2, /device:TPU:13, one launch (start us, length us, event | category | flops | bytes accessed | tf_op | source)
XLA Modules:
  0.0 974.2 jit_solution(4637317603499127587)
XLA Ops:
  8.9 17.8 %add_convert_fusion.2 = bf16[1,32,32,1024]{3,2,1,0:T(8,128)(2,1)} fusion(f32[1,32,32,1024]{3,2,1,0:T(8,128)} %bitcast.318, f32[1024]{0:T(1024)S(1)} %bitcast.386, f32[1024]{0:T(1024)S(1)} %bitcast.372, f32[1024]{0:T(1024)S(1)} %bitcast.374, f32[1024]{0:T(1024)S(1)} %bitcast.376, f32[1024]{0:T(1024)S(1)} %bitcast.378, f32[1024]{0:T(1024)S(1)} %bitcast.380, ...), kind=kLoop, calls=%fused_computation.165 | loop fusion | flops 18874368 | bytes 6328320 | tf_op jit(solution)/shard_map/convert_element_type | solution.py:740
  26.8 3.5 convolution_convert_fusion
  33.6 12.4 %while.45 = (s32[]{:T(128)}, bf16[2,512,4,64]{1,3,2,0:T(8,128)(2,1)}, f32[2,4,512]{2,1,0:T(4,128)S(1)}, bf16[2,512,4,64]{1,3,2,0:T(8,128)(2,1)S(1)}, bf16[1024,4...) while((s32[]{:T(128)}, bf16[2,512,4,64]{1,3,2,0:T(8,128)(2,1)}, ...), condition=%wide.region_5.6_spmd, body=%wide.region_2.5_spmd.sunk | while | flops 555874304 | bytes 33095860 | solution.py:92
  50.4 52.2 %shard_map.356 = f32[1024,1024]{1,0:T(8,128)S(1)} custom-call(f32[1024,1024]{1,0:T(8,128)S(1)} %fusion.125.x_ref), custom_call_target="tpu_custom_call" | custom-call | flops 1048576 | bytes 33554432 | tf_op jit(solution)/shard_map/pallas_call | solution.py:265
  107.9 7.9 fusion.114
  115.8 19.2 %fusion.57 = (bf16[1,32,32,1024]{3,2,1,0:T(8,128)(2,1)}, f32[1,32,32,1024]{3,2,1,0:T(8,128)}) fusion(f32[1024]{0:T(1024)S(1)} %bitcast.368, f32[1024]{0:T(1024)S(1)} %bitcast.354, f32[1024]{0:T(1024)S(1)} %bitcast.356, f32[1024]{0:T(1024)S(1)} %bitcast.358, f32[1,32,32,1024]{3,2,1,0:T(8,128)} %bitcast.322, f32[1024]{0:T(1024)S(1)} %bitcast.360, ...), kind=kLoop, calls=%fused_computation.90 | loop fusion | flops 27262976 | bytes 10522624 | tf_op jit(solution)/shard_map/convert_element_type | solution.py:761
  135.0 4.0 fusion.97
  142.7 3.6 multiply_convert_fusion.3
  146.4 4.3 fusion.111
  150.7 3.2 constant_dynamic-slice_fusion.15
  154.3 24.8 %multiply_reduce_fusion.10 = (f32[1024]{0:T(1024)}, f32[1024]{0:T(1024)}, f32[1024]{0:T(1024)}, f32[1024]{0:T(1024)}, f32[1024]{0:T(1024)}, /*index=5*/f32[1024]...) fusion(f32[1,32,32,1024]{3,2,1,0:T(8,128)} %bitcast.323, f32[1024,1024]{1,0:T(8,128)} %param.35, ...), kind=kOutput, calls=%fused_computation.142 | convolution fusion | flops 2193612800 | bytes 18911236 | tf_op jit(solution)/shard_map/isd,fd->isf/dot_general | solution.py:773
  179.1 13.5 %broadcast_multiply_fusion = (f32[1,32,32,1024]{3,2,1,0:T(8,128)}, f32[1,32,32,1024]{3,2,1,0:T(8,128)S(1)}, f32[1,32,32,1024]{3,2,1,0:T(8,128)}, f32[1,32,32,102...) fusion(f32[1,32,32,1024]{3,2,1,0:T(8,128)} %bitcast.324, ...), kind=kLoop, calls=%fused_computation.181 | loop fusion | flops 9437184 | bytes 41979904 | tf_op jit(solution)/shard_map/transpose(jvp())/mul | solution.py:54
  192.7 6.5 pad_add_fusion.1
  199.2 10.3 %fusion.60 = bf16[1,32,32,1024]{3,2,1,0:T(8,128)(2,1)S(1)} fusion(f32[1,32,32,1024]{3,2,1,0:T(8,128)S(1)} %get-tuple-element.410, f32[1,32,32,1024]{3,2,1,0:T(8,128)} %get-tuple-element.411, f32[1,32,32,1024]{3,2,1,0:T(8,128)} %get-tuple-element.412, f32[1,32,32,1024]{3,2,1,0:T(8,128)} %get-tuple-element.413, f32[1,32,32,1024]{3,2,1,0:T(8,128)} %get-tuple-element.414, ...), kind=kLoop, calls=%fused_computation.100 | loop fusion | flops 7340032 | bytes 31457280 | tf_op jit(solution)/shard_map/convert_element_type | solution.py:777
  217.1 6.3 dynamic-slice_add_fusion.1
  228.7 52.1 %shard_map.357 = f32[1024,1024]{1,0:T(8,128)S(1)} custom-call(f32[1024,1024]{1,0:T(8,128)S(1)} %fusion.85.x_ref), custom_call_target="tpu_custom_call" | custom-call | flops 1048576 | bytes 33554432 | tf_op jit(solution)/shard_map/pallas_call | solution.py:265
  305.0 4.1 fusion.117
  311.2 9.9 %collective-permute-done.7 = f32[128,1024]{1,0:T(8,128)} collective-permute-done((f32[128,1024]{1,0:T(8,128)}, f32[128,1024]{1,0:T(8,128)}, u32[]{:S(2)}, u32[]{:S(2)}) %collective-permute-start.7) | collective-permute-done | bytes 524320 | tf_op jit(solution)/shard_map/ppermute | solution.py:378
  321.9 32.9 %collective-permute-done.8 = f32[128,1024]{1,0:T(8,128)} collective-permute-done((f32[128,1024]{1,0:T(8,128)}, f32[128,1024]{1,0:T(8,128)}, u32[]{:S(2)}, u32[]{:S(2)}) %collective-permute-start.8) | collective-permute-done | bytes 524320 | tf_op jit(solution)/shard_map/ppermute | solution.py:378
  355.0 34.7 %while.46 = (s32[]{:T(128)}, f32[1024,4,64]{0,2,1:T(8,128)S(1)}, f32[1024,4,64]{0,2,1:T(8,128)S(1)}, bf16[2,512,4,64]{1,3,2,0:T(8,128)(2,1)}, bf16[2,512,4,64]{1...) while((s32[]{:T(128)}, f32[1024,4,64]{0,2,1:T(8,128)S(1)}, ...), condition=%wide.region_12.13_spmd.clone, body=%wide.region_10.12_spmd.clone.sunk | while | flops 1368782848 | bytes 164684176 | solution.py:135
  359.7 3.4 multiply_convert_fusion.6
  363.0 3.3 fusion.205
  376.8 3.4 multiply_convert_fusion.6
  380.2 3.3 fusion.205
  416.0 3.5 copy.55
  419.7 4.2 multiply_reduce_fusion.6
  428.6 52.1 %shard_map.358 = f32[1024,1024]{1,0:T(8,128)S(1)} custom-call(f32[1024,1024]{1,0:T(8,128)S(1)} %convolution_bitcast_fusion.x_ref), custom_call_target="tpu_custom_call" | custom-call | flops 1048576 | bytes 33554432 | tf_op jit(solution)/shard_map/pallas_call | solution.py:265
  492.2 12.0 %broadcast_multiply_fusion.9 = (f32[1,32,32,1024]{3,2,1,0:T(8,128)S(1)}, f32[1,32,32,1024]{3,2,1,0:T(8,128)}, f32[1,32,32,1024]{3,2,1,0:T(8,128)}, f32[1,32,32,1...) fusion(f32[1024]{0:T(1024)S(1)} %bitcast.387, ...), kind=kLoop, calls=%fused_computation.190 | loop fusion | flops 9437184 | bytes 41979904 | tf_op jit(solution)/shard_map/transpose(jvp())/mul | solution.py:54
  504.2 7.7 pad_add_fusion
  511.9 12.8 %fusion.145 = (f32[1024]{0:T(1024)S(1)}, f32[1,32,32,1024]{3,2,1,0:T(8,128)S(1)}) fusion(f32[1,32,32,1024]{3,2,1,0:T(8,128)} %get-tuple-element.408, f32[1,32,32,1024]{3,2,1,0:T(8,128)} %get-tuple-element.407, f32[1,32,32,1024]{3,2,1,0:T(8,128)} %get-tuple-element.406, f32[1,32,32,1024]{3,2,1,0:T(8,128)} %get-tuple-element.405, ...), kind=kLoop, calls=%fused_computation.316 | loop fusion | flops 7339008 | bytes 33558528 | tf_op jit(solution)/shard_map/transpose(jvp())/reduce_sum | solution.py:61
  525.8 3.3 fusion.47
  530.4 6.6 multiply_reduce_fusion.20
  537.0 7.0 multiply_reduce_fusion.19
  548.5 5.7 multiply_convert_fusion.1
  554.1 8.0 collective-permute-done.19
  564.2 17.1 %collective-permute-done.21 = f32[128,768]{1,0:T(8,128)S(1)} collective-permute-done((f32[128,768]{1,0:T(8,128)S(1)}, f32[128,768]{1,0:T(8,128)S(1)}, u32[]{:S(2)}, u32[]{:S(2)}) %collective-permute-start.21) | collective-permute-done | bytes 393248 | tf_op jit(solution)/shard_map/ppermute | solution.py:378
  589.8 32.9 %collective-permute-done.29 = f32[32,1024]{1,0:T(8,128)S(1)} collective-permute-done((f32[32,1024]{1,0:T(8,128)S(1)}, f32[32,1024]{1,0:T(8,128)S(1)}, u32[]{:S(2)}, u32[]{:S(2)}) %collective-permute-start.29) | collective-permute-done | bytes 131104 | tf_op jit(solution)/shard_map/ppermute | solution.py:378
  623.6 26.3 %shard_map.359 = (f32[32,1024]{1,0:T(8,128)S(1)}, f32[8,128]{1,0:T(8,128)S(1)}) custom-call(f32[32,1024]{1,0:T(8,128)S(1)} %select_maximum_fusion.x_ref), custom_call_target="tpu_custom_call" | custom-call | tf_op jit(solution)/shard_map/pallas_call | solution.py:355
  658.5 5.7 fusion.64
  668.2 4.3 fusion.62
  677.2 24.3 %collective-permute-done.34 = f32[128,1024]{1,0:T(8,128)S(1)} collective-permute-done((f32[128,1024]{1,0:T(8,128)S(1)}, f32[128,1024]{1,0:T(8,128)S(1)}, u32[]{:S(2)}, u32[]{:S(2)}) %collective-permute-start.34) | collective-permute-done | bytes 524320 | tf_op jit(solution)/shard_map/ppermute | solution.py:378
  711.0 88.9 %shard_map.360.g_ref = f32[1024,1024]{1,0:T(8,128)S(1)} custom-call(f32[4,128,1024]{2,1,0:T(8,128)S(1)} %pad_maximum_fusion.x_ref), custom_call_target="tpu_custom_call" | custom-call | tf_op jit(solution)/shard_map/pallas_call | solution.py:497
  802.0 75.9 %shard_map.361.q_ref = f32[1024,1024]{1,0:T(8,128)S(1)} custom-call(f32[1024,1024]{1,0:T(8,128)} %copy-done.3), custom_call_target="tpu_custom_call" | custom-call | flops 109521666048 | bytes 8388608 | tf_op jit(solution)/shard_map/pallas_call | solution.py:588
  879.9 60.4 %shard_map.362 = f32[4,1024,1024]{2,1,0:T(8,128)} custom-call(f32[1024,1024]{1,0:T(8,128)} %copy-done.2), custom_call_target="tpu_custom_call" | custom-call | tf_op jit(solution)/shard_map/pallas_call | solution.py:653
  940.3 9.7 multiply_subtract_fusion.2
  950.0 5.0 fusion.105
  955.0 10.2 %multiply_subtract_fusion.1 = f32[1024,1024]{1,0:T(8,128)} fusion(f32[1024,1024]{1,0:T(8,128)} %param.34, f32[1024,1024]{1,0:T(8,128)S(1)} %copy-done.19, f32[4,1024,1024]{2,1,0:T(8,128)S(1)} %copy-done.14), kind=kOutput, calls=%fused_computation.130 | convolution fusion | flops 6445596672 | bytes 16777216 | tf_op jit(solution)/shard_map/dot_general | solution.py:699
  965.2 8.6 multiply_subtract_fusion
  (431 shorter events, 187.9 us)
Async XLA Ops:
  1.7 152.6 %copy-start.103 = (f32[1,1,1024]{2,1,0:T(1,128)}, f32[1,1,1024]{2,1,0:T(1,128)S(1)}, u32[]{:S(2)}) copy-start(f32[1,1,1024]{2,1,0:T(1,128)S(1)} %get-tuple-element.458) | copy-start | bytes 12292
  5.9 20.8 %copy-start.79 = (f32[1024]{0:T(1024)}, f32[1024]{0:T(1024)S(1)}, u32[]{:S(2)}) copy-start(f32[1024]{0:T(1024)S(1)} %fusion.51) | copy-start | bytes 12292
  6.0 20.8 %copy-start.69 = (f32[1024]{0:T(1024)}, f32[1024]{0:T(1024)S(1)}, u32[]{:S(2)}) copy-start(f32[1024]{0:T(1024)S(1)} %fusion.135) | copy-start | bytes 12292
  6.0 20.7 %copy-start.81 = (f32[1,1024]{1,0:T(1,128)}, f32[1,1024]{1,0:T(1,128)S(1)}, u32[]{:S(2)}) copy-start(f32[1,1024]{1,0:T(1,128)S(1)} %get-tuple-element.449) | copy-start | bytes 12292
  6.0 20.7 %copy-start.83 = (f32[1,1024]{1,0:T(1,128)}, f32[1,1024]{1,0:T(1,128)S(1)}, u32[]{:S(2)}) copy-start(f32[1,1024]{1,0:T(1,128)S(1)} %get-tuple-element.450) | copy-start | bytes 12292
  6.0 20.7 %copy-start.85 = (f32[1,1024]{1,0:T(1,128)}, f32[1,1024]{1,0:T(1,128)S(1)}, u32[]{:S(2)}) copy-start(f32[1,1024]{1,0:T(1,128)S(1)} %get-tuple-element.451) | copy-start | bytes 12292
  50.4 52.2 %copy-start.59 = (f32[9,1024]{1,0:T(8,128)S(1)}, f32[9,1024]{1,0:T(8,128)}, u32[]{:S(2)}) copy-start(f32[9,1024]{1,0:T(8,128)} %param.31) | copy-start | bytes 110596
  142.5 74.6 %collective-permute-start = (f32[512,1024]{1,0:T(8,128)}, f32[512,1024]{1,0:T(8,128)}, u32[]{:S(2)}, u32[]{:S(2)}) collective-permute-start(f32[512,1024]{1,0:T(8,128)} %constant_dynamic-slice_fusion.16), channel_id=1, source_target_pairs={{0,4},{4,0},{8,12},{12,8},{16,20},{20,16},{24,28},{28,24},{1,5},{5... | collective-permute-start | bytes 6291464 | tf_op jit(solution)/shard_map/ppermute | solution.py:378
  153.9 63.2 %collective-permute-start.1 = (f32[512,1024]{1,0:T(8,128)}, f32[512,1024]{1,0:T(8,128)}, u32[]{:S(2)}, u32[]{:S(2)}) collective-permute-start(f32[512,1024]{1,0:T(8,128)} %constant_dynamic-slice_fusion.15), channel_id=1, source_target_pairs={{0,1},{1,0},{2,3},{3,2},{4,5},{5,4},{6,7},{7,6},{8,9},{9,8},{10,11... | collective-permute-start | bytes 6291464 | tf_op jit(solution)/shard_map/ppermute | solution.py:378
  215.8 65.0 %collective-permute-start.5 = (f32[512,1024]{1,0:T(8,128)}, f32[512,1024]{1,0:T(8,128)}, u32[]{:S(2)}, u32[]{:S(2)}) collective-permute-start(f32[512,1024]{1,0:T(8,128)} %constant_dynamic-slice_fusion.11), channel_id=1, source_target_pairs={{0,4},{4,0},{8,12},{12,8},{16,20},{20,16},{24,28},{28,24},{1,5},{5... | collective-permute-start | bytes 6291464 | tf_op jit(solution)/shard_map/ppermute | solution.py:378
  223.6 57.2 %collective-permute-start.2 = (f32[128,1024]{1,0:T(8,128)S(1)}, f32[128,1024]{1,0:T(8,128)S(1)}, u32[]{:S(2)}, u32[]{:S(2)}) collective-permute-start(f32[128,1024]{1,0:T(8,128)S(1)} %get-tuple-element.423), channel_id=1, source_target_pairs={{0,8},{4,12},{8,0},{12,4},{16,24},{20,28},{24,16},{28,20},{1,9},{5... | collective-permute-start | bytes 1572872 | tf_op jit(solution)/shard_map/ppermute | solution.py:378
  223.8 57.0 %collective-permute-start.3 = (f32[128,1024]{1,0:T(8,128)S(1)}, f32[128,1024]{1,0:T(8,128)S(1)}, u32[]{:S(2)}, u32[]{:S(2)}) collective-permute-start(f32[128,1024]{1,0:T(8,128)S(1)} %get-tuple-element.422), channel_id=1, source_target_pairs={{0,16},{4,20},{8,24},{12,28},{16,0},{20,4},{24,8},{28,12},{1,17},{... | collective-permute-start | bytes 1572872 | tf_op jit(solution)/shard_map/ppermute | solution.py:378
  226.1 54.7 %collective-permute-start.4 = (f32[128,1024]{1,0:T(8,128)S(1)}, f32[128,1024]{1,0:T(8,128)S(1)}, u32[]{:S(2)}, u32[]{:S(2)}) collective-permute-start(f32[128,1024]{1,0:T(8,128)S(1)} %get-tuple-element.421), channel_id=1, source_target_pairs={{0,24},{4,28},{8,16},{12,20},{16,8},{20,12},{24,0},{28,4},{1,25},{... | collective-permute-start | bytes 1572872 | tf_op jit(solution)/shard_map/ppermute | solution.py:378
  228.7 52.1 %copy-start.39 = (f32[1024,1024]{1,0:T(8,128)S(1)}, f32[1024,1024]{1,0:T(8,128)}, u32[]{:S(2)}) copy-start(f32[1024,1024]{1,0:T(8,128)} %copy-done.38) | copy-start | bytes 12582916
  283.9 27.0 %collective-permute-start.6 = (f32[128,1024]{1,0:T(8,128)}, f32[128,1024]{1,0:T(8,128)}, u32[]{:S(2)}, u32[]{:S(2)}) collective-permute-start(f32[128,1024]{1,0:T(8,128)} %add_add_fusion.4), channel_id=1, source_target_pairs={{0,8},{4,12},{8,0},{12,4},{16,24},{20,28},{24,16},{28,20},{1,9},{5... | collective-permute-start | bytes 1572872 | tf_op jit(solution)/shard_map/ppermute | solution.py:378
  284.9 36.2 %collective-permute-start.7 = (f32[128,1024]{1,0:T(8,128)}, f32[128,1024]{1,0:T(8,128)}, u32[]{:S(2)}, u32[]{:S(2)}) collective-permute-start(f32[128,1024]{1,0:T(8,128)} %add_add_fusion.4), channel_id=1, source_target_pairs={{0,16},{4,20},{8,24},{12,28},{16,0},{20,4},{24,8},{28,12},{1,17},{... | collective-permute-start | bytes 1572872 | tf_op jit(solution)/shard_map/ppermute | solution.py:378
  287.0 67.8 %collective-permute-start.8 = (f32[128,1024]{1,0:T(8,128)}, f32[128,1024]{1,0:T(8,128)}, u32[]{:S(2)}, u32[]{:S(2)}) collective-permute-start(f32[128,1024]{1,0:T(8,128)} %add_add_fusion.4), channel_id=1, source_target_pairs={{0,24},{4,28},{8,16},{12,20},{16,8},{20,12},{24,0},{28,4},{1,25},{... | collective-permute-start | bytes 1572872 | tf_op jit(solution)/shard_map/ppermute | solution.py:378
  288.5 107.3 %collective-permute-start.9 = (f32[128,1024]{1,0:T(8,128)}, f32[128,1024]{1,0:T(8,128)}, u32[]{:S(2)}, u32[]{:S(2)}) collective-permute-start(f32[128,1024]{1,0:T(8,128)} %get-tuple-element.420), channel_id=1, source_target_pairs={{0,8},{4,12},{8,0},{12,4},{16,24},{20,28},{24,16},{28,20},{1,9},{5... | collective-permute-start | bytes 1572872 | tf_op jit(solution)/shard_map/ppermute | solution.py:378
  289.7 106.1 %collective-permute-start.10 = (f32[128,1024]{1,0:T(8,128)}, f32[128,1024]{1,0:T(8,128)}, u32[]{:S(2)}, u32[]{:S(2)}) collective-permute-start(f32[128,1024]{1,0:T(8,128)} %get-tuple-element.419), channel_id=1, source_target_pairs={{0,16},{4,20},{8,24},{12,28},{16,0},{20,4},{24,8},{28,12},{1,17},{... | collective-permute-start | bytes 1572872 | tf_op jit(solution)/shard_map/ppermute | solution.py:378
  310.9 84.9 %collective-permute-start.11 = (f32[128,1024]{1,0:T(8,128)}, f32[128,1024]{1,0:T(8,128)}, u32[]{:S(2)}, u32[]{:S(2)}) collective-permute-start(f32[128,1024]{1,0:T(8,128)} %get-tuple-element.418), channel_id=1, source_target_pairs={{0,24},{4,28},{8,16},{12,20},{16,8},{20,12},{24,0},{28,4},{1,25},{... | collective-permute-start | bytes 1572872 | tf_op jit(solution)/shard_map/ppermute | solution.py:378
  321.1 74.7 %collective-permute-start.12 = (f32[512,1024]{1,0:T(8,128)}, f32[512,1024]{1,0:T(8,128)}, u32[]{:S(2)}, u32[]{:S(2)}) collective-permute-start(f32[512,1024]{1,0:T(8,128)} %get-tuple-element.192), channel_id=1, source_target_pairs={{0,2},{1,3},{2,0},{3,1},{4,6},{5,7},{6,4},{7,5},{8,10},{9,11},{10,... | collective-permute-start | bytes 6291464 | tf_op jit(solution)/shard_map/ppermute | solution.py:378
  354.8 41.0 %collective-permute-start.13 = (f32[128,1024]{1,0:T(8,128)}, f32[128,1024]{1,0:T(8,128)}, u32[]{:S(2)}, u32[]{:S(2)}) collective-permute-start(f32[128,1024]{1,0:T(8,128)} %constant_dynamic-slice_fusion.7), channel_id=1, source_target_pairs={{0,4},{4,0},{8,12},{12,8},{16,20},{20,16},{24,28},{28,24},{1,5},{5... | collective-permute-start | bytes 1572872 | tf_op jit(solution)/shard_map/ppermute | solution.py:378
  407.1 79.7 %collective-permute-start.17 = (f32[512,1024]{1,0:T(8,128)S(1)}, f32[512,1024]{1,0:T(8,128)}, u32[]{:S(2)}, u32[]{:S(2)}) collective-permute-start(f32[512,1024]{1,0:T(8,128)S(1)} %add.517), channel_id=1, source_target_pairs={{0,1},{1,0},{2,3},{3,2},{4,5},{5,4},{6,7},{7,6},{8,9},{9,8},{10,11... | collective-permute-start | bytes 6291464 | tf_op jit(solution)/shard_map/ppermute | solution.py:378
  414.8 71.8 %collective-permute-start.18 = (f32[512,768]{1,0:T(8,128)}, f32[512,768]{1,0:T(8,128)}, u32[]{:S(2)}, u32[]{:S(2)}) collective-permute-start(f32[512,768]{1,0:T(8,128)} %constant_dynamic-slice_fusion.6), channel_id=1, source_target_pairs={{0,4},{4,0},{8,12},{12,8},{16,20},{20,16},{24,28},{28,24},{1,5},{5... | collective-permute-start | bytes 4718600 | tf_op jit(solution)/shard_map/ppermute | solution.py:378
  424.0 60.0 %collective-permute-start.14 = (f32[128,1024]{1,0:T(8,128)S(1)}, f32[128,1024]{1,0:T(8,128)S(1)}, u32[]{:S(2)}, u32[]{:S(2)}) collective-permute-start(f32[128,1024]{1,0:T(8,128)S(1)} %add_add_fusion.3), channel_id=1, source_target_pairs={{0,8},{4,12},{8,0},{12,4},{16,24},{20,28},{24,16},{28,20},{1,9},{5... | collective-permute-start | bytes 1572872 | tf_op jit(solution)/shard_map/ppermute | solution.py:378
  424.1 60.7 %collective-permute-start.15 = (f32[128,1024]{1,0:T(8,128)S(1)}, f32[128,1024]{1,0:T(8,128)S(1)}, u32[]{:S(2)}, u32[]{:S(2)}) collective-permute-start(f32[128,1024]{1,0:T(8,128)S(1)} %add_add_fusion.3), channel_id=1, source_target_pairs={{0,16},{4,20},{8,24},{12,28},{16,0},{20,4},{24,8},{28,12},{1,17},{... | collective-permute-start | bytes 1572872 | tf_op jit(solution)/shard_map/ppermute | solution.py:378
  426.4 60.0 %collective-permute-start.16 = (f32[128,1024]{1,0:T(8,128)S(1)}, f32[128,1024]{1,0:T(8,128)S(1)}, u32[]{:S(2)}, u32[]{:S(2)}) collective-permute-start(f32[128,1024]{1,0:T(8,128)S(1)} %add_add_fusion.3), channel_id=1, source_target_pairs={{0,24},{4,28},{8,16},{12,20},{16,8},{20,12},{24,0},{28,4},{1,25},{... | collective-permute-start | bytes 1572872 | tf_op jit(solution)/shard_map/ppermute | solution.py:378
  428.6 58.3 %copy-start.46 = (f32[1024,768]{1,0:T(8,128)S(1)}, f32[1024,768]{1,0:T(8,128)}, u32[]{:S(2)}) copy-start(f32[1024,768]{1,0:T(8,128)} %copy-done.45) | copy-start | bytes 9437188
  483.9 61.5 %collective-permute-start.22 = (f32[32,1024]{1,0:T(8,128)}, f32[32,1024]{1,0:T(8,128)S(1)}, u32[]{:S(2)}, u32[]{:S(2)}) collective-permute-start(f32[32,1024]{1,0:T(8,128)} %get-tuple-element.436), channel_id=1, source_target_pairs={{0,8},{4,12},{8,0},{12,4},{16,24},{20,28},{24,16},{28,20},{1,9},{5... | collective-permute-start | bytes 393224 | tf_op jit(solution)/shard_map/ppermute | solution.py:378
  484.7 62.5 %collective-permute-start.23 = (f32[32,1024]{1,0:T(8,128)}, f32[32,1024]{1,0:T(8,128)}, u32[]{:S(2)}, u32[]{:S(2)}) collective-permute-start(f32[32,1024]{1,0:T(8,128)} %get-tuple-element.435), channel_id=1, source_target_pairs={{0,16},{4,20},{8,24},{12,28},{16,0},{20,4},{24,8},{28,12},{1,17},{... | collective-permute-start | bytes 393224 | tf_op jit(solution)/shard_map/ppermute | solution.py:378
  486.3 61.8 %collective-permute-start.24 = (f32[32,1024]{1,0:T(8,128)}, f32[32,1024]{1,0:T(8,128)S(1)}, u32[]{:S(2)}, u32[]{:S(2)}) collective-permute-start(f32[32,1024]{1,0:T(8,128)} %get-tuple-element.434), channel_id=1, source_target_pairs={{0,24},{4,28},{8,16},{12,20},{16,8},{20,12},{24,0},{28,4},{1,25},{... | collective-permute-start | bytes 393224 | tf_op jit(solution)/shard_map/ppermute | solution.py:378
  486.7 99.6 %collective-permute-start.31 = (f32[512,1024]{1,0:T(8,128)}, f32[512,1024]{1,0:T(8,128)}, u32[]{:S(2)}, u32[]{:S(2)}) collective-permute-start(f32[512,1024]{1,0:T(8,128)} %constant_dynamic-update-slice_fusion.12), channel_id=1, source_target_pairs={{0,4},{4,0},{8,12},{12,8},{16,20},{20,16},{24,28},{28,24},{1,5},{5... | collective-permute-start | bytes 6291464 | tf_op jit(solution)/shard_map/ppermute | solution.py:378
  529.0 121.1 %collective-permute-start.32 = (f32[512,1024]{1,0:T(8,128)}, f32[512,1024]{1,0:T(8,128)}, u32[]{:S(2)}, u32[]{:S(2)}) collective-permute-start(f32[512,1024]{1,0:T(8,128)} %constant_dynamic-update-slice_fusion.8), channel_id=1, source_target_pairs={{0,4},{4,0},{8,12},{12,8},{16,20},{20,16},{24,28},{28,24},{1,5},{5... | collective-permute-start | bytes 6291464 | tf_op jit(solution)/shard_map/ppermute | solution.py:378
  545.5 16.6 %collective-permute-start.19 = (f32[128,768]{1,0:T(8,128)S(1)}, f32[128,768]{1,0:T(8,128)S(1)}, u32[]{:S(2)}, u32[]{:S(2)}) collective-permute-start(f32[128,768]{1,0:T(8,128)S(1)} %get-tuple-element.426), channel_id=1, source_target_pairs={{0,8},{4,12},{8,0},{12,4},{16,24},{20,28},{24,16},{28,20},{1,9},{5... | collective-permute-start | bytes 1179656 | tf_op jit(solution)/shard_map/ppermute | solution.py:378
  547.2 17.1 %collective-permute-start.20 = (f32[128,768]{1,0:T(8,128)S(1)}, f32[128,768]{1,0:T(8,128)S(1)}, u32[]{:S(2)}, u32[]{:S(2)}) collective-permute-start(f32[128,768]{1,0:T(8,128)S(1)} %get-tuple-element.425), channel_id=1, source_target_pairs={{0,16},{4,20},{8,24},{12,28},{16,0},{20,4},{24,8},{28,12},{1,17},{... | collective-permute-start | bytes 1179656 | tf_op jit(solution)/shard_map/ppermute | solution.py:378
  548.1 33.2 %collective-permute-start.21 = (f32[128,768]{1,0:T(8,128)S(1)}, f32[128,768]{1,0:T(8,128)S(1)}, u32[]{:S(2)}, u32[]{:S(2)}) collective-permute-start(f32[128,768]{1,0:T(8,128)S(1)} %get-tuple-element.424), channel_id=1, source_target_pairs={{0,24},{4,28},{8,16},{12,20},{16,8},{20,12},{24,0},{28,4},{1,25},{... | collective-permute-start | bytes 1179656 | tf_op jit(solution)/shard_map/ppermute | solution.py:378
  582.5 4.2 collective-permute-start.28
  583.7 66.4 %collective-permute-start.25 = (f32[128,768]{1,0:T(8,128)S(1)}, f32[128,768]{1,0:T(8,128)}, u32[]{:S(2)}, u32[]{:S(2)}) collective-permute-start(f32[128,768]{1,0:T(8,128)S(1)} %get-tuple-element.386), channel_id=1, source_target_pairs={{0,8},{4,12},{8,0},{12,4},{16,24},{20,28},{24,16},{28,20},{1,9},{5... | collective-permute-start | bytes 1179656 | tf_op jit(solution)/shard_map/ppermute | solution.py:378
  585.2 65.0 %collective-permute-start.26 = (f32[128,768]{1,0:T(8,128)S(1)}, f32[128,768]{1,0:T(8,128)}, u32[]{:S(2)}, u32[]{:S(2)}) collective-permute-start(f32[128,768]{1,0:T(8,128)S(1)} %get-tuple-element.386), channel_id=1, source_target_pairs={{0,16},{4,20},{8,24},{12,28},{16,0},{20,4},{24,8},{28,12},{1,17},{... | collective-permute-start | bytes 1179656 | tf_op jit(solution)/shard_map/ppermute | solution.py:378
  586.3 63.9 %collective-permute-start.27 = (f32[128,768]{1,0:T(8,128)S(1)}, f32[128,768]{1,0:T(8,128)}, u32[]{:S(2)}, u32[]{:S(2)}) collective-permute-start(f32[128,768]{1,0:T(8,128)S(1)} %get-tuple-element.386), channel_id=1, source_target_pairs={{0,24},{4,28},{8,16},{12,20},{16,8},{20,12},{24,0},{28,4},{1,25},{... | collective-permute-start | bytes 1179656 | tf_op jit(solution)/shard_map/ppermute | solution.py:378
  586.7 36.0 %collective-permute-start.29 = (f32[32,1024]{1,0:T(8,128)S(1)}, f32[32,1024]{1,0:T(8,128)S(1)}, u32[]{:S(2)}, u32[]{:S(2)}) collective-permute-start(f32[32,1024]{1,0:T(8,128)S(1)} %get-tuple-element.384), channel_id=1, source_target_pairs={{0,16},{4,20},{8,24},{12,28},{16,0},{20,4},{24,8},{28,12},{1,17},{... | collective-permute-start | bytes 393224 | tf_op jit(solution)/shard_map/ppermute | solution.py:378
  622.7 27.4 %collective-permute-start.30 = (f32[32,1024]{1,0:T(8,128)S(1)}, f32[32,1024]{1,0:T(8,128)}, u32[]{:S(2)}, u32[]{:S(2)}) collective-permute-start(f32[32,1024]{1,0:T(8,128)S(1)} %get-tuple-element.384), channel_id=1, source_target_pairs={{0,24},{4,28},{8,16},{12,20},{16,8},{20,12},{24,0},{28,4},{1,25},{... | collective-permute-start | bytes 393224 | tf_op jit(solution)/shard_map/ppermute | solution.py:378
  654.3 48.6 %collective-permute-start.33 = (f32[512,768]{0,1:T(8,128)S(1)}, f32[512,768]{0,1:T(8,128)}, u32[]{:S(2)}, u32[]{:S(2)}) collective-permute-start(f32[512,768]{0,1:T(8,128)S(1)} %constant_dynamic-update-slice_fusion.4), channel_id=1, source_target_pairs={{0,4},{4,0},{8,12},{12,8},{16,20},{20,16},{24,28},{28,24},{1,5},{5... | collective-permute-start | bytes 4718600 | tf_op jit(solution)/shard_map/ppermute | solution.py:378
  657.9 43.5 %collective-permute-start.34 = (f32[128,1024]{1,0:T(8,128)S(1)}, f32[128,1024]{1,0:T(8,128)S(1)}, u32[]{:S(2)}, u32[]{:S(2)}) collective-permute-start(f32[128,1024]{1,0:T(8,128)S(1)} %constant_dynamic-update-slice_fusion), channel_id=1, source_target_pairs={{0,4},{4,0},{8,12},{12,8},{16,20},{20,16},{24,28},{28,24},{1,5},{5... | collective-permute-start | bytes 1572872 | tf_op jit(solution)/shard_map/ppermute | solution.py:378
  672.5 29.1 %copy-start.18 = (f32[1024,1024]{1,0:T(8,128)}, f32[1024,1024]{1,0:T(8,128)S(1)}, u32[]{:S(2)}) copy-start(f32[1024,1024]{1,0:T(8,128)S(1)} %fusion.62) | copy-start | bytes 12582916
  672.5 28.9 %copy-start.52 = (f32[256,1024]{1,0:T(8,128)S(1)}, f32[256,1024]{1,0:T(8,128)}, u32[]{:S(2)}) copy-start(f32[256,1024]{1,0:T(8,128)} %param.37) | copy-start | bytes 3145732
  674.1 28.9 %copy-start.27 = (f32[1024,3,256]{0,2,1:T(8,128)S(1)}, f32[1024,3,256]{0,2,1:T(8,128)}, u32[]{:S(2)}) copy-start(f32[1024,3,256]{0,2,1:T(8,128)} %copy.55) | copy-start | bytes 9437188
  674.1 28.9 %copy-start.32 = (f32[512,768]{0,1:T(8,128)S(1)}, f32[512,768]{0,1:T(8,128)}, u32[]{:S(2)}) copy-start(f32[512,768]{0,1:T(8,128)} %copy-done.31) | copy-start | bytes 4718596
  (111 other events, 702.1 us)

commit v3 on v1

v3 whole, which is shorter than its diff:
```python
import functools
import math

import jax
import jax.numpy as jnp
from jax import lax
from jax.experimental import pallas as pl
from jax.experimental.pallas import tpu as pltpu
from jax.sharding import PartitionSpec as P

D = 1024
HEAD = 64
FF = 4096
GRID = 32
NEWTON = 5
STEP = 10


first_decay = 0.9
second_decay = 0.999
adam_rate = 0.3
muon_rate = 0.15
muon_momentum = 0.5
weight_decay = 0.01
newton_terms = (3.4445, -4.775, 2.0315)
gelu_slope = 0.7978845608
gelu_cubic = 0.044715


def layer_norm(values):
    average = jnp.mean(values, axis=-1, keepdims=True)
    centred = values - average
    spread = jnp.mean(centred * centred, axis=-1, keepdims=True)
    return centred * lax.rsqrt(spread + 1e-06)


def entry_piece(hidden, offset, stretch):
    return layer_norm(hidden) * (1.0 + stretch) + offset


def attend_forward(queries, key_rows, value_rows):
    seq_len = queries.shape[0]
    block_rows = min(512, seq_len)
    blocks = queries.reshape(seq_len // block_rows, block_rows, queries.shape[1], queries.shape[2])
    scale_factor = HEAD ** (-0.5)

    def one_block(query_block):
        scores = (
            jnp.einsum("qhe,khe->hqk", query_block, key_rows, preferred_element_type=jnp.float32)
            * scale_factor
        )
        row_peak = jnp.max(scores, axis=-1, keepdims=True)
        weights = jnp.exp(scores - row_peak)
        summed = jnp.sum(weights, axis=-1, keepdims=True)
        soft_low = (weights / summed).astype(jnp.bfloat16)
        context = jnp.einsum(
            "hqk,khe->qhe", soft_low, value_rows, preferred_element_type=jnp.float32
        )
        return (context.astype(jnp.bfloat16), (row_peak + jnp.log(summed))[:, :, 0])

    context, logsum = lax.map(one_block, blocks)
    return (context.reshape(seq_len, -1), logsum)


def attend_backward(queries, key_rows, value_rows, logsum, grad_context):
    seq_len = queries.shape[0]
    block_rows = min(512, seq_len)
    block_count = seq_len // block_rows
    query_blocks = queries.reshape(block_count, block_rows, queries.shape[1], queries.shape[2])
    grad_blocks = grad_context.reshape(block_count, block_rows, queries.shape[1], queries.shape[2])
    scale_factor = HEAD ** (-0.5)

    def one_block(running, pieces):
        grad_keys, grad_values = running
        query_block, grad_block, logsum_block = pieces
        scores = (
            jnp.einsum("qhe,khe->hqk", query_block, key_rows, preferred_element_type=jnp.float32)
            * scale_factor
        )
        weights = jnp.exp(scores - logsum_block[:, :, None])
        soft_low = weights.astype(jnp.bfloat16)
        grad_values = grad_values + jnp.einsum(
            "hqk,qhe->khe", soft_low, grad_block, preferred_element_type=jnp.float32
        )
        grad_weights = jnp.einsum(
            "qhe,khe->hqk", grad_block, value_rows, preferred_element_type=jnp.float32
        )
        grad_scores = weights * (
            grad_weights - jnp.sum(weights * grad_weights, axis=-1, keepdims=True)
        )
        grad_low = grad_scores.astype(jnp.bfloat16)
        grad_query = (
            jnp.einsum("hqk,khe->qhe", grad_low, key_rows, preferred_element_type=jnp.float32)
            * scale_factor
        )
        grad_keys = (
            grad_keys
            + jnp.einsum("hqk,qhe->khe", grad_low, query_block, preferred_element_type=jnp.float32)
            * scale_factor
        )
        return ((grad_keys, grad_values), grad_query)

    start_sums = jnp.zeros(key_rows.shape, jnp.float32)
    finals, grad_queries = lax.scan(
        one_block, (start_sums, start_sums), (query_blocks, grad_blocks, logsum)
    )
    grad_queries = grad_queries.reshape(key_rows.shape)
    return jnp.stack([grad_queries, finals[0], finals[1]], axis=1)


MESH = pl.DeviceIdType.MESH
BLK = 256
LANES = 128
SLAB = 16
UNROLL = 4
MATRICES = 4


def partner(index, bit):
    return index + (1 - 2 * ((index // bit) % 2)) * bit


def bits_of(count):
    found = []
    bit = 1
    while bit < count:
        found.append(bit)
        bit *= 2
    return found


def place_at(axis, bit):
    place = {"wide": lax.axis_index("wide"), "narrow": lax.axis_index("narrow")}
    place[axis] = partner(place[axis], bit)
    return (place["wide"], place["narrow"])


def greet(places):
    barrier = pltpu.get_barrier_semaphore()
    for place in places:
        pl.semaphore_signal(barrier, inc=1, device_id=place, device_id_type=MESH)
    pl.semaphore_wait(barrier, len(places))


def send(src, dst, sends, arrivals, slot, place):
    copy = pltpu.make_async_remote_copy(
        src_ref=src,
        dst_ref=dst,
        send_sem=sends.at[slot],
        recv_sem=arrivals.at[slot],
        device_id=place,
        device_id_type=MESH,
    )
    copy.start()
    return copy


def core_scatter(values):
    rows = values.shape[0] // 2
    side = lax.axis_index("narrow") % 2
    give = lax.dynamic_slice_in_dim(values, (1 - side) * rows, rows, 0)
    keep = lax.dynamic_slice_in_dim(values, side * rows, rows, 0)
    return keep, permute(give, "narrow", 1)


def core_place(half, other):
    side = lax.axis_index("narrow") % 2
    return jnp.where(
        side == 0,
        jnp.concatenate([half, other], axis=0),
        jnp.concatenate([other, half], axis=0),
    )


def permute(values, axis, bit):
    size = lax.axis_size(axis)
    return lax.ppermute(values, axis, [(index, index ^ bit) for index in range(size)])


def together(*values):
    return lax.optimization_barrier(values)


def pair_scatter(values, axis):
    extent = values.shape[axis] // 2
    side = lax.axis_index("wide") % 2
    give = lax.dynamic_slice_in_dim(values, (1 - side) * extent, extent, axis)
    keep = lax.dynamic_slice_in_dim(values, side * extent, extent, axis)
    return keep, permute(give, "wide", 1)


def line_gather(share):
    count = lax.axis_size("wide") // 2
    return [permute(share, "wide", 2 * offset) for offset in range(1, count)]


def line_place(share, arrived):
    count = lax.axis_size("wide") // 2
    rows = share.shape[0]
    place = lax.axis_index("wide") // 2
    whole = jnp.zeros((count * rows,) + share.shape[1:], share.dtype)
    whole = lax.dynamic_update_slice_in_dim(whole, share, place * rows, 0)
    for offset, piece in zip(range(1, count), arrived):
        whole = lax.dynamic_update_slice_in_dim(whole, piece, (place ^ offset) * rows, 0)
    return whole


def pair_place(half, other, axis):
    side = lax.axis_index("wide") % 2
    return jnp.where(
        side == 0,
        jnp.concatenate([half, other], axis=axis),
        jnp.concatenate([other, half], axis=axis),
    )


def own_half(values, axis):
    extent = values.shape[axis] // 2
    side = lax.axis_index("wide") % 2
    return lax.dynamic_slice_in_dim(values, side * extent, extent, axis)


def wide_parts():
    w = lax.axis_index("wide")
    return w % 2, w // 2


def line_partner(z, offset):
    for bit in bits_of(2 * offset):
        if (offset // bit) % 2:
            z = partner(z, bit)
    return z


def block_of(ref, kind, y, z):
    count = lax.axis_size("wide") // 2
    if kind == "rows":
        rows = ref.shape[0] // (2 * count)
        return ref.at[pl.ds(pl.multiple_of((y * count + z) * rows, 8), rows), :]
    rows = ref.shape[0] // count
    if kind == "half":
        return ref.at[pl.ds(pl.multiple_of(z * rows, 8), rows), :]
    columns = ref.shape[1] // 2
    return ref.at[
        pl.ds(pl.multiple_of(z * rows, 8), rows), pl.ds(pl.multiple_of(y * columns, 128), columns)
    ]


def block_shape(shape, kind):
    count = lax.axis_size("wide") // 2
    if kind == "rows":
        return (shape[0] // (2 * count), shape[1])
    if kind == "half":
        return (shape[0] // count, shape[1])
    return (shape[0] // count, shape[1] // 2)


class Scatter:
    def __init__(self, src, kind, held, beside, inbox, sends, arrivals, local, base):
        self.src, self.kind, self.held, self.beside, self.inbox = src, kind, held, beside, inbox
        self.sends, self.arrivals, self.local, self.base = sends, arrivals, local, base
        self.count = lax.axis_size("wide") // 2
        self.copies = {}
        self.loads = {}

    @staticmethod
    def slots():
        return lax.axis_size("wide") - 1

    def start(self):
        y, z = wide_parts()
        for e in reversed(range(self.count)):
            spot = line_partner(z, e)
            load = pltpu.make_async_copy(
                block_of(self.src, self.kind, y, spot), self.held.at[e], self.local.at[e]
            )
            load.start()
            self.loads[e] = load
            if self.kind != "half":
                self.copies[("y", e)] = send(
                    block_of(self.src, self.kind, 1 - y, spot),
                    self.beside.at[e],
                    self.sends,
                    self.arrivals,
                    self.base + e,
                    place_at("wide", 1),
                )

    def step(self, e):
        self.loads[e].wait()
        if self.kind != "half":
            self.copies[("y", e)].wait_recv()
            self.held[e] = self.held[e] + self.beside[e]
        bit = 1
        while bit < self.count and e % (2 * bit) == 0:
            self.copies[("z", e + bit)].wait_recv()
            self.held[e] = self.held[e] + self.inbox[e + bit - 1]
            bit *= 2
        if e:
            low = e & -e
            self.copies[("z", e)] = send(
                self.held.at[e],
                self.inbox.at[e - 1],
                self.sends,
                self.arrivals,
                self.base + self.count + e - 1,
                place_at("wide", 2 * low),
            )

    def finish(self):
        for copy in self.copies.values():
            copy.wait_send()


def scatter_scratch(shape, kind):
    count = lax.axis_size("wide") // 2
    block = block_shape(shape, kind)
    return [
        pltpu.VMEM((count,) + block, jnp.float32),
        pltpu.VMEM((count if kind != "half" else 1,) + block, jnp.float32),
        pltpu.VMEM((max(count - 1, 1),) + block, jnp.float32),
        pltpu.SemaphoreType.DMA((count,)),
    ]


class Gather:
    def __init__(self, own, spot_of, hops, sends, arrivals, base):
        self.own, self.spot_of, self.hops = own, spot_of, hops
        self.sends, self.arrivals, self.base = sends, arrivals, base
        self.copies = {}
        self.order = sorted(range(2 ** len(hops)), key=lambda item: (bin(item).count("1"), item))

    def step(self, item):
        if item:
            self.copies[item].wait_recv()
        for index in reversed(range(item.bit_length(), len(self.hops))):
            later = item + 2**index
            spot = self.spot_of(item)
            axis, bit = self.hops[index]
            self.copies[later] = send(
                spot if item else self.own,
                spot,
                self.sends,
                self.arrivals,
                self.base + later - 1,
                place_at(axis, bit),
            )

    def finish(self):
        for copy in self.copies.values():
            copy.wait_send()


def line_hops():
    return [("wide", bit) for bit in reversed(bits_of(lax.axis_size("wide"))) if bit > 1]


class NarrowSum:
    def __init__(self, far_bits, pieces, x, o, near, far, held, sends, arrivals, local, base):
        self.bits, self.pieces = far_bits, pieces
        self.x, self.o, self.near, self.far, self.held = x, o, near, far, held
        self.sends, self.arrivals, self.local, self.base = sends, arrivals, local, base
        self.rows = x.shape[0] // 2
        self.core = lax.axis_index("narrow") % 2
        self.copies = []
        self.cross = {}
        self.keeps = []

    def block(self, side, p):
        step = self.rows // self.pieces
        return pl.ds(pl.multiple_of(side * self.rows + p * step, 8), step)

    def push(self, src, dst, slot, bit):
        copy = send(
            src, dst, self.sends, self.arrivals, self.base + slot, place_at("narrow", bit)
        )
        self.copies.append(copy)
        return copy

    def start(self):
        self.first = [
            self.push(self.x.at[self.block(1 - self.core, p)], self.near.at[p], p, 1)
            for p in range(self.pieces)
        ]
        self.loads = [
            pltpu.make_async_copy(
                self.x.at[self.block(self.core, p)], self.held.at[0, p], self.local.at[p]
            )
            for p in range(self.pieces)
        ]
        for load in self.loads:
            load.start()

    def hop(self, b, p):
        slot = (b + 1) * self.pieces + p
        self.cross[(b, p)] = self.push(
            self.held.at[b, p], self.far.at[b, p], slot, self.bits[b]
        )

    def begin(self, p):
        self.loads[p].wait()
        self.first[p].wait_recv()
        self.held[0, p] = self.held[0, p] + self.near[p]
        self.hop(0, p)

    def step(self, b, p):
        self.cross[(b, p)].wait_recv()
        self.held[b + 1, p] = self.held[b, p] + self.far[b, p]
        if b + 1 < len(self.bits):
            self.hop(b + 1, p)
            return
        spot = self.o.at[self.block(self.core, p)]
        slot = (b + 2) * self.pieces + p
        self.keeps.append(self.push(self.held.at[b + 1, p], spot, slot, 1))
        keep = pltpu.make_async_copy(self.held.at[b + 1, p], spot, self.local.at[p])
        keep.start()
        self.loads[p] = keep

    def finish(self):
        for copy in self.keeps:
            copy.wait_recv()
        for keep in self.loads:
            keep.wait()
        for copy in self.copies:
            copy.wait_send()


def narrow_scratch(shape, pieces):
    count = len(bits_of(lax.axis_size("narrow"))) - 1
    step = shape[0] // (2 * pieces)
    return [
        pltpu.VMEM((pieces, step, shape[1]), jnp.float32),
        pltpu.VMEM((count, pieces, step, shape[1]), jnp.float32),
        pltpu.VMEM((count + 1, pieces, step, shape[1]), jnp.float32),
        pltpu.SemaphoreType.DMA((pieces,)),
    ]


def sum_scatter_kernel(kinds, pieces, x_ref, *refs):
    total = len(kinds)
    sources, refs = refs[:total], refs[total:]
    o_ref, shares, refs = refs[0], refs[1 : 1 + total], refs[1 + total :]
    near, far, held, local = refs[:4]
    refs = refs[4:]
    sends, arrivals = refs[-2:]
    far_bits = bits_of(lax.axis_size("narrow"))[1:]
    wide_bits = bits_of(lax.axis_size("wide")) if total else []
    if total and all(kind == "half" for kind in kinds):
        wide_bits = wide_bits[1:]
    greet(
        [place_at("narrow", bit) for bit in [1] + far_bits]
        + [place_at("wide", bit) for bit in wide_bits]
    )
    base = (len(far_bits) + 2) * pieces
    narrow = NarrowSum(far_bits, pieces, x_ref, o_ref, near, far, held, sends, arrivals, local, 0)
    scatters = []
    for index, kind in enumerate(kinds):
        block, beside, inbox, loads = refs[4 * index : 4 * index + 4]
        scatters.append(
            Scatter(sources[index], kind, block, beside, inbox, sends, arrivals, loads, base)
        )
        base += Scatter.slots()
    narrow.start()
    for scatter in scatters:
        scatter.start()
    for p in range(pieces):
        narrow.begin(p)
    count = lax.axis_size("wide") // 2
    for scatter in scatters:
        if scatter.kind == "half":
            for e in reversed(range(1, count)):
                if e % 2:
                    scatter.step(e)
    left = {
        index: [
            e for e in reversed(range(count)) if scatter.kind != "half" or e % 2 == 0
        ]
        for index, scatter in enumerate(scatters)
    }
    for b in range(len(far_bits)):
        for p in range(pieces):
            narrow.step(b, p)
            for index, scatter in enumerate(scatters):
                if len(left[index]) > 1:
                    scatter.step(left[index].pop(0))
    outs = []
    for index, scatter in enumerate(scatters):
        while left[index]:
            scatter.step(left[index].pop(0))
        out = pltpu.make_async_copy(scatter.held.at[0], shares[index], scatter.local.at[0])
        out.start()
        outs.append(out)
    narrow.finish()
    for scatter in scatters:
        scatter.finish()
    for out in outs:
        out.wait()


def sum_scatter(values, gradients, kinds, number):
    pieces = 4
    narrow_bits = bits_of(lax.axis_size("narrow"))
    slots = (len(narrow_bits) + 1) * pieces + len(kinds) * Scatter.slots()
    anywhere = pl.BlockSpec(memory_space=pl.ANY)
    scratch = narrow_scratch(values.shape, pieces)
    shapes = [jax.ShapeDtypeStruct(values.shape, jnp.float32)]
    for gradient, kind in zip(gradients, kinds):
        scratch += scatter_scratch(gradient.shape, kind)
        shapes.append(jax.ShapeDtypeStruct(block_shape(gradient.shape, kind), jnp.float32))
    scratch += [pltpu.SemaphoreType.DMA((slots,)), pltpu.SemaphoreType.DMA((slots,))]
    return pl.pallas_call(
        functools.partial(sum_scatter_kernel, kinds, pieces),
        out_shape=tuple(shapes),
        in_specs=[anywhere] * (1 + len(kinds)),
        out_specs=(anywhere,) * len(shapes),
        scratch_shapes=scratch,
        compiler_params=pltpu.CompilerParams(
            collective_id=number, has_side_effects=True, vmem_limit_bytes=40 * 2**20
        ),
        cost_estimate=pl.CostEstimate(
            flops=values.size, bytes_accessed=values.size * 32, transcendentals=0
        ),
    )(values, *gradients)


def small_kernel(shared_rows, split_rows, x_ref, share_ref, o_ref, norm_ref, half_ref, *refs):
    slots, spare, spare_in, sends, arrivals, local = refs
    wide_bits = bits_of(lax.axis_size("wide"))
    narrow_bits = bits_of(lax.axis_size("narrow"))
    greet(
        [place_at("wide", bit) for bit in wide_bits]
        + [place_at("narrow", bit) for bit in narrow_bits]
    )
    y, z = wide_parts()
    count = len(wide_bits)
    copies = []
    slots[0] = x_ref[...]
    hops = line_hops()

    def spot_of(item):
        spot = z
        for index, (_, bit) in enumerate(hops):
            if (item >> index) % 2:
                spot = partner(spot, bit // 2)
        return block_of(half_ref, "half", y, spot)

    gather = Gather(share_ref, spot_of, hops, sends, arrivals, count + len(narrow_bits))
    keep = pltpu.make_async_copy(share_ref, spot_of(0), local.at[0])
    keep.start()
    for b in range(count):
        copy = send(
            slots.at[b], slots.at[count + 1 + b], sends, arrivals, b, place_at("wide", wide_bits[b])
        )
        copies.append(copy)
        copy.wait_recv()
        slots[b + 1] = slots[b] + slots[count + 1 + b]
    gather.step(0)
    total = slots[count]
    o_ref[...] = total
    shared_part = total[:shared_rows]
    split_part = total[shared_rows : shared_rows + split_rows]
    shared = jnp.sum(shared_part * shared_part)
    split_sum = jnp.sum(split_part * split_part) + jnp.sum(
        total[shared_rows + split_rows : shared_rows + split_rows + 1]
    )
    spare[0] = jnp.full(spare.shape[1:], split_sum, jnp.float32)
    for b in range(len(narrow_bits)):
        copy = send(
            spare.at[b], spare_in.at[b], sends, arrivals, count + b, place_at("narrow", narrow_bits[b])
        )
        copies.append(copy)
        copy.wait_recv()
        spare[b + 1] = spare[b] + spare_in[b]
    norm_ref[...] = jnp.sqrt(spare[len(narrow_bits)] + shared)
    for item in gather.order[1:]:
        gather.step(item)
    keep.wait()
    gather.finish()
    for copy in copies:
        copy.wait_send()


def small_sums(stacked, share, shared_rows, split_rows, number):
    wide_bits = bits_of(lax.axis_size("wide"))
    narrow_bits = bits_of(lax.axis_size("narrow"))
    vmem = pl.BlockSpec(memory_space=pltpu.VMEM)
    anywhere = pl.BlockSpec(memory_space=pl.ANY)
    count = len(wide_bits)
    line = lax.axis_size("wide") // 2
    total = count + len(narrow_bits) + line - 1
    return pl.pallas_call(
        functools.partial(small_kernel, shared_rows, split_rows),
        out_shape=(
            jax.ShapeDtypeStruct(stacked.shape, jnp.float32),
            jax.ShapeDtypeStruct((8, LANES), jnp.float32),
            jax.ShapeDtypeStruct((line * share.shape[0], share.shape[1]), jnp.float32),
        ),
        in_specs=[vmem, vmem],
        out_specs=(vmem, vmem, anywhere),
        scratch_shapes=[
            pltpu.VMEM((2 * count + 1,) + stacked.shape, jnp.float32),
            pltpu.VMEM((len(narrow_bits) + 1, 8, LANES), jnp.float32),
            pltpu.VMEM((len(narrow_bits), 8, LANES), jnp.float32),
            pltpu.SemaphoreType.DMA((total,)),
            pltpu.SemaphoreType.DMA((total,)),
            pltpu.SemaphoreType.DMA((1,)),
        ],
        compiler_params=pltpu.CompilerParams(
            collective_id=number, has_side_effects=True, vmem_limit_bytes=16 * 2**20
        ),
    )(stacked, share)


def gram_kernel(narrow_bits, hops, x_ref, o_ref, halves, inbox, beside, sends, arrivals, local):
    parts, rows = x_ref.shape[0], x_ref.shape[1] // 2
    sub = parts // MATRICES
    w, n = lax.axis_index("wide"), lax.axis_index("narrow")
    y = w % 2
    greeted = {("narrow", bit) for bit in narrow_bits} | set(hops)
    greet([place_at(axis, bit) for axis, bit in sorted(greeted)])
    load = pltpu.make_async_copy(x_ref, halves, local.at[0])
    load.start()
    load.wait()
    base = 0 * n
    size, at, slot = parts, 0, 0
    for bit in reversed(narrow_bits):
        size //= 2
        side = (n // bit) % 2
        copy = send(
            halves.at[pl.ds(base + (1 - side) * size, size)],
            inbox.at[pl.ds(at, size)],
            sends,
            arrivals,
            slot,
            place_at("narrow", bit),
        )
        base = base + side * size
        copy.wait()
        for s in range(size):
            halves[base + s] = halves[base + s] + inbox[at + s]
        at += size
        slot += 1
    row_half = lambda side: pl.ds(pl.multiple_of(side * rows, 8), rows)
    copy = send(
        halves.at[n, row_half(1 - y)], beside.at[0], sends, arrivals, slot, place_at("wide", 1)
    )
    copy.wait()
    beside[1] = halves[n, row_half(y)] + beside[0]
    slot += 1

    def spot_of(item):
        big, small = w, n % sub
        for index, (axis, bit) in enumerate(hops):
            if (item >> index) % 2:
                if axis == "wide":
                    big = partner(big, bit)
                else:
                    small = partner(small, bit)
        start = ((big // 2) * (2 * sub) + small * 2 + big % 2) * rows
        return o_ref.at[pl.ds(pl.multiple_of(start, 8), rows), :]

    keep = pltpu.make_async_copy(beside.at[1], spot_of(0), local.at[0])
    keep.start()
    gather = Gather(beside.at[1], spot_of, hops, sends, arrivals, slot)
    for item in gather.order:
        gather.step(item)
    keep.wait()
    gather.finish()


def gram_whole(partial, number):
    narrow_bits = bits_of(lax.axis_size("narrow"))
    wide_bits = bits_of(lax.axis_size("wide"))
    parts, rows, band = partial.shape
    sub = parts // MATRICES
    hops = [("narrow", bit) for bit in bits_of(sub)]
    hops += [("wide", bit) for bit in reversed(wide_bits)]
    slots = len(narrow_bits) + 2 ** len(hops)
    return pl.pallas_call(
        functools.partial(gram_kernel, narrow_bits, hops),
        out_shape=jax.ShapeDtypeStruct((rows * sub * len_of_line(), band), jnp.float32),
        in_specs=[pl.BlockSpec(memory_space=pl.ANY)],
        out_specs=pl.BlockSpec(memory_space=pl.ANY),
        scratch_shapes=[
            pltpu.VMEM(partial.shape, jnp.float32),
            pltpu.VMEM(partial.shape, jnp.float32),
            pltpu.VMEM((2, rows // 2, band), jnp.float32),
            pltpu.SemaphoreType.DMA((slots,)),
            pltpu.SemaphoreType.DMA((slots,)),
            pltpu.SemaphoreType.DMA((1,)),
        ],
        compiler_params=pltpu.CompilerParams(
            collective_id=number, has_side_effects=True, vmem_limit_bytes=24 * 2**20
        ),
    )(partial)


def len_of_line():
    return lax.axis_size("wide") // 2


def split(values):
    high = values.astype(jnp.bfloat16)
    return high, (values - high.astype(jnp.float32)).astype(jnp.bfloat16)


def product(left_high, left_low, right_high, right_low):
    dot = functools.partial(jnp.dot, preferred_element_type=jnp.float32)
    return dot(left_high, right_high) + (dot(left_high, right_low) + dot(left_low, right_high))


def polar_kernel(g_ref, q_ref, gh, gl, ph, pw, th, tl):
    size = g_ref.shape[0]
    blocks = size // BLK
    first, second, third = newton_terms
    rows = lambda block: pl.ds(block * BLK, BLK)
    square = (BLK, BLK)
    unit = (
        lax.broadcasted_iota(jnp.int32, square, 0) == lax.broadcasted_iota(jnp.int32, square, 1)
    ).astype(jnp.float32)
    count = size // LANES
    lanes = lambda block: pl.ds((block % count) * LANES, LANES)
    trace = jnp.zeros((), jnp.float32)
    for i in range(count):
        trace = trace + jnp.sum(g_ref[lanes(i), lanes(0)] * unit[:LANES, :LANES])
    factor = 1.0 / (jnp.sqrt(trace) + 1e-07)
    for i in range(count):
        for j in range(count // 2 + 1):
            values = g_ref[lanes(i), lanes(j)] * (factor * factor)
            gh[lanes(i), lanes(i + j)], gl[lanes(i), lanes(i + j)] = split(values)
            if 0 < j < count // 2:
                values = values.T
                gh[lanes(i + j), lanes(i)], gl[lanes(i + j), lanes(i)] = split(values)

    def put(high, low, i, j, values):
        high[rows(i), rows(j)], low[rows(i), rows(j)] = split(values)
        if i != j:
            high[rows(j), rows(i)], low[rows(j), rows(i)] = split(values.T)

    def symmetric(left, right, emit):
        for i in range(blocks):
            columns = pl.ds(i * BLK, size - i * BLK)
            values = product(
                left[0][rows(i), :], left[1][rows(i), :], right[0][:, columns], right[1][:, columns]
            )
            for j in range(i, blocks):
                emit(i, j, values[:, (j - i) * BLK : (j - i + 1) * BLK])

    def emit_terms(i, j, values):
        gram = gh[rows(i), rows(j)].astype(jnp.float32) + gl[rows(i), rows(j)].astype(jnp.float32)
        terms = second * gram + third * values
        if i == j:
            terms = terms + first * unit
        put(ph, pw, i, j, terms)

    def emit_total(i, j, values):
        q_ref[rows(i), rows(j)] = values
        if i != j:
            q_ref[rows(j), rows(i)] = values.T

    symmetric((gh, gl), (gh, gl), emit_terms)
    for i in range(blocks):
        q_ref[rows(i), :] = (
            ph[rows(i), :].astype(jnp.float32) + pw[rows(i), :].astype(jnp.float32)
        ) * factor

    def one_step(step, carry):
        symmetric((ph, pw), (gh, gl), functools.partial(put, th, tl))
        symmetric((th, tl), (ph, pw), functools.partial(put, gh, gl))
        symmetric((gh, gl), (gh, gl), emit_terms)
        for i in range(blocks):
            th[rows(i), :], tl[rows(i), :] = split(q_ref[rows(i), :])
        symmetric((ph, pw), (th, tl), emit_total)
        return carry

    lax.fori_loop(0, NEWTON - 1, one_step, 0)


def polar_factor(gramian):
    size = gramian.shape[0]
    vmem = pl.BlockSpec(memory_space=pltpu.VMEM)
    return pl.pallas_call(
        polar_kernel,
        out_shape=jax.ShapeDtypeStruct((size, size), jnp.float32),
        in_specs=[vmem],
        out_specs=vmem,
        scratch_shapes=[pltpu.VMEM((size, size), jnp.bfloat16)] * 6,
        compiler_params=pltpu.CompilerParams(vmem_limit_bytes=48 * 2**20),
        cost_estimate=pl.CostEstimate(
            flops=17 * 6 * size**3, bytes_accessed=8 * size * size, transcendentals=0
        ),
    )(gramian)


def spread_kernel(sub, pieces, q_ref, o_ref, sends, arrivals, local):
    size = q_ref.shape[0]
    half = size // 2
    step = half // pieces
    w, n = lax.axis_index("wide"), lax.axis_index("narrow")
    own = n // sub
    across = partner(own, 2)
    near_place, far_place = place_at("narrow", sub), place_at("narrow", 2 * sub)
    side_place = place_at("wide", 1)
    greet([near_place, far_place, side_place])
    top = w % 2
    rows = lambda side, p: pl.ds(pl.multiple_of(side * half + p * step, 8), step)
    keep = pltpu.make_async_copy(q_ref, o_ref.at[own], local.at[0])
    keep.start()
    copies = []

    def push(src, dst, place):
        copies.append(send(src, dst, sends, arrivals, len(copies), place))
        return copies[-1]

    cross = lambda p: push(q_ref.at[rows(top, p)], o_ref.at[own, rows(top, p)], far_place)
    crossing = [cross(p) for p in range(2)]
    landing = [push(q_ref, o_ref.at[own], near_place)]
    aside = []
    for p in range(pieces):
        crossing[p].wait()
        if p + 2 < pieces:
            crossing.append(cross(p + 2))
        if p >= 2:
            aside[p - 2].wait()
        spot = o_ref.at[across, rows(top, p)]
        aside.append(push(spot, spot, side_place))
        landing.append(push(spot, spot, near_place))
        if p >= 2:
            spot = o_ref.at[across, rows(1 - top, p - 2)]
            landing.append(push(spot, spot, near_place))
    for p in range(pieces - 2, pieces):
        aside[p].wait()
        spot = o_ref.at[across, rows(1 - top, p)]
        landing.append(push(spot, spot, near_place))
    keep.wait()
    for copy in landing:
        copy.wait_send()
    for copy in landing:
        copy.wait_recv()


def spread(factor, number):
    size = factor.shape[0]
    pieces = 8
    slots = 1 + 4 * pieces
    sub = lax.axis_size("narrow") // MATRICES
    return pl.pallas_call(
        functools.partial(spread_kernel, sub, pieces),
        out_shape=jax.ShapeDtypeStruct((MATRICES, size, size), jnp.float32),
        in_specs=[pl.BlockSpec(memory_space=pltpu.VMEM)],
        out_specs=pl.BlockSpec(memory_space=pl.ANY),
        scratch_shapes=[
            pltpu.SemaphoreType.DMA((slots,)),
            pltpu.SemaphoreType.DMA((slots,)),
            pltpu.SemaphoreType.DMA((1,)),
        ],
        compiler_params=pltpu.CompilerParams(collective_id=number, has_side_effects=True),
    )(factor)


def adam_update(weight, moment, square, gradient):
    moment_new = first_decay * moment + (1.0 - first_decay) * gradient
    square_new = second_decay * square + (1.0 - second_decay) * gradient * gradient
    moment_hat = moment_new / (1.0 - first_decay**STEP)
    square_hat = square_new / (1.0 - second_decay**STEP)
    weight_new = weight * (1.0 - adam_rate * weight_decay) - adam_rate * moment_hat / (
        jnp.sqrt(square_hat) + 1e-08
    )
    return (moment_new, square_new, weight_new)


def muon_finish(weight, polar_part, longest):
    return (
        weight * (1.0 - muon_rate * weight_decay)
        - muon_rate * 0.2 * math.sqrt(longest) * polar_part
    )


def column_shifts(strip, column):
    rows = strip.shape[0]
    left = jnp.where(column == 0, 0.0, pltpu.roll(strip, 1, 0))
    right = jnp.where(column == rows - 1, 0.0, pltpu.roll(strip, rows - 1, 0))
    return (left, strip, right)


def tap_rows(shifts, taps):
    return [
        taps[3 * i] * shifts[0] + taps[3 * i + 1] * shifts[1] + taps[3 * i + 2] * shifts[2]
        for i in range(3)
    ]


def strip_at(index):
    return pl.ds(pl.multiple_of(index * GRID, GRID), GRID)


def convolve(load, taps, emit):
    shape = load(0).shape
    column = lax.broadcasted_iota(jnp.int32, shape, 0)

    def one(r, carry):
        above, here = carry
        upper, middle, lower = tap_rows(column_shifts(load(r), column), taps)
        emit(r - 1, here + lower)
        return (upper, above + middle)

    upper, middle, _ = tap_rows(column_shifts(load(0), column), taps)
    above, here = lax.fori_loop(1, GRID, one, (upper, middle))
    emit(GRID - 1, here)


def kernel_sums(load, weigh, width):
    column = lax.broadcasted_iota(jnp.int32, (GRID, width), 0)
    fold = lambda values: values.reshape(GRID // 8, 8, width).sum(axis=0)
    zero = jnp.zeros((8, width), jnp.float32)

    def one(r, carry):
        sums = carry
        shifts = column_shifts(load(r), column)
        later = weigh(jnp.minimum(r + 1, GRID - 1)) * jnp.where(r < GRID - 1, 1.0, 0.0)
        earlier = weigh(jnp.maximum(r - 1, 0)) * jnp.where(r > 0, 1.0, 0.0)
        terms = (later, weigh(r), earlier)
        return tuple(
            sums[3 * i + j] + fold(terms[i] * shifts[j]) for i in range(3) for j in range(3)
        )

    return lax.fori_loop(0, GRID, one, (zero,) * 9)


def middle_kernel(
    entry_ref,
    entry_t_ref,
    grad_ffn_ref,
    expand_ref,
    reduce_ref,
    taps_ref,
    ffn_ref,
    entry_grad_ref,
    grad_reduce_ref,
    grad_expand_ref,
    grad_taps_ref,
    upward,
    slope,
    weight,
    active,
    grad_up,
):
    width = expand_ref.shape[1]
    step = pl.program_id(0)

    def dot(left, right, dims):
        return lax.dot_general(left, right, (dims, ((), ())), preferred_element_type=jnp.float32)

    taps = [taps_ref[t : t + 1, :] for t in range(9)]
    upward[...] = dot(entry_ref[...], expand_ref[...], ((1,), (0,)))
    weight[...] = dot(grad_ffn_ref[...], reduce_ref[...], ((1,), (1,)))

    def emit_middle(r, z):
        inner = gelu_slope * (z + gelu_cubic * z * z * z)
        bent = jnp.tanh(inner)
        active[strip_at(r), :] = (0.5 * z * (1.0 + bent)).astype(jnp.bfloat16)
        turn = 0.5 * (1.0 + bent) + 0.5 * z * (1.0 - bent * bent) * (
            gelu_slope * (1.0 + 3.0 * gelu_cubic * z * z)
        )
        weight[strip_at(r), :] = weight[strip_at(r), :] * turn

    convolve(lambda r: upward[strip_at(r), :], taps, emit_middle)

    def emit_grad(r, values):
        grad_up[strip_at(r), :] = values.astype(jnp.bfloat16)

    convolve(lambda r: weight[strip_at(r), :], taps[::-1], emit_grad)
    sums = kernel_sums(lambda r: upward[strip_at(r), :], lambda r: weight[strip_at(r), :], width)
    for t in range(9):
        grad_taps_ref[t : t + 1, :] = jnp.sum(sums[t], axis=0, keepdims=True)
    grad_reduce_ref[...] = dot(active[...], grad_ffn_ref[...], ((0,), (0,)))
    grad_expand_ref[...] = dot(entry_t_ref[...], grad_up[...], ((1,), (0,)))
    ffn = dot(active[...], reduce_ref[...], ((1,), (0,)))
    back = dot(grad_up[...], expand_ref[...], ((1,), (1,)))

    @pl.when(step == 0)
    def _():
        ffn_ref[...] = ffn
        entry_grad_ref[...] = back

    @pl.when(step > 0)
    def _():
        ffn_ref[...] += ffn
        entry_grad_ref[...] += back


def middle(entry, grad_ffn, expand, reduce, taps):
    tokens, width = entry.shape
    hidden_units = expand.shape[1]
    block = min(256, hidden_units)
    whole = lambda shape: pl.BlockSpec(shape, lambda i: (0, 0))
    f32 = lambda *shape: jax.ShapeDtypeStruct(shape, jnp.float32)
    return pl.pallas_call(
        middle_kernel,
        grid=(hidden_units // block,),
        out_shape=(
            f32(tokens, width),
            f32(tokens, width),
            f32(hidden_units, width),
            f32(width, hidden_units),
            f32(9, hidden_units),
        ),
        in_specs=[
            whole((tokens, width)),
            whole((width, tokens)),
            whole((tokens, width)),
            pl.BlockSpec((width, block), lambda i: (0, i)),
            pl.BlockSpec((block, width), lambda i: (i, 0)),
            pl.BlockSpec((9, block), lambda i: (0, i)),
        ],
        out_specs=(
            whole((tokens, width)),
            whole((tokens, width)),
            pl.BlockSpec((block, width), lambda i: (i, 0)),
            pl.BlockSpec((width, block), lambda i: (0, i)),
            pl.BlockSpec((9, block), lambda i: (0, i)),
        ),
        scratch_shapes=[
            pltpu.VMEM((tokens, block), jnp.float32),
            pltpu.VMEM((tokens, block), jnp.float32),
            pltpu.VMEM((tokens, block), jnp.float32),
            pltpu.VMEM((tokens, block), jnp.bfloat16),
            pltpu.VMEM((tokens, block), jnp.bfloat16),
        ],
        compiler_params=pltpu.CompilerParams(vmem_limit_bytes=52 * 2**20),
        cost_estimate=pl.CostEstimate(
            flops=12 * tokens * width * hidden_units,
            bytes_accessed=32 * tokens * width,
            transcendentals=tokens * hidden_units,
        ),
    )(entry, entry.T, grad_ffn, expand, reduce, taps)


def norm_strip(values):
    average = jnp.mean(values, axis=-1, keepdims=True)
    centred = values - average
    spread_of = jnp.mean(centred * centred, axis=-1, keepdims=True)
    inverse = lax.rsqrt(spread_of + 1e-06)
    return centred * inverse, inverse


def slab_at(index):
    return pl.ds(pl.multiple_of(index * SLAB, SLAB), SLAB)


def fold_rows(values):
    return values.reshape(values.shape[0] // 8, 8, values.shape[1]).sum(axis=0)


def mixer_kernel_forward(tokens_ref, shift_ref, scale_ref, taps_ref, out_ref, entered):
    stretch = 1.0 + scale_ref[...]
    offset = shift_ref[...]

    def enter(r, carry):
        normed, _ = norm_strip(tokens_ref[slab_at(r), :].astype(jnp.float32))
        entered[slab_at(r), :] = normed * stretch + offset
        return carry

    rows, width = tokens_ref.shape
    lax.fori_loop(0, rows // SLAB, enter, 0, unroll=UNROLL)
    for start in range(0, width, BLK):
        lanes = pl.ds(start, BLK)

        def emit(r, values, lanes=lanes):
            out_ref[strip_at(r), lanes] = values.astype(jnp.bfloat16)

        taps = [taps_ref[t : t + 1, lanes] for t in range(9)]
        convolve(lambda r, lanes=lanes: entered[strip_at(r), lanes], taps, emit)


def mixer_forward(tokens, shift, scale, taps):
    rows, width = tokens.shape
    vmem = pl.BlockSpec(memory_space=pltpu.VMEM)
    return pl.pallas_call(
        mixer_kernel_forward,
        out_shape=jax.ShapeDtypeStruct((rows, width), jnp.bfloat16),
        in_specs=[vmem] * 4,
        out_specs=vmem,
        scratch_shapes=[pltpu.VMEM((rows, width), jnp.float32)],
        compiler_params=pltpu.CompilerParams(vmem_limit_bytes=40 * 2**20),
        cost_estimate=pl.CostEstimate(
            flops=40 * rows * width, bytes_accessed=4 * rows * width, transcendentals=0
        ),
    )(tokens, shift, scale, taps)


def mixer_kernel_backward(
    tokens_ref,
    shift_ref,
    scale_ref,
    taps_ref,
    grad_mixed_ref,
    grad_hidden_ref,
    out_ref,
    grad_taps_ref,
    grad_shift_ref,
    grad_scale_ref,
    normed_ref,
    back_ref,
    inverse_ref,
):
    width = tokens_ref.shape[1]
    stretch = 1.0 + scale_ref[...]

    def enter(r, carry):
        normed, inverse = norm_strip(tokens_ref[slab_at(r), :].astype(jnp.float32))
        normed_ref[slab_at(r), :] = normed
        inverse_ref[slab_at(r), :] = jnp.broadcast_to(inverse, (SLAB, LANES))
        return carry

    rows = tokens_ref.shape[0]
    lax.fori_loop(0, rows // SLAB, enter, 0, unroll=UNROLL)
    for start in range(0, width, BLK):
        lanes = pl.ds(start, BLK)
        taps = [taps_ref[t : t + 1, lanes] for t in range(9)]
        stretch_part = 1.0 + scale_ref[:, lanes]
        offset_part = shift_ref[:, lanes]

        def emit(r, values, lanes=lanes):
            back_ref[strip_at(r), lanes] = values

        def entered(r, lanes=lanes, stretch_part=stretch_part, offset_part=offset_part):
            return normed_ref[strip_at(r), lanes] * stretch_part + offset_part

        weigh = lambda r, lanes=lanes: grad_mixed_ref[strip_at(r), lanes]
        convolve(weigh, taps[::-1], emit)
        sums = kernel_sums(entered, weigh, BLK)
        for t in range(9):
            grad_taps_ref[t : t + 1, lanes] = jnp.sum(sums[t], axis=0, keepdims=True)

    def leave(r, carry):
        shifts, scales = carry
        normed = normed_ref[slab_at(r), :]
        back = back_ref[slab_at(r), :]
        stretched = back * stretch
        first = jnp.mean(stretched, axis=-1, keepdims=True)
        second = jnp.mean(stretched * normed, axis=-1, keepdims=True)
        inverse = inverse_ref[slab_at(r), :][:, :1]
        out = grad_hidden_ref[slab_at(r), :] + (stretched - first - normed * second) * inverse
        out_ref[slab_at(r), :] = out.astype(jnp.bfloat16)
        return shifts + fold_rows(back), scales + fold_rows(back * normed)

    zero = jnp.zeros((8, width), jnp.float32)
    shifts, scales = lax.fori_loop(0, rows // SLAB, leave, (zero, zero), unroll=UNROLL)
    grad_shift_ref[...] = jnp.sum(shifts, axis=0, keepdims=True)
    grad_scale_ref[...] = jnp.sum(scales, axis=0, keepdims=True)


def mixer_backward(tokens, shift, scale, taps, grad_mixed, grad_hidden):
    rows, width = tokens.shape
    vmem = pl.BlockSpec(memory_space=pltpu.VMEM)
    f32 = lambda *shape: jax.ShapeDtypeStruct(shape, jnp.float32)
    return pl.pallas_call(
        mixer_kernel_backward,
        out_shape=(
            jax.ShapeDtypeStruct((rows, width), jnp.bfloat16),
            f32(9, width),
            f32(1, width),
            f32(1, width),
        ),
        in_specs=[vmem] * 6,
        out_specs=(vmem,) * 4,
        scratch_shapes=[
            pltpu.VMEM((rows, width), jnp.float32),
            pltpu.VMEM((rows, width), jnp.float32),
            pltpu.VMEM((rows, LANES), jnp.float32),
        ],
        compiler_params=pltpu.CompilerParams(vmem_limit_bytes=48 * 2**20),
        cost_estimate=pl.CostEstimate(
            flops=100 * rows * width, bytes_accessed=12 * rows * width, transcendentals=0
        ),
    )(tokens, shift, scale, taps, grad_mixed, grad_hidden)


def hidden_kernel_backward(
    hidden_ref,
    branch_ref,
    grad_entry_ref,
    grad_ffn_ref,
    scale_ref,
    gate_ref,
    grad_hidden_ref,
    grad_branch_ref,
    grad_shift_ref,
    grad_scale_ref,
    grad_gate_ref,
):
    width = hidden_ref.shape[1]
    stretch = 1.0 + scale_ref[...]
    gate = gate_ref[...]

    def one(r, carry):
        shifts, scales, gates = carry
        normed, inverse = norm_strip(hidden_ref[slab_at(r), :])
        back = grad_entry_ref[slab_at(r), :]
        stretched = back * stretch
        first = jnp.mean(stretched, axis=-1, keepdims=True)
        second = jnp.mean(stretched * normed, axis=-1, keepdims=True)
        grad = grad_ffn_ref[slab_at(r), :].astype(jnp.float32) + (
            stretched - first - normed * second
        ) * inverse
        grad_hidden_ref[slab_at(r), :] = grad
        grad_branch_ref[slab_at(r), :] = (gate * grad).astype(jnp.bfloat16)
        return (
            shifts + fold_rows(back),
            scales + fold_rows(back * normed),
            gates + fold_rows(branch_ref[slab_at(r), :] * grad),
        )

    zero = jnp.zeros((8, width), jnp.float32)
    shifts, scales, gates = lax.fori_loop(
        0, hidden_ref.shape[0] // SLAB, one, (zero, zero, zero), unroll=UNROLL
    )
    grad_shift_ref[...] = jnp.sum(shifts, axis=0, keepdims=True)
    grad_scale_ref[...] = jnp.sum(scales, axis=0, keepdims=True)
    grad_gate_ref[...] = jnp.sum(gates, axis=0, keepdims=True)


def hidden_backward(hidden, branch, grad_entry, grad_result, scale, gate):
    rows, width = hidden.shape
    vmem = pl.BlockSpec(memory_space=pltpu.VMEM)
    f32 = lambda *shape: jax.ShapeDtypeStruct(shape, jnp.float32)
    return pl.pallas_call(
        hidden_kernel_backward,
        out_shape=(
            f32(rows, width),
            jax.ShapeDtypeStruct((rows, width), jnp.bfloat16),
            f32(1, width),
            f32(1, width),
            f32(1, width),
        ),
        in_specs=[vmem] * 6,
        out_specs=(vmem,) * 5,
        compiler_params=pltpu.CompilerParams(vmem_limit_bytes=48 * 2**20),
        cost_estimate=pl.CostEstimate(
            flops=30 * rows * width, bytes_accessed=22 * rows * width, transcendentals=0
        ),
    )(hidden, branch, grad_entry, grad_result, scale, gate)


def interleave(first, second):
    count = lax.axis_size("wide")
    width = first.shape[1]
    both = [first.reshape(count, -1, width), second.reshape(count, -1, width)]
    return jnp.concatenate(both, axis=1).reshape(-1, width)


def part(rows, second_rows):
    width = rows.shape[1]
    size = second_rows // lax.axis_size("wide")
    total = 4 * size
    blocks = rows.reshape(-1, total, width)
    return blocks[:, : total - size].reshape(-1, width), blocks[:, total - size :].reshape(-1, width)


def gram_band(matrix, layout):
    axis = 0 if layout == "columns" else 1
    width = matrix.shape[axis]
    count = 2 * width // lax.axis_size("wide")
    start = (lax.axis_index("wide") // 2) * count
    rows = lax.dynamic_slice_in_dim(matrix, start, count, axis)
    product_rows = lax.dot_general(
        rows,
        matrix,
        (((1 - axis,), (1 - axis,)), ((), ())),
        precision=lax.Precision.HIGH,
        preferred_element_type=jnp.float32,
    )
    band = width // 2 + LANES
    twice = jnp.concatenate([product_rows, product_rows[:, :band]], axis=1)
    return jnp.concatenate(
        [
            lax.dynamic_slice_in_dim(twice[at : at + LANES], start + at, band, 1)
            for at in range(0, count, LANES)
        ],
        axis=0,
    )


def apply_factor(factor, matrix, layout):
    left, right = (factor, matrix) if layout == "columns" else (matrix, factor)
    return jnp.dot(
        left, right, precision=lax.Precision.HIGH, preferred_element_type=jnp.float32
    )


def local(
    tokens,
    conditions,
    item_live,
    cotangent,
    modulation_table,
    mixer_kernel,
    hidden_kernel,
    attend_weight,
    output_weight,
    expand_weight,
    reduce_weight,
    attend_moment,
    output_moment,
    expand_moment,
    reduce_moment,
    table_first,
    table_second,
    mixer_first,
    mixer_second,
    hidden_first,
    hidden_second,
):
    item_count = tokens.shape[0]
    seq_len = tokens.shape[1]
    local_heads = attend_weight.shape[2] // HEAD
    live_mask = item_live.astype(jnp.float32)[:, None, None]
    token_rows = tokens.astype(jnp.float32)
    modulation = modulation_table[None] + conditions
    shift_one = modulation[:, 0:1]
    scale_one = modulation[:, 1:2]
    gate_one = modulation[:, 2:3]
    shift_two = modulation[:, 3:4]
    scale_two = modulation[:, 4:5]
    gate_two = modulation[:, 5:6]
    width = tokens.shape[2]
    flat_tokens = tokens.reshape(-1, width)
    mixed_low = mixer_forward(flat_tokens, shift_one[0], scale_one[0], mixer_kernel)[None]
    attend_low = attend_weight.astype(jnp.bfloat16)
    triple = jnp.einsum(
        "isd,dkc->iskc", mixed_low, attend_low, preferred_element_type=jnp.float32
    ).astype(jnp.bfloat16)
    heads_split = triple.reshape(item_count, seq_len, 3, local_heads, HEAD)

    def attend_item(member):
        return attend_forward(member[:, 0], member[:, 1], member[:, 2])

    context, logsum = lax.map(attend_item, heads_split)
    output_low = output_weight.astype(jnp.bfloat16)
    branch_partial = jnp.einsum(
        "isc,cd->isd", context, output_low, preferred_element_type=jnp.float32
    )
    (branch,) = sum_scatter(branch_partial.reshape(-1, width), [], [], 1)
    branch = branch.reshape(tokens.shape)
    hidden = token_rows + gate_one * branch
    entry_low = entry_piece(hidden, shift_two, scale_two).astype(jnp.bfloat16)
    expand_low = expand_weight.astype(jnp.bfloat16)
    reduce_low = reduce_weight.astype(jnp.bfloat16)
    grad_result = cotangent.astype(jnp.float32) * live_mask
    grad_ffn_low = (gate_two * grad_result).astype(jnp.bfloat16)
    ffn_partial, entry_partial, grad_reduce, grad_expand, grad_hidden_kernel = middle(
        entry_low.reshape(-1, width),
        grad_ffn_low.reshape(-1, width),
        expand_low,
        reduce_low,
        hidden_kernel,
    )
    ffn_keep, ffn_other = core_scatter(ffn_partial)
    grad_entry, reduce_share = sum_scatter(entry_partial, [grad_reduce], ["rows"], 2)
    grad_entry, reduce_share, ffn_other, grad_expand = together(
        grad_entry, reduce_share, ffn_other, grad_expand
    )
    expand_keep, expand_other = pair_scatter(grad_expand, 1)
    reduce_pieces = line_gather(reduce_share)
    ffn_half = ffn_keep + ffn_other
    ffn_across = permute(ffn_half, "narrow", 2)
    grad_hidden, grad_branch_low, grad_shift_two, grad_scale_two, grad_gate_one = hidden_backward(
        hidden.reshape(-1, width),
        branch.reshape(-1, width),
        grad_entry,
        grad_result.reshape(-1, width),
        scale_two[0],
        gate_one[0],
    )
    grad_branch_low = grad_branch_low.reshape(tokens.shape)
    grad_output = jnp.einsum(
        "isc,isd->cd", context, grad_branch_low, preferred_element_type=jnp.float32
    )
    grad_context = jnp.einsum(
        "isd,cd->isc", grad_branch_low, output_low, preferred_element_type=jnp.float32
    ).astype(jnp.bfloat16)

    def attend_item_back(pieces):
        member, logsum_item, grad_item = pieces
        return attend_backward(
            member[:, 0],
            member[:, 1],
            member[:, 2],
            logsum_item,
            grad_item.reshape(seq_len, local_heads, HEAD),
        )

    grad_split = lax.map(attend_item_back, (heads_split, logsum, grad_context))
    grad_triple = grad_split.reshape(item_count, seq_len, 3, local_heads * HEAD).astype(
        jnp.bfloat16
    )
    *reduce_pieces, ffn_across, expand_other, grad_triple = together(
        *reduce_pieces, ffn_across, expand_other, grad_triple
    )
    ffn_half = ffn_half + ffn_across
    for bit in bits_of(lax.axis_size("narrow"))[2:]:
        ffn_half = ffn_half + permute(ffn_half, "narrow", bit)
    expand_half = expand_keep + expand_other
    reduce_line = line_place(reduce_share, reduce_pieces)
    ffn_other = permute(ffn_half, "narrow", 1)
    grad_attend = jnp.einsum(
        "iskc,isd->kcd", grad_triple, mixed_low, preferred_element_type=jnp.float32
    )
    attend_out = interleave(grad_attend.reshape(-1, width), grad_output)
    mixed_partial = jnp.einsum(
        "iskc,dkc->isd", grad_triple, attend_low, preferred_element_type=jnp.float32
    )
    grad_mixed, expand_share, attend_out_share = sum_scatter(
        mixed_partial.reshape(-1, width), [expand_half, attend_out], ["half", "rows"], 3
    )
    ffn_other, grad_mixed, expand_share, reduce_line = together(
        ffn_other, grad_mixed, expand_share, reduce_line
    )
    expand_pieces = line_gather(expand_share)
    reduce_other = permute(reduce_line, "wide", 1)
    ffn_branch = core_place(ffn_half, ffn_other).reshape(tokens.shape)
    block_out = (live_mask * (hidden + gate_two * ffn_branch)).astype(jnp.bfloat16)
    grad_gate_two = jnp.sum(ffn_branch * grad_result, axis=1)
    tokens_gradient, grad_mixer_kernel, grad_shift_one, grad_scale_one = mixer_backward(
        flat_tokens,
        shift_one[0],
        scale_one[0],
        mixer_kernel,
        grad_mixed,
        grad_hidden,
    )
    tokens_gradient = tokens_gradient.reshape(tokens.shape)
    grad_table = jnp.concatenate(
        [
            grad_shift_one,
            grad_scale_one,
            grad_gate_one,
            grad_shift_two,
            grad_scale_two,
            grad_gate_two,
        ],
        axis=0,
    )
    shares = [attend_out_share, expand_share, reduce_share]
    squares = sum(
        jnp.sum((share * share).reshape(-1, width), axis=0) for share in shares
    )
    shared_rows = grad_table.shape[0] + grad_mixer_kernel.shape[0]
    hidden_rows = -(-grad_hidden_kernel.size // width)
    padding = hidden_rows * width - grad_hidden_kernel.size
    hidden_flat = jnp.pad(grad_hidden_kernel.reshape(-1), (0, padding))
    stacked = jnp.concatenate(
        [grad_table, grad_mixer_kernel, hidden_flat.reshape(hidden_rows, width), squares[None]],
        axis=0,
    )
    stacked = jnp.pad(stacked, ((0, -stacked.shape[0] % 8), (0, 0)))
    small, norm, attend_out_line = small_sums(
        stacked, attend_out_share, shared_rows, hidden_rows, 4
    )
    summed_table = small[: grad_table.shape[0]]
    summed_mixer = small[grad_table.shape[0] : shared_rows]
    summed_hidden = small[shared_rows : shared_rows + hidden_rows].reshape(-1)
    summed_hidden = summed_hidden[: hidden_kernel.size].reshape(hidden_kernel.shape)
    *expand_pieces, norm = together(*expand_pieces, norm)
    gradient_norm = norm[0, 0]
    clip_factor = jnp.minimum(1.0, 1.0 / (gradient_norm + 1e-06))
    expand_line = line_place(expand_share, expand_pieces)
    attend_line, output_line = part(attend_out_line, grad_output.shape[0])
    attend_turned = attend_moment.reshape(width, -1).T
    blend = lambda moment, gradient: muon_momentum * moment + clip_factor * gradient
    halves = [
        (blend(own_half(attend_turned, 0), attend_line), "rows"),
        (blend(own_half(output_moment, 0), output_line), "rows"),
        (blend(own_half(expand_moment, 1), expand_line), "columns"),
        (blend(own_half(reduce_moment, 0), reduce_line), "rows"),
    ]
    bands = jnp.stack([gram_band(matrix, layout) for matrix, layout in halves])
    sub = lax.axis_size("narrow") // MATRICES
    gramian = gram_whole(bands.reshape(MATRICES * sub, -1, bands.shape[2]), 5)
    gramian, expand_line, attend_out_line = together(gramian, expand_line, attend_out_line)
    expand_other = permute(expand_line, "wide", 1)
    attend_out_other = permute(attend_out_line, "wide", 1)
    factors = spread(polar_factor(gramian), 6)
    factors, expand_other, attend_out_other, reduce_other = together(
        factors, expand_other, attend_out_other, reduce_other
    )
    attend_whole, output_whole = part(
        pair_place(attend_out_line, attend_out_other, 0), grad_output.shape[0]
    )
    carried = [
        blend(attend_moment, attend_whole.T.reshape(attend_moment.shape)),
        blend(output_moment, output_whole),
        blend(expand_moment, pair_place(expand_line, expand_other, 1)),
        blend(reduce_moment, pair_place(reduce_line, reduce_other, 0)),
    ]
    table_moment, table_square, table_result = adam_update(
        modulation_table, table_first, table_second, clip_factor * summed_table
    )
    mixer_moment, mixer_square, mixer_result = adam_update(
        mixer_kernel, mixer_first, mixer_second, clip_factor * summed_mixer
    )
    hidden_moment, hidden_square, hidden_result = adam_update(
        hidden_kernel, hidden_first, hidden_second, clip_factor * summed_hidden
    )
    matrices = [carried[0].reshape(width, -1), carried[1], carried[2], carried[3]]
    layouts = ("columns", "rows", "columns", "rows")
    polar_parts = [
        apply_factor(factors[position], matrix, layout)
        for position, (matrix, layout) in enumerate(zip(matrices, layouts))
    ]
    attend_result = muon_finish(attend_weight, polar_parts[0].reshape(attend_weight.shape), 3 * D)
    output_result = muon_finish(output_weight, polar_parts[1], D)
    expand_result = muon_finish(expand_weight, polar_parts[2], FF)
    reduce_result = muon_finish(reduce_weight, polar_parts[3], FF)
    return (
        block_out,
        tokens_gradient,
        gradient_norm,
        carried[0],
        carried[1],
        carried[2],
        carried[3],
        attend_result,
        output_result,
        expand_result,
        reduce_result,
        table_moment,
        table_square,
        table_result,
        mixer_moment,
        mixer_square,
        mixer_result,
        hidden_moment,
        hidden_square,
        hidden_result,
    )


def solution(mesh):
    placed = (
        P("wide", None, None),
        P("wide", None, None),
        P("wide"),
        P("wide", None, None),
        P(),
        P(),
        P(None, "narrow"),
        P(None, None, "narrow"),
        P("narrow", None),
        P(None, "narrow"),
        P("narrow", None),
        P(None, None, "narrow"),
        P("narrow", None),
        P(None, "narrow"),
        P("narrow", None),
        P(),
        P(),
        P(),
        P(),
        P(None, "narrow"),
        P(None, "narrow"),
    )
    return jax.shard_map(
        local,
        mesh=mesh,
        in_specs=placed,
        out_specs=(
            P("wide", None, None),
            P("wide", None, None),
            P(),
            P(None, None, "narrow"),
            P("narrow", None),
            P(None, "narrow"),
            P("narrow", None),
            P(None, None, "narrow"),
            P("narrow", None),
            P(None, "narrow"),
            P("narrow", None),
            P(),
            P(),
            P(),
            P(),
            P(),
            P(),
            P(None, "narrow"),
            P(None, "narrow"),
            P(None, "narrow"),
        ),
        check_vma=False,
    )
```

time: 1100 us -> 792 us (0.72)
  waiting for transfers between devices: 157 us -> 0.03 us
  other arithmetic: 214 us -> 67.2 us
  Pallas kernels: 480 us -> 548 us
  matrix products: 132 us -> 86.2 us
  starting transfers between devices: 39 us -> 12.3 us
    ppermute x27 -> x13, waiting for transfers between devices: 157 us -> 0.03 us  [permute(): lax.ppermute(values, axis, [(index, index ^ bit) for index in range(size)])]
    pallas_call x5 -> x9, Pallas kernels: 274 us -> 409 us  [the longest x3 192 us: sum_scatter(): pl.pallas_call(functools.partial(sum_scatter_kernel, kinds, pieces), out_...]
    pallas_call x1, Pallas kernels: 130 us -> 62.7 us  [spread(): pl.pallas_call(functools.partial(spread_kernel, sub, pieces), out_shape=j...]
    dot_general x11 -> x5, matrix products: 60.4 us -> 5.88 us  [the longest x4 4.09 us: gram_band(): lax.dot_general(rows, matrix, (((1 - axis,), (1 - axis,)), ((), ())), pre...]
    reduce_sum x9 -> x0, other arithmetic: 47.7 us -> none  [the longest x3 21.9 us: depthwise(): kernel[tap_row * 3 + tap_col]]
    convert_element_type x4 -> x2, other arithmetic: 49 us -> 5.68 us  [the longest x1 4 us: local(): expand_low = expand_weight.astype(jnp.bfloat16)]
    ppermute x27 -> x13, starting transfers between devices: 39 us -> 12.3 us  [permute(): lax.ppermute(values, axis, [(index, index ^ bit) for index in range(size)])]
    mul x3 -> x4, other arithmetic: 26.1 us -> 1.56 us  [local(): clip_factor * gradient]
  transfers between devices with their start and end apart: 27 -> 13, of which waited for: 10 -> 0; matrix products, arithmetic and copies ran while one was open for 24% -> 14% of each run, Pallas kernels for 12% -> 57%
where the time goes in v3:
time: 792 us; the launch traced here: 782 us
  Pallas kernels  548 us (69%)
  matrix products  86.2 us (11%)
  other arithmetic  67.2 us (8%)
  local copies, waits for them, and re-layouts  64.2 us (8%)
  starting transfers between devices  12.3 us (2%)
    pallas_call x3, Pallas kernels, sum_scatter(): pl.pallas_call(functools.partial(sum_scatter_kernel, kinds, pieces), out_...  192 us
    pallas_call x1, Pallas kernels, gram_whole(): pl.pallas_call(functools.partial(gram_kernel, narrow_bits, hops), out_sha...  86.1 us
    pallas_call x1, Pallas kernels, polar_factor(): pl.pallas_call(polar_kernel, out_shape=jax.ShapeDtypeStruct((size, size),...  75.9 us
    pallas_call x1, Pallas kernels, spread(): pl.pallas_call(functools.partial(spread_kernel, sub, pieces), out_shape=j...  62.7 us
    pallas_call x1, Pallas kernels, small_sums(): pl.pallas_call(functools.partial(small_kernel, shared_rows, split_rows),...  49.8 us
    pallas_call x1, Pallas kernels, middle(): pl.pallas_call(middle_kernel, grid=(hidden_units // block,), out_shape=(f...  39.9 us
    dot_general x4, matrix products, apply_factor(): jnp.dot(left, right, precision=lax.Precision.HIGH, preferred_element_type...  32.2 us
    unnamed x136, local copies, waits for them, and re-layouts  28.3 us
  transfers between devices with their start and end apart: 13, of which 0 were waited for; matrix products, arithmetic and copies ran while one was open for 14% of the time, Pallas kernels for 57%

profile of v3, /device:TPU:13, one launch (start us, length us, event | category | flops | bytes accessed | tf_op | source)
XLA Modules:
  0.0 782.0 jit_solution(8052928969911421304)
XLA Ops:
  4.0 7.4 shard_map.356
  13.9 12.4 %while.45 = (s32[]{:T(128)}, bf16[2,512,4,64]{1,3,2,0:T(8,128)(2,1)}, f32[2,4,512]{2,1,0:T(4,128)S(1)}, bf16[2,512,4,64]{1,3,2,0:T(8,128)(2,1)S(1)}, bf16[1024,4...) while((s32[]{:T(128)}, bf16[2,512,4,64]{1,3,2,0:T(8,128)(2,1)}, ...), condition=%wide.region_3.0_spmd, body=%wide.region_0.3_spmd.sunk | while | flops 555874304 | bytes 30998672 | solution.py:61
  29.1 52.2 %shard_map.357.branch_ref = f32[1024,1024]{1,0:T(8,128)S(1)} custom-call(f32[1024,1024]{1,0:T(8,128)S(1)} %fusion.96.x_ref), custom_call_target="tpu_custom_call" | custom-call | flops 1048576 | bytes 33554432 | tf_op jit(solution)/shard_map/pallas_call | solution.py:511
  87.5 2.7 copy.52.entry_t_ref
  91.0 4.0 convert_element_type.72.expand_ref
  97.3 3.5 fusion.56
  100.8 39.9 %shard_map.358 = (f32[1024,1024]{1,0:T(8,128)}, f32[1024,1024]{1,0:T(8,128)}, f32[1024,1024]{1,0:T(8,128)}, f32[1024,1024]{1,0:T(8,128)}, f32[9,1024]{1,0:T(8,128)S(1)}) custom-call(bf16[1024,1024]{1,0:T(8,128)(2,1)} %fusion.130.entry_ref, bf16[1024,1024]{1,0:T(8,128)(2,1)} %copy.52.entry_t_ref, bf16[1024,1024]{1,0:T(8,128)(2,1)} %get-tuple-element.350.grad_ffn_ref, ...), custom_call_target="tpu_custom_call" | custom-call | flops 12884901888 | bytes 33554432 | tf_op jit(solution)/shard_map/pallas_call | solution.py:998
  140.8 3.2 constant_dynamic-slice_fusion.1
  144.1 3.5 copy.58
  152.0 62.6 %shard_map.359 = (f32[1024,1024]{1,0:T(8,128)S(1)}, f32[128,1024]{1,0:T(8,128)S(1)}) custom-call(f32[1024,1024]{1,0:T(8,128)S(1)} %copy-done.4, f32[1024,1024]{1,0:T(8,128)S(1)} %copy-done.5), custom_call_target="tpu_custom_call" | custom-call | flops 1048576 | bytes 33554432 | tf_op jit(solution)/shard_map/pallas_call | solution.py:511
  216.6 2.4 collective-permute-start.1
  220.2 13.4 %shard_map.360 = (f32[1024,1024]{1,0:T(8,128)}, bf16[1024,1024]{1,0:T(8,128)(2,1)S(1)}, f32[1,1024]{1,0:T(1,128)S(1)}, f32[1,1024]{1,0:T(1,128)S(1)}, f32[1,1024]{1,0:T(1,128)S(1)}) custom-call(f32[1024,1024]{1,0:T(8,128)} %bitcast.232, f32[1024,1024]{1,0:T(8,128)} %copy-done, f32[1024,1024]{1,0:T(8,128)} %copy-done.7, ...), custom_call_target="tpu_custom_call" | custom-call | flops 31457280 | bytes 23068672 | tf_op jit(solution)/shard_map/pallas_call | solution.py:1228
  235.2 2.8 reshape.403
  237.9 2.3 copy.55
  240.2 3.2 constant_dynamic-slice_fusion
  244.0 3.3 dynamic-slice_add_fusion.1
  248.1 42.4 %while.46 = (s32[]{:T(128)}, f32[1024,4,64]{0,2,1:T(8,128)}, f32[1024,4,64]{0,2,1:T(8,128)}, bf16[2,512,4,64]{1,3,2,0:T(8,128)(2,1)}, bf16[2,512,4,64]{1,3,2,0:T...) while((s32[]{:T(128)}, f32[1024,4,64]{0,2,1:T(8,128)}, ...), condition=%wide.region_8.9_spmd.clone, body=%wide.region_6.8_spmd.clone.sunk | while | flops 1368782848 | bytes 143714064 | solution.py:104
  248.5 2.3 fusion.161
  250.9 2.8 multiply_reduce_fusion.9
  254.2 3.3 multiply_convert_fusion.4
  257.5 4.2 fusion.162
  261.8 4.4 fusion.164
  266.1 2.7 fusion.163
  268.8 2.3 fusion.161
  271.2 2.8 multiply_reduce_fusion.9
  274.5 3.3 multiply_convert_fusion.4
  277.8 4.5 fusion.162
  282.4 4.4 fusion.164
  286.8 3.7 fusion.163
  290.5 2.4 copy.56
  299.7 2.9 add.258
  306.9 2.7 pad_maximum_fusion
  310.6 2.2 dynamic-slice_add_fusion.refs_0_
  315.0 77.7 %shard_map.361 = (f32[1024,1024]{1,0:T(8,128)S(1)}, f32[256,512]{1,0:T(8,128)S(1)}, f32[128,1024]{1,0:T(8,128)S(1)}) custom-call(f32[1024,1024]{1,0:T(8,128)S(1)} %convolution_bitcast_fusion.x_ref, f32[1024,512]{1,0:T(8,128)S(1)} %dynamic-slice_add_fusion.refs_0_, f32[1024,1024]{1,0:T(8,128)} %bitcast.238), custom_call_target="tpu_custom_call" | custom-call | flops 1048576 | bytes 33554432 | tf_op jit(solution)/shard_map/pallas_call | solution.py:511
  406.8 20.3 %shard_map.362 = (bf16[1024,1024]{1,0:T(8,128)(2,1)}, f32[9,1024]{1,0:T(8,128)S(1)}, f32[1,1024]{1,0:T(1,128)S(1)}, f32[1,1024]{1,0:T(1,128)S(1)}) custom-call(bf16[1024,1024]{1,0:T(8,128)(2,1)S(1)} %bitcast.229, f32[1,1024]{1,0:T(1,128)S(1)} %copy-done.17, f32[1,1024]{1,0:T(1,128)S(1)} %copy-done.15, f32[9,1024]{1,0:T(8,128)S(1)} %copy-done.11, ...), custom_call_target="tpu_custom_call" | custom-call | flops 104857600 | bytes 12582912 | tf_op jit(solution)/shard_map/pallas_call | solution.py:1158
  427.1 4.5 multiply_reduce_fusion.2
  432.0 49.8 %shard_map.363 = (f32[32,1024]{1,0:T(8,128)S(1)}, f32[8,128]{1,0:T(8,128)S(1)}, f32[512,1024]{1,0:T(8,128)S(1)}) custom-call(f32[32,1024]{1,0:T(8,128)S(1)} %pad.4.x_ref, f32[128,1024]{1,0:T(8,128)S(1)} %get-tuple-element.212.share_ref), custom_call_target="tpu_custom_call" | custom-call | tf_op jit(solution)/shard_map/pallas_call | solution.py:591
  501.7 86.1 %shard_map.364.g_ref = f32[1024,640]{1,0:T(8,128)S(1)} custom-call(f32[4,256,640]{2,1,0:T(8,128)S(1)} %pad_maximum_fusion.1.x_ref), custom_call_target="tpu_custom_call" | custom-call | tf_op jit(solution)/shard_map/pallas_call | solution.py:679
  589.3 75.9 %shard_map.365.q_ref = f32[1024,1024]{1,0:T(8,128)} custom-call(f32[1024,640]{1,0:T(8,128)S(1)} %shard_map.364.g_ref), custom_call_target="tpu_custom_call" | custom-call | flops 109521666048 | bytes 8388608 | tf_op jit(solution)/shard_map/pallas_call | solution.py:782
  665.3 62.7 %shard_map.366 = f32[4,1024,1024]{2,1,0:T(8,128)} custom-call(f32[1024,1024]{1,0:T(8,128)} %shard_map.365.q_ref), custom_call_target="tpu_custom_call" | custom-call | tf_op jit(solution)/shard_map/pallas_call | solution.py:847
  729.6 2.9 maximum_select_fusion.1
  735.7 4.6 fusion.43
  741.0 2.4 copy.60
  743.4 9.7 %multiply_subtract_fusion.2 = f32[1024,3,256]{2,0,1:T(8,128)} fusion(f32[1024,3,256]{2,0,1:T(8,128)} %param.32, f32[1024,3,256]{0,2,1:T(8,128)S(1)} %multiply_add_fusion, f32[4,1024,1024]{2,1,0:T(8,128)} %shard_map.366), kind=kOutput, calls=%fused_computation.78 | convolution fusion | flops 4834197504 | bytes 13631488 | tf_op jit(solution)/shard_map/dot_general | solution.py:1287
  753.1 10.3 %multiply_subtract_fusion = f32[1024,1024]{1,0:T(8,128)} fusion(f32[1024,1024]{1,0:T(8,128)S(1)} %copy-done.35, f32[1024,1024]{1,0:T(8,128)S(1)} %copy-done.32, f32[4,1024,1024]{2,1,0:T(8,128)} %shard_map.366), kind=kOutput, calls=%fused_computation.63 | convolution fusion | flops 6445596672 | bytes 16777216 | tf_op jit(solution)/shard_map/dot_general | solution.py:1287
  763.4 4.9 fusion.41
  769.4 8.9 %multiply_subtract_fusion.1 = f32[1024,1024]{1,0:T(8,128)} fusion(f32[1024,1024]{1,0:T(8,128)S(1)} %copy-done.36, f32[1024,1024]{1,0:T(8,128)S(1)} %fusion.41, f32[4,1024,1024]{2,1,0:T(8,128)S(1)} %bitcast.234), kind=kOutput, calls=%fused_computation.65 | convolution fusion | flops 6445596672 | bytes 16777216 | tf_op jit(solution)/shard_map/dot_general | solution.py:1287
  778.5 3.3 fusion.80
  (279 shorter events, 96.5 us)
Async XLA Ops:
  1.5 11.8 %copy-start.14 = (f32[1,1024]{1,0:T(1,128)}, f32[1,1024]{1,0:T(1,128)S(1)}, u32[]{:S(2)}) copy-start(f32[1,1024]{1,0:T(1,128)S(1)} %get-tuple-element.366.scale_ref) | copy-start | bytes 12292
  1.5 11.8 %copy-start.16 = (f32[1,1024]{1,0:T(1,128)}, f32[1,1024]{1,0:T(1,128)S(1)}, u32[]{:S(2)}) copy-start(f32[1,1024]{1,0:T(1,128)S(1)} %get-tuple-element.367.shift_ref) | copy-start | bytes 12292
  1.5 95.2 %copy-start.65 = (f32[1,1,1024]{2,1,0:T(1,128)}, f32[1,1,1024]{2,1,0:T(1,128)S(1)}, u32[]{:S(2)}) copy-start(f32[1,1,1024]{2,1,0:T(1,128)S(1)} %get-tuple-element.365) | copy-start | bytes 12292
  13.9 14.5 %copy-start.53 = (f32[256,1024]{1,0:T(8,128)S(1)}, f32[256,1024]{1,0:T(8,128)}, u32[]{:S(2)}) copy-start(f32[256,1024]{1,0:T(8,128)} %param.33) | copy-start | bytes 3145732
  26.3 55.0 %copy-start.27 = (bf16[1024,4,64]{0,2,1:T(8,128)(2,1)}, bf16[1024,4,64]{0,2,1:T(8,128)(2,1)S(1)}, u32[]{:S(2)}) copy-start(bf16[1024,4,64]{0,2,1:T(8,128)(2,1)S(1)} %get-tuple-element.540) | copy-start | bytes 1572868
  26.3 55.7 %copy-start.22 = (bf16[2,512,4,64]{1,3,2,0:T(8,128)(2,1)}, bf16[2,512,4,64]{1,3,2,0:T(8,128)(2,1)S(1)}, u32[]{:S(2)}) copy-start(bf16[2,512,4,64]{1,3,2,0:T(8,128)(2,1)S(1)} %get-tuple-element.539) | copy-start | bytes 1572868
  28.3 53.0 %copy-start.47 = (bf16[32,8,2,512]{3,1,2,0:T(8,128)(2,1)}, bf16[32,8,2,512]{3,1,2,0:T(8,128)(2,1)S(1)}, u32[]{:S(2)}) copy-start(bf16[32,8,2,512]{3,1,2,0:T(8,128)(2,1)S(1)} %copy.65) | copy-start | bytes 1572868
  29.1 52.3 %copy-start.2 = (bf16[1,1024,1024]{2,1,0:T(8,128)(2,1)S(1)}, bf16[1,1024,1024]{2,1,0:T(8,128)(2,1)}, u32[]{:S(2)}) copy-start(bf16[1,1024,1024]{2,1,0:T(8,128)(2,1)} %param.25) | copy-start | bytes 6291460
  143.9 72.6 %collective-permute-start = (f32[512,1024]{1,0:T(8,128)}, f32[512,1024]{1,0:T(8,128)S(1)}, u32[]{:S(2)}, u32[]{:S(2)}) collective-permute-start(f32[512,1024]{1,0:T(8,128)} %constant_dynamic-slice_fusion.1), channel_id=1, source_target_pairs={{0,1},{1,0},{2,3},{3,2},{4,5},{5,4},{6,7},{7,6},{8,9},{9,8},{10,11... | collective-permute-start | bytes 6291464 | tf_op jit(solution)/shard_map/ppermute | solution.py:177
  216.6 83.1 %collective-permute-start.1 = (f32[128,1024]{1,0:T(8,128)S(1)}, f32[128,1024]{1,0:T(8,128)}, u32[]{:S(2)}, u32[]{:S(2)}) collective-permute-start(f32[128,1024]{1,0:T(8,128)S(1)} %get-tuple-element.184), channel_id=1, source_target_pairs={{0,8},{4,12},{8,0},{12,4},{16,24},{20,28},{24,16},{28,20},{1,9},{5... | collective-permute-start | bytes 1572872 | tf_op jit(solution)/shard_map/ppermute | solution.py:177
  219.0 80.7 %collective-permute-start.2 = (f32[128,1024]{1,0:T(8,128)S(1)}, f32[128,1024]{1,0:T(8,128)}, u32[]{:S(2)}, u32[]{:S(2)}) collective-permute-start(f32[128,1024]{1,0:T(8,128)S(1)} %get-tuple-element.184), channel_id=1, source_target_pairs={{0,16},{4,20},{8,24},{12,28},{16,0},{20,4},{24,8},{28,12},{1,17},{... | collective-permute-start | bytes 1572872 | tf_op jit(solution)/shard_map/ppermute | solution.py:177
  219.0 80.7 %collective-permute-start.3 = (f32[128,1024]{1,0:T(8,128)S(1)}, f32[128,1024]{1,0:T(8,128)}, u32[]{:S(2)}, u32[]{:S(2)}) collective-permute-start(f32[128,1024]{1,0:T(8,128)S(1)} %get-tuple-element.184), channel_id=1, source_target_pairs={{0,24},{4,28},{8,16},{12,20},{16,8},{20,12},{24,0},{28,4},{1,25},{... | collective-permute-start | bytes 1572872 | tf_op jit(solution)/shard_map/ppermute | solution.py:177
  220.2 13.4 %copy-start.54 = (f32[256,1024]{1,0:T(8,128)S(1)}, f32[256,1024]{1,0:T(8,128)}, u32[]{:S(2)}) copy-start(f32[256,1024]{1,0:T(8,128)} %param.33) | copy-start | bytes 3145732
  243.4 56.3 %collective-permute-start.5 = (f32[1024,512]{1,0:T(8,128)}, f32[1024,512]{1,0:T(8,128)}, u32[]{:S(2)}, u32[]{:S(2)}) collective-permute-start(f32[1024,512]{1,0:T(8,128)} %constant_dynamic-slice_fusion), channel_id=1, source_target_pairs={{0,4},{4,0},{8,12},{12,8},{16,20},{20,16},{24,28},{28,24},{1,5},{5... | collective-permute-start | bytes 6291464 | tf_op jit(solution)/shard_map/ppermute | solution.py:177
  247.3 52.4 %collective-permute-start.4 = (f32[512,1024]{1,0:T(8,128)}, f32[512,1024]{1,0:T(8,128)}, u32[]{:S(2)}, u32[]{:S(2)}) collective-permute-start(f32[512,1024]{1,0:T(8,128)} %dynamic-slice_add_fusion.1), channel_id=1, source_target_pairs={{0,2},{1,3},{2,0},{3,1},{4,6},{5,7},{6,4},{7,5},{8,10},{9,11},{10,... | collective-permute-start | bytes 6291464 | tf_op jit(solution)/shard_map/ppermute | solution.py:177
  277.8 8.9 %copy-start.19 = (f32[4,512,1024]{2,1,0:T(8,128)S(1)}, f32[4,512,1024]{2,1,0:T(8,128)}, u32[]{:S(2)}) copy-start(f32[4,512,1024]{2,1,0:T(8,128)} %copy-done.18) | copy-start | bytes 25165828 | tf_op jit(solution)/shard_map/while/body/eval_jaxpr/while
  302.6 95.6 %collective-permute-start.6 = (f32[512,1024]{1,0:T(8,128)S(1)}, f32[512,1024]{1,0:T(8,128)}, u32[]{:S(2)}, u32[]{:S(2)}) collective-permute-start(f32[512,1024]{1,0:T(8,128)S(1)} %add.258), channel_id=1, source_target_pairs={{0,1},{1,0},{2,3},{3,2},{4,5},{5,4},{6,7},{7,6},{8,9},{9,8},{10,11... | collective-permute-start | bytes 6291464 | tf_op jit(solution)/shard_map/ppermute | solution.py:177
  395.8 10.9 %copy-start.3 = (bf16[1,1024,1024]{2,1,0:T(8,128)(2,1)S(1)}, bf16[1,1024,1024]{2,1,0:T(8,128)(2,1)}, u32[]{:S(2)}) copy-start(bf16[1,1024,1024]{2,1,0:T(8,128)(2,1)} %param.25) | copy-start | bytes 6291460
  395.8 10.9 %copy-start.11 = (f32[9,1024]{1,0:T(8,128)S(1)}, f32[9,1024]{1,0:T(8,128)}, u32[]{:S(2)}) copy-start(f32[9,1024]{1,0:T(8,128)} %taps_ref.5) | copy-start | bytes 110596
  395.8 10.9 %copy-start.15 = (f32[1,1024]{1,0:T(1,128)S(1)}, f32[1,1024]{1,0:T(1,128)}, u32[]{:S(2)}) copy-start(f32[1,1024]{1,0:T(1,128)} %copy-done.14) | copy-start | bytes 12292
  395.8 10.9 %copy-start.17 = (f32[1,1024]{1,0:T(1,128)S(1)}, f32[1,1024]{1,0:T(1,128)}, u32[]{:S(2)}) copy-start(f32[1,1024]{1,0:T(1,128)} %copy-done.16) | copy-start | bytes 12292
  398.3 84.2 %collective-permute-start.7 = (f32[256,512]{1,0:T(8,128)S(1)}, f32[256,512]{1,0:T(8,128)}, u32[]{:S(2)}, u32[]{:S(2)}) collective-permute-start(f32[256,512]{1,0:T(8,128)S(1)} %get-tuple-element.204), channel_id=1, source_target_pairs={{0,8},{4,12},{8,0},{12,4},{16,24},{20,28},{24,16},{28,20},{1,9},{5... | collective-permute-start | bytes 1572872 | tf_op jit(solution)/shard_map/ppermute | solution.py:177
  398.5 84.0 %collective-permute-start.8 = (f32[256,512]{1,0:T(8,128)S(1)}, f32[256,512]{1,0:T(8,128)}, u32[]{:S(2)}, u32[]{:S(2)}) collective-permute-start(f32[256,512]{1,0:T(8,128)S(1)} %get-tuple-element.204), channel_id=1, source_target_pairs={{0,16},{4,20},{8,24},{12,28},{16,0},{20,4},{24,8},{28,12},{1,17},{... | collective-permute-start | bytes 1572872 | tf_op jit(solution)/shard_map/ppermute | solution.py:177
  400.7 81.8 %collective-permute-start.9 = (f32[256,512]{1,0:T(8,128)S(1)}, f32[256,512]{1,0:T(8,128)}, u32[]{:S(2)}, u32[]{:S(2)}) collective-permute-start(f32[256,512]{1,0:T(8,128)S(1)} %get-tuple-element.204), channel_id=1, source_target_pairs={{0,24},{4,28},{8,16},{12,20},{16,8},{20,12},{24,0},{28,4},{1,25},{... | collective-permute-start | bytes 1572872 | tf_op jit(solution)/shard_map/ppermute | solution.py:177
  406.8 20.3 %copy-start.21 = (f32[1,1024,1024]{2,1,0:T(8,128)S(1)}, f32[1,1024,1024]{2,1,0:T(8,128)}, u32[]{:S(2)}) copy-start(f32[1,1024,1024]{2,1,0:T(8,128)} %copy-done.20) | copy-start | bytes 12582916
  406.8 20.3 %copy-start.42 = (f32[512,1024]{1,0:T(8,128)S(1)}, f32[512,1024]{1,0:T(8,128)}, u32[]{:S(2)}) copy-start(f32[512,1024]{1,0:T(8,128)} %copy-done.41) | copy-start | bytes 6291460
  406.8 20.3 %copy-start.44 = (bf16[1,1024,1024]{2,1,0:T(8,128)(2,1)S(1)}, bf16[1,1024,1024]{2,1,0:T(8,128)(2,1)}, u32[]{:S(2)}) copy-start(bf16[1,1024,1024]{2,1,0:T(8,128)(2,1)} %param.28) | copy-start | bytes 6291460
  406.8 20.3 %copy-start.66 = (f32[1,1,1024]{2,1,0:T(1,128)S(1)}, f32[1,1,1024]{2,1,0:T(1,128)}, u32[]{:S(2)}) copy-start(f32[1,1,1024]{2,1,0:T(1,128)} %copy-done.65) | copy-start | bytes 12292
  481.7 247.8 %collective-permute-start.12 = (f32[512,1024]{1,0:T(8,128)}, f32[512,1024]{1,0:T(8,128)}, u32[]{:S(2)}, u32[]{:S(2)}) collective-permute-start(f32[512,1024]{1,0:T(8,128)} %copy-done.29), channel_id=1, source_target_pairs={{0,4},{4,0},{8,12},{12,8},{16,20},{20,16},{24,28},{28,24},{1,5},{5... | collective-permute-start | bytes 6291464 | tf_op jit(solution)/shard_map/ppermute | solution.py:177
  587.8 141.8 %collective-permute-start.10 = (f32[1024,512]{1,0:T(8,128)}, f32[1024,512]{1,0:T(8,128)}, u32[]{:S(2)}, u32[]{:S(2)}) collective-permute-start(f32[1024,512]{1,0:T(8,128)} %constant_dynamic-update-slice_fusion), channel_id=1, source_target_pairs={{0,4},{4,0},{8,12},{12,8},{16,20},{20,16},{24,28},{28,24},{1,5},{5... | collective-permute-start | bytes 6291464 | tf_op jit(solution)/shard_map/ppermute | solution.py:177
  588.4 141.2 %collective-permute-start.11 = (f32[512,1024]{1,0:T(8,128)S(1)}, f32[512,1024]{1,0:T(8,128)}, u32[]{:S(2)}, u32[]{:S(2)}) collective-permute-start(f32[512,1024]{1,0:T(8,128)S(1)} %get-tuple-element.220), channel_id=1, source_target_pairs={{0,4},{4,0},{8,12},{12,8},{16,20},{20,16},{24,28},{28,24},{1,5},{5... | collective-permute-start | bytes 6291464 | tf_op jit(solution)/shard_map/ppermute | solution.py:177
  665.2 62.8 %copy-start.60 = (f32[6,1024]{1,0:T(8,128)S(1)}, f32[6,1024]{1,0:T(8,128)}, u32[]{:S(2)}) copy-start(f32[6,1024]{1,0:T(8,128)} %param.29) | copy-start | bytes 73732
  665.2 62.8 %copy-start.67 = (f32[6,1024]{1,0:T(8,128)S(1)}, f32[6,1024]{1,0:T(8,128)}, u32[]{:S(2)}) copy-start(f32[6,1024]{1,0:T(8,128)} %param.41) | copy-start | bytes 73732
  665.2 62.8 %copy-start.68 = (f32[6,1024]{1,0:T(8,128)S(1)}, f32[6,1024]{1,0:T(8,128)}, u32[]{:S(2)}) copy-start(f32[6,1024]{1,0:T(8,128)} %param.40) | copy-start | bytes 73732
  665.2 63.5 %copy-start.13 = (f32[9,1024]{1,0:T(8,128)S(1)}, f32[9,1024]{1,0:T(8,128)}, u32[]{:S(2)}) copy-start(f32[9,1024]{1,0:T(8,128)} %taps_ref.4) | copy-start | bytes 110596
  665.3 63.5 %copy-start.61 = (f32[9,1024]{1,0:T(8,128)S(1)}, f32[9,1024]{1,0:T(8,128)}, u32[]{:S(2)}) copy-start(f32[9,1024]{1,0:T(8,128)} %param.45) | copy-start | bytes 110596
  665.3 63.5 %copy-start.62 = (f32[9,1024]{1,0:T(8,128)S(1)}, f32[9,1024]{1,0:T(8,128)}, u32[]{:S(2)}) copy-start(f32[9,1024]{1,0:T(8,128)} %param.44) | copy-start | bytes 110596
  665.3 63.5 %copy-start.63 = (f32[9,1024]{1,0:T(8,128)S(1)}, f32[9,1024]{1,0:T(8,128)}, u32[]{:S(2)}) copy-start(f32[9,1024]{1,0:T(8,128)} %param.43) | copy-start | bytes 110596
  665.3 63.5 %copy-start.64 = (f32[9,1024]{1,0:T(8,128)S(1)}, f32[9,1024]{1,0:T(8,128)}, u32[]{:S(2)}) copy-start(f32[9,1024]{1,0:T(8,128)} %param.42) | copy-start | bytes 110596
  743.4 9.7 %copy-start.32 = (f32[1024,1024]{1,0:T(8,128)S(1)}, f32[1024,1024]{1,0:T(8,128)}, u32[]{:S(2)}) copy-start(f32[1024,1024]{1,0:T(8,128)} %fusion.43) | copy-start | bytes 12582916
  743.4 9.7 %copy-start.35 = (f32[1024,1024]{1,0:T(8,128)S(1)}, f32[1024,1024]{1,0:T(8,128)}, u32[]{:S(2)}) copy-start(f32[1024,1024]{1,0:T(8,128)} %param.35) | copy-start | bytes 12582916
  743.4 25.0 %slice-start = ((s8[16777216]{0:T(1024)(128)(4,1)}), s8[4194304]{0:T(1024)(128)(4,1)S(1)}, s32[]{:S(2)}) async-start(s8[16777216]{0:T(1024)(128)(4,1)} %bitcast.233), calls=%async_computation | async-start | bytes 8388608
  743.4 25.0 %slice-start.1 = ((s8[16777216]{0:T(1024)(128)(4,1)}), s8[4194304]{0:T(1024)(128)(4,1)S(1)}, s32[]{:S(2)}) async-start(s8[16777216]{0:T(1024)(128)(4,1)} %bitcast.233), calls=%async_computation.1 | async-start | bytes 8388608
  753.1 10.3 %copy-start.40 = (f32[1024,1024]{1,0:T(8,128)S(1)}, f32[1024,1024]{1,0:T(8,128)}, u32[]{:S(2)}) copy-start(f32[1024,1024]{1,0:T(8,128)} %param.38) | copy-start | bytes 12582916
  753.1 15.3 %slice-start.2 = ((s8[16777216]{0:T(1024)(128)(4,1)}), s8[4194304]{0:T(1024)(128)(4,1)S(1)}, s32[]{:S(2)}) async-start(s8[16777216]{0:T(1024)(128)(4,1)} %bitcast.233), calls=%async_computation.2 | async-start | bytes 8388608
  769.4 8.9 %copy-start.50 = (f32[8,32,1024]{2,1,0:T(8,128)S(1)}, f32[8,32,1024]{2,1,0:T(8,128)}, u32[]{:S(2)}) copy-start(f32[8,32,1024]{2,1,0:T(8,128)} %slice_multiply_fusion.2) | copy-start | bytes 3145732
  769.4 8.9 %copy-start.56 = (f32[256,1024]{1,0:T(8,128)S(1)}, f32[256,1024]{1,0:T(8,128)}, u32[]{:S(2)}) copy-start(f32[256,1024]{1,0:T(8,128)} %param.37) | copy-start | bytes 3145732
  769.4 9.1 %copy-start.55 = (f32[256,1024]{1,0:T(8,128)S(1)}, f32[256,1024]{1,0:T(8,128)}, u32[]{:S(2)}) copy-start(f32[256,1024]{1,0:T(8,128)} %param.33) | copy-start | bytes 3145732
  (45 other events, 157.2 us)

commit v4 on v3

--- a/solution.py
+++ b/solution.py
@@ -27,91 +27,11 @@
 gelu_cubic = 0.044715
 
 
-def layer_norm(values):
-    average = jnp.mean(values, axis=-1, keepdims=True)
-    centred = values - average
-    spread = jnp.mean(centred * centred, axis=-1, keepdims=True)
-    return centred * lax.rsqrt(spread + 1e-06)
-
-
-def entry_piece(hidden, offset, stretch):
-    return layer_norm(hidden) * (1.0 + stretch) + offset
-
-
-def attend_forward(queries, key_rows, value_rows):
-    seq_len = queries.shape[0]
-    block_rows = min(512, seq_len)
-    blocks = queries.reshape(seq_len // block_rows, block_rows, queries.shape[1], queries.shape[2])
-    scale_factor = HEAD ** (-0.5)
-
-    def one_block(query_block):
-        scores = (
-            jnp.einsum("qhe,khe->hqk", query_block, key_rows, preferred_element_type=jnp.float32)
-            * scale_factor
-        )
-        row_peak = jnp.max(scores, axis=-1, keepdims=True)
-        weights = jnp.exp(scores - row_peak)
-        summed = jnp.sum(weights, axis=-1, keepdims=True)
-        soft_low = (weights / summed).astype(jnp.bfloat16)
-        context = jnp.einsum(
-            "hqk,khe->qhe", soft_low, value_rows, preferred_element_type=jnp.float32
-        )
-        return (context.astype(jnp.bfloat16), (row_peak + jnp.log(summed))[:, :, 0])
-
-    context, logsum = lax.map(one_block, blocks)
-    return (context.reshape(seq_len, -1), logsum)
-
-
-def attend_backward(queries, key_rows, value_rows, logsum, grad_context):
-    seq_len = queries.shape[0]
-    block_rows = min(512, seq_len)
-    block_count = seq_len // block_rows
-    query_blocks = queries.reshape(block_count, block_rows, queries.shape[1], queries.shape[2])
-    grad_blocks = grad_context.reshape(block_count, block_rows, queries.shape[1], queries.shape[2])
-    scale_factor = HEAD ** (-0.5)
-
-    def one_block(running, pieces):
-        grad_keys, grad_values = running
-        query_block, grad_block, logsum_block = pieces
-        scores = (
-            jnp.einsum("qhe,khe->hqk", query_block, key_rows, preferred_element_type=jnp.float32)
-            * scale_factor
-        )
-        weights = jnp.exp(scores - logsum_block[:, :, None])
-        soft_low = weights.astype(jnp.bfloat16)
-        grad_values = grad_values + jnp.einsum(
-            "hqk,qhe->khe", soft_low, grad_block, preferred_element_type=jnp.float32
-        )
-        grad_weights = jnp.einsum(
-            "qhe,khe->hqk", grad_block, value_rows, preferred_element_type=jnp.float32
-        )
-        grad_scores = weights * (
-            grad_weights - jnp.sum(weights * grad_weights, axis=-1, keepdims=True)
-        )
-        grad_low = grad_scores.astype(jnp.bfloat16)
-        grad_query = (
-            jnp.einsum("hqk,khe->qhe", grad_low, key_rows, preferred_element_type=jnp.float32)
-            * scale_factor
-        )
-        grad_keys = (
-            grad_keys
-            + jnp.einsum("hqk,qhe->khe", grad_low, query_block, preferred_element_type=jnp.float32)
-            * scale_factor
-        )
-        return ((grad_keys, grad_values), grad_query)
-
-    start_sums = jnp.zeros(key_rows.shape, jnp.float32)
-    finals, grad_queries = lax.scan(
-        one_block, (start_sums, start_sums), (query_blocks, grad_blocks, logsum)
-    )
-    grad_queries = grad_queries.reshape(key_rows.shape)
-    return jnp.stack([grad_queries, finals[0], finals[1]], axis=1)
-
-
 MESH = pl.DeviceIdType.MESH
 BLK = 256
 LANES = 128
 SLAB = 16
+QUERIES = 1024
 UNROLL = 4
 MATRICES = 4
 
@@ -203,15 +123,6 @@
     for offset, piece in zip(range(1, count), arrived):
         whole = lax.dynamic_update_slice_in_dim(whole, piece, (place ^ offset) * rows, 0)
     return whole
-
-
-def pair_place(half, other, axis):
-    side = lax.axis_index("wide") % 2
-    return jnp.where(
-        side == 0,
-        jnp.concatenate([half, other], axis=axis),
-        jnp.concatenate([other, half], axis=axis),
-    )
 
 
 def own_half(values, axis):
@@ -792,70 +703,220 @@
     )(gramian)
 
 
-def spread_kernel(sub, pieces, q_ref, o_ref, sends, arrivals, local):
+def finish_kernel(sub, pieces, norm_ref, q_ref, *refs):
+    lines, others, refs = refs[0:6:2], refs[1:6:2], refs[6:]
+    moments, weights, refs = refs[:4], refs[4:8], refs[8:]
+    carried, results, refs = refs[:4], refs[4:8], refs[8:]
+    qs, refs = refs[0], refs[1:]
+    staged, values, highs, lows = refs[:3], refs[3:7], refs[7:11], refs[11:15]
+    sends, arrivals, near_sems, load_sems, value_sems, out_sems = refs[15:]
     size = q_ref.shape[0]
     half = size // 2
     step = half // pieces
     w, n = lax.axis_index("wide"), lax.axis_index("narrow")
     own = n // sub
     across = partner(own, 2)
+    far = own // 2
     near_place, far_place = place_at("narrow", sub), place_at("narrow", 2 * sub)
     side_place = place_at("wide", 1)
     greet([near_place, far_place, side_place])
-    top = w % 2
+    y = w % 2
     rows = lambda side, p: pl.ds(pl.multiple_of(side * half + p * step, 8), step)
-    keep = pltpu.make_async_copy(q_ref, o_ref.at[own], local.at[0])
+    slot = iter(range(1 + 4 * pieces))
+    copies = []
+
+    def push(src, dst, place):
+        copies.append(send(src, dst, sends, arrivals, next(slot), place))
+        return copies[-1]
+
+    crossing = [
+        push(q_ref.at[rows(y, p)], qs.at[own, rows(y, p)], far_place) for p in range(pieces)
+    ]
+    near_own = push(q_ref, qs.at[own], near_place)
+    keep = pltpu.make_async_copy(q_ref, qs.at[own], near_sems.at[0])
     keep.start()
-    copies = []
-
-    def push(src, dst, place):
-        copies.append(send(src, dst, sends, arrivals, len(copies), place))
-        return copies[-1]
-
-    cross = lambda p: push(q_ref.at[rows(top, p)], o_ref.at[own, rows(top, p)], far_place)
-    crossing = [cross(p) for p in range(2)]
-    landing = [push(q_ref, o_ref.at[own], near_place)]
-    aside = []
-    for p in range(pieces):
-        crossing[p].wait()
-        if p + 2 < pieces:
-            crossing.append(cross(p + 2))
-        if p >= 2:
-            aside[p - 2].wait()
-        spot = o_ref.at[across, rows(top, p)]
+    loads = []
+    for index, (line, other, stage) in enumerate(zip(lines, others, staged)):
+        for side, part_ref in ((y, line), (1 - y, other)):
+            if index == 1:
+                extent = stage.shape[1] // 2
+                spot = stage.at[:, pl.ds(pl.multiple_of(side * extent, 128), extent)]
+            else:
+                extent = stage.shape[0] // 2
+                spot = stage.at[pl.ds(pl.multiple_of(side * extent, 8), extent), :]
+            loads.append(
+                pltpu.make_async_copy(part_ref, spot, load_sems.at[len(loads)])
+            )
+            loads[-1].start()
+    fills = []
+    for k in range(MATRICES):
+        fills.append(pltpu.make_async_copy(moments[k], values[k], value_sems.at[k]))
+        fills[-1].start()
+    norm = norm_ref[0:1, 0:1]
+    clip = jnp.minimum(1.0, 1.0 / (norm + 1e-06))
+
+    def blend(value, start, stage, stage_start, count):
+        slab = 16 if count % 16 == 0 else 8
+
+        def one(i, carry):
+            spot = pl.ds(pl.multiple_of(start + i * slab, 8), slab)
+            source = pl.ds(pl.multiple_of(stage_start + i * slab, 8), slab)
+            value[spot, :] = muon_momentum * value[spot, :] + clip * stage[source, :]
+            return carry
+
+        lax.fori_loop(0, count // slab, one, 0, unroll=min(4, count // slab))
+
+    blocks = lax.axis_size("wide")
+    shares = [values[k].shape[0] // blocks for k in range(2)]
+    outs = []
+    for load in loads[:2]:
+        load.wait()
+    for k in range(2):
+        fills[k].wait()
+
+    def one_block(b, carry):
+        stage_start = b * (shares[0] + shares[1])
+        blend(values[0], b * shares[0], staged[0], stage_start, shares[0])
+        blend(values[1], b * shares[1], staged[0], stage_start + shares[0], shares[1])
+        return carry
+
+    lax.fori_loop(0, blocks, one_block, 0)
+    for k in (2, 3):
+        loads[2 * k - 2].wait()
+        loads[2 * k - 1].wait()
+        fills[k].wait()
+        blend(values[k], 0, staged[k - 1], 0, values[k].shape[0])
+    for k in range(MATRICES):
+        outs.append(pltpu.make_async_copy(values[k], carried[k], out_sems.at[k]))
+        outs[-1].start()
+    for k in range(MATRICES):
+
+        def cut(i, carry, k=k):
+            spot = pl.ds(pl.multiple_of(i * SLAB, SLAB), SLAB)
+            highs[k][spot, :], lows[k][spot, :] = split(values[k][spot, :])
+            return carry
+
+        lax.fori_loop(0, values[k].shape[0] // SLAB, cut, 0, unroll=UNROLL)
+    for k in range(MATRICES):
+        outs[k].wait()
+        fills[k] = pltpu.make_async_copy(weights[k], values[k], value_sems.at[k])
+        fills[k].start()
+
+    dot = lambda left, right, dims: lax.dot_general(
+        left, right, (dims, ((), ())), preferred_element_type=jnp.float32
+    )
+    lengths = (3 * D, D, FF, FF)
+
+    def process(k, start):
+        spot = pl.ds(pl.multiple_of(start, BLK), BLK)
+        q_high, q_low = split(qs[k, spot, :])
+        high, low = highs[k], lows[k]
+        scale = muon_rate * 0.2 * math.sqrt(lengths[k])
+        if k == 2:
+            dims = ((1,), (0,))
+            polar = dot(q_high, high[...], dims) + (
+                dot(q_high, low[...], dims) + dot(q_low, high[...], dims)
+            )
+            where = (spot, slice(None))
+        else:
+            dims = ((1,), (1,))
+            polar = dot(high[...], q_high, dims) + (
+                dot(low[...], q_high, dims) + dot(high[...], q_low, dims)
+            )
+            where = (slice(None), spot)
+        values[k][where] = values[k][where] * (1.0 - muon_rate * weight_decay) - scale * polar
+        pltpu.make_async_copy(
+            values[k].at[where], results[k].at[where], out_sems.at[k]
+        ).start()
+
+    def pair(first, starts):
+        for side in range(2):
+            matrices = (0, 1) if first == (side == 0) else (2, 3)
+
+            @pl.when(far == side)
+            def _(matrices=matrices):
+                for k in matrices:
+                    lax.fori_loop(
+                        0, len(starts), lambda i, c, k=k: (process(k, starts[0] + i * BLK), c)[1], 0
+                    )
+
+    aside, near_across, near_side = [], [], []
+
+    def forward(p):
+        crossing[p].wait_recv()
+        spot = qs.at[across, rows(y, p)]
         aside.append(push(spot, spot, side_place))
-        landing.append(push(spot, spot, near_place))
-        if p >= 2:
-            spot = o_ref.at[across, rows(1 - top, p - 2)]
-            landing.append(push(spot, spot, near_place))
-    for p in range(pieces - 2, pieces):
-        aside[p].wait()
-        spot = o_ref.at[across, rows(1 - top, p)]
-        landing.append(push(spot, spot, near_place))
+        near_across.append(push(spot, spot, near_place))
+
+    def forward_side(p):
+        aside[p].wait_recv()
+        spot = qs.at[across, rows(1 - y, p)]
+        near_side.append(push(spot, spot, near_place))
+
+    forward(0)
     keep.wait()
-    for copy in landing:
+    near_own.wait_recv()
+    for k in range(MATRICES):
+        fills[k].wait()
+    pair(True, [0, BLK])
+    forward(1)
+    pair(True, [2 * BLK, 3 * BLK])
+    forward_side(0)
+    for p in range(2, pieces):
+        forward(p)
+        forward_side(p - 1)
+    group = BLK // step
+    for copy in near_across:
+        copy.wait_recv()
+    pair(False, [y * half + i * BLK for i in range(half // BLK)])
+    for copy in near_side[:group]:
+        copy.wait_recv()
+    pair(False, [(1 - y) * half])
+    forward_side(pieces - 1)
+    for copy in near_side[group:]:
+        copy.wait_recv()
+    pair(False, [(1 - y) * half + BLK])
+    for copy in copies:
         copy.wait_send()
-    for copy in landing:
-        copy.wait_recv()
-
-
-def spread(factor, number):
+    for k in range(MATRICES):
+        pltpu.make_async_copy(values[k], results[k], out_sems.at[k]).wait()
+
+
+def finish(norm, factor, lines, others, moments, weights, number):
+    pieces = 4
     size = factor.shape[0]
-    pieces = 8
+    sub = lax.axis_size("narrow") // MATRICES
+    anywhere = pl.BlockSpec(memory_space=pl.ANY)
+    operands = [part for both in zip(lines, others) for part in both]
+    shapes = [jax.ShapeDtypeStruct(moment.shape, jnp.float32) for moment in moments]
+    staged = [(moments[0].shape[0] + moments[1].shape[0], size), moments[2].shape, moments[3].shape]
     slots = 1 + 4 * pieces
-    sub = lax.axis_size("narrow") // MATRICES
-    return pl.pallas_call(
-        functools.partial(spread_kernel, sub, pieces),
-        out_shape=jax.ShapeDtypeStruct((MATRICES, size, size), jnp.float32),
-        in_specs=[pl.BlockSpec(memory_space=pltpu.VMEM)],
-        out_specs=pl.BlockSpec(memory_space=pl.ANY),
-        scratch_shapes=[
+    outs = pl.pallas_call(
+        functools.partial(finish_kernel, sub, pieces),
+        out_shape=tuple(shapes + shapes),
+        in_specs=[pl.BlockSpec(memory_space=pltpu.VMEM)] + [anywhere] * (1 + len(operands) + 8),
+        out_specs=(anywhere,) * 8,
+        scratch_shapes=[pltpu.VMEM((MATRICES, size, size), jnp.float32)]
+        + [pltpu.VMEM(shape, jnp.float32) for shape in staged]
+        + [pltpu.VMEM(moment.shape, jnp.float32) for moment in moments]
+        + [pltpu.VMEM(moment.shape, jnp.bfloat16) for moment in moments]
+        + [pltpu.VMEM(moment.shape, jnp.bfloat16) for moment in moments]
+        + [
             pltpu.SemaphoreType.DMA((slots,)),
             pltpu.SemaphoreType.DMA((slots,)),
             pltpu.SemaphoreType.DMA((1,)),
+            pltpu.SemaphoreType.DMA((6,)),
+            pltpu.SemaphoreType.DMA((MATRICES,)),
+            pltpu.SemaphoreType.DMA((MATRICES,)),
         ],
-        compiler_params=pltpu.CompilerParams(collective_id=number, has_side_effects=True),
-    )(factor)
+        compiler_params=pltpu.CompilerParams(
+            collective_id=number, has_side_effects=True, vmem_limit_bytes=60 * 2**20
+        ),
+        cost_estimate=pl.CostEstimate(
+            flops=18 * size * size * size, bytes_accessed=80 * size * size, transcendentals=0
+        ),
+    )(norm, factor, *operands, *moments, *weights)
+    return outs[:4], outs[4:]
 
 
 def adam_update(weight, moment, square, gradient):
@@ -867,13 +928,6 @@
         jnp.sqrt(square_hat) + 1e-08
     )
     return (moment_new, square_new, weight_new)
-
-
-def muon_finish(weight, polar_part, longest):
-    return (
-        weight * (1.0 - muon_rate * weight_decay)
-        - muon_rate * 0.2 * math.sqrt(longest) * polar_part
-    )
 
 
 def column_shifts(strip, column):
@@ -989,7 +1043,7 @@
         entry_grad_ref[...] += back
 
 
-def middle(entry, grad_ffn, expand, reduce, taps):
+def middle(entry, entry_t, grad_ffn, expand, reduce, taps):
     tokens, width = entry.shape
     hidden_units = expand.shape[1]
     block = min(256, hidden_units)
@@ -1033,7 +1087,7 @@
             bytes_accessed=32 * tokens * width,
             transcendentals=tokens * hidden_units,
         ),
-    )(entry, entry.T, grad_ffn, expand, reduce, taps)
+    )(entry, entry_t, grad_ffn, expand, reduce, taps)
 
 
 def norm_strip(values):
@@ -1243,6 +1297,281 @@
     )(hidden, branch, grad_entry, grad_result, scale, gate)
 
 
+def dot_of(left, right, left_axis, right_axis):
+    return lax.dot_general(
+        left,
+        right,
+        (((left_axis,), (right_axis,)), ((), ())),
+        preferred_element_type=jnp.float32,
+    )
+
+
+def head_only(values, head):
+    lane = lax.broadcasted_iota(jnp.int32, values.shape, 1)
+    return jnp.where(lane // HEAD == head, values, jnp.zeros_like(values))
+
+
+def attend_kernel(
+    mixed_ref, attend_ref, triple_ref, context_ref, logsum_ref, turned, values_t
+):
+    tokens = mixed_ref.shape[0]
+    width = context_ref.shape[1]
+    step = min(BLK, width)
+    for start in range(0, 3 * width, step):
+        columns = pl.ds(start, step)
+        triple_ref[:, columns] = dot_of(mixed_ref[...], attend_ref[:, columns], 1, 0).astype(
+            jnp.bfloat16
+        )
+    values_t[...] = triple_ref[:, pl.ds(2 * width, width)].T
+    scale = jnp.bfloat16(HEAD ** (-0.5))
+    for head in range(width // HEAD):
+        pair = head * HEAD // LANES * LANES
+        inside = head % (LANES // HEAD)
+
+        def one(block, carry, head=head, pair=pair, inside=inside):
+            spot = pl.ds(pl.multiple_of(block * QUERIES, QUERIES), QUERIES)
+            queries = head_only(triple_ref[spot, pl.ds(pair, LANES)], inside) * scale
+            scores = dot_of(triple_ref[:, pl.ds(width + pair, LANES)], queries, 1, 1)
+            peak = jnp.max(scores, axis=0, keepdims=True)
+            weights = jnp.exp(scores - peak)
+            total = jnp.sum(weights, axis=0, keepdims=True)
+            soft_low = (weights * (1.0 / total)).astype(jnp.bfloat16)
+            turned[pl.ds(head * HEAD, HEAD), spot] = dot_of(
+                values_t[pl.ds(head * HEAD, HEAD), :], soft_low, 1, 0
+            )
+            logsum_ref[pl.ds(head, 1), spot] = peak + jnp.log(total)
+            return carry
+
+        lax.fori_loop(0, tokens // QUERIES, one, 0)
+    context_ref[...] = turned[...].T.astype(jnp.bfloat16)
+
+
+def attend(mixed, attend_low):
+    tokens, width = mixed.shape
+    own = attend_low.shape[1] // 3
+    vmem = pl.BlockSpec(memory_space=pltpu.VMEM)
+    return pl.pallas_call(
+        attend_kernel,
+        out_shape=(
+            jax.ShapeDtypeStruct((tokens, 3 * own), jnp.bfloat16),
+            jax.ShapeDtypeStruct((tokens, own), jnp.bfloat16),
+            jax.ShapeDtypeStruct((8, tokens), jnp.float32),
+        ),
+        in_specs=[vmem] * 2,
+        out_specs=(vmem,) * 3,
+        scratch_shapes=[
+            pltpu.VMEM((own, tokens), jnp.float32),
+            pltpu.VMEM((own, tokens), jnp.bfloat16),
+        ],
+        compiler_params=pltpu.CompilerParams(vmem_limit_bytes=40 * 2**20),
+        cost_estimate=pl.CostEstimate(
+            flops=16 * tokens * tokens * own,
+            bytes_accessed=12 * tokens * width,
+            transcendentals=tokens * tokens * own // HEAD,
+        ),
+    )(mixed, attend_low)
+
+
+def attend_back_kernel(
+    mixed_ref,
+    attend_ref,
+    output_ref,
+    triple_ref,
+    context_ref,
+    logsum_ref,
+    grad_branch_ref,
+    grad_output_ref,
+    grad_attend_ref,
+    grad_mixed_ref,
+    grad_context,
+    keys_t,
+    grad_queries_t,
+    grad_keys,
+    grad_values,
+    grad_triple,
+):
+    tokens = mixed_ref.shape[0]
+    width = output_ref.shape[0]
+    grad_context[...] = dot_of(grad_branch_ref[...], output_ref[...], 1, 1).astype(jnp.bfloat16)
+    keys_t[...] = triple_ref[:, pl.ds(width, width)].T
+    grad_keys[...] = jnp.zeros_like(grad_keys)
+    grad_values[...] = jnp.zeros_like(grad_values)
+    scale = HEAD ** (-0.5)
+    low_scale = jnp.bfloat16(scale)
+    for head in range(width // HEAD):
+        pair = head * HEAD // LANES * LANES
+        inside = head % (LANES // HEAD)
+        lanes = pl.ds(pair, LANES)
+
+        def one(block, carry, head=head, pair=pair, inside=inside, lanes=lanes):
+            spot = pl.ds(pl.multiple_of(block * QUERIES, QUERIES), QUERIES)
+            queries = head_only(triple_ref[spot, lanes], inside)
+            back = head_only(grad_context[spot, lanes], inside)
+            scores = dot_of(triple_ref[:, pl.ds(width + pair, LANES)], queries * low_scale, 1, 1)
+            weights = jnp.exp(scores - logsum_ref[pl.ds(head, 1), spot])
+            grad_weights = dot_of(triple_ref[:, pl.ds(2 * width + pair, LANES)], back, 1, 1)
+            grad_values[:, lanes] += dot_of(weights.astype(jnp.bfloat16), back, 1, 0)
+            inner = jnp.sum(weights * grad_weights, axis=0, keepdims=True)
+            grad_low = (weights * (grad_weights - inner)).astype(jnp.bfloat16)
+            grad_keys[:, lanes] += dot_of(grad_low, queries, 1, 0)
+            grad_queries_t[pl.ds(head * HEAD, HEAD), spot] = dot_of(
+                keys_t[pl.ds(head * HEAD, HEAD), :], grad_low, 1, 0
+            )
+            return carry
+
+        lax.fori_loop(0, tokens // QUERIES, one, 0)
+    grad_triple[:, pl.ds(0, width)] = (grad_queries_t[...].T * scale).astype(jnp.bfloat16)
+    grad_triple[:, pl.ds(width, width)] = (grad_keys[...] * scale).astype(jnp.bfloat16)
+    grad_triple[:, pl.ds(2 * width, width)] = grad_values[...].astype(jnp.bfloat16)
+    grad_output_ref[...] = dot_of(context_ref[...], grad_branch_ref[...], 0, 0)
+    grad_attend_ref[...] = dot_of(grad_triple[...], mixed_ref[...], 0, 0)
+    grad_mixed_ref[...] = dot_of(grad_triple[...], attend_ref[...], 1, 1)
+
+
+def attend_back(mixed, attend_low, output_low, triple, context, logsum, grad_branch):
+    tokens, width = mixed.shape
+    own = output_low.shape[0]
+    vmem = pl.BlockSpec(memory_space=pltpu.VMEM)
+    f32 = lambda *shape: jax.ShapeDtypeStruct(shape, jnp.float32)
+    return pl.pallas_call(
+        attend_back_kernel,
+        out_shape=(f32(own, width), f32(3 * own, width), f32(tokens, width)),
+        in_specs=[vmem] * 7,
+        out_specs=(vmem,) * 3,
+        scratch_shapes=[
+            pltpu.VMEM((tokens, own), jnp.bfloat16),
+            pltpu.VMEM((own, tokens), jnp.bfloat16),
+            pltpu.VMEM((own, tokens), jnp.float32),
+            pltpu.VMEM((tokens, own), jnp.float32),
+            pltpu.VMEM((tokens, own), jnp.float32),
+            pltpu.VMEM((tokens, 3 * own), jnp.bfloat16),
+        ],
+        compiler_params=pltpu.CompilerParams(vmem_limit_bytes=52 * 2**20),
+        cost_estimate=pl.CostEstimate(
+            flops=40 * tokens * tokens * own,
+            bytes_accessed=20 * tokens * width,
+            transcendentals=tokens * tokens * own // HEAD,
+        ),
+    )(mixed, attend_low, output_low, triple, context, logsum, grad_branch)
+
+
+def narrow_hops():
+    return [("narrow", bit) for bit in reversed(bits_of(lax.axis_size("narrow")))]
+
+
+def narrow_position(item):
+    n = lax.axis_index("narrow")
+    position = 0
+    for index, (_, bit) in enumerate(narrow_hops()):
+        value = (n // bit) % 2
+        if (item >> index) % 2:
+            value = 1 - value
+        position = position + value * 2**index
+    return position
+
+
+def entry_kernel(
+    pieces,
+    context_ref,
+    tokens_ref,
+    output_ref,
+    gate_ref,
+    shift_ref,
+    scale_ref,
+    branch_ref,
+    hidden_ref,
+    entry_ref,
+    entry_t_ref,
+    slots,
+    output_low,
+    sends,
+    arrivals,
+):
+    rows, own = context_ref.shape
+    step = rows // pieces
+    hops = narrow_hops()
+    count = 2 ** len(hops)
+    greet([place_at(axis, bit) for axis, bit in hops])
+    chunk = lambda p: pl.ds(p * step, step)
+    slots[narrow_position(0)] = context_ref[...].astype(jnp.float32)
+    gathers = []
+    for p in range(pieces):
+        spot_of = lambda item, p=p: slots.at[narrow_position(item), chunk(p)]
+        gathers.append(Gather(spot_of(0), spot_of, hops, sends, arrivals, p * (count - 1)))
+        gathers[p].step(0)
+    output_low[...] = output_ref[...].astype(jnp.bfloat16)
+    gate, offset, stretch = gate_ref[...], shift_ref[...], 1.0 + scale_ref[...]
+    for p in range(pieces):
+        for item in gathers[p].order[1:]:
+            gathers[p].step(item)
+        branch = jnp.zeros((step, output_ref.shape[1]), jnp.float32)
+        for position in range(count):
+            branch = branch + dot_of(
+                slots[position, chunk(p)].astype(jnp.bfloat16),
+                output_low[pl.ds(position * own, own), :],
+                1,
+                0,
+            )
+        branch_ref[chunk(p), :] = branch
+
+        def one(i, carry, p=p):
+            spot = pl.ds(pl.multiple_of(p * step + i * SLAB, SLAB), SLAB)
+            hidden = tokens_ref[spot, :].astype(jnp.float32) + gate * branch_ref[spot, :]
+            hidden_ref[spot, :] = hidden
+            normed, _ = norm_strip(hidden)
+            entry_ref[spot, :] = (normed * stretch + offset).astype(jnp.bfloat16)
+            return carry
+
+        lax.fori_loop(0, step // SLAB, one, 0, unroll=UNROLL)
+        entry_t_ref[:, chunk(p)] = entry_ref[chunk(p), :].T
+    for gather in gathers:
+        gather.finish()
+
+
+def enter(context, tokens, output_all, gate, shift, scale, number):
+    pieces = 4
+    rows, own = context.shape
+    width = tokens.shape[1]
+    count = lax.axis_size("narrow")
+    vmem = pl.BlockSpec(memory_space=pltpu.VMEM)
+    slots = pieces * (count - 1)
+    return pl.pallas_call(
+        functools.partial(entry_kernel, pieces),
+        out_shape=(
+            jax.ShapeDtypeStruct((rows, width), jnp.float32),
+            jax.ShapeDtypeStruct((rows, width), jnp.float32),
+            jax.ShapeDtypeStruct((rows, width), jnp.bfloat16),
+            jax.ShapeDtypeStruct((width, rows), jnp.bfloat16),
+        ),
+        in_specs=[vmem] * 6,
+        out_specs=(vmem,) * 4,
+        scratch_shapes=[
+            pltpu.VMEM((count, rows, own), jnp.float32),
+            pltpu.VMEM(output_all.shape, jnp.bfloat16),
+            pltpu.SemaphoreType.DMA((slots,)),
+            pltpu.SemaphoreType.DMA((slots,)),
+        ],
+        compiler_params=pltpu.CompilerParams(
+            collective_id=number, has_side_effects=True, vmem_limit_bytes=40 * 2**20
+        ),
+        cost_estimate=pl.CostEstimate(
+            flops=2 * rows * width * width, bytes_accessed=100 * rows * width, transcendentals=0
+        ),
+    )(context, tokens, output_all, gate, shift, scale)
+
+
+def all_rows(values):
+    for _, bit in narrow_hops():
+        side = (lax.axis_index("narrow") // bit) % 2
+        other = permute(values, "narrow", bit)
+        values = jnp.where(
+            side == 0,
+            jnp.concatenate([values, other], axis=0),
+            jnp.concatenate([other, values], axis=0),
+        )
+    return values
+
+
 def interleave(first, second):
     count = lax.axis_size("wide")
     width = first.shape[1]
@@ -1279,13 +1608,6 @@
             for at in range(0, count, LANES)
         ],
         axis=0,
-    )
-
-
-def apply_factor(factor, matrix, layout):
-    left, right = (factor, matrix) if layout == "columns" else (matrix, factor)
-    return jnp.dot(
-        left, right, precision=lax.Precision.HIGH, preferred_element_type=jnp.float32
     )
 
 
@@ -1312,11 +1634,7 @@
     hidden_first,
     hidden_second,
 ):
-    item_count = tokens.shape[0]
-    seq_len = tokens.shape[1]
-    local_heads = attend_weight.shape[2] // HEAD
     live_mask = item_live.astype(jnp.float32)[:, None, None]
-    token_rows = tokens.astype(jnp.float32)
     modulation = modulation_table[None] + conditions
     shift_one = modulation[:, 0:1]
     scale_one = modulation[:, 1:2]
@@ -1326,31 +1644,21 @@
     gate_two = modulation[:, 5:6]
     width = tokens.shape[2]
     flat_tokens = tokens.reshape(-1, width)
-    mixed_low = mixer_forward(flat_tokens, shift_one[0], scale_one[0], mixer_kernel)[None]
-    attend_low = attend_weight.astype(jnp.bfloat16)
-    triple = jnp.einsum(
-        "isd,dkc->iskc", mixed_low, attend_low, preferred_element_type=jnp.float32
-    ).astype(jnp.bfloat16)
-    heads_split = triple.reshape(item_count, seq_len, 3, local_heads, HEAD)
-
-    def attend_item(member):
-        return attend_forward(member[:, 0], member[:, 1], member[:, 2])
-
-    context, logsum = lax.map(attend_item, heads_split)
+    mixed_low = mixer_forward(flat_tokens, shift_one[0], scale_one[0], mixer_kernel)
+    output_all = all_rows(output_weight)
     output_low = output_weight.astype(jnp.bfloat16)
-    branch_partial = jnp.einsum(
-        "isc,cd->isd", context, output_low, preferred_element_type=jnp.float32
-    )
-    (branch,) = sum_scatter(branch_partial.reshape(-1, width), [], [], 1)
-    branch = branch.reshape(tokens.shape)
-    hidden = token_rows + gate_one * branch
-    entry_low = entry_piece(hidden, shift_two, scale_two).astype(jnp.bfloat16)
+    attend_low = attend_weight.astype(jnp.bfloat16).reshape(width, -1)
+    triple, context, logsum = attend(mixed_low, attend_low)
+    branch, hidden, entry_low, entry_turned = enter(
+        context, flat_tokens, output_all, gate_one[0], shift_two[0], scale_two[0], 1
+    )
     expand_low = expand_weight.astype(jnp.bfloat16)
     reduce_low = reduce_weight.astype(jnp.bfloat16)
     grad_result = cotangent.astype(jnp.float32) * live_mask
     grad_ffn_low = (gate_two * grad_result).astype(jnp.bfloat16)
     ffn_partial, entry_partial, grad_reduce, grad_expand, grad_hidden_kernel = middle(
-        entry_low.reshape(-1, width),
+        entry_low,
+        entry_turned,
         grad_ffn_low.reshape(-1, width),
         expand_low,
         reduce_low,
@@ -1366,37 +1674,18 @@
     ffn_half = ffn_keep + ffn_other
     ffn_across = permute(ffn_half, "narrow", 2)
     grad_hidden, grad_branch_low, grad_shift_two, grad_scale_two, grad_gate_one = hidden_backward(
-        hidden.reshape(-1, width),
-        branch.reshape(-1, width),
+        hidden,
+        branch,
         grad_entry,
         grad_result.reshape(-1, width),
         scale_two[0],
         gate_one[0],
     )
-    grad_branch_low = grad_branch_low.reshape(tokens.shape)
-    grad_output = jnp.einsum(
-        "isc,isd->cd", context, grad_branch_low, preferred_element_type=jnp.float32
-    )
-    grad_context = jnp.einsum(
-        "isd,cd->isc", grad_branch_low, output_low, preferred_element_type=jnp.float32
-    ).astype(jnp.bfloat16)
-
-    def attend_item_back(pieces):
-        member, logsum_item, grad_item = pieces
-        return attend_backward(
-            member[:, 0],
-            member[:, 1],
-            member[:, 2],
-            logsum_item,
-            grad_item.reshape(seq_len, local_heads, HEAD),
-        )
-
-    grad_split = lax.map(attend_item_back, (heads_split, logsum, grad_context))
-    grad_triple = grad_split.reshape(item_count, seq_len, 3, local_heads * HEAD).astype(
-        jnp.bfloat16
-    )
-    *reduce_pieces, ffn_across, expand_other, grad_triple = together(
-        *reduce_pieces, ffn_across, expand_other, grad_triple
+    grad_output, grad_attend, mixed_partial = attend_back(
+        mixed_low, attend_low, output_low, triple, context, logsum, grad_branch_low
+    )
+    *reduce_pieces, ffn_across, expand_other, mixed_partial = together(
+        *reduce_pieces, ffn_across, expand_other, mixed_partial
     )
     ffn_half = ffn_half + ffn_across
     for bit in bits_of(lax.axis_size("narrow"))[2:]:
@@ -1404,15 +1693,9 @@
     expand_half = expand_keep + expand_other
     reduce_line = line_place(reduce_share, reduce_pieces)
     ffn_other = permute(ffn_half, "narrow", 1)
-    grad_attend = jnp.einsum(
-        "iskc,isd->kcd", grad_triple, mixed_low, preferred_element_type=jnp.float32
-    )
-    attend_out = interleave(grad_attend.reshape(-1, width), grad_output)
-    mixed_partial = jnp.einsum(
-        "iskc,dkc->isd", grad_triple, attend_low, preferred_element_type=jnp.float32
-    )
+    attend_out = interleave(grad_attend, grad_output)
     grad_mixed, expand_share, attend_out_share = sum_scatter(
-        mixed_partial.reshape(-1, width), [expand_half, attend_out], ["half", "rows"], 3
+        mixed_partial, [expand_half, attend_out], ["half", "rows"], 3
     )
     ffn_other, grad_mixed, expand_share, reduce_line = together(
         ffn_other, grad_mixed, expand_share, reduce_line
@@ -1420,7 +1703,7 @@
     expand_pieces = line_gather(expand_share)
     reduce_other = permute(reduce_line, "wide", 1)
     ffn_branch = core_place(ffn_half, ffn_other).reshape(tokens.shape)
-    block_out = (live_mask * (hidden + gate_two * ffn_branch)).astype(jnp.bfloat16)
+    block_out = (live_mask * (hidden[None] + gate_two * ffn_branch)).astype(jnp.bfloat16)
     grad_gate_two = jnp.sum(ffn_branch * grad_result, axis=1)
     tokens_gradient, grad_mixer_kernel, grad_shift_one, grad_scale_one = mixer_backward(
         flat_tokens,
@@ -1481,19 +1764,22 @@
     gramian, expand_line, attend_out_line = together(gramian, expand_line, attend_out_line)
     expand_other = permute(expand_line, "wide", 1)
     attend_out_other = permute(attend_out_line, "wide", 1)
-    factors = spread(polar_factor(gramian), 6)
-    factors, expand_other, attend_out_other, reduce_other = together(
-        factors, expand_other, attend_out_other, reduce_other
-    )
-    attend_whole, output_whole = part(
-        pair_place(attend_out_line, attend_out_other, 0), grad_output.shape[0]
-    )
-    carried = [
-        blend(attend_moment, attend_whole.T.reshape(attend_moment.shape)),
-        blend(output_moment, output_whole),
-        blend(expand_moment, pair_place(expand_line, expand_other, 1)),
-        blend(reduce_moment, pair_place(reduce_line, reduce_other, 0)),
-    ]
+    factor = polar_factor(gramian)
+    factor, expand_other, attend_out_other, reduce_other = together(
+        factor, expand_other, attend_out_other, reduce_other
+    )
+    turn = lambda matrix: matrix.reshape(width, -1).T
+    carried, results = finish(
+        norm,
+        factor,
+        [attend_out_line, expand_line, reduce_line],
+        [attend_out_other, expand_other, reduce_other],
+        [attend_turned, output_moment, expand_moment, reduce_moment],
+        [turn(attend_weight), output_weight, expand_weight, reduce_weight],
+        6,
+    )
+    attend_carried = carried[0].T.reshape(attend_weight.shape)
+    attend_result = results[0].T.reshape(attend_weight.shape)
     table_moment, table_square, table_result = adam_update(
         modulation_table, table_first, table_second, clip_factor * summed_table
     )
@@ -1503,28 +1789,18 @@
     hidden_moment, hidden_square, hidden_result = adam_update(
         hidden_kernel, hidden_first, hidden_second, clip_factor * summed_hidden
     )
-    matrices = [carried[0].reshape(width, -1), carried[1], carried[2], carried[3]]
-    layouts = ("columns", "rows", "columns", "rows")
-    polar_parts = [
-        apply_factor(factors[position], matrix, layout)
-        for position, (matrix, layout) in enumerate(zip(matrices, layouts))
-    ]
-    attend_result = muon_finish(attend_weight, polar_parts[0].reshape(attend_weight.shape), 3 * D)
-    output_result = muon_finish(output_weight, polar_parts[1], D)
-    expand_result = muon_finish(expand_weight, polar_parts[2], FF)
-    reduce_result = muon_finish(reduce_weight, polar_parts[3], FF)
     return (
         block_out,
         tokens_gradient,
         gradient_norm,
-        carried[0],
+        attend_carried,
         carried[1],
         carried[2],
         carried[3],
         attend_result,
-        output_result,
-        expand_result,
-        reduce_result,
+        results[1],
+        results[2],
+        results[3],
         table_moment,
         table_square,
         table_result,

time: 792 us -> 764 us (0.965)
  matrix products: 86.2 us -> 3.91 us
  waiting for transfers between devices: 0.03 us -> 42.1 us
  Pallas kernels: 548 us -> 567 us
  other arithmetic: 67.2 us -> 54.4 us
    dot_general x24 -> x0, matrix products: 82.2 us -> none  [the longest x4 32.2 us: apply_factor(): jnp.dot(left, right, precision=lax.Precision.HIGH, preferred_element_type...]
    pallas_call x1 -> x4, Pallas kernels: 62.7 us -> 137 us  [the longest x1 74.1 us: finish(): pl.pallas_call(functools.partial(finish_kernel, sub, pieces), out_shape=t...]
    pallas_call x3 -> x2, Pallas kernels: 192 us -> 138 us  [sum_scatter(): pl.pallas_call(functools.partial(sum_scatter_kernel, kinds, pieces), out_...]
    ppermute x13 -> x15, waiting for transfers between devices: 0.03 us -> 42.1 us  [permute(): lax.ppermute(values, axis, [(index, index ^ bit) for index in range(size)])]
    unnamed x136 -> x126, local copies, waits for them, and re-layouts: 28.3 us -> 52.2 us
    add x8 -> x4, other arithmetic: 14.6 us -> 3.88 us  [local(): muon_momentum * moment + clip_factor * gradient]
    ppermute x13 -> x15, starting transfers between devices: 12.3 us -> 16.2 us  [permute(): lax.ppermute(values, axis, [(index, index ^ bit) for index in range(size)])]
  transfers between devices with their start and end apart: 13 -> 15, of which waited for: 0 -> 3; matrix products, arithmetic and copies ran while one was open for 14% -> 8% of each run, Pallas kernels for 57% -> 56%
where the time goes in v4:
time: 764 us; the launch traced here: 754 us
  Pallas kernels  567 us (74%)
  local copies, waits for them, and re-layouts  67.3 us (9%)
  other arithmetic  54.4 us (7%)
  waiting for transfers between devices  42.1 us (6%)
  starting transfers between devices  16.2 us (2%)
    pallas_call x2, Pallas kernels, sum_scatter(): pl.pallas_call(functools.partial(sum_scatter_kernel, kinds, pieces), out_...  138 us
    pallas_call x1, Pallas kernels, gram_whole(): pl.pallas_call(functools.partial(gram_kernel, narrow_bits, hops), out_sha...  84.5 us
    pallas_call x1, Pallas kernels, polar_factor(): pl.pallas_call(polar_kernel, out_shape=jax.ShapeDtypeStruct((size, size),...  75.7 us
    pallas_call x1, Pallas kernels, finish(): pl.pallas_call(functools.partial(finish_kernel, sub, pieces), out_shape=t...  74.1 us
    unnamed x126, local copies, waits for them, and re-layouts  52.2 us
    pallas_call x1, Pallas kernels, small_sums(): pl.pallas_call(functools.partial(small_kernel, shared_rows, split_rows),...  51.3 us
    ppermute x15, waiting for transfers between devices, permute(): lax.ppermute(values, axis, [(index, index ^ bit) for index in range(size)])  42.1 us
    pallas_call x1, Pallas kernels, middle(): pl.pallas_call(middle_kernel, grid=(hidden_units // block,), out_shape=(f...  39.9 us
  transfers between devices with their start and end apart: 15, of which 3 were waited for; matrix products, arithmetic and copies ran while one was open for 8% of the time, Pallas kernels for 56%

profile of v4, /device:TPU:13, one launch (start us, length us, event | category | flops | bytes accessed | tf_op | source)
XLA Modules:
  0.0 754.4 jit_solution(16370410356678671647)
XLA Ops:
  1.9 23.0 %collective-permute-done = f32[256,1024]{1,0:T(8,128)S(1)} collective-permute-done((f32[256,1024]{1,0:T(8,128)}, f32[256,1024]{1,0:T(8,128)S(1)}, u32[]{:S(2)}, u32[]{:S(2)}) %collective-permute-start) | collective-permute-done | bytes 1048608 | tf_op jit(solution)/shard_map/ppermute | solution.py:97
  25.0 3.3 maximum_select_fusion.3
  29.8 2.4 copy.48
  34.3 2.6 copy.49.attend_ref
  37.6 4.0 convert_element_type.33.expand_ref
  41.6 1.7 convert_element_type.34.reduce_ref
  43.9 7.4 shard_map.356.mixed_ref
  51.4 8.0 %shard_map.357 = (bf16[1024,768]{1,0:T(8,128)(2,1)S(1)}, bf16[1024,256]{1,0:T(8,128)(2,1)S(1)}, f32[8,1024]{1,0:T(8,128)S(1)}) custom-call(bf16[1024,1024]{1,0:T(8,128)(2,1)S(1)} %shard_map.356.mixed_ref, bf16[1024,768]{1,0:T(8,128)(2,1)S(1)} %copy-done.9), custom_call_target="tpu_custom_call" | custom-call | flops 4294967296 | bytes 12582912 | tf_op jit(solution)/shard_map/pallas_call | solution.py:1353
  59.5 3.5 fusion.6
  63.0 6.8 maximum_select_fusion.output_ref
  69.9 32.9 %shard_map.358 = (f32[1024,1024]{1,0:T(8,128)S(1)}, f32[1024,1024]{1,0:T(8,128)}, bf16[1024,1024]{1,0:T(8,128)(2,1)S(1)}, bf16[1024,1024]{1,0:T(8,128)(2,1)S(1)}) custom-call(bf16[1024,256]{1,0:T(8,128)(2,1)S(1)} %get-tuple-element.85.context_ref, bf16[1024,1024]{1,0:T(8,128)(2,1)S(1)} %bitcast.63, f32[1024,1024]{1,0:T(8,128)} %maximum_select_fusion.output_ref, ...), custom_call_target="tpu_custom_call" | custom-call | flops 2147483648 | bytes 104857600 | tf_op jit(solution)/shard_map/pallas_call | solution.py:1538
  102.8 2.1 copy-done.5
  107.5 39.9 %shard_map.359 = (f32[1024,1024]{1,0:T(8,128)}, f32[1024,1024]{1,0:T(8,128)}, f32[1024,1024]{1,0:T(8,128)}, f32[1024,1024]{1,0:T(8,128)}, f32[9,1024]{1,0:T(8,128)S(1)}) custom-call(bf16[1024,1024]{1,0:T(8,128)(2,1)} %copy-done.15, bf16[1024,1024]{1,0:T(8,128)(2,1)} %copy-done.16, bf16[1024,1024]{1,0:T(8,128)(2,1)} %get-tuple-element.200.grad_ffn_ref, ...), custom_call_target="tpu_custom_call" | custom-call | flops 12884901888 | bytes 33554432 | tf_op jit(solution)/shard_map/pallas_call | solution.py:1052
  147.4 3.2 constant_dynamic-slice_fusion.1
  150.6 2.2 copy-done.2
  152.8 2.2 copy-done.3
  155.0 62.2 %shard_map.360 = (f32[1024,1024]{1,0:T(8,128)S(1)}, f32[128,1024]{1,0:T(8,128)S(1)}) custom-call(f32[1024,1024]{1,0:T(8,128)S(1)} %copy-done.2, f32[1024,1024]{1,0:T(8,128)S(1)} %copy-done.3), custom_call_target="tpu_custom_call" | custom-call | flops 1048576 | bytes 33554432 | tf_op jit(solution)/shard_map/pallas_call | solution.py:422
  217.2 3.7 dynamic-slice_add_fusion.1
  220.9 2.0 collective-permute-start.6
  225.1 2.5 collective-permute-start.3
  228.8 13.4 %shard_map.361 = (f32[1024,1024]{1,0:T(8,128)}, bf16[1024,1024]{1,0:T(8,128)(2,1)S(1)}, f32[1,1024]{1,0:T(1,128)S(1)}, f32[1,1024]{1,0:T(1,128)S(1)}, f32[1,1024]{1,0:T(1,128)S(1)}) custom-call(f32[1024,1024]{1,0:T(8,128)} %get-tuple-element.86.hidden_ref, f32[1024,1024]{1,0:T(8,128)} %copy-done.5, f32[1024,1024]{1,0:T(8,128)} %copy-done.6, ...), custom_call_target="tpu_custom_call" | custom-call | flops 31457280 | bytes 23068672 | tf_op jit(solution)/shard_map/pallas_call | solution.py:1282
  243.5 21.6 %shard_map.362 = (f32[256,1024]{1,0:T(8,128)}, f32[768,1024]{1,0:T(8,128)}, f32[1024,1024]{1,0:T(8,128)}) custom-call(bf16[1024,1024]{1,0:T(8,128)(2,1)} %copy-done.7, bf16[1024,768]{1,0:T(8,128)(2,1)} %copy.49.attend_ref, bf16[256,1024]{1,0:T(8,128)(2,1)S(1)} %convert_element_type.35.output_ref, bf16[1024,768]{1,0:T(8,128)(2,1)} %copy-done.19, ...), custom_call_target="tpu_custom_call" | custom-call | flops 10737418240 | bytes 20971520 | tf_op jit(solution)/shard_map/pallas_call | solution.py:1436
  265.1 8.5 %collective-permute-done.5 = f32[128,1024]{1,0:T(8,128)S(1)} collective-permute-done((f32[128,1024]{1,0:T(8,128)S(1)}, f32[128,1024]{1,0:T(8,128)S(1)}, u32[]{:S(2)}, u32[]{:S(2)}) %collective-permute-start.5) | collective-permute-done | bytes 524320 | tf_op jit(solution)/shard_map/ppermute | solution.py:97
  273.6 4.4 add.182
  278.0 1.9 collective-permute-start.8
  279.9 3.5 copy.51
  283.5 5.0 pad_maximum_fusion
  290.5 1.7 copy-done.1
  292.2 76.0 %shard_map.363 = (f32[1024,1024]{1,0:T(8,128)S(1)}, f32[256,512]{1,0:T(8,128)S(1)}, f32[128,1024]{1,0:T(8,128)S(1)}) custom-call(f32[1024,1024]{1,0:T(8,128)S(1)} %copy-done.1, f32[1024,512]{1,0:T(8,128)S(1)} %dynamic-slice_add_fusion.refs_0_, f32[1024,1024]{1,0:T(8,128)} %bitcast.67), custom_call_target="tpu_custom_call" | custom-call | flops 1048576 | bytes 33554432 | tf_op jit(solution)/shard_map/pallas_call | solution.py:422
  369.8 1.9 collective-permute-start.9
  375.5 2.0 reshape.184
  378.6 4.6 fusion.5
  383.1 20.1 %shard_map.364 = (bf16[1024,1024]{1,0:T(8,128)(2,1)}, f32[9,1024]{1,0:T(8,128)S(1)}, f32[1,1024]{1,0:T(1,128)S(1)}, f32[1,1024]{1,0:T(1,128)S(1)}) custom-call(bf16[1024,1024]{1,0:T(8,128)(2,1)S(1)} %bitcast.64, f32[1,1024]{1,0:T(1,128)S(1)} %get-tuple-element.213.shift_ref, f32[1,1024]{1,0:T(1,128)S(1)} %get-tuple-element.212.scale_ref, ...), custom_call_target="tpu_custom_call" | custom-call | flops 104857600 | bytes 12582912 | tf_op jit(solution)/shard_map/pallas_call | solution.py:1212
  403.6 51.3 %shard_map.365 = (f32[32,1024]{1,0:T(8,128)S(1)}, f32[8,128]{1,0:T(8,128)S(1)}, f32[512,1024]{1,0:T(8,128)S(1)}) custom-call(f32[32,1024]{1,0:T(8,128)S(1)} %pad.4.x_ref, f32[128,1024]{1,0:T(8,128)S(1)} %get-tuple-element.126.share_ref), custom_call_target="tpu_custom_call" | custom-call | tf_op jit(solution)/shard_map/pallas_call | solution.py:502
  455.5 6.9 fusion.8
  463.7 2.9 multiply_add_fusion
  476.9 1.7 copy-done.26
  481.1 84.5 %shard_map.366.g_ref = f32[1024,640]{1,0:T(8,128)S(1)} custom-call(f32[4,256,640]{2,1,0:T(8,128)S(1)} %pad_maximum_fusion.1.x_ref), custom_call_target="tpu_custom_call" | custom-call | tf_op jit(solution)/shard_map/pallas_call | solution.py:590
  567.3 75.7 %shard_map.367.q_ref = f32[1024,1024]{1,0:T(8,128)} custom-call(f32[1024,640]{1,0:T(8,128)S(1)} %shard_map.366.g_ref), custom_call_target="tpu_custom_call" | custom-call | flops 109521666048 | bytes 8388608 | tf_op jit(solution)/shard_map/pallas_call | solution.py:693
  644.5 10.6 %collective-permute-done.13.refs_1_ = f32[512,1024]{1,0:T(8,128)S(1)} collective-permute-done((f32[512,1024]{1,0:T(8,128)S(1)}, f32[512,1024]{1,0:T(8,128)S(1)}, u32[]{:S(2)}, u32[]{:S(2)}) %collective-permute-start.13) | collective-permute-done | bytes 2097184 | tf_op jit(solution)/shard_map/ppermute | solution.py:97
  656.4 74.1 %shard_map.368 = (f32[768,1024]{1,0:T(8,128)}, f32[256,1024]{1,0:T(8,128)}, f32[1024,1024]{1,0:T(8,128)}, f32[1024,1024]{1,0:T(8,128)}, f32[768,1024]{1,0:T(8,12...) custom-call(f32[8,128]{1,0:T(8,128)} %copy-done.14, f32[1024,1024]{1,0:T(8,128)} %shard_map.367.q_ref, ...), custom_call_target="tpu_custom_call" | custom-call | flops 19327352832 | bytes 83886080 | tf_op jit(solution)/shard_map/pallas_call | solution.py:894
  730.5 3.7 copy.53
  734.2 2.4 copy.54
  736.6 2.3 copy.71
  738.9 4.9 copy.72
  743.8 2.1 copy.73
  748.2 2.1 copy.75
  751.9 2.0 copy.76
  (189 shorter events, 43.7 us)
Async XLA Ops:
  0.7 24.3 %collective-permute-start = (f32[256,1024]{1,0:T(8,128)}, f32[256,1024]{1,0:T(8,128)S(1)}, u32[]{:S(2)}, u32[]{:S(2)}) collective-permute-start(f32[256,1024]{1,0:T(8,128)} %refs_11_.1), channel_id=1, source_target_pairs={{0,2},{1,3},{2,0},{3,1},{4,6},{5,7},{6,4},{7,5},{8,10},{9,11},{10,... | collective-permute-start | bytes 3145736 | tf_op jit(solution)/shard_map/ppermute | solution.py:97
  28.2 34.8 %collective-permute-start.1 = (f32[512,1024]{1,0:T(8,128)}, f32[512,1024]{1,0:T(8,128)}, u32[]{:S(2)}, u32[]{:S(2)}) collective-permute-start(f32[512,1024]{1,0:T(8,128)} %maximum_select_fusion.3), channel_id=1, source_target_pairs={{0,1},{1,0},{2,3},{3,2},{4,5},{5,4},{6,7},{7,6},{8,9},{9,8},{10,11... | collective-permute-start | bytes 6291464 | tf_op jit(solution)/shard_map/ppermute | solution.py:97
  43.9 7.4 copy-start.9
  51.4 8.1 %copy-start.7 = (bf16[1024,1024]{1,0:T(8,128)(2,1)}, bf16[1024,1024]{1,0:T(8,128)(2,1)S(1)}, u32[]{:S(2)}) copy-start(bf16[1024,1024]{1,0:T(8,128)(2,1)S(1)} %shard_map.356.mixed_ref) | copy-start | bytes 6291460
  51.4 8.1 %copy-start.21 = (bf16[1,1024,1024]{2,1,0:T(8,128)(2,1)S(1)}, bf16[1,1024,1024]{2,1,0:T(8,128)(2,1)}, u32[]{:S(2)}) copy-start(bf16[1,1024,1024]{2,1,0:T(8,128)(2,1)} %param.24) | copy-start | bytes 6291460
  59.4 10.4 %copy-start.17 = (bf16[1024,256]{1,0:T(8,128)(2,1)}, bf16[1024,256]{1,0:T(8,128)(2,1)S(1)}, u32[]{:S(2)}) copy-start(bf16[1024,256]{1,0:T(8,128)(2,1)S(1)} %get-tuple-element.85.context_ref) | copy-start | bytes 1572868
  69.9 37.6 %copy-start.11 = (f32[9,1024]{1,0:T(8,128)S(1)}, f32[9,1024]{1,0:T(8,128)}, u32[]{:S(2)}) copy-start(f32[9,1024]{1,0:T(8,128)} %taps_ref.4) | copy-start | bytes 110596
  150.6 66.6 %collective-permute-start.2 = (f32[512,1024]{1,0:T(8,128)}, f32[512,1024]{1,0:T(8,128)}, u32[]{:S(2)}, u32[]{:S(2)}) collective-permute-start(f32[512,1024]{1,0:T(8,128)} %constant_dynamic-slice_fusion.1), channel_id=1, source_target_pairs={{0,1},{1,0},{2,3},{3,2},{4,5},{5,4},{6,7},{7,6},{8,9},{9,8},{10,11... | collective-permute-start | bytes 6291464 | tf_op jit(solution)/shard_map/ppermute | solution.py:97
  155.0 62.2 %copy-start.29 = (f32[1024,1024]{1,0:T(8,128)S(1)}, f32[1024,1024]{1,0:T(8,128)}, u32[]{:S(2)}) copy-start(f32[1024,1024]{1,0:T(8,128)} %get-tuple-element.89) | copy-start | bytes 12582916
  217.2 5.7 copy-start.27
  220.9 4.0 copy-start.30
  220.9 52.6 %collective-permute-start.6 = (f32[512,1024]{1,0:T(8,128)S(1)}, f32[512,1024]{1,0:T(8,128)}, u32[]{:S(2)}, u32[]{:S(2)}) collective-permute-start(f32[512,1024]{1,0:T(8,128)S(1)} %dynamic-slice_add_fusion.1), channel_id=1, source_target_pairs={{0,2},{1,3},{2,0},{3,1},{4,6},{5,7},{6,4},{7,5},{8,10},{9,11},{10,... | collective-permute-start | bytes 6291464 | tf_op jit(solution)/shard_map/ppermute | solution.py:97
  224.5 49.1 %collective-permute-start.7 = (f32[1024,512]{1,0:T(8,128)}, f32[1024,512]{1,0:T(8,128)S(1)}, u32[]{:S(2)}, u32[]{:S(2)}) collective-permute-start(f32[1024,512]{1,0:T(8,128)} %constant_dynamic-slice_fusion), channel_id=1, source_target_pairs={{0,4},{4,0},{8,12},{12,8},{16,20},{20,16},{24,28},{28,24},{1,5},{5... | collective-permute-start | bytes 6291464 | tf_op jit(solution)/shard_map/ppermute | solution.py:97
  225.1 40.0 %collective-permute-start.3 = (f32[128,1024]{1,0:T(8,128)S(1)}, f32[128,1024]{1,0:T(8,128)S(1)}, u32[]{:S(2)}, u32[]{:S(2)}) collective-permute-start(f32[128,1024]{1,0:T(8,128)S(1)} %get-tuple-element.96), channel_id=1, source_target_pairs={{0,8},{4,12},{8,0},{12,4},{16,24},{20,28},{24,16},{28,20},{1,9},{5... | collective-permute-start | bytes 1572872 | tf_op jit(solution)/shard_map/ppermute | solution.py:97
  227.5 37.6 %collective-permute-start.4 = (f32[128,1024]{1,0:T(8,128)S(1)}, f32[128,1024]{1,0:T(8,128)S(1)}, u32[]{:S(2)}, u32[]{:S(2)}) collective-permute-start(f32[128,1024]{1,0:T(8,128)S(1)} %get-tuple-element.96), channel_id=1, source_target_pairs={{0,16},{4,20},{8,24},{12,28},{16,0},{20,4},{24,8},{28,12},{1,17},{... | collective-permute-start | bytes 1572872 | tf_op jit(solution)/shard_map/ppermute | solution.py:97
  227.5 46.0 %collective-permute-start.5 = (f32[128,1024]{1,0:T(8,128)S(1)}, f32[128,1024]{1,0:T(8,128)S(1)}, u32[]{:S(2)}, u32[]{:S(2)}) collective-permute-start(f32[128,1024]{1,0:T(8,128)S(1)} %get-tuple-element.96), channel_id=1, source_target_pairs={{0,24},{4,28},{8,16},{12,20},{16,8},{20,12},{24,0},{28,4},{1,25},{... | collective-permute-start | bytes 1572872 | tf_op jit(solution)/shard_map/ppermute | solution.py:97
  228.8 14.7 %copy-start.18 = (bf16[1024,256]{1,0:T(8,128)(2,1)S(1)}, bf16[1024,256]{1,0:T(8,128)(2,1)}, u32[]{:S(2)}) copy-start(bf16[1024,256]{1,0:T(8,128)(2,1)} %copy-done.17) | copy-start | bytes 1572868
  265.1 12.9 %copy-start.40 = (f32[128,1024]{1,0:T(8,128)}, f32[128,1024]{1,0:T(8,128)S(1)}, u32[]{:S(2)}) copy-start(f32[128,1024]{1,0:T(8,128)S(1)} %collective-permute-done.3) | copy-start | bytes 1572868
  265.1 12.9 %copy-start.42 = (f32[128,1024]{1,0:T(8,128)}, f32[128,1024]{1,0:T(8,128)S(1)}, u32[]{:S(2)}) copy-start(f32[128,1024]{1,0:T(8,128)S(1)} %collective-permute-done.4) | copy-start | bytes 1572868
  273.6 4.4 copy-start.44
  273.6 4.4 copy-start.36
  278.0 91.8 %collective-permute-start.8 = (f32[512,1024]{1,0:T(8,128)}, f32[512,1024]{1,0:T(8,128)}, u32[]{:S(2)}, u32[]{:S(2)}) collective-permute-start(f32[512,1024]{1,0:T(8,128)} %add.182), channel_id=1, source_target_pairs={{0,1},{1,0},{2,3},{3,2},{4,5},{5,4},{6,7},{7,6},{8,9},{9,8},{10,11... | collective-permute-start | bytes 6291464 | tf_op jit(solution)/shard_map/ppermute | solution.py:97
  283.5 5.3 copy-start.28
  292.2 76.1 %copy-start.41 = (f32[128,1024]{1,0:T(8,128)S(1)}, f32[128,1024]{1,0:T(8,128)}, u32[]{:S(2)}) copy-start(f32[128,1024]{1,0:T(8,128)} %copy-done.40) | copy-start | bytes 1572868
  292.2 76.1 %copy-start.43 = (f32[128,1024]{1,0:T(8,128)S(1)}, f32[128,1024]{1,0:T(8,128)}, u32[]{:S(2)}) copy-start(f32[128,1024]{1,0:T(8,128)} %copy-done.42) | copy-start | bytes 1572868
  368.2 5.0 copy-start.4
  369.7 4.4 copy-start.22
  369.8 92.6 %collective-permute-start.9 = (f32[256,512]{1,0:T(8,128)S(1)}, f32[256,512]{1,0:T(8,128)}, u32[]{:S(2)}, u32[]{:S(2)}) collective-permute-start(f32[256,512]{1,0:T(8,128)S(1)} %get-tuple-element.118), channel_id=1, source_target_pairs={{0,8},{4,12},{8,0},{12,4},{16,24},{20,28},{24,16},{28,20},{1,9},{5... | collective-permute-start | bytes 1572872 | tf_op jit(solution)/shard_map/ppermute | solution.py:97
  371.7 90.7 %collective-permute-start.10 = (f32[256,512]{1,0:T(8,128)S(1)}, f32[256,512]{1,0:T(8,128)}, u32[]{:S(2)}, u32[]{:S(2)}) collective-permute-start(f32[256,512]{1,0:T(8,128)S(1)} %get-tuple-element.118), channel_id=1, source_target_pairs={{0,16},{4,20},{8,24},{12,28},{16,0},{20,4},{24,8},{28,12},{1,17},{... | collective-permute-start | bytes 1572872 | tf_op jit(solution)/shard_map/ppermute | solution.py:97
  371.7 90.8 %collective-permute-start.11 = (f32[256,512]{1,0:T(8,128)S(1)}, f32[256,512]{1,0:T(8,128)}, u32[]{:S(2)}, u32[]{:S(2)}) collective-permute-start(f32[256,512]{1,0:T(8,128)S(1)} %get-tuple-element.118), channel_id=1, source_target_pairs={{0,24},{4,28},{8,16},{12,20},{16,8},{20,12},{24,0},{28,4},{1,25},{... | collective-permute-start | bytes 1572872 | tf_op jit(solution)/shard_map/ppermute | solution.py:97
  454.9 7.6 %copy-start.14 = (f32[8,128]{1,0:T(8,128)}, f32[8,128]{1,0:T(8,128)S(1)}, u32[]{:S(2)}) copy-start(f32[8,128]{1,0:T(8,128)S(1)} %get-tuple-element.128.norm_ref) | copy-start | bytes 12292
  454.9 111.4 %copy-start.8 = (f32[512,1024]{1,0:T(8,128)}, f32[512,1024]{1,0:T(8,128)S(1)}, u32[]{:S(2)}) copy-start(f32[512,1024]{1,0:T(8,128)S(1)} %get-tuple-element.136.refs_0_) | copy-start | bytes 6291460
  454.9 189.6 %collective-permute-start.14 = (f32[512,1024]{1,0:T(8,128)}, f32[512,1024]{1,0:T(8,128)}, u32[]{:S(2)}, u32[]{:S(2)}) collective-permute-start(f32[512,1024]{1,0:T(8,128)} %copy-done.22), channel_id=1, source_target_pairs={{0,4},{4,0},{8,12},{12,8},{16,20},{20,16},{24,28},{28,24},{1,5},{5... | collective-permute-start | bytes 6291464 | tf_op jit(solution)/shard_map/ppermute | solution.py:97
  467.8 5.0 copy-start.38
  472.8 92.9 %copy-start.25 = (f32[1024,512]{1,0:T(8,128)}, f32[1024,512]{1,0:T(8,128)S(1)}, u32[]{:S(2)}) copy-start(f32[1024,512]{1,0:T(8,128)S(1)} %constant_dynamic-update-slice_fusion.refs_2_) | copy-start | bytes 6291460
  565.7 77.4 %copy-start.48 = (f32[6,1024]{1,0:T(8,128)S(1)}, f32[6,1024]{1,0:T(8,128)}, u32[]{:S(2)}) copy-start(f32[6,1024]{1,0:T(8,128)} %param.25) | copy-start | bytes 73732
  565.7 77.4 %copy-start.53 = (f32[6,1024]{1,0:T(8,128)S(1)}, f32[6,1024]{1,0:T(8,128)}, u32[]{:S(2)}) copy-start(f32[6,1024]{1,0:T(8,128)} %param.37) | copy-start | bytes 73732
  565.7 77.4 %copy-start.54 = (f32[6,1024]{1,0:T(8,128)S(1)}, f32[6,1024]{1,0:T(8,128)}, u32[]{:S(2)}) copy-start(f32[6,1024]{1,0:T(8,128)} %param.36) | copy-start | bytes 73732
  565.7 78.0 %copy-start.12 = (f32[9,1024]{1,0:T(8,128)S(1)}, f32[9,1024]{1,0:T(8,128)}, u32[]{:S(2)}) copy-start(f32[9,1024]{1,0:T(8,128)} %taps_ref.4) | copy-start | bytes 110596
  565.7 78.0 %copy-start.49 = (f32[9,1024]{1,0:T(8,128)S(1)}, f32[9,1024]{1,0:T(8,128)}, u32[]{:S(2)}) copy-start(f32[9,1024]{1,0:T(8,128)} %param.41) | copy-start | bytes 110596
  565.7 78.0 %copy-start.50 = (f32[9,1024]{1,0:T(8,128)S(1)}, f32[9,1024]{1,0:T(8,128)}, u32[]{:S(2)}) copy-start(f32[9,1024]{1,0:T(8,128)} %param.40) | copy-start | bytes 110596
  565.7 78.0 %copy-start.51 = (f32[9,1024]{1,0:T(8,128)S(1)}, f32[9,1024]{1,0:T(8,128)}, u32[]{:S(2)}) copy-start(f32[9,1024]{1,0:T(8,128)} %param.39) | copy-start | bytes 110596
  565.8 78.0 %copy-start.52 = (f32[9,1024]{1,0:T(8,128)S(1)}, f32[9,1024]{1,0:T(8,128)}, u32[]{:S(2)}) copy-start(f32[9,1024]{1,0:T(8,128)} %param.38) | copy-start | bytes 110596
  565.8 78.8 %collective-permute-start.12 = (f32[1024,512]{1,0:T(8,128)S(1)}, f32[1024,512]{1,0:T(8,128)S(1)}, u32[]{:S(2)}, u32[]{:S(2)}) collective-permute-start(f32[1024,512]{1,0:T(8,128)S(1)} %constant_dynamic-update-slice_fusion.refs_2_), channel_id=1, source_target_pairs={{0,4},{4,0},{8,12},{12,8},{16,20},{20,16},{24,28},{28,24},{1,5},{5... | collective-permute-start | bytes 6291464 | tf_op jit(solution)/shard_map/ppermute | solution.py:97
  566.4 88.7 %collective-permute-start.13 = (f32[512,1024]{1,0:T(8,128)S(1)}, f32[512,1024]{1,0:T(8,128)S(1)}, u32[]{:S(2)}, u32[]{:S(2)}) collective-permute-start(f32[512,1024]{1,0:T(8,128)S(1)} %get-tuple-element.136.refs_0_), channel_id=1, source_target_pairs={{0,4},{4,0},{8,12},{12,8},{16,20},{20,16},{24,28},{28,24},{1,5},{5... | collective-permute-start | bytes 6291464 | tf_op jit(solution)/shard_map/ppermute | solution.py:97
  644.5 10.6 %copy-start.56 = (f32[1024,512]{1,0:T(8,128)}, f32[1024,512]{1,0:T(8,128)S(1)}, u32[]{:S(2)}) copy-start(f32[1024,512]{1,0:T(8,128)S(1)} %collective-permute-done.12.refs_3_) | copy-start | bytes 6291460
  738.9 4.9 copy-start.34
  743.8 4.4 copy-start.33
  (25 other events, 54.0 us)

commit v5 on v4

--- a/solution.py
+++ b/solution.py
@@ -34,6 +34,7 @@
 QUERIES = 1024
 UNROLL = 4
 MATRICES = 4
+COLUMNS = (0, 2)
 
 
 def partner(index, bit):
@@ -75,14 +76,6 @@
     return copy
 
 
-def core_scatter(values):
-    rows = values.shape[0] // 2
-    side = lax.axis_index("narrow") % 2
-    give = lax.dynamic_slice_in_dim(values, (1 - side) * rows, rows, 0)
-    keep = lax.dynamic_slice_in_dim(values, side * rows, rows, 0)
-    return keep, permute(give, "narrow", 1)
-
-
 def core_place(half, other):
     side = lax.axis_index("narrow") % 2
     return jnp.where(
@@ -99,14 +92,6 @@
 
 def together(*values):
     return lax.optimization_barrier(values)
-
-
-def pair_scatter(values, axis):
-    extent = values.shape[axis] // 2
-    side = lax.axis_index("wide") % 2
-    give = lax.dynamic_slice_in_dim(values, (1 - side) * extent, extent, axis)
-    keep = lax.dynamic_slice_in_dim(values, side * extent, extent, axis)
-    return keep, permute(give, "wide", 1)
 
 
 def line_gather(share):
@@ -143,32 +128,24 @@
     return z
 
 
-def block_of(ref, kind, y, z):
+def block_of(ref, y, z):
     count = lax.axis_size("wide") // 2
-    if kind == "rows":
-        rows = ref.shape[0] // (2 * count)
-        return ref.at[pl.ds(pl.multiple_of((y * count + z) * rows, 8), rows), :]
-    rows = ref.shape[0] // count
-    if kind == "half":
-        return ref.at[pl.ds(pl.multiple_of(z * rows, 8), rows), :]
-    columns = ref.shape[1] // 2
-    return ref.at[
-        pl.ds(pl.multiple_of(z * rows, 8), rows), pl.ds(pl.multiple_of(y * columns, 128), columns)
-    ]
-
-
-def block_shape(shape, kind):
-    count = lax.axis_size("wide") // 2
-    if kind == "rows":
-        return (shape[0] // (2 * count), shape[1])
-    if kind == "half":
-        return (shape[0] // count, shape[1])
-    return (shape[0] // count, shape[1] // 2)
+    rows = ref.shape[0] // (2 * count)
+    return ref.at[pl.ds(pl.multiple_of((y * count + z) * rows, 8), rows), :]
+
+
+def line_block(ref, z):
+    rows = ref.shape[0] // (lax.axis_size("wide") // 2)
+    return ref.at[pl.ds(pl.multiple_of(z * rows, 8), rows), :]
+
+
+def block_shape(shape):
+    return (shape[0] // lax.axis_size("wide"), shape[1])
 
 
 class Scatter:
-    def __init__(self, src, kind, held, beside, inbox, sends, arrivals, local, base):
-        self.src, self.kind, self.held, self.beside, self.inbox = src, kind, held, beside, inbox
+    def __init__(self, src, held, beside, inbox, sends, arrivals, local, base):
+        self.src, self.held, self.beside, self.inbox = src, held, beside, inbox
         self.sends, self.arrivals, self.local, self.base = sends, arrivals, local, base
         self.count = lax.axis_size("wide") // 2
         self.copies = {}
@@ -178,30 +155,34 @@
     def slots():
         return lax.axis_size("wide") - 1
 
-    def start(self):
+    def load(self):
         y, z = wide_parts()
         for e in reversed(range(self.count)):
-            spot = line_partner(z, e)
-            load = pltpu.make_async_copy(
-                block_of(self.src, self.kind, y, spot), self.held.at[e], self.local.at[e]
+            self.loads[e] = pltpu.make_async_copy(
+                block_of(self.src, y, line_partner(z, e)), self.held.at[e], self.local.at[e]
             )
-            load.start()
-            self.loads[e] = load
-            if self.kind != "half":
-                self.copies[("y", e)] = send(
-                    block_of(self.src, self.kind, 1 - y, spot),
-                    self.beside.at[e],
-                    self.sends,
-                    self.arrivals,
-                    self.base + e,
-                    place_at("wide", 1),
-                )
+            self.loads[e].start()
+
+    def give(self, e):
+        y, z = wide_parts()
+        self.copies[("y", e)] = send(
+            block_of(self.src, 1 - y, line_partner(z, e)),
+            self.beside.at[e],
+            self.sends,
+            self.arrivals,
+            self.base + e,
+            place_at("wide", 1),
+        )
+
+    def start(self):
+        self.load()
+        for e in reversed(range(self.count)):
+            self.give(e)
 
     def step(self, e):
         self.loads[e].wait()
-        if self.kind != "half":
-            self.copies[("y", e)].wait_recv()
-            self.held[e] = self.held[e] + self.beside[e]
+        self.copies[("y", e)].wait_recv()
+        self.held[e] = self.held[e] + self.beside[e]
         bit = 1
         while bit < self.count and e % (2 * bit) == 0:
             self.copies[("z", e + bit)].wait_recv()
@@ -223,12 +204,12 @@
             copy.wait_send()
 
 
-def scatter_scratch(shape, kind):
+def scatter_scratch(shape):
     count = lax.axis_size("wide") // 2
-    block = block_shape(shape, kind)
+    block = block_shape(shape)
     return [
         pltpu.VMEM((count,) + block, jnp.float32),
-        pltpu.VMEM((count if kind != "half" else 1,) + block, jnp.float32),
+        pltpu.VMEM((count,) + block, jnp.float32),
         pltpu.VMEM((max(count - 1, 1),) + block, jnp.float32),
         pltpu.SemaphoreType.DMA((count,)),
     ]
@@ -347,91 +328,58 @@
     ]
 
 
-def sum_scatter_kernel(kinds, pieces, x_ref, *refs):
-    total = len(kinds)
-    sources, refs = refs[:total], refs[total:]
-    o_ref, shares, refs = refs[0], refs[1 : 1 + total], refs[1 + total :]
-    near, far, held, local = refs[:4]
-    refs = refs[4:]
-    sends, arrivals = refs[-2:]
+def sum_scatter_kernel(pieces, x_ref, source_ref, o_ref, share_ref, *refs):
+    near, far, held, local, block, beside, inbox, loads, sends, arrivals = refs
     far_bits = bits_of(lax.axis_size("narrow"))[1:]
-    wide_bits = bits_of(lax.axis_size("wide")) if total else []
-    if total and all(kind == "half" for kind in kinds):
-        wide_bits = wide_bits[1:]
     greet(
         [place_at("narrow", bit) for bit in [1] + far_bits]
-        + [place_at("wide", bit) for bit in wide_bits]
-    )
+        + [place_at("wide", bit) for bit in bits_of(lax.axis_size("wide"))]
+    )
+    narrow = NarrowSum(far_bits, pieces, x_ref, o_ref, near, far, held, sends, arrivals, local, 0)
     base = (len(far_bits) + 2) * pieces
-    narrow = NarrowSum(far_bits, pieces, x_ref, o_ref, near, far, held, sends, arrivals, local, 0)
-    scatters = []
-    for index, kind in enumerate(kinds):
-        block, beside, inbox, loads = refs[4 * index : 4 * index + 4]
-        scatters.append(
-            Scatter(sources[index], kind, block, beside, inbox, sends, arrivals, loads, base)
-        )
-        base += Scatter.slots()
+    scatter = Scatter(source_ref, block, beside, inbox, sends, arrivals, loads, base)
     narrow.start()
-    for scatter in scatters:
-        scatter.start()
+    scatter.start()
     for p in range(pieces):
         narrow.begin(p)
-    count = lax.axis_size("wide") // 2
-    for scatter in scatters:
-        if scatter.kind == "half":
-            for e in reversed(range(1, count)):
-                if e % 2:
-                    scatter.step(e)
-    left = {
-        index: [
-            e for e in reversed(range(count)) if scatter.kind != "half" or e % 2 == 0
-        ]
-        for index, scatter in enumerate(scatters)
-    }
+    left = list(reversed(range(lax.axis_size("wide") // 2)))
     for b in range(len(far_bits)):
         for p in range(pieces):
             narrow.step(b, p)
-            for index, scatter in enumerate(scatters):
-                if len(left[index]) > 1:
-                    scatter.step(left[index].pop(0))
-    outs = []
-    for index, scatter in enumerate(scatters):
-        while left[index]:
-            scatter.step(left[index].pop(0))
-        out = pltpu.make_async_copy(scatter.held.at[0], shares[index], scatter.local.at[0])
-        out.start()
-        outs.append(out)
+            if len(left) > 1:
+                scatter.step(left.pop(0))
+    while left:
+        scatter.step(left.pop(0))
+    out = pltpu.make_async_copy(scatter.held.at[0], share_ref, scatter.local.at[0])
+    out.start()
     narrow.finish()
-    for scatter in scatters:
-        scatter.finish()
-    for out in outs:
-        out.wait()
-
-
-def sum_scatter(values, gradients, kinds, number):
+    scatter.finish()
+    out.wait()
+
+
+def sum_scatter(values, gradient, number):
     pieces = 4
     narrow_bits = bits_of(lax.axis_size("narrow"))
-    slots = (len(narrow_bits) + 1) * pieces + len(kinds) * Scatter.slots()
+    slots = (len(narrow_bits) + 1) * pieces + Scatter.slots()
     anywhere = pl.BlockSpec(memory_space=pl.ANY)
-    scratch = narrow_scratch(values.shape, pieces)
-    shapes = [jax.ShapeDtypeStruct(values.shape, jnp.float32)]
-    for gradient, kind in zip(gradients, kinds):
-        scratch += scatter_scratch(gradient.shape, kind)
-        shapes.append(jax.ShapeDtypeStruct(block_shape(gradient.shape, kind), jnp.float32))
-    scratch += [pltpu.SemaphoreType.DMA((slots,)), pltpu.SemaphoreType.DMA((slots,))]
+    scratch = narrow_scratch(values.shape, pieces) + scatter_scratch(gradient.shape)
     return pl.pallas_call(
-        functools.partial(sum_scatter_kernel, kinds, pieces),
-        out_shape=tuple(shapes),
-        in_specs=[anywhere] * (1 + len(kinds)),
-        out_specs=(anywhere,) * len(shapes),
-        scratch_shapes=scratch,
+        functools.partial(sum_scatter_kernel, pieces),
+        out_shape=(
+            jax.ShapeDtypeStruct(values.shape, jnp.float32),
+            jax.ShapeDtypeStruct(block_shape(gradient.shape), jnp.float32),
+        ),
+        in_specs=[anywhere] * 2,
+        out_specs=(anywhere,) * 2,
+        scratch_shapes=scratch
+        + [pltpu.SemaphoreType.DMA((slots,)), pltpu.SemaphoreType.DMA((slots,))],
         compiler_params=pltpu.CompilerParams(
             collective_id=number, has_side_effects=True, vmem_limit_bytes=40 * 2**20
         ),
         cost_estimate=pl.CostEstimate(
             flops=values.size, bytes_accessed=values.size * 32, transcendentals=0
         ),
-    )(values, *gradients)
+    )(values, gradient)
 
 
 def small_kernel(shared_rows, split_rows, x_ref, share_ref, o_ref, norm_ref, half_ref, *refs):
@@ -442,7 +390,7 @@
         [place_at("wide", bit) for bit in wide_bits]
         + [place_at("narrow", bit) for bit in narrow_bits]
     )
-    y, z = wide_parts()
+    _, z = wide_parts()
     count = len(wide_bits)
     copies = []
     slots[0] = x_ref[...]
@@ -453,7 +401,7 @@
         for index, (_, bit) in enumerate(hops):
             if (item >> index) % 2:
                 spot = partner(spot, bit // 2)
-        return block_of(half_ref, "half", y, spot)
+        return line_block(half_ref, spot)
 
     gather = Gather(share_ref, spot_of, hops, sends, arrivals, count + len(narrow_bits))
     keep = pltpu.make_async_copy(share_ref, spot_of(0), local.at[0])
@@ -708,8 +656,8 @@
     moments, weights, refs = refs[:4], refs[4:8], refs[8:]
     carried, results, refs = refs[:4], refs[4:8], refs[8:]
     qs, refs = refs[0], refs[1:]
-    staged, values, highs, lows = refs[:3], refs[3:7], refs[7:11], refs[11:15]
-    sends, arrivals, near_sems, load_sems, value_sems, out_sems = refs[15:]
+    staged, values, highs, lows = refs[:4], refs[4:8], refs[8:12], refs[12:16]
+    sends, arrivals, near_sems, load_sems, value_sems, out_sems = refs[16:]
     size = q_ref.shape[0]
     half = size // 2
     step = half // pieces
@@ -735,19 +683,27 @@
     near_own = push(q_ref, qs.at[own], near_place)
     keep = pltpu.make_async_copy(q_ref, qs.at[own], near_sems.at[0])
     keep.start()
-    loads = []
-    for index, (line, other, stage) in enumerate(zip(lines, others, staged)):
-        for side, part_ref in ((y, line), (1 - y, other)):
-            if index == 1:
-                extent = stage.shape[1] // 2
-                spot = stage.at[:, pl.ds(pl.multiple_of(side * extent, 128), extent)]
-            else:
-                extent = stage.shape[0] // 2
-                spot = stage.at[pl.ds(pl.multiple_of(side * extent, 8), extent), :]
-            loads.append(
-                pltpu.make_async_copy(part_ref, spot, load_sems.at[len(loads)])
-            )
-            loads[-1].start()
+    blocks = lax.axis_size("wide")
+    stages = staged
+    whole = []
+    for k in range(MATRICES):
+        sources = (lines[max(k - 1, 0)], others[max(k - 1, 0)])
+        extent = stages[k].shape[0] // 2
+        for side, source in zip((y, 1 - y), sources):
+            if k >= 2:
+                spot = stages[k].at[pl.ds(pl.multiple_of(side * extent, 8), extent), :]
+                pltpu.make_async_copy(source, spot, load_sems.at[k]).start()
+                continue
+            share = (stages[0].shape[0] // blocks, stages[1].shape[0] // blocks)
+            for b in range(blocks // 2):
+                start = b * (share[0] + share[1]) + k * share[0]
+                to = pl.multiple_of(side * extent + b * share[k], 8)
+                pltpu.make_async_copy(
+                    source.at[pl.ds(start, share[k]), :],
+                    stages[k].at[pl.ds(to, share[k]), :],
+                    load_sems.at[k],
+                ).start()
+        whole.append(pltpu.make_async_copy(stages[k], stages[k], load_sems.at[k]))
     fills = []
     for k in range(MATRICES):
         fills.append(pltpu.make_async_copy(moments[k], values[k], value_sems.at[k]))
@@ -755,37 +711,30 @@
     norm = norm_ref[0:1, 0:1]
     clip = jnp.minimum(1.0, 1.0 / (norm + 1e-06))
 
-    def blend(value, start, stage, stage_start, count):
-        slab = 16 if count % 16 == 0 else 8
+    def blend_rows(value, stage):
+        slab = 16
 
         def one(i, carry):
-            spot = pl.ds(pl.multiple_of(start + i * slab, 8), slab)
-            source = pl.ds(pl.multiple_of(stage_start + i * slab, 8), slab)
-            value[spot, :] = muon_momentum * value[spot, :] + clip * stage[source, :]
+            spot = pl.ds(pl.multiple_of(i * slab, 8), slab)
+            value[spot, :] = muon_momentum * value[spot, :] + clip * stage[spot, :]
             return carry
 
-        lax.fori_loop(0, count // slab, one, 0, unroll=min(4, count // slab))
-
-    blocks = lax.axis_size("wide")
-    shares = [values[k].shape[0] // blocks for k in range(2)]
+        lax.fori_loop(0, value.shape[0] // slab, one, 0, unroll=UNROLL)
+
+    def blend_columns(value, stage):
+        def one(i, carry):
+            spot = pl.ds(pl.multiple_of(i * LANES, LANES), LANES)
+            value[:, spot] = muon_momentum * value[:, spot] + clip * stage[spot, :].T
+            return carry
+
+        lax.fori_loop(0, value.shape[1] // LANES, one, 0)
+
     outs = []
-    for load in loads[:2]:
-        load.wait()
-    for k in range(2):
+    for k in range(MATRICES):
+        whole[k].wait()
         fills[k].wait()
-
-    def one_block(b, carry):
-        stage_start = b * (shares[0] + shares[1])
-        blend(values[0], b * shares[0], staged[0], stage_start, shares[0])
-        blend(values[1], b * shares[1], staged[0], stage_start + shares[0], shares[1])
-        return carry
-
-    lax.fori_loop(0, blocks, one_block, 0)
-    for k in (2, 3):
-        loads[2 * k - 2].wait()
-        loads[2 * k - 1].wait()
-        fills[k].wait()
-        blend(values[k], 0, staged[k - 1], 0, values[k].shape[0])
+        blend = blend_columns if k in COLUMNS else blend_rows
+        blend(values[k], stages[k])
     for k in range(MATRICES):
         outs.append(pltpu.make_async_copy(values[k], carried[k], out_sems.at[k]))
         outs[-1].start()
@@ -812,7 +761,7 @@
         q_high, q_low = split(qs[k, spot, :])
         high, low = highs[k], lows[k]
         scale = muon_rate * 0.2 * math.sqrt(lengths[k])
-        if k == 2:
+        if k in COLUMNS:
             dims = ((1,), (0,))
             polar = dot(q_high, high[...], dims) + (
                 dot(q_high, low[...], dims) + dot(q_low, high[...], dims)
@@ -889,7 +838,7 @@
     anywhere = pl.BlockSpec(memory_space=pl.ANY)
     operands = [part for both in zip(lines, others) for part in both]
     shapes = [jax.ShapeDtypeStruct(moment.shape, jnp.float32) for moment in moments]
-    staged = [(moments[0].shape[0] + moments[1].shape[0], size), moments[2].shape, moments[3].shape]
+    staged = [(moment.size // size, size) for moment in moments]
     slots = 1 + 4 * pieces
     outs = pl.pallas_call(
         functools.partial(finish_kernel, sub, pieces),
@@ -905,7 +854,7 @@
             pltpu.SemaphoreType.DMA((slots,)),
             pltpu.SemaphoreType.DMA((slots,)),
             pltpu.SemaphoreType.DMA((1,)),
-            pltpu.SemaphoreType.DMA((6,)),
+            pltpu.SemaphoreType.DMA((MATRICES,)),
             pltpu.SemaphoreType.DMA((MATRICES,)),
             pltpu.SemaphoreType.DMA((MATRICES,)),
         ],
@@ -982,112 +931,261 @@
 
 
 def middle_kernel(
+    pieces,
     entry_ref,
-    entry_t_ref,
-    grad_ffn_ref,
-    expand_ref,
-    reduce_ref,
+    cotangent_ref,
+    live_ref,
+    gate_ref,
+    expand_any,
+    reduce_any,
     taps_ref,
-    ffn_ref,
-    entry_grad_ref,
-    grad_reduce_ref,
-    grad_expand_ref,
+    ffn_half_ref,
+    grad_entry_any,
+    reduce_share,
+    expand_share,
     grad_taps_ref,
+    expand_full,
+    reduce_full,
+    grad_ffn,
     upward,
-    slope,
     weight,
     active,
     grad_up,
+    ffn,
+    back,
+    grad_reduce,
+    grad_expand,
+    ffn_inbox,
+    near,
+    far,
+    held,
+    local,
+    reduce_held,
+    reduce_beside,
+    reduce_inbox,
+    reduce_loads,
+    expand_held,
+    expand_beside,
+    expand_inbox,
+    expand_loads,
+    weight_sems,
+    sends,
+    arrivals,
 ):
-    width = expand_ref.shape[1]
-    step = pl.program_id(0)
-
-    def dot(left, right, dims):
-        return lax.dot_general(left, right, (dims, ((), ())), preferred_element_type=jnp.float32)
-
-    taps = [taps_ref[t : t + 1, :] for t in range(9)]
-    upward[...] = dot(entry_ref[...], expand_ref[...], ((1,), (0,)))
-    weight[...] = dot(grad_ffn_ref[...], reduce_ref[...], ((1,), (1,)))
-
-    def emit_middle(r, z):
-        inner = gelu_slope * (z + gelu_cubic * z * z * z)
-        bent = jnp.tanh(inner)
-        active[strip_at(r), :] = (0.5 * z * (1.0 + bent)).astype(jnp.bfloat16)
-        turn = 0.5 * (1.0 + bent) + 0.5 * z * (1.0 - bent * bent) * (
-            gelu_slope * (1.0 + 3.0 * gelu_cubic * z * z)
+    units = expand_any.shape[1]
+    block = min(BLK, units // 2)
+    steps = units // block
+    groups = steps // 2
+    y, z = wide_parts()
+    count = lax.axis_size("wide") // 2
+    far_bits = bits_of(lax.axis_size("narrow"))[1:]
+    greet(
+        [place_at("narrow", bit) for bit in [1] + far_bits]
+        + [place_at("wide", bit) for bit in bits_of(lax.axis_size("wide"))]
+    )
+
+    def block_index(step):
+        side = 1 - y if step < groups else y
+        return side * groups + line_partner(z // (count // groups), groups - 1 - step % groups)
+
+    fetches = []
+    for step in range(steps):
+        spot = pl.ds(pl.multiple_of(block_index(step) * block, LANES), block)
+        pair = (
+            pltpu.make_async_copy(
+                expand_any.at[:, spot], expand_full.at[:, spot], weight_sems.at[step]
+            ),
+            pltpu.make_async_copy(
+                reduce_any.at[spot, :], reduce_full.at[spot, :], weight_sems.at[steps + step]
+            ),
         )
-        weight[strip_at(r), :] = weight[strip_at(r), :] * turn
-
-    convolve(lambda r: upward[strip_at(r), :], taps, emit_middle)
-
-    def emit_grad(r, values):
-        grad_up[strip_at(r), :] = values.astype(jnp.bfloat16)
-
-    convolve(lambda r: weight[strip_at(r), :], taps[::-1], emit_grad)
-    sums = kernel_sums(lambda r: upward[strip_at(r), :], lambda r: weight[strip_at(r), :], width)
-    for t in range(9):
-        grad_taps_ref[t : t + 1, :] = jnp.sum(sums[t], axis=0, keepdims=True)
-    grad_reduce_ref[...] = dot(active[...], grad_ffn_ref[...], ((0,), (0,)))
-    grad_expand_ref[...] = dot(entry_t_ref[...], grad_up[...], ((1,), (0,)))
-    ffn = dot(active[...], reduce_ref[...], ((1,), (0,)))
-    back = dot(grad_up[...], expand_ref[...], ((1,), (1,)))
-
-    @pl.when(step == 0)
-    def _():
-        ffn_ref[...] = ffn
-        entry_grad_ref[...] = back
-
-    @pl.when(step > 0)
-    def _():
-        ffn_ref[...] += ffn
-        entry_grad_ref[...] += back
-
-
-def middle(entry, entry_t, grad_ffn, expand, reduce, taps):
+        for copy in pair:
+            copy.start()
+        fetches.append(pair)
+    gate, live = gate_ref[...], live_ref[...]
+
+    def gated(i, carry):
+        spot = slab_at(i)
+        result = cotangent_ref[spot, :].astype(jnp.float32) * live
+        grad_ffn[spot, :] = (gate * result).astype(jnp.bfloat16)
+        return carry
+
+    lax.fori_loop(0, grad_ffn.shape[0] // SLAB, gated, 0, unroll=UNROLL)
+
+    def work(spot, fresh):
+        expand_low = expand_full[:, spot].astype(jnp.bfloat16)
+        reduce_low = reduce_full[spot, :].astype(jnp.bfloat16)
+        taps = [taps_ref[t : t + 1, spot] for t in range(9)]
+        upward[...] = dot_of(entry_ref[...], expand_low, 1, 0)
+        weight[...] = dot_of(grad_ffn[...], reduce_low, 1, 1)
+
+        def emit_middle(r, values):
+            inner = gelu_slope * (values + gelu_cubic * values * values * values)
+            bent = jnp.tanh(inner)
+            active[strip_at(r), :] = (0.5 * values * (1.0 + bent)).astype(jnp.bfloat16)
+            turn = 0.5 * (1.0 + bent) + 0.5 * values * (1.0 - bent * bent) * (
+                gelu_slope * (1.0 + 3.0 * gelu_cubic * values * values)
+            )
+            weight[strip_at(r), :] = weight[strip_at(r), :] * turn
+
+        convolve(lambda r: upward[strip_at(r), :], taps, emit_middle)
+
+        def emit_grad(r, values):
+            grad_up[strip_at(r), :] = values.astype(jnp.bfloat16)
+
+        convolve(lambda r: weight[strip_at(r), :], taps[::-1], emit_grad)
+        sums = kernel_sums(
+            lambda r: upward[strip_at(r), :], lambda r: weight[strip_at(r), :], block
+        )
+        for t in range(9):
+            grad_taps_ref[t : t + 1, spot] = jnp.sum(sums[t], axis=0, keepdims=True)
+        grad_reduce[spot, :] = dot_of(active[...], grad_ffn[...], 0, 0)
+        grad_expand[spot, :] = dot_of(grad_up[...], entry_ref[...], 0, 0)
+        if fresh:
+            ffn[...] = dot_of(active[...], reduce_low, 1, 0)
+            back[...] = dot_of(grad_up[...], expand_low, 1, 1)
+        else:
+            ffn[...] += dot_of(active[...], reduce_low, 1, 0)
+            back[...] += dot_of(grad_up[...], expand_low, 1, 1)
+
+    base = (len(far_bits) + 2) * pieces + 1
+    reduce_sum = Scatter(
+        grad_reduce, reduce_held, reduce_beside, reduce_inbox, sends, arrivals, reduce_loads, base
+    )
+    expand_sum = Scatter(
+        grad_expand,
+        expand_held,
+        expand_beside,
+        expand_inbox,
+        sends,
+        arrivals,
+        expand_loads,
+        base + Scatter.slots(),
+    )
+    for step in range(groups):
+        for copy in fetches[step]:
+            copy.wait()
+        work(pl.ds(pl.multiple_of(block_index(step) * block, LANES), block), step == 0)
+        size = count // groups
+        ready = [(groups - 1 - step) * size + e for e in reversed(range(size))]
+        for scatter in (reduce_sum, expand_sum):
+            for e in ready:
+                scatter.give(e)
+    for step in range(groups, steps):
+        for copy in fetches[step]:
+            copy.wait()
+
+    def later(i, carry):
+        side_block = line_partner_of(z // (count // groups), i, groups)
+        work(pl.ds(pl.multiple_of((y * groups + side_block) * block, LANES), block), False)
+        return carry
+
+    lax.fori_loop(0, groups, later, 0)
+    narrow = NarrowSum(
+        far_bits, pieces, back, grad_entry_any, near, far, held, sends, arrivals, local, 0
+    )
+    narrow.start()
+    core = lax.axis_index("narrow") % 2
+    half = ffn.shape[0] // 2
+    side_rows = lambda side: pl.ds(pl.multiple_of(side * half, 8), half)
+    ffn_copy = send(
+        ffn.at[side_rows(1 - core)], ffn_inbox, sends, arrivals, base - 1, place_at("narrow", 1)
+    )
+    for scatter in (reduce_sum, expand_sum):
+        scatter.load()
+    for p in range(pieces):
+        narrow.begin(p)
+    left = [list(reversed(range(count))), list(reversed(range(count)))]
+    scatters = (reduce_sum, expand_sum)
+    scatters[0].step(left[0].pop(0))
+    scatters[1].step(left[1].pop(0))
+    ffn_copy.wait_recv()
+    ffn_half_ref[...] = ffn[side_rows(core), :] + ffn_inbox[...]
+    turns = [0, 1, 0, 0, 1, 1]
+    for b in range(len(far_bits)):
+        for p in range(pieces):
+            narrow.step(b, p)
+            if turns and len(left[turns[0]]) > 1:
+                which = turns.pop(0)
+                scatters[which].step(left[which].pop(0))
+    outs = []
+    for which, share in ((0, reduce_share), (1, expand_share)):
+        while left[which]:
+            scatters[which].step(left[which].pop(0))
+        out = pltpu.make_async_copy(scatters[which].held.at[0], share, scatters[which].local.at[0])
+        out.start()
+        outs.append(out)
+    narrow.finish()
+    ffn_copy.wait_send()
+    for scatter in scatters:
+        scatter.finish()
+    for out in outs:
+        out.wait()
+
+
+def line_partner_of(place, index, count):
+    flipped = 0 * place
+    for bit in bits_of(count):
+        one, two = (place // bit) % 2, (index // bit) % 2
+        flipped = flipped + (one + two - 2 * one * two) * bit
+    return flipped
+
+
+def middle(entry, cotangent, live, gate, expand, reduce, taps, number):
     tokens, width = entry.shape
-    hidden_units = expand.shape[1]
-    block = min(256, hidden_units)
-    whole = lambda shape: pl.BlockSpec(shape, lambda i: (0, 0))
+    units = expand.shape[1]
+    block = min(BLK, units // 2)
+    steps = units // block
+    pieces = 4
+    narrow_bits = bits_of(lax.axis_size("narrow"))
+    slots = (len(narrow_bits) + 1) * pieces + 1 + 2 * Scatter.slots()
+    vmem = pl.BlockSpec(memory_space=pltpu.VMEM)
+    anywhere = pl.BlockSpec(memory_space=pl.ANY)
     f32 = lambda *shape: jax.ShapeDtypeStruct(shape, jnp.float32)
+    wide = lambda *shape: pltpu.VMEM(shape, jnp.float32)
+    low = lambda *shape: pltpu.VMEM(shape, jnp.bfloat16)
+    share = block_shape((units, width))
     return pl.pallas_call(
-        middle_kernel,
-        grid=(hidden_units // block,),
+        functools.partial(middle_kernel, pieces),
         out_shape=(
+            f32(tokens // 2, width),
             f32(tokens, width),
-            f32(tokens, width),
-            f32(hidden_units, width),
-            f32(width, hidden_units),
-            f32(9, hidden_units),
-        ),
-        in_specs=[
-            whole((tokens, width)),
-            whole((width, tokens)),
-            whole((tokens, width)),
-            pl.BlockSpec((width, block), lambda i: (0, i)),
-            pl.BlockSpec((block, width), lambda i: (i, 0)),
-            pl.BlockSpec((9, block), lambda i: (0, i)),
+            f32(*share),
+            f32(*share),
+            f32(9, units),
+        ),
+        in_specs=[vmem, vmem, vmem, vmem, anywhere, anywhere, vmem],
+        out_specs=(vmem, anywhere, anywhere, anywhere, vmem),
+        scratch_shapes=[
+            wide(width, units),
+            wide(units, width),
+            low(tokens, width),
+            wide(tokens, block),
+            wide(tokens, block),
+            low(tokens, block),
+            low(tokens, block),
+            wide(tokens, width),
+            wide(tokens, width),
+            wide(units, width),
+            wide(units, width),
+            wide(tokens // 2, width),
+        ]
+        + narrow_scratch((tokens, width), pieces)
+        + scatter_scratch((units, width)) * 2
+        + [
+            pltpu.SemaphoreType.DMA((2 * steps,)),
+            pltpu.SemaphoreType.DMA((slots,)),
+            pltpu.SemaphoreType.DMA((slots,)),
         ],
-        out_specs=(
-            whole((tokens, width)),
-            whole((tokens, width)),
-            pl.BlockSpec((block, width), lambda i: (i, 0)),
-            pl.BlockSpec((width, block), lambda i: (0, i)),
-            pl.BlockSpec((9, block), lambda i: (0, i)),
-        ),
-        scratch_shapes=[
-            pltpu.VMEM((tokens, block), jnp.float32),
-            pltpu.VMEM((tokens, block), jnp.float32),
-            pltpu.VMEM((tokens, block), jnp.float32),
-            pltpu.VMEM((tokens, block), jnp.bfloat16),
-            pltpu.VMEM((tokens, block), jnp.bfloat16),
-        ],
-        compiler_params=pltpu.CompilerParams(vmem_limit_bytes=52 * 2**20),
+        compiler_params=pltpu.CompilerParams(
+            collective_id=number, has_side_effects=True, vmem_limit_bytes=60 * 2**20
+        ),
         cost_estimate=pl.CostEstimate(
-            flops=12 * tokens * width * hidden_units,
-            bytes_accessed=32 * tokens * width,
-            transcendentals=tokens * hidden_units,
-        ),
-    )(entry, entry_t, grad_ffn, expand, reduce, taps)
+            flops=12 * tokens * width * units,
+            bytes_accessed=200 * tokens * width,
+            transcendentals=tokens * units,
+        ),
+    )(entry, cotangent, live, gate, expand, reduce, taps)
 
 
 def norm_strip(values):
@@ -1235,7 +1333,8 @@
     hidden_ref,
     branch_ref,
     grad_entry_ref,
-    grad_ffn_ref,
+    cotangent_ref,
+    live_ref,
     scale_ref,
     gate_ref,
     grad_hidden_ref,
@@ -1247,6 +1346,7 @@
     width = hidden_ref.shape[1]
     stretch = 1.0 + scale_ref[...]
     gate = gate_ref[...]
+    live = live_ref[...]
 
     def one(r, carry):
         shifts, scales, gates = carry
@@ -1255,7 +1355,7 @@
         stretched = back * stretch
         first = jnp.mean(stretched, axis=-1, keepdims=True)
         second = jnp.mean(stretched * normed, axis=-1, keepdims=True)
-        grad = grad_ffn_ref[slab_at(r), :].astype(jnp.float32) + (
+        grad = cotangent_ref[slab_at(r), :].astype(jnp.float32) * live + (
             stretched - first - normed * second
         ) * inverse
         grad_hidden_ref[slab_at(r), :] = grad
@@ -1275,7 +1375,7 @@
     grad_gate_ref[...] = jnp.sum(gates, axis=0, keepdims=True)
 
 
-def hidden_backward(hidden, branch, grad_entry, grad_result, scale, gate):
+def hidden_backward(hidden, branch, grad_entry, cotangent, live, scale, gate):
     rows, width = hidden.shape
     vmem = pl.BlockSpec(memory_space=pltpu.VMEM)
     f32 = lambda *shape: jax.ShapeDtypeStruct(shape, jnp.float32)
@@ -1288,13 +1388,13 @@
             f32(1, width),
             f32(1, width),
         ),
-        in_specs=[vmem] * 6,
+        in_specs=[vmem] * 7,
         out_specs=(vmem,) * 5,
         compiler_params=pltpu.CompilerParams(vmem_limit_bytes=48 * 2**20),
         cost_estimate=pl.CostEstimate(
             flops=30 * rows * width, bytes_accessed=22 * rows * width, transcendentals=0
         ),
-    )(hidden, branch, grad_entry, grad_result, scale, gate)
+    )(hidden, branch, grad_entry, cotangent, live, scale, gate)
 
 
 def dot_of(left, right, left_axis, right_axis):
@@ -1312,14 +1412,15 @@
 
 
 def attend_kernel(
-    mixed_ref, attend_ref, triple_ref, context_ref, logsum_ref, turned, values_t
+    mixed_ref, attend_ref, triple_ref, context_ref, logsum_ref, low_ref, turned, values_t
 ):
     tokens = mixed_ref.shape[0]
     width = context_ref.shape[1]
     step = min(BLK, width)
     for start in range(0, 3 * width, step):
         columns = pl.ds(start, step)
-        triple_ref[:, columns] = dot_of(mixed_ref[...], attend_ref[:, columns], 1, 0).astype(
+        low_ref[:, columns] = attend_ref[:, columns].astype(jnp.bfloat16)
+        triple_ref[:, columns] = dot_of(mixed_ref[...], low_ref[:, columns], 1, 0).astype(
             jnp.bfloat16
         )
     values_t[...] = triple_ref[:, pl.ds(2 * width, width)].T
@@ -1346,9 +1447,9 @@
     context_ref[...] = turned[...].T.astype(jnp.bfloat16)
 
 
-def attend(mixed, attend_low):
+def attend(mixed, attend_weight):
     tokens, width = mixed.shape
-    own = attend_low.shape[1] // 3
+    own = attend_weight.shape[1] // 3
     vmem = pl.BlockSpec(memory_space=pltpu.VMEM)
     return pl.pallas_call(
         attend_kernel,
@@ -1356,9 +1457,10 @@
             jax.ShapeDtypeStruct((tokens, 3 * own), jnp.bfloat16),
             jax.ShapeDtypeStruct((tokens, own), jnp.bfloat16),
             jax.ShapeDtypeStruct((8, tokens), jnp.float32),
+            jax.ShapeDtypeStruct(attend_weight.shape, jnp.bfloat16),
         ),
         in_specs=[vmem] * 2,
-        out_specs=(vmem,) * 3,
+        out_specs=(vmem,) * 4,
         scratch_shapes=[
             pltpu.VMEM((own, tokens), jnp.float32),
             pltpu.VMEM((own, tokens), jnp.bfloat16),
@@ -1369,7 +1471,7 @@
             bytes_accessed=12 * tokens * width,
             transcendentals=tokens * tokens * own // HEAD,
         ),
-    )(mixed, attend_low)
+    )(mixed, attend_weight)
 
 
 def attend_back_kernel(
@@ -1380,8 +1482,7 @@
     context_ref,
     logsum_ref,
     grad_branch_ref,
-    grad_output_ref,
-    grad_attend_ref,
+    attend_out_ref,
     grad_mixed_ref,
     grad_context,
     keys_t,
@@ -1423,8 +1524,14 @@
     grad_triple[:, pl.ds(0, width)] = (grad_queries_t[...].T * scale).astype(jnp.bfloat16)
     grad_triple[:, pl.ds(width, width)] = (grad_keys[...] * scale).astype(jnp.bfloat16)
     grad_triple[:, pl.ds(2 * width, width)] = grad_values[...].astype(jnp.bfloat16)
-    grad_output_ref[...] = dot_of(context_ref[...], grad_branch_ref[...], 0, 0)
-    grad_attend_ref[...] = dot_of(grad_triple[...], mixed_ref[...], 0, 0)
+    grad_output = dot_of(context_ref[...], grad_branch_ref[...], 0, 0)
+    grad_attend = dot_of(grad_triple[...], mixed_ref[...], 0, 0)
+    blocks = lax.axis_size("wide")
+    first, second = 3 * width // blocks, width // blocks
+    for b in range(blocks):
+        start = b * (first + second)
+        attend_out_ref[pl.ds(start, first), :] = grad_attend[b * first : (b + 1) * first]
+        attend_out_ref[pl.ds(start + first, second), :] = grad_output[b * second : (b + 1) * second]
     grad_mixed_ref[...] = dot_of(grad_triple[...], attend_ref[...], 1, 1)
 
 
@@ -1435,9 +1542,9 @@
     f32 = lambda *shape: jax.ShapeDtypeStruct(shape, jnp.float32)
     return pl.pallas_call(
         attend_back_kernel,
-        out_shape=(f32(own, width), f32(3 * own, width), f32(tokens, width)),
+        out_shape=(f32(4 * own, width), f32(tokens, width)),
         in_specs=[vmem] * 7,
-        out_specs=(vmem,) * 3,
+        out_specs=(vmem,) * 2,
         scratch_shapes=[
             pltpu.VMEM((tokens, own), jnp.bfloat16),
             pltpu.VMEM((own, tokens), jnp.bfloat16),
@@ -1481,9 +1588,9 @@
     branch_ref,
     hidden_ref,
     entry_ref,
-    entry_t_ref,
     slots,
     output_low,
+    output_inbox,
     sends,
     arrivals,
 ):
@@ -1494,12 +1601,23 @@
     greet([place_at(axis, bit) for axis, bit in hops])
     chunk = lambda p: pl.ds(p * step, step)
     slots[narrow_position(0)] = context_ref[...].astype(jnp.float32)
+    output_copy = send(
+        output_ref, output_inbox, sends, arrivals, pieces * (count - 1), place_at("narrow", 1)
+    )
     gathers = []
     for p in range(pieces):
         spot_of = lambda item, p=p: slots.at[narrow_position(item), chunk(p)]
         gathers.append(Gather(spot_of(0), spot_of, hops, sends, arrivals, p * (count - 1)))
         gathers[p].step(0)
-    output_low[...] = output_ref[...].astype(jnp.bfloat16)
+    core = lax.axis_index("narrow") % 2
+    half = output_ref.shape[0]
+    output_low[pl.ds(pl.multiple_of(core * half, SLAB), half), :] = output_ref[...].astype(
+        jnp.bfloat16
+    )
+    output_copy.wait_recv()
+    output_low[pl.ds(pl.multiple_of((1 - core) * half, SLAB), half), :] = output_inbox[...].astype(
+        jnp.bfloat16
+    )
     gate, offset, stretch = gate_ref[...], shift_ref[...], 1.0 + scale_ref[...]
     for p in range(pieces):
         for item in gathers[p].order[1:]:
@@ -1523,31 +1641,31 @@
             return carry
 
         lax.fori_loop(0, step // SLAB, one, 0, unroll=UNROLL)
-        entry_t_ref[:, chunk(p)] = entry_ref[chunk(p), :].T
     for gather in gathers:
         gather.finish()
-
-
-def enter(context, tokens, output_all, gate, shift, scale, number):
+    output_copy.wait_send()
+
+
+def enter(context, tokens, output_rows, gate, shift, scale, number):
     pieces = 4
     rows, own = context.shape
     width = tokens.shape[1]
     count = lax.axis_size("narrow")
     vmem = pl.BlockSpec(memory_space=pltpu.VMEM)
-    slots = pieces * (count - 1)
+    slots = pieces * (count - 1) + 1
     return pl.pallas_call(
         functools.partial(entry_kernel, pieces),
         out_shape=(
             jax.ShapeDtypeStruct((rows, width), jnp.float32),
             jax.ShapeDtypeStruct((rows, width), jnp.float32),
             jax.ShapeDtypeStruct((rows, width), jnp.bfloat16),
-            jax.ShapeDtypeStruct((width, rows), jnp.bfloat16),
         ),
         in_specs=[vmem] * 6,
-        out_specs=(vmem,) * 4,
+        out_specs=(vmem,) * 3,
         scratch_shapes=[
             pltpu.VMEM((count, rows, own), jnp.float32),
-            pltpu.VMEM(output_all.shape, jnp.bfloat16),
+            pltpu.VMEM((width, width), jnp.bfloat16),
+            pltpu.VMEM(output_rows.shape, jnp.float32),
             pltpu.SemaphoreType.DMA((slots,)),
             pltpu.SemaphoreType.DMA((slots,)),
         ],
@@ -1557,11 +1675,11 @@
         cost_estimate=pl.CostEstimate(
             flops=2 * rows * width * width, bytes_accessed=100 * rows * width, transcendentals=0
         ),
-    )(context, tokens, output_all, gate, shift, scale)
+    )(context, tokens, output_rows, gate, shift, scale)
 
 
 def all_rows(values):
-    for _, bit in narrow_hops():
+    for _, bit in narrow_hops()[:-1]:
         side = (lax.axis_index("narrow") // bit) % 2
         other = permute(values, "narrow", bit)
         values = jnp.where(
@@ -1572,13 +1690,6 @@
     return values
 
 
-def interleave(first, second):
-    count = lax.axis_size("wide")
-    width = first.shape[1]
-    both = [first.reshape(count, -1, width), second.reshape(count, -1, width)]
-    return jnp.concatenate(both, axis=1).reshape(-1, width)
-
-
 def part(rows, second_rows):
     width = rows.shape[1]
     size = second_rows // lax.axis_size("wide")
@@ -1587,16 +1698,15 @@
     return blocks[:, : total - size].reshape(-1, width), blocks[:, total - size :].reshape(-1, width)
 
 
-def gram_band(matrix, layout):
-    axis = 0 if layout == "columns" else 1
-    width = matrix.shape[axis]
+def gram_band(matrix):
+    width = matrix.shape[1]
     count = 2 * width // lax.axis_size("wide")
     start = (lax.axis_index("wide") // 2) * count
-    rows = lax.dynamic_slice_in_dim(matrix, start, count, axis)
+    rows = lax.dynamic_slice_in_dim(matrix, start, count, 1)
     product_rows = lax.dot_general(
         rows,
         matrix,
-        (((1 - axis,), (1 - axis,)), ((), ())),
+        (((0,), (0,)), ((), ())),
         precision=lax.Precision.HIGH,
         preferred_element_type=jnp.float32,
     )
@@ -1645,65 +1755,59 @@
     width = tokens.shape[2]
     flat_tokens = tokens.reshape(-1, width)
     mixed_low = mixer_forward(flat_tokens, shift_one[0], scale_one[0], mixer_kernel)
-    output_all = all_rows(output_weight)
+    attend_flat = attend_weight.reshape(width, -1)
+    triple, context, logsum, attend_low = attend(mixed_low, attend_flat)
     output_low = output_weight.astype(jnp.bfloat16)
-    attend_low = attend_weight.astype(jnp.bfloat16).reshape(width, -1)
-    triple, context, logsum = attend(mixed_low, attend_low)
-    branch, hidden, entry_low, entry_turned = enter(
-        context, flat_tokens, output_all, gate_one[0], shift_two[0], scale_two[0], 1
-    )
-    expand_low = expand_weight.astype(jnp.bfloat16)
-    reduce_low = reduce_weight.astype(jnp.bfloat16)
-    grad_result = cotangent.astype(jnp.float32) * live_mask
-    grad_ffn_low = (gate_two * grad_result).astype(jnp.bfloat16)
-    ffn_partial, entry_partial, grad_reduce, grad_expand, grad_hidden_kernel = middle(
+    output_rows, context = together(all_rows(output_weight), context)
+    branch, hidden, entry_low = enter(
+        context, flat_tokens, output_rows, gate_one[0], shift_two[0], scale_two[0], 1
+    )
+    flat_cotangent = cotangent.reshape(-1, width)
+    live_row = jnp.broadcast_to(live_mask[0], (1, width))
+    ffn_half, grad_entry, reduce_share, expand_share, grad_hidden_kernel = middle(
         entry_low,
-        entry_turned,
-        grad_ffn_low.reshape(-1, width),
-        expand_low,
-        reduce_low,
+        flat_cotangent,
+        live_row,
+        gate_two[0],
+        expand_weight,
+        reduce_weight,
         hidden_kernel,
-    )
-    ffn_keep, ffn_other = core_scatter(ffn_partial)
-    grad_entry, reduce_share = sum_scatter(entry_partial, [grad_reduce], ["rows"], 2)
-    grad_entry, reduce_share, ffn_other, grad_expand = together(
-        grad_entry, reduce_share, ffn_other, grad_expand
-    )
-    expand_keep, expand_other = pair_scatter(grad_expand, 1)
+        2,
+    )
+    grad_entry, reduce_share, expand_share, ffn_half = together(
+        grad_entry, reduce_share, expand_share, ffn_half
+    )
     reduce_pieces = line_gather(reduce_share)
-    ffn_half = ffn_keep + ffn_other
     ffn_across = permute(ffn_half, "narrow", 2)
     grad_hidden, grad_branch_low, grad_shift_two, grad_scale_two, grad_gate_one = hidden_backward(
         hidden,
         branch,
         grad_entry,
-        grad_result.reshape(-1, width),
+        flat_cotangent,
+        live_row,
         scale_two[0],
         gate_one[0],
     )
-    grad_output, grad_attend, mixed_partial = attend_back(
+    attend_out, mixed_partial = attend_back(
         mixed_low, attend_low, output_low, triple, context, logsum, grad_branch_low
     )
-    *reduce_pieces, ffn_across, expand_other, mixed_partial = together(
-        *reduce_pieces, ffn_across, expand_other, mixed_partial
+    *reduce_pieces, ffn_across, mixed_partial = together(
+        *reduce_pieces, ffn_across, mixed_partial
     )
     ffn_half = ffn_half + ffn_across
     for bit in bits_of(lax.axis_size("narrow"))[2:]:
         ffn_half = ffn_half + permute(ffn_half, "narrow", bit)
-    expand_half = expand_keep + expand_other
     reduce_line = line_place(reduce_share, reduce_pieces)
     ffn_other = permute(ffn_half, "narrow", 1)
-    attend_out = interleave(grad_attend, grad_output)
-    grad_mixed, expand_share, attend_out_share = sum_scatter(
-        mixed_partial, [expand_half, attend_out], ["half", "rows"], 3
-    )
-    ffn_other, grad_mixed, expand_share, reduce_line = together(
-        ffn_other, grad_mixed, expand_share, reduce_line
+    grad_mixed, attend_out_share = sum_scatter(mixed_partial, attend_out, 3)
+    ffn_other, grad_mixed, attend_out_share, reduce_line, expand_share = together(
+        ffn_other, grad_mixed, attend_out_share, reduce_line, expand_share
     )
     expand_pieces = line_gather(expand_share)
     reduce_other = permute(reduce_line, "wide", 1)
     ffn_branch = core_place(ffn_half, ffn_other).reshape(tokens.shape)
     block_out = (live_mask * (hidden[None] + gate_two * ffn_branch)).astype(jnp.bfloat16)
+    grad_result = cotangent.astype(jnp.float32) * live_mask
     grad_gate_two = jnp.sum(ffn_branch * grad_result, axis=1)
     tokens_gradient, grad_mixer_kernel, grad_shift_one, grad_scale_one = mixer_backward(
         flat_tokens,
@@ -1749,16 +1853,16 @@
     gradient_norm = norm[0, 0]
     clip_factor = jnp.minimum(1.0, 1.0 / (gradient_norm + 1e-06))
     expand_line = line_place(expand_share, expand_pieces)
-    attend_line, output_line = part(attend_out_line, grad_output.shape[0])
-    attend_turned = attend_moment.reshape(width, -1).T
+    attend_line, output_line = part(attend_out_line, output_weight.shape[0])
+    attend_moment_flat = attend_moment.reshape(width, -1)
     blend = lambda moment, gradient: muon_momentum * moment + clip_factor * gradient
     halves = [
-        (blend(own_half(attend_turned, 0), attend_line), "rows"),
-        (blend(own_half(output_moment, 0), output_line), "rows"),
-        (blend(own_half(expand_moment, 1), expand_line), "columns"),
-        (blend(own_half(reduce_moment, 0), reduce_line), "rows"),
+        blend(own_half(attend_moment_flat, 1).T, attend_line),
+        blend(own_half(output_moment, 0), output_line),
+        blend(own_half(expand_moment, 1).T, expand_line),
+        blend(own_half(reduce_moment, 0), reduce_line),
     ]
-    bands = jnp.stack([gram_band(matrix, layout) for matrix, layout in halves])
+    bands = jnp.stack([gram_band(matrix) for matrix in halves])
     sub = lax.axis_size("narrow") // MATRICES
     gramian = gram_whole(bands.reshape(MATRICES * sub, -1, bands.shape[2]), 5)
     gramian, expand_line, attend_out_line = together(gramian, expand_line, attend_out_line)
@@ -1768,18 +1872,17 @@
     factor, expand_other, attend_out_other, reduce_other = together(
         factor, expand_other, attend_out_other, reduce_other
     )
-    turn = lambda matrix: matrix.reshape(width, -1).T
     carried, results = finish(
         norm,
         factor,
         [attend_out_line, expand_line, reduce_line],
         [attend_out_other, expand_other, reduce_other],
-        [attend_turned, output_moment, expand_moment, reduce_moment],
-        [turn(attend_weight), output_weight, expand_weight, reduce_weight],
+        [attend_moment_flat, output_moment, expand_moment, reduce_moment],
+        [attend_flat, output_weight, expand_weight, reduce_weight],
         6,
     )
-    attend_carried = carried[0].T.reshape(attend_weight.shape)
-    attend_result = results[0].T.reshape(attend_weight.shape)
+    attend_carried = carried[0].reshape(attend_weight.shape)
+    attend_result = results[0].reshape(attend_weight.shape)
     table_moment, table_square, table_result = adam_update(
         modulation_table, table_first, table_second, clip_factor * summed_table
     )

time: 764 us -> 705 us (0.923)
  other arithmetic: 54.4 us -> 23.4 us
  waiting for transfers between devices: 42.1 us -> 14.7 us
    ppermute x15 -> x12, waiting for transfers between devices: 42.1 us -> 14.7 us  [permute(): lax.ppermute(values, axis, [(index, index ^ bit) for index in range(size)])]
    pallas_call x4 -> x3, Pallas kernels: 200 us -> 192 us  [the longest x1 109 us: middle(): pl.pallas_call(functools.partial(middle_kernel, pieces), out_shape=(f32(t...]
    ppermute x15 -> x12, starting transfers between devices: 16.2 us -> 15.3 us  [permute(): lax.ppermute(values, axis, [(index, index ^ bit) for index in range(size)])]
    unnamed x126 -> x111, local copies, waits for them, and re-layouts: 52.2 us -> 52.3 us
  transfers between devices with their start and end apart: 15 -> 12, of which waited for: 3 -> 2; matrix products, arithmetic and copies ran while one was open for 8% -> 7% of each run, Pallas kernels for 56% -> 50%
where the time goes in v5:
time: 705 us; the launch traced here: 695 us
  Pallas kernels  561 us (80%)
  local copies, waits for them, and re-layouts  74 us (10%)
  other arithmetic  23.4 us (3%)
  starting transfers between devices  15.3 us (2%)
  waiting for transfers between devices  14.7 us (2%)
    pallas_call x1, Pallas kernels, middle(): pl.pallas_call(functools.partial(middle_kernel, pieces), out_shape=(f32(t...  109 us
    pallas_call x1, Pallas kernels, gram_whole(): pl.pallas_call(functools.partial(gram_kernel, narrow_bits, hops), out_sha...  85.6 us
    pallas_call x1, Pallas kernels, polar_factor(): pl.pallas_call(polar_kernel, out_shape=jax.ShapeDtypeStruct((size, size),...  75.9 us
    pallas_call x1, Pallas kernels, finish(): pl.pallas_call(functools.partial(finish_kernel, sub, pieces), out_shape=t...  74 us
    pallas_call x1, Pallas kernels, sum_scatter(): pl.pallas_call(functools.partial(sum_scatter_kernel, pieces), out_shape=(...  61 us
    pallas_call x1, Pallas kernels, small_sums(): pl.pallas_call(functools.partial(small_kernel, shared_rows, split_rows),...  55 us
    unnamed x111, local copies, waits for them, and re-layouts  52.3 us
    pallas_call x1, Pallas kernels, enter(): pl.pallas_call(functools.partial(entry_kernel, pieces), out_shape=(jax.Sh...  30.5 us
  transfers between devices with their start and end apart: 12, of which 2 were waited for; matrix products, arithmetic and copies ran while one was open for 7% of the time, Pallas kernels for 50%

profile of v5, /device:TPU:13, one launch (start us, length us, event | category | flops | bytes accessed | tf_op | source)
XLA Modules:
  0.0 695.4 jit_solution(16691417556804235991)
XLA Ops:
  1.9 3.5 copy.49
  5.5 3.7 copy.50.attend_ref.refs_10_
  10.5 7.4 %shard_map.356.mixed_ref = bf16[1024,1024]{1,0:T(8,128)(2,1)S(1)} custom-call(bf16[1024,1024]{1,0:T(8,128)(2,1)S(1)} %bitcast.51, f32[1,1024]{1,0:T(1,128)S(1)} %get-tuple-element.208.shift_ref, f32[1,1024]{1,0:T(1,128)S(1)} %get-tuple-element.207.scale_ref, f32[9,1024]{1,0:T(8,128)S(1)} %copy-done.10), custom_call_target="tpu_custom_call" | custom-call | flops 41943040 | bytes 4194304 | tf_op jit(solution)/shard_map/pallas_call | solution.py:1231
  17.9 8.1 %shard_map.357 = (bf16[1024,768]{1,0:T(8,128)(2,1)S(1)}, bf16[1024,256]{1,0:T(8,128)(2,1)S(1)}, f32[8,1024]{1,0:T(8,128)S(1)}, bf16[1024,768]{1,0:T(8,128)(2,1)S(1)}) custom-call(bf16[1024,1024]{1,0:T(8,128)(2,1)S(1)} %shard_map.356.mixed_ref, f32[1024,768]{1,0:T(8,128)S(1)} %copy-done.7), custom_call_target="tpu_custom_call" | custom-call | flops 4294967296 | bytes 12582912 | tf_op jit(solution)/shard_map/pallas_call | solution.py:1454
  26.1 3.0 maximum_select_fusion.2.output_ref
  29.2 30.5 %shard_map.358 = (f32[1024,1024]{1,0:T(8,128)S(1)}, f32[1024,1024]{1,0:T(8,128)}, bf16[1024,1024]{1,0:T(8,128)(2,1)S(1)}) custom-call(bf16[1024,256]{1,0:T(8,128)(2,1)S(1)} %get-tuple-element.84.context_ref, bf16[1024,1024]{1,0:T(8,128)(2,1)S(1)} %bitcast.52, f32[512,1024]{1,0:T(8,128)S(1)} %maximum_select_fusion.2.output_ref, ...), custom_call_target="tpu_custom_call" | custom-call | flops 2147483648 | bytes 104857600 | tf_op jit(solution)/shard_map/pallas_call | solution.py:1656
  59.7 2.0 copy-done.6
  61.7 1.3 copy-done.14
  63.6 109.3 %shard_map.359 = (f32[512,1024]{1,0:T(8,128)}, f32[1024,1024]{1,0:T(8,128)}, f32[128,1024]{1,0:T(8,128)}, f32[128,1024]{1,0:T(8,128)}, f32[9,1024]{1,0:T(8,128)}) custom-call(bf16[1024,1024]{1,0:T(8,128)(2,1)} %copy-done.14, bf16[1024,1024]{1,0:T(8,128)(2,1)} %bitcast.54, f32[1,1024]{1,0:T(1,128)} %broadcast_in_dim.5.live_ref, ...), custom_call_target="tpu_custom_call" | custom-call | flops 12884901888 | bytes 209715200 | tf_op jit(solution)/shard_map/pallas_call | solution.py:1148
  173.0 1.6 collective-permute-start.4
  175.2 1.6 collective-permute-start.2
  177.4 1.6 copy-done.1
  179.0 12.1 %shard_map.360 = (f32[1024,1024]{1,0:T(8,128)}, bf16[1024,1024]{1,0:T(8,128)(2,1)S(1)}, f32[1,1024]{1,0:T(1,128)S(1)}, f32[1,1024]{1,0:T(1,128)S(1)}, f32[1,1024]{1,0:T(1,128)S(1)}) custom-call(f32[1024,1024]{1,0:T(8,128)} %get-tuple-element.86.hidden_ref, f32[1024,1024]{1,0:T(8,128)} %copy-done.6, f32[1024,1024]{1,0:T(8,128)} %get-tuple-element.98.grad_entry_ref, ...), custom_call_target="tpu_custom_call" | custom-call | flops 31457280 | bytes 23068672 | tf_op jit(solution)/shard_map/pallas_call | solution.py:1382
  192.4 21.8 %shard_map.361 = (f32[1024,1024]{1,0:T(8,128)}, f32[1024,1024]{1,0:T(8,128)}) custom-call(bf16[1024,1024]{1,0:T(8,128)(2,1)} %copy-done.8, bf16[1024,768]{1,0:T(8,128)(2,1)} %copy-done.16, bf16[256,1024]{1,0:T(8,128)(2,1)S(1)} %convert_element_type.18.output_ref, bf16[1024,768]{1,0:T(8,128)(2,1)} %copy-done.15, ...), custom_call_target="tpu_custom_call" | custom-call | flops 10737418240 | bytes 20971520 | tf_op jit(solution)/shard_map/pallas_call | solution.py:1543
  214.2 5.5 collective-permute-done.3
  219.8 1.9 add.151
  221.7 4.5 collective-permute-start.5
  226.3 3.1 constant_dynamic-slice_fusion
  229.3 2.9 copy.59
  232.3 3.5 copy.51
  235.8 3.5 copy.53.refs_6_
  240.5 2.2 copy-done.3
  242.7 2.2 copy-done.4
  244.8 61.0 %shard_map.362 = (f32[1024,1024]{1,0:T(8,128)S(1)}, f32[128,1024]{1,0:T(8,128)S(1)}) custom-call(f32[1024,1024]{1,0:T(8,128)S(1)} %copy-done.4, f32[1024,1024]{1,0:T(8,128)S(1)} %copy-done.3), custom_call_target="tpu_custom_call" | custom-call | flops 1048576 | bytes 33554432 | tf_op jit(solution)/shard_map/pallas_call | solution.py:366
  307.8 2.4 collective-permute-start.6
  311.8 1.4 copy-done.19
  313.2 4.3 fusion.5
  317.5 20.1 %shard_map.363 = (bf16[1024,1024]{1,0:T(8,128)(2,1)}, f32[9,1024]{1,0:T(8,128)S(1)}, f32[1,1024]{1,0:T(1,128)S(1)}, f32[1,1024]{1,0:T(1,128)S(1)}) custom-call(bf16[1024,1024]{1,0:T(8,128)(2,1)S(1)} %bitcast.53, f32[1,1024]{1,0:T(1,128)S(1)} %get-tuple-element.208.shift_ref, f32[1,1024]{1,0:T(1,128)S(1)} %get-tuple-element.207.scale_ref, ...), custom_call_target="tpu_custom_call" | custom-call | flops 104857600 | bytes 12582912 | tf_op jit(solution)/shard_map/pallas_call | solution.py:1310
  338.0 55.0 %shard_map.364 = (f32[32,1024]{1,0:T(8,128)S(1)}, f32[8,128]{1,0:T(8,128)S(1)}, f32[512,1024]{1,0:T(8,128)S(1)}) custom-call(f32[32,1024]{1,0:T(8,128)S(1)} %pad.4.x_ref, f32[128,1024]{1,0:T(8,128)S(1)} %get-tuple-element.122.share_ref), custom_call_target="tpu_custom_call" | custom-call | tf_op jit(solution)/shard_map/pallas_call | solution.py:450
  393.1 7.5 %fusion.6 = bf16[1,1024,1024]{2,1,0:T(8,128)(2,1)} fusion(f32[1024,1024]{1,0:T(8,128)} %get-tuple-element.86.hidden_ref, f32[512,1024]{1,0:T(8,128)} %add.151, f32[512,1024]{1,0:T(8,128)} %collective-permute-done.5, f32[1024]{0:T(1024)S(1)} %bitcast.63, f32[]{:T(128)} %bitcast, pred[]{:T(512)S(6)} %eq.14), kind=kLoop, calls=%fused_computation.12 | loop fusion | flops 7340032 | bytes 10489861 | tf_op jit(solution)/shard_map/convert_element_type | solution.py:1809
  401.8 2.9 multiply_add_fusion
  406.1 1.4 copy-done.20
  415.1 1.7 copy-done.17
  419.2 85.6 %shard_map.365.g_ref = f32[1024,640]{1,0:T(8,128)S(1)} custom-call(f32[4,256,640]{2,1,0:T(8,128)S(1)} %pad_maximum_fusion.x_ref), custom_call_target="tpu_custom_call" | custom-call | tf_op jit(solution)/shard_map/pallas_call | solution.py:538
  505.1 1.3 collective-permute-start.10
  506.4 75.9 %shard_map.366.q_ref = f32[1024,1024]{1,0:T(8,128)} custom-call(f32[1024,640]{1,0:T(8,128)S(1)} %shard_map.365.g_ref), custom_call_target="tpu_custom_call" | custom-call | flops 109521666048 | bytes 8388608 | tf_op jit(solution)/shard_map/pallas_call | solution.py:641
  585.2 9.1 %collective-permute-done.10.refs_1_ = f32[512,1024]{1,0:T(8,128)} collective-permute-done((f32[512,1024]{1,0:T(8,128)S(1)}, f32[512,1024]{1,0:T(8,128)}, u32[]{:S(2)}, u32[]{:S(2)}) %collective-permute-start.10) | collective-permute-done | bytes 2097184 | tf_op jit(solution)/shard_map/ppermute | solution.py:90
  594.3 74.0 %shard_map.367 = (f32[1024,768]{1,0:T(8,128)}, f32[256,1024]{1,0:T(8,128)}, f32[1024,1024]{1,0:T(8,128)}, f32[1024,1024]{1,0:T(8,128)}, f32[1024,768]{1,0:T(8,12...) custom-call(f32[8,128]{1,0:T(8,128)} %copy-done.13, f32[1024,1024]{1,0:T(8,128)} %shard_map.366.q_ref, ...), custom_call_target="tpu_custom_call" | custom-call | flops 19327352832 | bytes 83886080 | tf_op jit(solution)/shard_map/pallas_call | solution.py:843
  668.3 2.4 copy.55
  670.7 2.4 copy.57
  673.1 2.4 copy.56
  675.5 2.4 copy.58
  677.8 2.3 copy.77
  680.1 4.9 copy.78
  685.1 2.1 copy.79
  689.5 2.1 copy.81
  691.6 1.6 copy-done.24
  693.2 2.0 copy.82
  (163 shorter events, 27.0 us)
Async XLA Ops:
  0.7 25.4 %collective-permute-start = (f32[256,1024]{1,0:T(8,128)}, f32[256,1024]{1,0:T(8,128)}, u32[]{:S(2)}, u32[]{:S(2)}) collective-permute-start(f32[256,1024]{1,0:T(8,128)} %refs_11_.1), channel_id=1, source_target_pairs={{0,2},{1,3},{2,0},{3,1},{4,6},{5,7},{6,4},{7,5},{8,10},{9,11},{10,... | collective-permute-start | bytes 3145736 | tf_op jit(solution)/shard_map/ppermute | solution.py:90
  5.5 4.4 copy-start.38
  5.5 4.4 copy-start.48
  5.5 5.0 copy-start
  5.5 5.0 copy-start.10
  10.5 7.4 %copy-start.7 = (f32[1024,768]{1,0:T(8,128)S(1)}, f32[1024,768]{1,0:T(8,128)}, u32[]{:S(2)}) copy-start(f32[1024,768]{1,0:T(8,128)} %copy.50.attend_ref.refs_10_) | copy-start | bytes 9437188
  17.9 8.1 %copy-start.8 = (bf16[1024,1024]{1,0:T(8,128)(2,1)}, bf16[1024,1024]{1,0:T(8,128)(2,1)S(1)}, u32[]{:S(2)}) copy-start(bf16[1024,1024]{1,0:T(8,128)(2,1)S(1)} %shard_map.356.mixed_ref) | copy-start | bytes 6291460
  17.9 8.2 %copy-start.23 = (f32[256,1024]{1,0:T(8,128)S(1)}, f32[256,1024]{1,0:T(8,128)}, u32[]{:S(2)}) copy-start(f32[256,1024]{1,0:T(8,128)} %refs_11_.1) | copy-start | bytes 3145732
  26.1 3.1 copy-start.15
  26.1 3.1 copy-start.16
  63.6 113.8 %copy-start.11 = (f32[1,1024]{1,0:T(1,128)S(1)}, f32[1,1024]{1,0:T(1,128)}, u32[]{:S(2)}) copy-start(f32[1,1024]{1,0:T(1,128)} %broadcast_in_dim.5.live_ref) | copy-start | bytes 12292
  173.0 46.8 %collective-permute-start.4 = (f32[512,1024]{1,0:T(8,128)}, f32[512,1024]{1,0:T(8,128)S(1)}, u32[]{:S(2)}, u32[]{:S(2)}) collective-permute-start(f32[512,1024]{1,0:T(8,128)} %get-tuple-element.92), channel_id=1, source_target_pairs={{0,2},{1,3},{2,0},{3,1},{4,6},{5,7},{6,4},{7,5},{8,10},{9,11},{10,... | collective-permute-start | bytes 6291464 | tf_op jit(solution)/shard_map/ppermute | solution.py:90
  174.7 39.5 %collective-permute-start.1 = (f32[128,1024]{1,0:T(8,128)}, f32[128,1024]{1,0:T(8,128)S(1)}, u32[]{:S(2)}, u32[]{:S(2)}) collective-permute-start(f32[128,1024]{1,0:T(8,128)} %get-tuple-element.93), channel_id=1, source_target_pairs={{0,8},{4,12},{8,0},{12,4},{16,24},{20,28},{24,16},{28,20},{1,9},{5... | collective-permute-start | bytes 1572872 | tf_op jit(solution)/shard_map/ppermute | solution.py:90
  175.2 39.1 %collective-permute-start.2 = (f32[128,1024]{1,0:T(8,128)}, f32[128,1024]{1,0:T(8,128)S(1)}, u32[]{:S(2)}, u32[]{:S(2)}) collective-permute-start(f32[128,1024]{1,0:T(8,128)} %get-tuple-element.93), channel_id=1, source_target_pairs={{0,16},{4,20},{8,24},{12,28},{16,0},{20,4},{24,8},{28,12},{1,17},{... | collective-permute-start | bytes 1572872 | tf_op jit(solution)/shard_map/ppermute | solution.py:90
  176.8 43.0 %collective-permute-start.3 = (f32[128,1024]{1,0:T(8,128)}, f32[128,1024]{1,0:T(8,128)S(1)}, u32[]{:S(2)}, u32[]{:S(2)}) collective-permute-start(f32[128,1024]{1,0:T(8,128)} %get-tuple-element.93), channel_id=1, source_target_pairs={{0,24},{4,28},{8,16},{12,20},{16,8},{20,12},{24,0},{28,4},{1,25},{... | collective-permute-start | bytes 1572872 | tf_op jit(solution)/shard_map/ppermute | solution.py:90
  192.4 27.3 %copy-start.27 = (f32[512,1024]{1,0:T(8,128)S(1)}, f32[512,1024]{1,0:T(8,128)}, u32[]{:S(2)}) copy-start(f32[512,1024]{1,0:T(8,128)} %get-tuple-element.92) | copy-start | bytes 6291460
  214.2 7.5 %copy-start.31 = (f32[128,1024]{1,0:T(8,128)}, f32[128,1024]{1,0:T(8,128)S(1)}, u32[]{:S(2)}) copy-start(f32[128,1024]{1,0:T(8,128)S(1)} %collective-permute-done.1) | copy-start | bytes 1572868
  214.2 7.5 %copy-start.33 = (f32[128,1024]{1,0:T(8,128)}, f32[128,1024]{1,0:T(8,128)S(1)}, u32[]{:S(2)}) copy-start(f32[128,1024]{1,0:T(8,128)S(1)} %collective-permute-done.2) | copy-start | bytes 1572868
  221.7 85.6 %collective-permute-start.5 = (f32[512,1024]{1,0:T(8,128)}, f32[512,1024]{1,0:T(8,128)}, u32[]{:S(2)}, u32[]{:S(2)}) collective-permute-start(f32[512,1024]{1,0:T(8,128)} %add.151), channel_id=1, source_target_pairs={{0,1},{1,0},{2,3},{3,2},{4,5},{5,4},{6,7},{7,6},{8,9},{9,8},{10,11... | collective-permute-start | bytes 6291464 | tf_op jit(solution)/shard_map/ppermute | solution.py:90
  240.5 2.2 copy-start.3
  242.7 2.2 copy-start.4
  244.8 61.0 %copy-start.32 = (f32[128,1024]{1,0:T(8,128)S(1)}, f32[128,1024]{1,0:T(8,128)}, u32[]{:S(2)}) copy-start(f32[128,1024]{1,0:T(8,128)} %copy-done.31) | copy-start | bytes 1572868
  244.8 61.1 %copy-start.34 = (f32[128,1024]{1,0:T(8,128)S(1)}, f32[128,1024]{1,0:T(8,128)}, u32[]{:S(2)}) copy-start(f32[128,1024]{1,0:T(8,128)} %copy-done.33) | copy-start | bytes 1572868
  305.8 5.8 copy-start.5
  307.3 10.1 %copy-start.22 = (f32[512,1024]{1,0:T(8,128)}, f32[512,1024]{1,0:T(8,128)S(1)}, u32[]{:S(2)}) copy-start(f32[512,1024]{1,0:T(8,128)S(1)} %constant_dynamic-update-slice_fusion.4.refs_4_) | copy-start | bytes 6291460
  307.3 5.9 copy-start.2
  307.8 92.8 %collective-permute-start.6 = (f32[128,1024]{1,0:T(8,128)S(1)}, f32[128,1024]{1,0:T(8,128)}, u32[]{:S(2)}, u32[]{:S(2)}) collective-permute-start(f32[128,1024]{1,0:T(8,128)S(1)} %copy-done.29), channel_id=1, source_target_pairs={{0,8},{4,12},{8,0},{12,4},{16,24},{20,28},{24,16},{28,20},{1,9},{5... | collective-permute-start | bytes 1572872 | tf_op jit(solution)/shard_map/ppermute | solution.py:90
  310.2 90.4 %collective-permute-start.7 = (f32[128,1024]{1,0:T(8,128)S(1)}, f32[128,1024]{1,0:T(8,128)}, u32[]{:S(2)}, u32[]{:S(2)}) collective-permute-start(f32[128,1024]{1,0:T(8,128)S(1)} %copy-done.29), channel_id=1, source_target_pairs={{0,16},{4,20},{8,24},{12,28},{16,0},{20,4},{24,8},{28,12},{1,17},{... | collective-permute-start | bytes 1572872 | tf_op jit(solution)/shard_map/ppermute | solution.py:90
  310.2 90.4 %collective-permute-start.8 = (f32[128,1024]{1,0:T(8,128)S(1)}, f32[128,1024]{1,0:T(8,128)}, u32[]{:S(2)}, u32[]{:S(2)}) collective-permute-start(f32[128,1024]{1,0:T(8,128)S(1)} %copy-done.29), channel_id=1, source_target_pairs={{0,24},{4,28},{8,16},{12,20},{16,8},{20,12},{24,0},{28,4},{1,25},{... | collective-permute-start | bytes 1572872 | tf_op jit(solution)/shard_map/ppermute | solution.py:90
  317.5 20.2 %copy-start.45 = (f32[9,1024]{1,0:T(8,128)S(1)}, f32[9,1024]{1,0:T(8,128)}, u32[]{:S(2)}) copy-start(f32[9,1024]{1,0:T(8,128)} %get-tuple-element.121) | copy-start | bytes 110596
  393.0 7.6 %copy-start.13 = (f32[8,128]{1,0:T(8,128)}, f32[8,128]{1,0:T(8,128)S(1)}, u32[]{:S(2)}) copy-start(f32[8,128]{1,0:T(8,128)S(1)} %get-tuple-element.124.norm_ref) | copy-start | bytes 12292
  393.0 112.1 %copy-start.9 = (f32[512,1024]{1,0:T(8,128)}, f32[512,1024]{1,0:T(8,128)S(1)}, u32[]{:S(2)}) copy-start(f32[512,1024]{1,0:T(8,128)S(1)} %get-tuple-element.132.refs_0_) | copy-start | bytes 6291460
  393.0 190.8 %collective-permute-start.11 = (f32[512,1024]{1,0:T(8,128)}, f32[512,1024]{1,0:T(8,128)}, u32[]{:S(2)}, u32[]{:S(2)}) collective-permute-start(f32[512,1024]{1,0:T(8,128)} %copy-done.22), channel_id=1, source_target_pairs={{0,4},{4,0},{8,12},{12,8},{16,20},{20,16},{24,28},{28,24},{1,5},{5... | collective-permute-start | bytes 6291464 | tf_op jit(solution)/shard_map/ppermute | solution.py:90
  406.0 4.8 copy-start.18
  410.8 93.9 %copy-start.21 = (f32[512,1024]{1,0:T(8,128)}, f32[512,1024]{1,0:T(8,128)S(1)}, u32[]{:S(2)}) copy-start(f32[512,1024]{1,0:T(8,128)S(1)} %constant_dynamic-update-slice_fusion.refs_2_) | copy-start | bytes 6291460
  504.8 77.6 %copy-start.39 = (f32[6,1024]{1,0:T(8,128)S(1)}, f32[6,1024]{1,0:T(8,128)}, u32[]{:S(2)}) copy-start(f32[6,1024]{1,0:T(8,128)} %param.25) | copy-start | bytes 73732
  504.8 77.6 %copy-start.46 = (f32[6,1024]{1,0:T(8,128)S(1)}, f32[6,1024]{1,0:T(8,128)}, u32[]{:S(2)}) copy-start(f32[6,1024]{1,0:T(8,128)} %param.37) | copy-start | bytes 73732
  504.8 77.6 %copy-start.47 = (f32[6,1024]{1,0:T(8,128)S(1)}, f32[6,1024]{1,0:T(8,128)}, u32[]{:S(2)}) copy-start(f32[6,1024]{1,0:T(8,128)} %param.36) | copy-start | bytes 73732
  504.8 78.2 %copy-start.40 = (f32[9,1024]{1,0:T(8,128)S(1)}, f32[9,1024]{1,0:T(8,128)}, u32[]{:S(2)}) copy-start(f32[9,1024]{1,0:T(8,128)} %taps_ref.4) | copy-start | bytes 110596
  504.8 78.2 %copy-start.41 = (f32[9,1024]{1,0:T(8,128)S(1)}, f32[9,1024]{1,0:T(8,128)}, u32[]{:S(2)}) copy-start(f32[9,1024]{1,0:T(8,128)} %param.41) | copy-start | bytes 110596
  504.8 78.2 %copy-start.42 = (f32[9,1024]{1,0:T(8,128)S(1)}, f32[9,1024]{1,0:T(8,128)}, u32[]{:S(2)}) copy-start(f32[9,1024]{1,0:T(8,128)} %param.40) | copy-start | bytes 110596
  504.8 78.2 %copy-start.43 = (f32[9,1024]{1,0:T(8,128)S(1)}, f32[9,1024]{1,0:T(8,128)}, u32[]{:S(2)}) copy-start(f32[9,1024]{1,0:T(8,128)} %param.39) | copy-start | bytes 110596
  504.9 78.2 %copy-start.44 = (f32[9,1024]{1,0:T(8,128)S(1)}, f32[9,1024]{1,0:T(8,128)}, u32[]{:S(2)}) copy-start(f32[9,1024]{1,0:T(8,128)} %param.38) | copy-start | bytes 110596
  504.9 79.0 %collective-permute-start.9 = (f32[512,1024]{1,0:T(8,128)S(1)}, f32[512,1024]{1,0:T(8,128)S(1)}, u32[]{:S(2)}, u32[]{:S(2)}) collective-permute-start(f32[512,1024]{1,0:T(8,128)S(1)} %constant_dynamic-update-slice_fusion.refs_2_), channel_id=1, source_target_pairs={{0,4},{4,0},{8,12},{12,8},{16,20},{20,16},{24,28},{28,24},{1,5},{5... | collective-permute-start | bytes 6291464 | tf_op jit(solution)/shard_map/ppermute | solution.py:90
  505.1 89.2 %collective-permute-start.10 = (f32[512,1024]{1,0:T(8,128)S(1)}, f32[512,1024]{1,0:T(8,128)}, u32[]{:S(2)}, u32[]{:S(2)}) collective-permute-start(f32[512,1024]{1,0:T(8,128)S(1)} %get-tuple-element.132.refs_0_), channel_id=1, source_target_pairs={{0,4},{4,0},{8,12},{12,8},{16,20},{20,16},{24,28},{28,24},{1,5},{5... | collective-permute-start | bytes 6291464 | tf_op jit(solution)/shard_map/ppermute | solution.py:90
  680.1 4.9 copy-start.26
  685.1 4.4 copy-start.25
  689.5 3.7 copy-start.24
  (14 other events, 22.2 us)

commit v6 on v5

--- a/solution.py
+++ b/solution.py
@@ -31,7 +31,7 @@
 BLK = 256
 LANES = 128
 SLAB = 16
-QUERIES = 1024
+QUERIES = 512
 UNROLL = 4
 MATRICES = 4
 COLUMNS = (0, 2)
@@ -76,15 +76,6 @@
     return copy
 
 
-def core_place(half, other):
-    side = lax.axis_index("narrow") % 2
-    return jnp.where(
-        side == 0,
-        jnp.concatenate([half, other], axis=0),
-        jnp.concatenate([other, half], axis=0),
-    )
-
-
 def permute(values, axis, bit):
     size = lax.axis_size(axis)
     return lax.ppermute(values, axis, [(index, index ^ bit) for index in range(size)])
@@ -92,22 +83,6 @@
 
 def together(*values):
     return lax.optimization_barrier(values)
-
-
-def line_gather(share):
-    count = lax.axis_size("wide") // 2
-    return [permute(share, "wide", 2 * offset) for offset in range(1, count)]
-
-
-def line_place(share, arrived):
-    count = lax.axis_size("wide") // 2
-    rows = share.shape[0]
-    place = lax.axis_index("wide") // 2
-    whole = jnp.zeros((count * rows,) + share.shape[1:], share.dtype)
-    whole = lax.dynamic_update_slice_in_dim(whole, share, place * rows, 0)
-    for offset, piece in zip(range(1, count), arrived):
-        whole = lax.dynamic_update_slice_in_dim(whole, piece, (place ^ offset) * rows, 0)
-    return whole
 
 
 def own_half(values, axis):
@@ -225,7 +200,7 @@
     def step(self, item):
         if item:
             self.copies[item].wait_recv()
-        for index in reversed(range(item.bit_length(), len(self.hops))):
+        for index in range(item.bit_length(), len(self.hops)):
             later = item + 2**index
             spot = self.spot_of(item)
             axis, bit = self.hops[index]
@@ -328,184 +303,164 @@
     ]
 
 
-def sum_scatter_kernel(pieces, x_ref, source_ref, o_ref, share_ref, *refs):
-    near, far, held, local, block, beside, inbox, loads, sends, arrivals = refs
-    far_bits = bits_of(lax.axis_size("narrow"))[1:]
+def gram_kernel(
+    norm_ref,
+    attend_out_any,
+    expand_any,
+    reduce_any,
+    attend_moment_any,
+    output_moment_any,
+    expand_moment_any,
+    reduce_moment_any,
+    band_ref,
+    attend_out,
+    expand,
+    reduce,
+    attend_moment,
+    output_moment,
+    expand_moment,
+    reduce_moment,
+    *refs,
+):
+    highs, lows, refs = refs[:MATRICES], refs[MATRICES : 2 * MATRICES], refs[2 * MATRICES :]
+    twice, halves, inbox, block, load_sems, sends, arrivals, local = refs
+    narrow_bits = bits_of(lax.axis_size("narrow"))
+    wide_bits = bits_of(lax.axis_size("wide"))
+    parts, rows = halves.shape[0], halves.shape[1]
+    sub = parts // MATRICES
+    size = attend_out.shape[1]
+    hops = [("narrow", bit) for bit in bits_of(sub)]
+    hops += [("wide", bit) for bit in reversed(wide_bits)]
+    w, n = lax.axis_index("wide"), lax.axis_index("narrow")
+    y, z = wide_parts()
     greet(
-        [place_at("narrow", bit) for bit in [1] + far_bits]
-        + [place_at("wide", bit) for bit in bits_of(lax.axis_size("wide"))]
-    )
-    narrow = NarrowSum(far_bits, pieces, x_ref, o_ref, near, far, held, sends, arrivals, local, 0)
-    base = (len(far_bits) + 2) * pieces
-    scatter = Scatter(source_ref, block, beside, inbox, sends, arrivals, loads, base)
-    narrow.start()
-    scatter.start()
-    for p in range(pieces):
-        narrow.begin(p)
-    left = list(reversed(range(lax.axis_size("wide") // 2)))
-    for b in range(len(far_bits)):
-        for p in range(pieces):
-            narrow.step(b, p)
-            if len(left) > 1:
-                scatter.step(left.pop(0))
-    while left:
-        scatter.step(left.pop(0))
-    out = pltpu.make_async_copy(scatter.held.at[0], share_ref, scatter.local.at[0])
-    out.start()
-    narrow.finish()
-    scatter.finish()
-    out.wait()
-
-
-def sum_scatter(values, gradient, number):
-    pieces = 4
-    narrow_bits = bits_of(lax.axis_size("narrow"))
-    slots = (len(narrow_bits) + 1) * pieces + Scatter.slots()
-    anywhere = pl.BlockSpec(memory_space=pl.ANY)
-    scratch = narrow_scratch(values.shape, pieces) + scatter_scratch(gradient.shape)
-    return pl.pallas_call(
-        functools.partial(sum_scatter_kernel, pieces),
-        out_shape=(
-            jax.ShapeDtypeStruct(values.shape, jnp.float32),
-            jax.ShapeDtypeStruct(block_shape(gradient.shape), jnp.float32),
-        ),
-        in_specs=[anywhere] * 2,
-        out_specs=(anywhere,) * 2,
-        scratch_shapes=scratch
-        + [pltpu.SemaphoreType.DMA((slots,)), pltpu.SemaphoreType.DMA((slots,))],
-        compiler_params=pltpu.CompilerParams(
-            collective_id=number, has_side_effects=True, vmem_limit_bytes=40 * 2**20
-        ),
-        cost_estimate=pl.CostEstimate(
-            flops=values.size, bytes_accessed=values.size * 32, transcendentals=0
-        ),
-    )(values, gradient)
-
-
-def small_kernel(shared_rows, split_rows, x_ref, share_ref, o_ref, norm_ref, half_ref, *refs):
-    slots, spare, spare_in, sends, arrivals, local = refs
-    wide_bits = bits_of(lax.axis_size("wide"))
-    narrow_bits = bits_of(lax.axis_size("narrow"))
-    greet(
-        [place_at("wide", bit) for bit in wide_bits]
-        + [place_at("narrow", bit) for bit in narrow_bits]
-    )
-    _, z = wide_parts()
-    count = len(wide_bits)
+        [place_at("narrow", bit) for bit in narrow_bits]
+        + [place_at("wide", bit) for bit in wide_bits]
+    )
+    own_rows = lambda ref: ref.at[
+        pl.ds(pl.multiple_of(y * (ref.shape[0] // 2), 8), ref.shape[0] // 2), :
+    ]
+    own_columns = lambda ref: ref.at[
+        :, pl.ds(pl.multiple_of(y * (ref.shape[1] // 2), LANES), ref.shape[1] // 2)
+    ]
+    loads = []
+    for src, dst in (
+        (attend_out_any, attend_out),
+        (attend_moment_any, attend_moment),
+        (own_rows(output_moment_any), output_moment),
+        (expand_any, expand),
+        (own_columns(expand_moment_any), expand_moment),
+        (reduce_any, reduce),
+        (own_rows(reduce_moment_any), reduce_moment),
+    ):
+        loads.append(pltpu.make_async_copy(src, dst, load_sems.at[len(loads)]))
+        loads[-1].start()
+    clip = jnp.minimum(1.0, 1.0 / (norm_ref[0:1, 0:1] + 1e-06))
+    count = halves.shape[1] * sub
+    start = z * count
+    lines = lax.axis_size("wide") // 2
+    band = halves.shape[2]
+
+    def blend(k, moment, gradient):
+        total = highs[k].shape[0]
+
+        def one(i, carry):
+            spot = slab_at(i)
+            highs[k][spot, :], lows[k][spot, :] = split(
+                muon_momentum * moment[spot, :] + clip * gradient[spot, :]
+            )
+            return carry
+
+        lax.fori_loop(0, total // SLAB, one, 0, unroll=UNROLL)
+
+    def multiply(k):
+        columns = pl.ds(pl.multiple_of(start, LANES), count)
+        high, low = highs[k][:, columns], lows[k][:, columns]
+        values = dot_of(high, highs[k][...], 0, 0) + (
+            dot_of(high, lows[k][...], 0, 0) + dot_of(low, highs[k][...], 0, 0)
+        )
+        twice[:, :size] = values
+        twice[:, size:] = values[:, :band]
+        for s in range(sub):
+            for at in range(0, rows, LANES):
+                extent = min(LANES, rows)
+                first = s * rows + at
+                lanes = pl.ds(pl.multiple_of(start + first // LANES * LANES, LANES), band)
+                halves[k * sub + s, at : at + extent, :] = twice[first : first + extent, lanes]
+
+    share = attend_out.shape[0] // lines
+    first_rows, second_rows = 3 * share // 4, share // 4
+    loads[0].wait()
+    loads[1].wait()
+    loads[2].wait()
+    for b in range(lines):
+        for moment, gradient_at, extent in (
+            (attend_moment, b * share, first_rows),
+            (output_moment, b * share + first_rows, second_rows),
+        ):
+            spot = pl.ds(b * extent, extent)
+            moment[spot, :] = (
+                muon_momentum * moment[spot, :]
+                + clip * attend_out[gradient_at : gradient_at + extent, :]
+            )
+
+    def cut(k, values):
+        def one(i, carry):
+            spot = slab_at(i)
+            highs[k][spot, :], lows[k][spot, :] = split(values[spot, :])
+            return carry
+
+        lax.fori_loop(0, highs[k].shape[0] // SLAB, one, 0, unroll=UNROLL)
+
+    cut(0, attend_moment)
+    multiply(0)
+    cut(1, output_moment)
+    multiply(1)
+    loads[3].wait()
+    loads[4].wait()
+    for at in range(0, expand.shape[0], LANES):
+        spot = pl.ds(at, LANES)
+        highs[2][spot, :], lows[2][spot, :] = split(
+            muon_momentum * expand_moment[:, spot].T + clip * expand[spot, :]
+        )
+    multiply(2)
+    loads[5].wait()
+    loads[6].wait()
+    blend(3, reduce_moment, reduce)
+    multiply(3)
+    half = rows // 2
+    row_half = lambda side: pl.ds(pl.multiple_of(side * half, 8), half)
+    slot = iter(range(sends.shape[0]))
     copies = []
-    slots[0] = x_ref[...]
-    hops = line_hops()
-
-    def spot_of(item):
-        spot = z
-        for index, (_, bit) in enumerate(hops):
-            if (item >> index) % 2:
-                spot = partner(spot, bit // 2)
-        return line_block(half_ref, spot)
-
-    gather = Gather(share_ref, spot_of, hops, sends, arrivals, count + len(narrow_bits))
-    keep = pltpu.make_async_copy(share_ref, spot_of(0), local.at[0])
-    keep.start()
-    for b in range(count):
-        copy = send(
-            slots.at[b], slots.at[count + 1 + b], sends, arrivals, b, place_at("wide", wide_bits[b])
-        )
-        copies.append(copy)
-        copy.wait_recv()
-        slots[b + 1] = slots[b] + slots[count + 1 + b]
-    gather.step(0)
-    total = slots[count]
-    o_ref[...] = total
-    shared_part = total[:shared_rows]
-    split_part = total[shared_rows : shared_rows + split_rows]
-    shared = jnp.sum(shared_part * shared_part)
-    split_sum = jnp.sum(split_part * split_part) + jnp.sum(
-        total[shared_rows + split_rows : shared_rows + split_rows + 1]
-    )
-    spare[0] = jnp.full(spare.shape[1:], split_sum, jnp.float32)
-    for b in range(len(narrow_bits)):
-        copy = send(
-            spare.at[b], spare_in.at[b], sends, arrivals, count + b, place_at("narrow", narrow_bits[b])
-        )
-        copies.append(copy)
-        copy.wait_recv()
-        spare[b + 1] = spare[b] + spare_in[b]
-    norm_ref[...] = jnp.sqrt(spare[len(narrow_bits)] + shared)
-    for item in gather.order[1:]:
-        gather.step(item)
-    keep.wait()
-    gather.finish()
-    for copy in copies:
-        copy.wait_send()
-
-
-def small_sums(stacked, share, shared_rows, split_rows, number):
-    wide_bits = bits_of(lax.axis_size("wide"))
-    narrow_bits = bits_of(lax.axis_size("narrow"))
-    vmem = pl.BlockSpec(memory_space=pltpu.VMEM)
-    anywhere = pl.BlockSpec(memory_space=pl.ANY)
-    count = len(wide_bits)
-    line = lax.axis_size("wide") // 2
-    total = count + len(narrow_bits) + line - 1
-    return pl.pallas_call(
-        functools.partial(small_kernel, shared_rows, split_rows),
-        out_shape=(
-            jax.ShapeDtypeStruct(stacked.shape, jnp.float32),
-            jax.ShapeDtypeStruct((8, LANES), jnp.float32),
-            jax.ShapeDtypeStruct((line * share.shape[0], share.shape[1]), jnp.float32),
-        ),
-        in_specs=[vmem, vmem],
-        out_specs=(vmem, vmem, anywhere),
-        scratch_shapes=[
-            pltpu.VMEM((2 * count + 1,) + stacked.shape, jnp.float32),
-            pltpu.VMEM((len(narrow_bits) + 1, 8, LANES), jnp.float32),
-            pltpu.VMEM((len(narrow_bits), 8, LANES), jnp.float32),
-            pltpu.SemaphoreType.DMA((total,)),
-            pltpu.SemaphoreType.DMA((total,)),
-            pltpu.SemaphoreType.DMA((1,)),
-        ],
-        compiler_params=pltpu.CompilerParams(
-            collective_id=number, has_side_effects=True, vmem_limit_bytes=16 * 2**20
-        ),
-    )(stacked, share)
-
-
-def gram_kernel(narrow_bits, hops, x_ref, o_ref, halves, inbox, beside, sends, arrivals, local):
-    parts, rows = x_ref.shape[0], x_ref.shape[1] // 2
-    sub = parts // MATRICES
-    w, n = lax.axis_index("wide"), lax.axis_index("narrow")
-    y = w % 2
-    greeted = {("narrow", bit) for bit in narrow_bits} | set(hops)
-    greet([place_at(axis, bit) for axis, bit in sorted(greeted)])
-    load = pltpu.make_async_copy(x_ref, halves, local.at[0])
-    load.start()
-    load.wait()
-    base = 0 * n
-    size, at, slot = parts, 0, 0
-    for bit in reversed(narrow_bits):
-        size //= 2
-        side = (n // bit) % 2
-        copy = send(
-            halves.at[pl.ds(base + (1 - side) * size, size)],
-            inbox.at[pl.ds(at, size)],
-            sends,
-            arrivals,
-            slot,
-            place_at("narrow", bit),
-        )
-        base = base + side * size
-        copy.wait()
-        for s in range(size):
-            halves[base + s] = halves[base + s] + inbox[at + s]
-        at += size
-        slot += 1
-    row_half = lambda side: pl.ds(pl.multiple_of(side * rows, 8), rows)
-    copy = send(
-        halves.at[n, row_half(1 - y)], beside.at[0], sends, arrivals, slot, place_at("wide", 1)
-    )
-    copy.wait()
-    beside[1] = halves[n, row_half(y)] + beside[0]
-    slot += 1
+
+    def push(src, dst, place):
+        copies.append(send(src, dst, sends, arrivals, next(slot), place))
+        return copies[-1]
+
+    at = 0
+    for bit in narrow_bits:
+        value = (n // bit) % 2
+        last = 2 * bit == parts
+        waits = []
+        for j in range(parts // (2 * bit)):
+            mine = n % bit + value * bit + j * 2 * bit
+            theirs = n % bit + (1 - value) * bit + j * 2 * bit
+            for side in (1 - y, y) if last else (None,):
+                spot = slice(None) if side is None else row_half(side)
+                copy = push(
+                    halves.at[theirs] if side is None else halves.at[theirs, spot],
+                    inbox.at[at + j] if side is None else inbox.at[at + j, spot],
+                    place_at("narrow", bit),
+                )
+                waits.append((copy, mine, at + j, spot))
+        at += parts // (2 * bit)
+        for copy, mine, where, spot in waits:
+            copy.wait_recv()
+            halves[mine, spot] = halves[mine, spot] + inbox[where, spot]
+            if last and copy is waits[0][0]:
+                side_copy = push(halves.at[n, row_half(1 - y)], block.at[0], place_at("wide", 1))
+    side_copy.wait_recv()
+    block[1] = halves[n, row_half(y)] + block[0]
 
     def spot_of(item):
         big, small = w, n % sub
@@ -515,47 +470,68 @@
                     big = partner(big, bit)
                 else:
                     small = partner(small, bit)
-        start = ((big // 2) * (2 * sub) + small * 2 + big % 2) * rows
-        return o_ref.at[pl.ds(pl.multiple_of(start, 8), rows), :]
-
-    keep = pltpu.make_async_copy(beside.at[1], spot_of(0), local.at[0])
+        first = ((big // 2) * (2 * sub) + small * 2 + big % 2) * half
+        return band_ref.at[pl.ds(pl.multiple_of(first, 8), half), :]
+
+    keep = pltpu.make_async_copy(block.at[1], spot_of(0), local.at[0])
     keep.start()
-    gather = Gather(beside.at[1], spot_of, hops, sends, arrivals, slot)
+    gather = Gather(block.at[1], spot_of, hops, sends, arrivals, next(slot))
     for item in gather.order:
         gather.step(item)
     keep.wait()
     gather.finish()
-
-
-def gram_whole(partial, number):
+    for copy in copies:
+        copy.wait_send()
+
+
+def gram_whole(norm, lines, moments, number):
     narrow_bits = bits_of(lax.axis_size("narrow"))
     wide_bits = bits_of(lax.axis_size("wide"))
-    parts, rows, band = partial.shape
-    sub = parts // MATRICES
-    hops = [("narrow", bit) for bit in bits_of(sub)]
-    hops += [("wide", bit) for bit in reversed(wide_bits)]
-    slots = len(narrow_bits) + 2 ** len(hops)
+    size = lines[0].shape[1]
+    sub = lax.axis_size("narrow") // MATRICES
+    parts = lax.axis_size("narrow")
+    count = 2 * size // lax.axis_size("wide")
+    band = size // 2 + LANES
+    halves = (parts, count // sub, band)
+    line_rows = [lines[0].shape[0] * 3 // 4, lines[0].shape[0] // 4]
+    line_rows += [lines[1].shape[0], lines[2].shape[0]]
+    gathers = len(bits_of(sub)) + len(wide_bits)
+    slots = parts + 2 + 2**gathers
+    vmem = pl.BlockSpec(memory_space=pltpu.VMEM)
+    anywhere = pl.BlockSpec(memory_space=pl.ANY)
+    wide = lambda *shape: pltpu.VMEM(shape, jnp.float32)
     return pl.pallas_call(
-        functools.partial(gram_kernel, narrow_bits, hops),
-        out_shape=jax.ShapeDtypeStruct((rows * sub * len_of_line(), band), jnp.float32),
-        in_specs=[pl.BlockSpec(memory_space=pl.ANY)],
-        out_specs=pl.BlockSpec(memory_space=pl.ANY),
+        gram_kernel,
+        out_shape=jax.ShapeDtypeStruct((size, band), jnp.float32),
+        in_specs=[vmem] + [anywhere] * 7,
+        out_specs=anywhere,
         scratch_shapes=[
-            pltpu.VMEM(partial.shape, jnp.float32),
-            pltpu.VMEM(partial.shape, jnp.float32),
-            pltpu.VMEM((2, rows // 2, band), jnp.float32),
+            wide(*lines[0].shape),
+            wide(*lines[1].shape),
+            wide(*lines[2].shape),
+            wide(line_rows[0], size),
+            wide(line_rows[1], size),
+            wide(size, line_rows[2]),
+            wide(line_rows[3], size),
+        ]
+        + [pltpu.VMEM((rows, size), jnp.bfloat16) for rows in line_rows] * 2
+        + [
+            wide(count, size + band),
+            wide(*halves),
+            wide(*halves),
+            wide(2, halves[1] // 2, band),
+            pltpu.SemaphoreType.DMA((7,)),
             pltpu.SemaphoreType.DMA((slots,)),
             pltpu.SemaphoreType.DMA((slots,)),
             pltpu.SemaphoreType.DMA((1,)),
         ],
         compiler_params=pltpu.CompilerParams(
-            collective_id=number, has_side_effects=True, vmem_limit_bytes=24 * 2**20
+            collective_id=number, has_side_effects=True, vmem_limit_bytes=48 * 2**20
         ),
-    )(partial)
-
-
-def len_of_line():
-    return lax.axis_size("wide") // 2
+        cost_estimate=pl.CostEstimate(
+            flops=3 * size * size * size, bytes_accessed=80 * size * size, transcendentals=0
+        ),
+    )(norm, *lines, *moments)
 
 
 def split(values):
@@ -568,7 +544,7 @@
     return dot(left_high, right_high) + (dot(left_high, right_low) + dot(left_low, right_high))
 
 
-def polar_kernel(g_ref, q_ref, gh, gl, ph, pw, th, tl):
+def polar_kernel(g_ref, band_ref, q_ref, gh, gl, ph, pw, th, tl):
     size = g_ref.shape[0]
     blocks = size // BLK
     first, second, third = newton_terms
@@ -633,6 +609,9 @@
         return carry
 
     lax.fori_loop(0, NEWTON - 1, one_step, 0)
+    for i in range(count):
+        for j in range(count // 2 + 1):
+            band_ref[lanes(i), lanes(j)] = q_ref[lanes(i), lanes(i + j)]
 
 
 def polar_factor(gramian):
@@ -640,10 +619,11 @@
     vmem = pl.BlockSpec(memory_space=pltpu.VMEM)
     return pl.pallas_call(
         polar_kernel,
-        out_shape=jax.ShapeDtypeStruct((size, size), jnp.float32),
+        out_shape=jax.ShapeDtypeStruct(gramian.shape, jnp.float32),
         in_specs=[vmem],
         out_specs=vmem,
-        scratch_shapes=[pltpu.VMEM((size, size), jnp.bfloat16)] * 6,
+        scratch_shapes=[pltpu.VMEM((size, size), jnp.float32)]
+        + [pltpu.VMEM((size, size), jnp.bfloat16)] * 6,
         compiler_params=pltpu.CompilerParams(vmem_limit_bytes=48 * 2**20),
         cost_estimate=pl.CostEstimate(
             flops=17 * 6 * size**3, bytes_accessed=8 * size * size, transcendentals=0
@@ -651,75 +631,117 @@
     )(gramian)
 
 
-def finish_kernel(sub, pieces, norm_ref, q_ref, *refs):
-    lines, others, refs = refs[0:6:2], refs[1:6:2], refs[6:]
-    moments, weights, refs = refs[:4], refs[4:8], refs[8:]
-    carried, results, refs = refs[:4], refs[4:8], refs[8:]
-    qs, refs = refs[0], refs[1:]
-    staged, values, highs, lows = refs[:4], refs[4:8], refs[8:12], refs[12:16]
-    sends, arrivals, near_sems, load_sems, value_sems, out_sems = refs[16:]
-    size = q_ref.shape[0]
-    half = size // 2
+def spread_kernel(sub, pieces, q_ref, o_ref, sends, arrivals, local):
+    half = q_ref.shape[0] // 2
     step = half // pieces
     w, n = lax.axis_index("wide"), lax.axis_index("narrow")
     own = n // sub
     across = partner(own, 2)
-    far = own // 2
     near_place, far_place = place_at("narrow", sub), place_at("narrow", 2 * sub)
     side_place = place_at("wide", 1)
     greet([near_place, far_place, side_place])
     y = w % 2
     rows = lambda side, p: pl.ds(pl.multiple_of(side * half + p * step, 8), step)
-    slot = iter(range(1 + 4 * pieces))
     copies = []
 
     def push(src, dst, place):
-        copies.append(send(src, dst, sends, arrivals, next(slot), place))
+        copies.append(send(src, dst, sends, arrivals, len(copies), place))
         return copies[-1]
 
     crossing = [
-        push(q_ref.at[rows(y, p)], qs.at[own, rows(y, p)], far_place) for p in range(pieces)
+        push(q_ref.at[rows(y, p)], o_ref.at[own, rows(y, p)], far_place) for p in range(pieces)
     ]
-    near_own = push(q_ref, qs.at[own], near_place)
-    keep = pltpu.make_async_copy(q_ref, qs.at[own], near_sems.at[0])
+    landing = [push(q_ref, o_ref.at[own], near_place)]
+    keep = pltpu.make_async_copy(q_ref, o_ref.at[own], local.at[0])
     keep.start()
+    aside = []
+
+    def forward(p):
+        crossing[p].wait_recv()
+        spot = o_ref.at[across, rows(y, p)]
+        aside.append(push(spot, spot, side_place))
+        landing.append(push(spot, spot, near_place))
+
+    def forward_side(p):
+        aside[p].wait_recv()
+        spot = o_ref.at[across, rows(1 - y, p)]
+        landing.append(push(spot, spot, near_place))
+
+    forward(0)
+    for p in range(1, pieces):
+        forward(p)
+        forward_side(p - 1)
+    forward_side(pieces - 1)
+    keep.wait()
+    for copy in landing:
+        copy.wait_recv()
+    for copy in copies:
+        copy.wait_send()
+
+
+def spread(band, number):
+    pieces = 4
+    slots = 1 + 4 * pieces
+    sub = lax.axis_size("narrow") // MATRICES
+    return pl.pallas_call(
+        functools.partial(spread_kernel, sub, pieces),
+        out_shape=jax.ShapeDtypeStruct((MATRICES,) + band.shape, jnp.float32),
+        in_specs=[pl.BlockSpec(memory_space=pltpu.VMEM)],
+        out_specs=pl.BlockSpec(memory_space=pl.ANY),
+        scratch_shapes=[
+            pltpu.SemaphoreType.DMA((slots,)),
+            pltpu.SemaphoreType.DMA((slots,)),
+            pltpu.SemaphoreType.DMA((1,)),
+        ],
+        compiler_params=pltpu.CompilerParams(collective_id=number, has_side_effects=True),
+    )(band)
+
+
+def finish_kernel(norm_ref, bands_any, *refs):
+    lines, others, refs = refs[0:6:2], refs[1:6:2], refs[6:]
+    moments, weights, refs = refs[:4], refs[4:8], refs[8:]
+    carried, results, refs = refs[:4], refs[4:8], refs[8:]
+    bands, factor_high, factor_low = refs[:3]
+    staged, values, highs, lows = refs[3:7], refs[7:11], refs[11:15], refs[15:19]
+    load_sems, value_sems, out_sems, band_sems = refs[19:]
+    size = factor_high.shape[0]
+    y, _ = wide_parts()
     blocks = lax.axis_size("wide")
-    stages = staged
     whole = []
+    fills = []
     for k in range(MATRICES):
         sources = (lines[max(k - 1, 0)], others[max(k - 1, 0)])
-        extent = stages[k].shape[0] // 2
+        extent = staged[k].shape[0] // 2
         for side, source in zip((y, 1 - y), sources):
             if k >= 2:
-                spot = stages[k].at[pl.ds(pl.multiple_of(side * extent, 8), extent), :]
+                spot = staged[k].at[pl.ds(pl.multiple_of(side * extent, 8), extent), :]
                 pltpu.make_async_copy(source, spot, load_sems.at[k]).start()
                 continue
-            share = (stages[0].shape[0] // blocks, stages[1].shape[0] // blocks)
+            share = (staged[0].shape[0] // blocks, staged[1].shape[0] // blocks)
             for b in range(blocks // 2):
                 start = b * (share[0] + share[1]) + k * share[0]
                 to = pl.multiple_of(side * extent + b * share[k], 8)
                 pltpu.make_async_copy(
                     source.at[pl.ds(start, share[k]), :],
-                    stages[k].at[pl.ds(to, share[k]), :],
+                    staged[k].at[pl.ds(to, share[k]), :],
                     load_sems.at[k],
                 ).start()
-        whole.append(pltpu.make_async_copy(stages[k], stages[k], load_sems.at[k]))
-    fills = []
-    for k in range(MATRICES):
+        whole.append(pltpu.make_async_copy(staged[k], staged[k], load_sems.at[k]))
         fills.append(pltpu.make_async_copy(moments[k], values[k], value_sems.at[k]))
         fills[-1].start()
-    norm = norm_ref[0:1, 0:1]
-    clip = jnp.minimum(1.0, 1.0 / (norm + 1e-06))
+    arrivals = []
+    for k in range(MATRICES):
+        arrivals.append(pltpu.make_async_copy(bands_any.at[k], bands.at[k], band_sems.at[k]))
+        arrivals[-1].start()
+    clip = jnp.minimum(1.0, 1.0 / (norm_ref[0:1, 0:1] + 1e-06))
 
     def blend_rows(value, stage):
-        slab = 16
-
         def one(i, carry):
-            spot = pl.ds(pl.multiple_of(i * slab, 8), slab)
+            spot = slab_at(i)
             value[spot, :] = muon_momentum * value[spot, :] + clip * stage[spot, :]
             return carry
 
-        lax.fori_loop(0, value.shape[0] // slab, one, 0, unroll=UNROLL)
+        lax.fori_loop(0, value.shape[0] // SLAB, one, 0, unroll=UNROLL)
 
     def blend_columns(value, stage):
         def one(i, carry):
@@ -734,15 +756,12 @@
         whole[k].wait()
         fills[k].wait()
         blend = blend_columns if k in COLUMNS else blend_rows
-        blend(values[k], stages[k])
-    for k in range(MATRICES):
+        blend(values[k], staged[k])
         outs.append(pltpu.make_async_copy(values[k], carried[k], out_sems.at[k]))
         outs[-1].start()
-    for k in range(MATRICES):
 
         def cut(i, carry, k=k):
-            spot = pl.ds(pl.multiple_of(i * SLAB, SLAB), SLAB)
-            highs[k][spot, :], lows[k][spot, :] = split(values[k][spot, :])
+            highs[k][slab_at(i), :], lows[k][slab_at(i), :] = split(values[k][slab_at(i), :])
             return carry
 
         lax.fori_loop(0, values[k].shape[0] // SLAB, cut, 0, unroll=UNROLL)
@@ -750,121 +769,73 @@
         outs[k].wait()
         fills[k] = pltpu.make_async_copy(weights[k], values[k], value_sems.at[k])
         fills[k].start()
-
-    dot = lambda left, right, dims: lax.dot_general(
-        left, right, (dims, ((), ())), preferred_element_type=jnp.float32
-    )
     lengths = (3 * D, D, FF, FF)
-
-    def process(k, start):
-        spot = pl.ds(pl.multiple_of(start, BLK), BLK)
-        q_high, q_low = split(qs[k, spot, :])
-        high, low = highs[k], lows[k]
-        scale = muon_rate * 0.2 * math.sqrt(lengths[k])
-        if k in COLUMNS:
-            dims = ((1,), (0,))
-            polar = dot(q_high, high[...], dims) + (
-                dot(q_high, low[...], dims) + dot(q_low, high[...], dims)
-            )
-            where = (spot, slice(None))
-        else:
-            dims = ((1,), (1,))
-            polar = dot(high[...], q_high, dims) + (
-                dot(low[...], q_high, dims) + dot(high[...], q_low, dims)
-            )
-            where = (slice(None), spot)
-        values[k][where] = values[k][where] * (1.0 - muon_rate * weight_decay) - scale * polar
-        pltpu.make_async_copy(
-            values[k].at[where], results[k].at[where], out_sems.at[k]
-        ).start()
-
-    def pair(first, starts):
-        for side in range(2):
-            matrices = (0, 1) if first == (side == 0) else (2, 3)
-
-            @pl.when(far == side)
-            def _(matrices=matrices):
-                for k in matrices:
-                    lax.fori_loop(
-                        0, len(starts), lambda i, c, k=k: (process(k, starts[0] + i * BLK), c)[1], 0
-                    )
-
-    aside, near_across, near_side = [], [], []
-
-    def forward(p):
-        crossing[p].wait_recv()
-        spot = qs.at[across, rows(y, p)]
-        aside.append(push(spot, spot, side_place))
-        near_across.append(push(spot, spot, near_place))
-
-    def forward_side(p):
-        aside[p].wait_recv()
-        spot = qs.at[across, rows(1 - y, p)]
-        near_side.append(push(spot, spot, near_place))
-
-    forward(0)
-    keep.wait()
-    near_own.wait_recv()
+    count = size // LANES
+    lanes = lambda block: pl.ds((block % count) * LANES, LANES)
     for k in range(MATRICES):
+        arrivals[k].wait()
+        for i in range(count):
+            for j in range(count // 2 + 1):
+                part = bands[k, lanes(i), lanes(j)]
+                spot = (lanes(i), lanes(i + j))
+                factor_high[spot], factor_low[spot] = split(part)
+                if 0 < j < count // 2:
+                    spot = (lanes(i + j), lanes(i))
+                    factor_high[spot], factor_low[spot] = split(part.T)
         fills[k].wait()
-    pair(True, [0, BLK])
-    forward(1)
-    pair(True, [2 * BLK, 3 * BLK])
-    forward_side(0)
-    for p in range(2, pieces):
-        forward(p)
-        forward_side(p - 1)
-    group = BLK // step
-    for copy in near_across:
-        copy.wait_recv()
-    pair(False, [y * half + i * BLK for i in range(half // BLK)])
-    for copy in near_side[:group]:
-        copy.wait_recv()
-    pair(False, [(1 - y) * half])
-    forward_side(pieces - 1)
-    for copy in near_side[group:]:
-        copy.wait_recv()
-    pair(False, [(1 - y) * half + BLK])
-    for copy in copies:
-        copy.wait_send()
+
+        def process(i, carry, k=k):
+            spot = pl.ds(pl.multiple_of(i * BLK, BLK), BLK)
+            q_high, q_low = factor_high[spot, :], factor_low[spot, :]
+            high, low = highs[k], lows[k]
+            if k in COLUMNS:
+                polar = dot_of(q_high, high[...], 1, 0) + (
+                    dot_of(q_high, low[...], 1, 0) + dot_of(q_low, high[...], 1, 0)
+                )
+                where = (spot, slice(None))
+            else:
+                polar = dot_of(high[...], q_high, 1, 1) + (
+                    dot_of(low[...], q_high, 1, 1) + dot_of(high[...], q_low, 1, 1)
+                )
+                where = (slice(None), spot)
+            scale = muon_rate * 0.2 * math.sqrt(lengths[k])
+            values[k][where] = values[k][where] * (1.0 - muon_rate * weight_decay) - scale * polar
+            pltpu.make_async_copy(
+                values[k].at[where], results[k].at[where], out_sems.at[k]
+            ).start()
+            return carry
+
+        lax.fori_loop(0, size // BLK, process, 0)
     for k in range(MATRICES):
         pltpu.make_async_copy(values[k], results[k], out_sems.at[k]).wait()
 
 
-def finish(norm, factor, lines, others, moments, weights, number):
-    pieces = 4
-    size = factor.shape[0]
-    sub = lax.axis_size("narrow") // MATRICES
+def finish(norm, bands, lines, others, moments, weights):
+    size = bands.shape[1]
     anywhere = pl.BlockSpec(memory_space=pl.ANY)
     operands = [part for both in zip(lines, others) for part in both]
     shapes = [jax.ShapeDtypeStruct(moment.shape, jnp.float32) for moment in moments]
     staged = [(moment.size // size, size) for moment in moments]
-    slots = 1 + 4 * pieces
     outs = pl.pallas_call(
-        functools.partial(finish_kernel, sub, pieces),
+        finish_kernel,
         out_shape=tuple(shapes + shapes),
         in_specs=[pl.BlockSpec(memory_space=pltpu.VMEM)] + [anywhere] * (1 + len(operands) + 8),
         out_specs=(anywhere,) * 8,
-        scratch_shapes=[pltpu.VMEM((MATRICES, size, size), jnp.float32)]
+        scratch_shapes=[
+            pltpu.VMEM(bands.shape, jnp.float32),
+            pltpu.VMEM((size, size), jnp.bfloat16),
+            pltpu.VMEM((size, size), jnp.bfloat16),
+        ]
         + [pltpu.VMEM(shape, jnp.float32) for shape in staged]
         + [pltpu.VMEM(moment.shape, jnp.float32) for moment in moments]
         + [pltpu.VMEM(moment.shape, jnp.bfloat16) for moment in moments]
         + [pltpu.VMEM(moment.shape, jnp.bfloat16) for moment in moments]
-        + [
-            pltpu.SemaphoreType.DMA((slots,)),
-            pltpu.SemaphoreType.DMA((slots,)),
-            pltpu.SemaphoreType.DMA((1,)),
-            pltpu.SemaphoreType.DMA((MATRICES,)),
-            pltpu.SemaphoreType.DMA((MATRICES,)),
-            pltpu.SemaphoreType.DMA((MATRICES,)),
-        ],
-        compiler_params=pltpu.CompilerParams(
-            collective_id=number, has_side_effects=True, vmem_limit_bytes=60 * 2**20
-        ),
+        + [pltpu.SemaphoreType.DMA((MATRICES,))] * 4,
+        compiler_params=pltpu.CompilerParams(vmem_limit_bytes=60 * 2**20),
         cost_estimate=pl.CostEstimate(
             flops=18 * size * size * size, bytes_accessed=80 * size * size, transcendentals=0
         ),
-    )(norm, factor, *operands, *moments, *weights)
+    )(norm, bands, *operands, *moments, *weights)
     return outs[:4], outs[4:]
 
 
@@ -1303,100 +1274,6 @@
     grad_scale_ref[...] = jnp.sum(scales, axis=0, keepdims=True)
 
 
-def mixer_backward(tokens, shift, scale, taps, grad_mixed, grad_hidden):
-    rows, width = tokens.shape
-    vmem = pl.BlockSpec(memory_space=pltpu.VMEM)
-    f32 = lambda *shape: jax.ShapeDtypeStruct(shape, jnp.float32)
-    return pl.pallas_call(
-        mixer_kernel_backward,
-        out_shape=(
-            jax.ShapeDtypeStruct((rows, width), jnp.bfloat16),
-            f32(9, width),
-            f32(1, width),
-            f32(1, width),
-        ),
-        in_specs=[vmem] * 6,
-        out_specs=(vmem,) * 4,
-        scratch_shapes=[
-            pltpu.VMEM((rows, width), jnp.float32),
-            pltpu.VMEM((rows, width), jnp.float32),
-            pltpu.VMEM((rows, LANES), jnp.float32),
-        ],
-        compiler_params=pltpu.CompilerParams(vmem_limit_bytes=48 * 2**20),
-        cost_estimate=pl.CostEstimate(
-            flops=100 * rows * width, bytes_accessed=12 * rows * width, transcendentals=0
-        ),
-    )(tokens, shift, scale, taps, grad_mixed, grad_hidden)
-
-
-def hidden_kernel_backward(
-    hidden_ref,
-    branch_ref,
-    grad_entry_ref,
-    cotangent_ref,
-    live_ref,
-    scale_ref,
-    gate_ref,
-    grad_hidden_ref,
-    grad_branch_ref,
-    grad_shift_ref,
-    grad_scale_ref,
-    grad_gate_ref,
-):
-    width = hidden_ref.shape[1]
-    stretch = 1.0 + scale_ref[...]
-    gate = gate_ref[...]
-    live = live_ref[...]
-
-    def one(r, carry):
-        shifts, scales, gates = carry
-        normed, inverse = norm_strip(hidden_ref[slab_at(r), :])
-        back = grad_entry_ref[slab_at(r), :]
-        stretched = back * stretch
-        first = jnp.mean(stretched, axis=-1, keepdims=True)
-        second = jnp.mean(stretched * normed, axis=-1, keepdims=True)
-        grad = cotangent_ref[slab_at(r), :].astype(jnp.float32) * live + (
-            stretched - first - normed * second
-        ) * inverse
-        grad_hidden_ref[slab_at(r), :] = grad
-        grad_branch_ref[slab_at(r), :] = (gate * grad).astype(jnp.bfloat16)
-        return (
-            shifts + fold_rows(back),
-            scales + fold_rows(back * normed),
-            gates + fold_rows(branch_ref[slab_at(r), :] * grad),
-        )
-
-    zero = jnp.zeros((8, width), jnp.float32)
-    shifts, scales, gates = lax.fori_loop(
-        0, hidden_ref.shape[0] // SLAB, one, (zero, zero, zero), unroll=UNROLL
-    )
-    grad_shift_ref[...] = jnp.sum(shifts, axis=0, keepdims=True)
-    grad_scale_ref[...] = jnp.sum(scales, axis=0, keepdims=True)
-    grad_gate_ref[...] = jnp.sum(gates, axis=0, keepdims=True)
-
-
-def hidden_backward(hidden, branch, grad_entry, cotangent, live, scale, gate):
-    rows, width = hidden.shape
-    vmem = pl.BlockSpec(memory_space=pltpu.VMEM)
-    f32 = lambda *shape: jax.ShapeDtypeStruct(shape, jnp.float32)
-    return pl.pallas_call(
-        hidden_kernel_backward,
-        out_shape=(
-            f32(rows, width),
-            jax.ShapeDtypeStruct((rows, width), jnp.bfloat16),
-            f32(1, width),
-            f32(1, width),
-            f32(1, width),
-        ),
-        in_specs=[vmem] * 7,
-        out_specs=(vmem,) * 5,
-        compiler_params=pltpu.CompilerParams(vmem_limit_bytes=48 * 2**20),
-        cost_estimate=pl.CostEstimate(
-            flops=30 * rows * width, bytes_accessed=22 * rows * width, transcendentals=0
-        ),
-    )(hidden, branch, grad_entry, cotangent, live, scale, gate)
-
-
 def dot_of(left, right, left_axis, right_axis):
     return lax.dot_general(
         left,
@@ -1472,94 +1349,6 @@
             transcendentals=tokens * tokens * own // HEAD,
         ),
     )(mixed, attend_weight)
-
-
-def attend_back_kernel(
-    mixed_ref,
-    attend_ref,
-    output_ref,
-    triple_ref,
-    context_ref,
-    logsum_ref,
-    grad_branch_ref,
-    attend_out_ref,
-    grad_mixed_ref,
-    grad_context,
-    keys_t,
-    grad_queries_t,
-    grad_keys,
-    grad_values,
-    grad_triple,
-):
-    tokens = mixed_ref.shape[0]
-    width = output_ref.shape[0]
-    grad_context[...] = dot_of(grad_branch_ref[...], output_ref[...], 1, 1).astype(jnp.bfloat16)
-    keys_t[...] = triple_ref[:, pl.ds(width, width)].T
-    grad_keys[...] = jnp.zeros_like(grad_keys)
-    grad_values[...] = jnp.zeros_like(grad_values)
-    scale = HEAD ** (-0.5)
-    low_scale = jnp.bfloat16(scale)
-    for head in range(width // HEAD):
-        pair = head * HEAD // LANES * LANES
-        inside = head % (LANES // HEAD)
-        lanes = pl.ds(pair, LANES)
-
-        def one(block, carry, head=head, pair=pair, inside=inside, lanes=lanes):
-            spot = pl.ds(pl.multiple_of(block * QUERIES, QUERIES), QUERIES)
-            queries = head_only(triple_ref[spot, lanes], inside)
-            back = head_only(grad_context[spot, lanes], inside)
-            scores = dot_of(triple_ref[:, pl.ds(width + pair, LANES)], queries * low_scale, 1, 1)
-            weights = jnp.exp(scores - logsum_ref[pl.ds(head, 1), spot])
-            grad_weights = dot_of(triple_ref[:, pl.ds(2 * width + pair, LANES)], back, 1, 1)
-            grad_values[:, lanes] += dot_of(weights.astype(jnp.bfloat16), back, 1, 0)
-            inner = jnp.sum(weights * grad_weights, axis=0, keepdims=True)
-            grad_low = (weights * (grad_weights - inner)).astype(jnp.bfloat16)
-            grad_keys[:, lanes] += dot_of(grad_low, queries, 1, 0)
-            grad_queries_t[pl.ds(head * HEAD, HEAD), spot] = dot_of(
-                keys_t[pl.ds(head * HEAD, HEAD), :], grad_low, 1, 0
-            )
-            return carry
-
-        lax.fori_loop(0, tokens // QUERIES, one, 0)
-    grad_triple[:, pl.ds(0, width)] = (grad_queries_t[...].T * scale).astype(jnp.bfloat16)
-    grad_triple[:, pl.ds(width, width)] = (grad_keys[...] * scale).astype(jnp.bfloat16)
-    grad_triple[:, pl.ds(2 * width, width)] = grad_values[...].astype(jnp.bfloat16)
-    grad_output = dot_of(context_ref[...], grad_branch_ref[...], 0, 0)
-    grad_attend = dot_of(grad_triple[...], mixed_ref[...], 0, 0)
-    blocks = lax.axis_size("wide")
-    first, second = 3 * width // blocks, width // blocks
-    for b in range(blocks):
-        start = b * (first + second)
-        attend_out_ref[pl.ds(start, first), :] = grad_attend[b * first : (b + 1) * first]
-        attend_out_ref[pl.ds(start + first, second), :] = grad_output[b * second : (b + 1) * second]
-    grad_mixed_ref[...] = dot_of(grad_triple[...], attend_ref[...], 1, 1)
-
-
-def attend_back(mixed, attend_low, output_low, triple, context, logsum, grad_branch):
-    tokens, width = mixed.shape
-    own = output_low.shape[0]
-    vmem = pl.BlockSpec(memory_space=pltpu.VMEM)
-    f32 = lambda *shape: jax.ShapeDtypeStruct(shape, jnp.float32)
-    return pl.pallas_call(
-        attend_back_kernel,
-        out_shape=(f32(4 * own, width), f32(tokens, width)),
-        in_specs=[vmem] * 7,
-        out_specs=(vmem,) * 2,
-        scratch_shapes=[
-            pltpu.VMEM((tokens, own), jnp.bfloat16),
-            pltpu.VMEM((own, tokens), jnp.bfloat16),
-            pltpu.VMEM((own, tokens), jnp.float32),
-            pltpu.VMEM((tokens, own), jnp.float32),
-            pltpu.VMEM((tokens, own), jnp.float32),
-            pltpu.VMEM((tokens, 3 * own), jnp.bfloat16),
-        ],
-        compiler_params=pltpu.CompilerParams(vmem_limit_bytes=52 * 2**20),
-        cost_estimate=pl.CostEstimate(
-            flops=40 * tokens * tokens * own,
-            bytes_accessed=20 * tokens * width,
-            transcendentals=tokens * tokens * own // HEAD,
-        ),
-    )(mixed, attend_low, output_low, triple, context, logsum, grad_branch)
 
 
 def narrow_hops():
@@ -1690,34 +1479,536 @@
     return values
 
 
-def part(rows, second_rows):
-    width = rows.shape[1]
-    size = second_rows // lax.axis_size("wide")
-    total = 4 * size
-    blocks = rows.reshape(-1, total, width)
-    return blocks[:, : total - size].reshape(-1, width), blocks[:, total - size :].reshape(-1, width)
-
-
-def gram_band(matrix):
-    width = matrix.shape[1]
-    count = 2 * width // lax.axis_size("wide")
-    start = (lax.axis_index("wide") // 2) * count
-    rows = lax.dynamic_slice_in_dim(matrix, start, count, 1)
-    product_rows = lax.dot_general(
-        rows,
-        matrix,
-        (((0,), (0,)), ((), ())),
-        precision=lax.Precision.HIGH,
-        preferred_element_type=jnp.float32,
-    )
-    band = width // 2 + LANES
-    twice = jnp.concatenate([product_rows, product_rows[:, :band]], axis=1)
-    return jnp.concatenate(
-        [
-            lax.dynamic_slice_in_dim(twice[at : at + LANES], start + at, band, 1)
-            for at in range(0, count, LANES)
+def back_kernel(
+    pieces,
+    hidden_any,
+    branch_any,
+    grad_entry_any,
+    cotangent_any,
+    live_ref,
+    scale_ref,
+    gate_ref,
+    mixed_ref,
+    attend_ref,
+    output_ref,
+    triple_ref,
+    context_ref,
+    logsum_ref,
+    reduce_share_ref,
+    expand_share_ref,
+    grad_hidden_ref,
+    grad_shift_ref,
+    grad_scale_ref,
+    grad_gate_ref,
+    grad_mixed_any,
+    attend_out_share,
+    reduce_line,
+    expand_line,
+    hidden,
+    branch,
+    grad_entry,
+    cotangent,
+    grad_branch,
+    output_low,
+    grad_context,
+    keys_t,
+    grad_queries_t,
+    grad_keys,
+    grad_values,
+    grad_triple,
+    near,
+    far,
+    held,
+    local,
+    scatter_held,
+    scatter_beside,
+    scatter_inbox,
+    scatter_loads,
+    load_sems,
+    keep_sems,
+    sends,
+    arrivals,
+):
+    tokens, width = hidden.shape
+    own = output_ref.shape[0]
+    _, z = wide_parts()
+    far_bits = bits_of(lax.axis_size("narrow"))[1:]
+    greet(
+        [place_at("narrow", bit) for bit in [1] + far_bits]
+        + [place_at("wide", bit) for bit in bits_of(lax.axis_size("wide"))]
+    )
+    hops = line_hops()
+    base = (len(far_bits) + 2) * pieces + Scatter.slots()
+
+    def spot_in(line):
+        def spot_of(item):
+            spot = z
+            for index, (_, bit) in enumerate(hops):
+                if (item >> index) % 2:
+                    spot = partner(spot, bit // 2)
+            return line_block(line, spot)
+
+        return spot_of
+
+    gathers, keeps = [], []
+    for index, (share, line) in enumerate(
+        ((reduce_share_ref, reduce_line), (expand_share_ref, expand_line))
+    ):
+        start = base + index * (2 ** len(hops) - 1)
+        gathers.append(Gather(share, spot_in(line), hops, sends, arrivals, start))
+        gathers[index].step(0)
+        keeps.append(pltpu.make_async_copy(share, spot_in(line)(0), keep_sems.at[index]))
+        keeps[index].start()
+    step = tokens // pieces
+    loads = []
+    for p in range(pieces):
+        spot = pl.ds(p * step, step)
+        pairs = (
+            (hidden_any, hidden),
+            (branch_any, branch),
+            (grad_entry_any, grad_entry),
+            (cotangent_any, cotangent),
+        )
+        loads.append(
+            [
+                pltpu.make_async_copy(src.at[spot, :], dst.at[spot, :], load_sems.at[4 * p + i])
+                for i, (src, dst) in enumerate(pairs)
+            ]
+        )
+        for load in loads[p]:
+            load.start()
+    output_low[...] = output_ref[...].astype(jnp.bfloat16)
+    stretch, gate, live = 1.0 + scale_ref[...], gate_ref[...], live_ref[...]
+
+    def one_slab(r, carry):
+        shifts, scales, gates = carry
+        spot = slab_at(r)
+        normed, inverse = norm_strip(hidden[spot, :])
+        back = grad_entry[spot, :]
+        stretched = back * stretch
+        first = jnp.mean(stretched, axis=-1, keepdims=True)
+        second = jnp.mean(stretched * normed, axis=-1, keepdims=True)
+        grad = cotangent[spot, :].astype(jnp.float32) * live + (
+            stretched - first - normed * second
+        ) * inverse
+        grad_hidden_ref[spot, :] = grad
+        grad_branch[spot, :] = (gate * grad).astype(jnp.bfloat16)
+        return (
+            shifts + fold_rows(back),
+            scales + fold_rows(back * normed),
+            gates + fold_rows(branch[spot, :] * grad),
+        )
+
+    sums = (jnp.zeros((8, width), jnp.float32),) * 3
+    for p in range(pieces):
+        for load in loads[p]:
+            load.wait()
+        first_slab = p * step // SLAB
+        sums = lax.fori_loop(
+            first_slab, first_slab + step // SLAB, one_slab, sums, unroll=UNROLL
+        )
+    for ref, total in zip((grad_shift_ref, grad_scale_ref, grad_gate_ref), sums):
+        ref[...] = jnp.sum(total, axis=0, keepdims=True)
+    grad_context[...] = dot_of(grad_branch[...], output_low[...], 1, 1).astype(jnp.bfloat16)
+    keys_t[...] = triple_ref[:, pl.ds(own, own)].T
+    grad_keys[...] = jnp.zeros_like(grad_keys)
+    grad_values[...] = jnp.zeros_like(grad_values)
+    scale = HEAD ** (-0.5)
+    low_scale = jnp.bfloat16(scale)
+    heads = own // HEAD
+    for head in range(heads):
+        pair = head * HEAD // LANES * LANES
+        inside = head % (LANES // HEAD)
+        lanes = pl.ds(pair, LANES)
+
+        def one(block, carry, head=head, pair=pair, inside=inside, lanes=lanes):
+            spot = pl.ds(pl.multiple_of(block * QUERIES, QUERIES), QUERIES)
+            queries = head_only(triple_ref[spot, lanes], inside)
+            back = head_only(grad_context[spot, lanes], inside)
+            scores = dot_of(triple_ref[:, pl.ds(own + pair, LANES)], queries * low_scale, 1, 1)
+            weights = jnp.exp(scores - logsum_ref[pl.ds(head, 1), spot])
+            grad_weights = dot_of(triple_ref[:, pl.ds(2 * own + pair, LANES)], back, 1, 1)
+            grad_values[:, lanes] += dot_of(weights.astype(jnp.bfloat16), back, 1, 0)
+            inner = jnp.sum(weights * grad_weights, axis=0, keepdims=True)
+            grad_low = (weights * (grad_weights - inner)).astype(jnp.bfloat16)
+            grad_keys[:, lanes] += dot_of(grad_low, queries, 1, 0)
+            grad_queries_t[pl.ds(head * HEAD, HEAD), spot] = dot_of(
+                keys_t[pl.ds(head * HEAD, HEAD), :], grad_low, 1, 0
+            )
+            return carry
+
+        lax.fori_loop(0, tokens // QUERIES, one, 0)
+        if head == max(heads - 2, 0):
+            gathers[0].step(1)
+    grad_triple[:, pl.ds(0, own)] = (grad_queries_t[...].T * scale).astype(jnp.bfloat16)
+    grad_triple[:, pl.ds(own, own)] = (grad_keys[...] * scale).astype(jnp.bfloat16)
+    grad_triple[:, pl.ds(2 * own, own)] = grad_values[...].astype(jnp.bfloat16)
+    mixed_partial, attend_out = grad_entry, branch.at[pl.ds(0, 4 * own), :]
+    mixed_partial[...] = dot_of(grad_triple[...], attend_ref[...], 1, 1)
+    narrow = NarrowSum(
+        far_bits, pieces, mixed_partial, grad_mixed_any, near, far, held, sends, arrivals, local, 0
+    )
+    narrow.start()
+    grad_attend = dot_of(grad_triple[...], mixed_ref[...], 0, 0)
+    grad_output = dot_of(context_ref[...], grad_branch[...], 0, 0)
+    blocks = lax.axis_size("wide")
+    first, second = 3 * own // blocks, own // blocks
+    for b in range(blocks):
+        start = b * (first + second)
+        attend_out[pl.ds(start, first), :] = grad_attend[b * first : (b + 1) * first]
+        attend_out[pl.ds(start + first, second), :] = grad_output[b * second : (b + 1) * second]
+    scatter = Scatter(
+        attend_out,
+        scatter_held,
+        scatter_beside,
+        scatter_inbox,
+        sends,
+        arrivals,
+        scatter_loads,
+        (len(far_bits) + 2) * pieces,
+    )
+    for p in range(pieces):
+        narrow.begin(p)
+    scatter.start()
+    left = list(reversed(range(blocks // 2)))
+    forwards = [(0, item) for item in gathers[0].order[2:]] + [
+        (1, item) for item in gathers[1].order[1:]
+    ]
+    urgent = [(1, 1)]
+    for b in range(len(far_bits)):
+        for p in range(pieces):
+            narrow.step(b, p)
+            if urgent:
+                index, item = urgent.pop(0)
+                gathers[index].step(item)
+            if len(left) > 1:
+                scatter.step(left.pop(0))
+    for index, item in forwards:
+        if (index, item) != (1, 1):
+            gathers[index].step(item)
+    while left:
+        scatter.step(left.pop(0))
+    out = pltpu.make_async_copy(scatter.held.at[0], attend_out_share, scatter.local.at[0])
+    out.start()
+    narrow.finish()
+    scatter.finish()
+    for gather in gathers:
+        gather.finish()
+    for keep in keeps:
+        keep.wait()
+    out.wait()
+
+
+def back(
+    hidden,
+    branch,
+    grad_entry,
+    cotangent,
+    live,
+    scale,
+    gate,
+    mixed,
+    attend_low,
+    output_weight,
+    triple,
+    context,
+    logsum,
+    reduce_share,
+    expand_share,
+    number,
+):
+    tokens, width = hidden.shape
+    own = output_weight.shape[0]
+    pieces = 4
+    line = lax.axis_size("wide") // 2
+    narrow_bits = bits_of(lax.axis_size("narrow"))
+    slots = (len(narrow_bits) + 1) * pieces + Scatter.slots() + 2 * (line - 1)
+    vmem = pl.BlockSpec(memory_space=pltpu.VMEM)
+    anywhere = pl.BlockSpec(memory_space=pl.ANY)
+    f32 = lambda *shape: jax.ShapeDtypeStruct(shape, jnp.float32)
+    wide = lambda *shape: pltpu.VMEM(shape, jnp.float32)
+    low = lambda *shape: pltpu.VMEM(shape, jnp.bfloat16)
+    return pl.pallas_call(
+        functools.partial(back_kernel, pieces),
+        out_shape=(
+            f32(tokens, width),
+            f32(1, width),
+            f32(1, width),
+            f32(1, width),
+            f32(tokens, width),
+            f32(4 * own // (2 * line), width),
+            f32(line * reduce_share.shape[0], width),
+            f32(line * expand_share.shape[0], width),
+        ),
+        in_specs=[anywhere] * 4 + [vmem] * 11,
+        out_specs=(vmem,) * 4 + (anywhere,) * 4,
+        scratch_shapes=[
+            wide(tokens, width),
+            wide(max(tokens, 4 * own), width),
+            wide(tokens, width),
+            low(tokens, width),
+            low(tokens, width),
+            low(own, width),
+            low(tokens, own),
+            low(own, tokens),
+            wide(own, tokens),
+            wide(tokens, own),
+            wide(tokens, own),
+            low(tokens, 3 * own),
+        ]
+        + narrow_scratch((tokens, width), pieces)
+        + scatter_scratch((4 * own, width))
+        + [
+            pltpu.SemaphoreType.DMA((4 * pieces,)),
+            pltpu.SemaphoreType.DMA((2,)),
+            pltpu.SemaphoreType.DMA((slots,)),
+            pltpu.SemaphoreType.DMA((slots,)),
         ],
-        axis=0,
+        compiler_params=pltpu.CompilerParams(
+            collective_id=number, has_side_effects=True, vmem_limit_bytes=60 * 2**20
+        ),
+        cost_estimate=pl.CostEstimate(
+            flops=40 * tokens * tokens * own,
+            bytes_accessed=150 * tokens * width,
+            transcendentals=tokens * tokens * own // HEAD,
+        ),
+    )(
+        hidden,
+        branch,
+        grad_entry,
+        cotangent,
+        live,
+        scale,
+        gate,
+        mixed,
+        attend_low,
+        output_weight,
+        triple,
+        context,
+        logsum,
+        reduce_share,
+        expand_share,
+    )
+
+
+def tail_kernel(
+    tokens_ref,
+    shift_ref,
+    scale_ref,
+    taps_ref,
+    grad_mixed_ref,
+    grad_hidden_ref,
+    hidden_ref,
+    ffn_half_ref,
+    ffn_across_ref,
+    cotangent_ref,
+    live_ref,
+    gate_ref,
+    rows_ref,
+    split_ref,
+    attend_out_ref,
+    reduce_ref,
+    expand_ref,
+    tokens_grad_ref,
+    block_out_ref,
+    small_ref,
+    norm_ref,
+    line_ref,
+    ffn,
+    normed_ref,
+    back_ref,
+    inverse_ref,
+    grad_taps,
+    grad_shift,
+    grad_scale,
+    slots,
+    spare,
+    spare_in,
+    keep_sems,
+    sends,
+    arrivals,
+):
+    width = tokens_ref.shape[1]
+    wide_bits = bits_of(lax.axis_size("wide"))
+    narrow_bits = bits_of(lax.axis_size("narrow"))
+    greet(
+        [place_at("wide", bit) for bit in wide_bits]
+        + [place_at("narrow", bit) for bit in narrow_bits]
+    )
+    _, z = wide_parts()
+    count = len(wide_bits)
+    hops = line_hops()
+
+    def spot_of(item):
+        spot = z
+        for index, (_, bit) in enumerate(hops):
+            if (item >> index) % 2:
+                spot = partner(spot, bit // 2)
+        return line_block(line_ref, spot)
+
+    gather = Gather(attend_out_ref, spot_of, hops, sends, arrivals, count + len(narrow_bits))
+    gather.step(0)
+    keep = pltpu.make_async_copy(attend_out_ref, spot_of(0), keep_sems.at[0])
+    keep.start()
+    core = lax.axis_index("narrow") % 2
+    half = ffn.shape[0] // 2
+    mine = pl.ds(pl.multiple_of(core * half, SLAB), half)
+    ffn[mine, :] = ffn_half_ref[...] + ffn_across_ref[...]
+    last = count + len(narrow_bits) + 2 ** len(hops) - 1
+    ffn_copy = send(ffn.at[mine, :], ffn.at[mine, :], sends, arrivals, last, place_at("narrow", 1))
+    mixer_kernel_backward(
+        tokens_ref,
+        shift_ref,
+        scale_ref,
+        taps_ref,
+        grad_mixed_ref,
+        grad_hidden_ref,
+        tokens_grad_ref,
+        grad_taps,
+        grad_shift,
+        grad_scale,
+        normed_ref,
+        back_ref,
+        inverse_ref,
+    )
+    ffn_copy.wait_recv()
+    gate, live = gate_ref[...], live_ref[...]
+
+    def leave(r, gates):
+        spot = slab_at(r)
+        branch = ffn[spot, :]
+        block_out_ref[spot, :] = (live * (hidden_ref[spot, :] + gate * branch)).astype(jnp.bfloat16)
+        return gates + fold_rows(branch * (cotangent_ref[spot, :].astype(jnp.float32) * live))
+
+    gates = lax.fori_loop(
+        0, ffn.shape[0] // SLAB, leave, jnp.zeros((8, width), jnp.float32), unroll=UNROLL
+    )
+    slots[0] = jnp.zeros(slots.shape[1:], jnp.float32)
+    slots[0, 0:1, :] = grad_shift[...]
+    slots[0, 1:2, :] = grad_scale[...]
+    slots[0, 2:5, :] = rows_ref[...]
+    slots[0, 5:6, :] = jnp.sum(gates, axis=0, keepdims=True)
+    shared_rows = 6 + taps_ref.shape[0]
+    slots[0, 6:shared_rows, :] = grad_taps[...]
+    split_rows = split_ref.shape[0]
+    slots[0, shared_rows : shared_rows + split_rows, :] = split_ref[...]
+    squares = jnp.zeros((8, width), jnp.float32)
+    for share in (attend_out_ref, reduce_ref, expand_ref):
+        squares = squares + fold_rows(share[...] * share[...])
+    end = shared_rows + split_rows
+    slots[0, end : end + 1, :] = jnp.sum(squares, axis=0, keepdims=True)
+    copies = []
+    for b in range(count):
+        copy = send(
+            slots.at[b], slots.at[count + 1 + b], sends, arrivals, b, place_at("wide", wide_bits[b])
+        )
+        copies.append(copy)
+        if b == 0:
+            gather.step(1)
+        copy.wait_recv()
+        slots[b + 1] = slots[b] + slots[count + 1 + b]
+    total = slots[count]
+    small_ref[...] = total
+    shared_part = total[:shared_rows]
+    split_part = total[shared_rows:end]
+    shared = jnp.sum(shared_part * shared_part)
+    split_sum = jnp.sum(split_part * split_part) + jnp.sum(total[end : end + 1])
+    spare[0] = jnp.full(spare.shape[1:], split_sum, jnp.float32)
+    for b in range(len(narrow_bits)):
+        copy = send(
+            spare.at[b], spare_in.at[b], sends, arrivals, count + b, place_at("narrow", narrow_bits[b])
+        )
+        copies.append(copy)
+        copy.wait_recv()
+        spare[b + 1] = spare[b] + spare_in[b]
+    norm_ref[...] = jnp.sqrt(spare[len(narrow_bits)] + shared)
+    for item in gather.order[2:]:
+        gather.step(item)
+    keep.wait()
+    gather.finish()
+    ffn_copy.wait_send()
+    for copy in copies:
+        copy.wait_send()
+
+
+def tail(
+    tokens,
+    shift,
+    scale,
+    taps,
+    grad_mixed,
+    grad_hidden,
+    hidden,
+    ffn_half,
+    ffn_across,
+    cotangent,
+    live,
+    gate,
+    table_rows,
+    split_rows,
+    shares,
+    number,
+):
+    rows, width = tokens.shape
+    wide_bits = bits_of(lax.axis_size("wide"))
+    narrow_bits = bits_of(lax.axis_size("narrow"))
+    count = len(wide_bits)
+    line = lax.axis_size("wide") // 2
+    total = count + len(narrow_bits) + line
+    small = -(-(6 + taps.shape[0] + split_rows.shape[0] + 1) // 8) * 8
+    vmem = pl.BlockSpec(memory_space=pltpu.VMEM)
+    anywhere = pl.BlockSpec(memory_space=pl.ANY)
+    f32 = lambda *shape: jax.ShapeDtypeStruct(shape, jnp.float32)
+    low = lambda *shape: jax.ShapeDtypeStruct(shape, jnp.bfloat16)
+    wide = lambda *shape: pltpu.VMEM(shape, jnp.float32)
+    return pl.pallas_call(
+        tail_kernel,
+        out_shape=(
+            low(rows, width),
+            low(rows, width),
+            f32(small, width),
+            f32(8, LANES),
+            f32(line * shares[0].shape[0], width),
+        ),
+        in_specs=[vmem] * 17,
+        out_specs=(vmem,) * 4 + (anywhere,),
+        scratch_shapes=[
+            wide(rows, width),
+            wide(rows, width),
+            wide(rows, width),
+            wide(rows, LANES),
+            wide(9, width),
+            wide(1, width),
+            wide(1, width),
+            wide(2 * count + 1, small, width),
+            wide(len(narrow_bits) + 1, 8, LANES),
+            wide(len(narrow_bits), 8, LANES),
+            pltpu.SemaphoreType.DMA((1,)),
+            pltpu.SemaphoreType.DMA((total,)),
+            pltpu.SemaphoreType.DMA((total,)),
+        ],
+        compiler_params=pltpu.CompilerParams(
+            collective_id=number, has_side_effects=True, vmem_limit_bytes=56 * 2**20
+        ),
+        cost_estimate=pl.CostEstimate(
+            flops=100 * rows * width, bytes_accessed=60 * rows * width, transcendentals=0
+        ),
+    )(
+        tokens,
+        shift,
+        scale,
+        taps,
+        grad_mixed,
+        grad_hidden,
+        hidden,
+        ffn_half,
+        ffn_across,
+        cotangent,
+        live,
+        gate,
+        table_rows,
+        split_rows,
+        *shares,
     )
 
 
@@ -1757,7 +2048,6 @@
     mixed_low = mixer_forward(flat_tokens, shift_one[0], scale_one[0], mixer_kernel)
     attend_flat = attend_weight.reshape(width, -1)
     triple, context, logsum, attend_low = attend(mixed_low, attend_flat)
-    output_low = output_weight.astype(jnp.bfloat16)
     output_rows, context = together(all_rows(output_weight), context)
     branch, hidden, entry_low = enter(
         context, flat_tokens, output_rows, gate_one[0], shift_two[0], scale_two[0], 1
@@ -1777,9 +2067,19 @@
     grad_entry, reduce_share, expand_share, ffn_half = together(
         grad_entry, reduce_share, expand_share, ffn_half
     )
-    reduce_pieces = line_gather(reduce_share)
-    ffn_across = permute(ffn_half, "narrow", 2)
-    grad_hidden, grad_branch_low, grad_shift_two, grad_scale_two, grad_gate_one = hidden_backward(
+    for bit in bits_of(lax.axis_size("narrow"))[1:-1]:
+        ffn_half = ffn_half + permute(ffn_half, "narrow", bit)
+    ffn_across = permute(ffn_half, "narrow", lax.axis_size("narrow") // 2)
+    (
+        grad_hidden,
+        grad_shift_two,
+        grad_scale_two,
+        grad_gate_one,
+        grad_mixed,
+        attend_out_share,
+        reduce_line,
+        expand_line,
+    ) = back(
         hidden,
         branch,
         grad_entry,
@@ -1787,88 +2087,62 @@
         live_row,
         scale_two[0],
         gate_one[0],
-    )
-    attend_out, mixed_partial = attend_back(
-        mixed_low, attend_low, output_low, triple, context, logsum, grad_branch_low
-    )
-    *reduce_pieces, ffn_across, mixed_partial = together(
-        *reduce_pieces, ffn_across, mixed_partial
-    )
-    ffn_half = ffn_half + ffn_across
-    for bit in bits_of(lax.axis_size("narrow"))[2:]:
-        ffn_half = ffn_half + permute(ffn_half, "narrow", bit)
-    reduce_line = line_place(reduce_share, reduce_pieces)
-    ffn_other = permute(ffn_half, "narrow", 1)
-    grad_mixed, attend_out_share = sum_scatter(mixed_partial, attend_out, 3)
-    ffn_other, grad_mixed, attend_out_share, reduce_line, expand_share = together(
-        ffn_other, grad_mixed, attend_out_share, reduce_line, expand_share
-    )
-    expand_pieces = line_gather(expand_share)
+        mixed_low,
+        attend_low,
+        output_weight,
+        triple,
+        context,
+        logsum,
+        reduce_share,
+        expand_share,
+        3,
+    )
+    ffn_across, grad_mixed, reduce_line, attend_out_share = together(
+        ffn_across, grad_mixed, reduce_line, attend_out_share
+    )
     reduce_other = permute(reduce_line, "wide", 1)
-    ffn_branch = core_place(ffn_half, ffn_other).reshape(tokens.shape)
-    block_out = (live_mask * (hidden[None] + gate_two * ffn_branch)).astype(jnp.bfloat16)
-    grad_result = cotangent.astype(jnp.float32) * live_mask
-    grad_gate_two = jnp.sum(ffn_branch * grad_result, axis=1)
-    tokens_gradient, grad_mixer_kernel, grad_shift_one, grad_scale_one = mixer_backward(
+    shared_rows = modulation_table.shape[0] + mixer_kernel.shape[0]
+    hidden_rows = -(-grad_hidden_kernel.size // width)
+    padding = hidden_rows * width - grad_hidden_kernel.size
+    hidden_flat = jnp.pad(grad_hidden_kernel.reshape(-1), (0, padding))
+    tokens_gradient, block_out, small, norm, attend_out_line = tail(
         flat_tokens,
         shift_one[0],
         scale_one[0],
         mixer_kernel,
         grad_mixed,
         grad_hidden,
+        hidden,
+        ffn_half,
+        ffn_across,
+        flat_cotangent,
+        live_row,
+        gate_two[0],
+        jnp.concatenate([grad_gate_one, grad_shift_two, grad_scale_two], axis=0),
+        hidden_flat.reshape(hidden_rows, width),
+        [attend_out_share, reduce_share, expand_share],
+        4,
     )
     tokens_gradient = tokens_gradient.reshape(tokens.shape)
-    grad_table = jnp.concatenate(
-        [
-            grad_shift_one,
-            grad_scale_one,
-            grad_gate_one,
-            grad_shift_two,
-            grad_scale_two,
-            grad_gate_two,
-        ],
-        axis=0,
-    )
-    shares = [attend_out_share, expand_share, reduce_share]
-    squares = sum(
-        jnp.sum((share * share).reshape(-1, width), axis=0) for share in shares
-    )
-    shared_rows = grad_table.shape[0] + grad_mixer_kernel.shape[0]
-    hidden_rows = -(-grad_hidden_kernel.size // width)
-    padding = hidden_rows * width - grad_hidden_kernel.size
-    hidden_flat = jnp.pad(grad_hidden_kernel.reshape(-1), (0, padding))
-    stacked = jnp.concatenate(
-        [grad_table, grad_mixer_kernel, hidden_flat.reshape(hidden_rows, width), squares[None]],
-        axis=0,
-    )
-    stacked = jnp.pad(stacked, ((0, -stacked.shape[0] % 8), (0, 0)))
-    small, norm, attend_out_line = small_sums(
-        stacked, attend_out_share, shared_rows, hidden_rows, 4
-    )
-    summed_table = small[: grad_table.shape[0]]
-    summed_mixer = small[grad_table.shape[0] : shared_rows]
+    block_out = block_out.reshape(tokens.shape)
+    summed_table = small[: modulation_table.shape[0]]
+    summed_mixer = small[modulation_table.shape[0] : shared_rows]
     summed_hidden = small[shared_rows : shared_rows + hidden_rows].reshape(-1)
     summed_hidden = summed_hidden[: hidden_kernel.size].reshape(hidden_kernel.shape)
-    *expand_pieces, norm = together(*expand_pieces, norm)
     gradient_norm = norm[0, 0]
     clip_factor = jnp.minimum(1.0, 1.0 / (gradient_norm + 1e-06))
-    expand_line = line_place(expand_share, expand_pieces)
-    attend_line, output_line = part(attend_out_line, output_weight.shape[0])
     attend_moment_flat = attend_moment.reshape(width, -1)
-    blend = lambda moment, gradient: muon_momentum * moment + clip_factor * gradient
-    halves = [
-        blend(own_half(attend_moment_flat, 1).T, attend_line),
-        blend(own_half(output_moment, 0), output_line),
-        blend(own_half(expand_moment, 1).T, expand_line),
-        blend(own_half(reduce_moment, 0), reduce_line),
-    ]
-    bands = jnp.stack([gram_band(matrix) for matrix in halves])
-    sub = lax.axis_size("narrow") // MATRICES
-    gramian = gram_whole(bands.reshape(MATRICES * sub, -1, bands.shape[2]), 5)
+    attend_half = own_half(attend_moment_flat, 1).T
+    gramian = gram_whole(
+        norm,
+        [attend_out_line, expand_line, reduce_line],
+        [attend_half, output_moment, expand_moment, reduce_moment],
+        5,
+    )
     gramian, expand_line, attend_out_line = together(gramian, expand_line, attend_out_line)
     expand_other = permute(expand_line, "wide", 1)
     attend_out_other = permute(attend_out_line, "wide", 1)
-    factor = polar_factor(gramian)
+    factor = spread(polar_factor(gramian), 6)
     factor, expand_other, attend_out_other, reduce_other = together(
         factor, expand_other, attend_out_other, reduce_other
     )
@@ -1879,7 +2153,6 @@
         [attend_out_other, expand_other, reduce_other],
         [attend_moment_flat, output_moment, expand_moment, reduce_moment],
         [attend_flat, output_weight, expand_weight, reduce_weight],
-        6,
     )
     attend_carried = carried[0].reshape(attend_weight.shape)
     attend_result = results[0].reshape(attend_weight.shape)

time: 705 us -> 627 us (0.89)
  the two profiles are of different devices: /device:TPU:13 before, /device:TPU:0 now
where the time goes in v6:
time: 627 us; the launch traced here: 619 us
  Pallas kernels  566 us (90%)
  local copies, waits for them, and re-layouts  39 us (6%)
  starting transfers between devices  8.26 us (1%)
    pallas_call x1, Pallas kernels, middle(): pl.pallas_call(functools.partial(middle_kernel, pieces), out_shape=(f32(t...  116 us
    pallas_call x1, Pallas kernels, back(): pl.pallas_call(functools.partial(back_kernel, pieces), out_shape=(f32(tok...  111 us
    pallas_call x1, Pallas kernels, polar_factor(): pl.pallas_call(polar_kernel, out_shape=jax.ShapeDtypeStruct(gramian.shape...  73.9 us
    pallas_call x1, Pallas kernels, gram_whole(): pl.pallas_call(gram_kernel, out_shape=jax.ShapeDtypeStruct((size, band),...  68.5 us
    pallas_call x1, Pallas kernels, tail(): pl.pallas_call(tail_kernel, out_shape=(low(rows, width), low(rows, width)...  63.2 us
    pallas_call x1, Pallas kernels, finish(): pl.pallas_call(finish_kernel, out_shape=tuple(shapes + shapes), in_specs=...  45.1 us
    pallas_call x1, Pallas kernels, spread(): pl.pallas_call(functools.partial(spread_kernel, sub, pieces), out_shape=j...  42 us
    pallas_call x1, Pallas kernels, enter(): pl.pallas_call(functools.partial(entry_kernel, pieces), out_shape=(jax.Sh...  28.6 us
  transfers between devices with their start and end apart: 5, of which 0 were waited for; matrix products, arithmetic and copies ran while one was open for 3% of the time, Pallas kernels for 61%

profile of v6, /device:TPU:0, one launch (start us, length us, event | category | flops | bytes accessed | tf_op | source)
XLA Modules:
  0.0 619.3 jit_solution(13810049791963726233)
XLA Ops:
  0.7 3.0 collective-permute-start
  3.7 3.5 copy.48
  7.2 3.7 copy.49.attend_ref.refs_10_
  11.8 0.6 slice_bitcast_fusion
  12.4 7.4 %shard_map.356.mixed_ref = bf16[1024,1024]{1,0:T(8,128)(2,1)S(1)} custom-call(bf16[1024,1024]{1,0:T(8,128)(2,1)S(1)} %bitcast.27, f32[1,1024]{1,0:T(1,128)S(1)} %get-tuple-element.177.shift_ref, f32[1,1024]{1,0:T(1,128)S(1)} %get-tuple-element.176.scale_ref, f32[9,1024]{1,0:T(8,128)S(1)} %copy-done.6), custom_call_target="tpu_custom_call" | custom-call | flops 41943040 | bytes 4194304 | tf_op jit(solution)/shard_map/pallas_call | solution.py:1202
  19.8 0.0 copy-start.4
  19.8 0.0 copy-start.22
  19.9 10.7 %shard_map.357 = (bf16[1024,768]{1,0:T(8,128)(2,1)S(1)}, bf16[1024,256]{1,0:T(8,128)(2,1)S(1)}, f32[8,1024]{1,0:T(8,128)S(1)}, bf16[1024,768]{1,0:T(8,128)(2,1)S(1)}) custom-call(bf16[1024,1024]{1,0:T(8,128)(2,1)S(1)} %shard_map.356.mixed_ref, f32[1024,768]{1,0:T(8,128)S(1)} %copy-done.1), custom_call_target="tpu_custom_call" | custom-call | flops 4294967296 | bytes 12582912 | tf_op jit(solution)/shard_map/pallas_call | solution.py:1331
  30.5 0.0 copy-start.16
  30.6 0.0 copy-start.18
  30.6 0.2 maximum_select_fusion.output_ref
  30.8 0.9 copy-done.16
  31.7 0.5 copy-done.17
  32.2 28.6 %shard_map.358 = (f32[1024,1024]{1,0:T(8,128)S(1)}, f32[1024,1024]{1,0:T(8,128)}, bf16[1024,1024]{1,0:T(8,128)(2,1)S(1)}) custom-call(bf16[1024,256]{1,0:T(8,128)(2,1)S(1)} %get-tuple-element.71.context_ref, bf16[1024,1024]{1,0:T(8,128)(2,1)S(1)} %bitcast.28, f32[512,1024]{1,0:T(8,128)S(1)} %maximum_select_fusion.output_ref, ...), custom_call_target="tpu_custom_call" | custom-call | flops 2147483648 | bytes 104857600 | tf_op jit(solution)/shard_map/pallas_call | solution.py:1445
  60.8 0.0 copy-start.13
  60.8 2.0 copy-done.13
  62.8 1.3 copy-done.14
  64.1 0.6 broadcast_in_dim.12.live_ref
  64.7 115.6 %shard_map.359 = (f32[512,1024]{1,0:T(8,128)}, f32[1024,1024]{1,0:T(8,128)}, f32[128,1024]{1,0:T(8,128)}, f32[128,1024]{1,0:T(8,128)}, f32[9,1024]{1,0:T(8,128)}) custom-call(bf16[1024,1024]{1,0:T(8,128)(2,1)} %copy-done.14, bf16[1024,1024]{1,0:T(8,128)(2,1)} %bitcast.36, f32[1,1024]{1,0:T(1,128)} %broadcast_in_dim.12.live_ref, ...), custom_call_target="tpu_custom_call" | custom-call | flops 12884901888 | bytes 209715200 | tf_op jit(solution)/shard_map/pallas_call | solution.py:1119
  180.4 1.6 collective-permute-start.1
  182.0 2.4 copy.50
  184.4 2.7 copy.51.refs_6_
  187.1 1.6 dynamic-slice_bitcast_fusion.attend_moment_any
  188.7 111.0 %shard_map.360 = (f32[1024,1024]{1,0:T(8,128)}, f32[1,1024]{1,0:T(1,128)}, f32[1,1024]{1,0:T(1,128)}, f32[1,1024]{1,0:T(1,128)}, f32[1024,1024]{1,0:T(8,128)}, /...) custom-call(f32[1024,1024]{1,0:T(8,128)} %get-tuple-element.79.hidden_any.hidden_ref, ...), custom_call_target="tpu_custom_call" | custom-call | flops 10737418240 | bytes 157286400 | tf_op jit(solution)/shard_map/pallas_call | solution.py:1731
  299.7 1.3 pad_maximum_fusion.rows_ref
  301.0 1.5 collective-permute-start.4
  302.5 63.2 %shard_map.361 = (bf16[1024,1024]{1,0:T(8,128)(2,1)}, bf16[1024,1024]{1,0:T(8,128)(2,1)}, f32[32,1024]{1,0:T(8,128)}, f32[8,128]{1,0:T(8,128)}, f32[512,1024]{1,0:T(8,128)}) custom-call(bf16[1024,1024]{1,0:T(8,128)(2,1)} %bitcast.26, f32[1,1024]{1,0:T(1,128)} %copy-done.9, f32[1,1024]{1,0:T(1,128)} %copy-done.8, f32[9,1024]{1,0:T(8,128)} %taps_ref.5, ...), custom_call_target="tpu_custom_call" | custom-call | flops 104857600 | bytes 62914560 | tf_op jit(solution)/shard_map/pallas_call | solution.py:1964
  365.7 0.7 copy-done.12
  366.4 68.5 %shard_map.362.g_ref = f32[1024,640]{1,0:T(8,128)} custom-call(f32[8,128]{1,0:T(8,128)S(1)} %copy-done.12, f32[512,1024]{1,0:T(8,128)} %get-tuple-element.106.attend_out_any.refs_0_, f32[512,1024]{1,0:T(8,128)} %get-tuple-element.105.expand_any.refs_2_, f32[512,1024]{1,0:T(8,128)} %get-tuple-element.103.reduce_any.refs_4_, ...), custom_call_target="tpu_custom_call" | custom-call | flops 3221225472 | bytes 83886080 | tf_op jit(solution)/shard_map/pallas_call | solution.py:503
  434.9 1.0 collective-permute-start.2
  435.9 1.1 collective-permute-start.3
  437.0 1.7 copy-done.3
  438.7 73.9 %shard_map.363.q_ref = f32[1024,640]{1,0:T(8,128)S(1)} custom-call(f32[1024,640]{1,0:T(8,128)S(1)} %copy-done.3), custom_call_target="tpu_custom_call" | custom-call | flops 109521666048 | bytes 8388608 | tf_op jit(solution)/shard_map/pallas_call | solution.py:620
  512.7 1.5 copy-done.2
  514.2 1.2 slice.36
  515.4 0.0 copy-start.7
  515.4 0.0 copy-start.28
  515.4 0.0 copy-start.29
  515.4 42.0 %shard_map.364.bands_any = f32[4,1024,640]{2,1,0:T(8,128)} custom-call(f32[1024,640]{1,0:T(8,128)} %copy-done.2), custom_call_target="tpu_custom_call" | custom-call | tf_op jit(solution)/shard_map/pallas_call | solution.py:686
  558.2 0.7 divide_subtract_fusion.2
  558.9 0.8 divide_subtract_fusion
  559.7 45.1 %shard_map.365 = (f32[1024,768]{1,0:T(8,128)}, f32[256,1024]{1,0:T(8,128)}, f32[1024,1024]{1,0:T(8,128)}, f32[1024,1024]{1,0:T(8,128)}, f32[1024,768]{1,0:T(8,12...) custom-call(f32[8,128]{1,0:T(8,128)} %get-tuple-element.100.norm_ref, ...), custom_call_target="tpu_custom_call" | custom-call | flops 19327352832 | bytes 83886080 | tf_op jit(solution)/shard_map/pallas_call | solution.py:819
  604.8 2.4 copy.53
  607.2 2.4 copy.55
  609.5 2.4 copy.54
  611.9 2.4 copy.56
  614.3 3.2 copy.61
  617.5 1.3 copy.62
  (59 shorter events, 0.1 us)
Async XLA Ops:
  0.7 29.9 %collective-permute-start = (f32[256,1024]{1,0:T(8,128)}, f32[256,1024]{1,0:T(8,128)S(1)}, u32[]{:S(2)}, u32[]{:S(2)}) collective-permute-start(f32[256,1024]{1,0:T(8,128)} %refs_11_.1), channel_id=1, source_target_pairs={{0,2},{1,3},{2,0},{3,1},{4,6},{5,7},{6,4},{7,5},{8,10},{9,11},{10,... | collective-permute-start | bytes 3145736 | tf_op jit(solution)/shard_map/ppermute | solution.py:81
  7.2 4.5 copy-start.24
  7.2 4.5 copy-start.33
  7.2 5.2 copy-start
  7.2 5.2 copy-start.6
  10.9 8.9 %copy-start.1 = (f32[1024,768]{1,0:T(8,128)S(1)}, f32[1024,768]{1,0:T(8,128)}, u32[]{:S(2)}) copy-start(f32[1024,768]{1,0:T(8,128)} %copy.49.attend_ref.refs_10_) | copy-start | bytes 9437188
  12.4 18.2 %copy-start.8 = (f32[1,1024]{1,0:T(1,128)}, f32[1,1024]{1,0:T(1,128)S(1)}, u32[]{:S(2)}) copy-start(f32[1,1024]{1,0:T(1,128)S(1)} %get-tuple-element.176.scale_ref) | copy-start | bytes 12292
  12.4 18.2 %copy-start.9 = (f32[1,1024]{1,0:T(1,128)}, f32[1,1024]{1,0:T(1,128)S(1)}, u32[]{:S(2)}) copy-start(f32[1,1024]{1,0:T(1,128)S(1)} %get-tuple-element.177.shift_ref) | copy-start | bytes 12292
  12.4 19.8 %copy-start.10 = (f32[1,1024]{1,0:T(1,128)}, f32[1,1024]{1,0:T(1,128)S(1)}, u32[]{:S(2)}) copy-start(f32[1,1024]{1,0:T(1,128)S(1)} %get-tuple-element.173.scale_ref) | copy-start | bytes 12292
  12.4 19.8 %copy-start.11 = (f32[1,1024]{1,0:T(1,128)}, f32[1,1024]{1,0:T(1,128)S(1)}, u32[]{:S(2)}) copy-start(f32[1,1024]{1,0:T(1,128)S(1)} %get-tuple-element.175.gate_ref) | copy-start | bytes 12292
  19.8 10.7 %copy-start.4 = (bf16[1024,1024]{1,0:T(8,128)(2,1)}, bf16[1024,1024]{1,0:T(8,128)(2,1)S(1)}, u32[]{:S(2)}) copy-start(bf16[1024,1024]{1,0:T(8,128)(2,1)S(1)} %shard_map.356.mixed_ref) | copy-start | bytes 6291460
  19.8 10.8 %copy-start.22 = (f32[256,1024]{1,0:T(8,128)S(1)}, f32[256,1024]{1,0:T(8,128)}, u32[]{:S(2)}) copy-start(f32[256,1024]{1,0:T(8,128)} %refs_11_.1) | copy-start | bytes 3145732
  30.5 1.1 copy-start.16
  30.6 1.7 copy-start.17
  30.6 30.2 %copy-start.15 = (bf16[1024,256]{1,0:T(8,128)(2,1)}, bf16[1024,256]{1,0:T(8,128)(2,1)S(1)}, u32[]{:S(2)}) copy-start(bf16[1024,256]{1,0:T(8,128)(2,1)S(1)} %get-tuple-element.71.context_ref) | copy-start | bytes 1572868
  30.6 30.2 %copy-start.18 = (f32[8,1024]{1,0:T(8,128)}, f32[8,1024]{1,0:T(8,128)S(1)}, u32[]{:S(2)}) copy-start(f32[8,1024]{1,0:T(8,128)S(1)} %get-tuple-element.84.logsum_ref) | copy-start | bytes 98308
  60.8 2.0 copy-start.13
  62.8 1.3 copy-start.14
  180.4 120.6 %collective-permute-start.1 = (f32[512,1024]{1,0:T(8,128)}, f32[512,1024]{1,0:T(8,128)}, u32[]{:S(2)}, u32[]{:S(2)}) collective-permute-start(f32[512,1024]{1,0:T(8,128)} %get-tuple-element.78.ffn_half_ref), channel_id=1, source_target_pairs={{0,2},{1,3},{2,0},{3,1},{4,6},{5,7},{6,4},{7,5},{8,10},{9,11},{10,... | collective-permute-start | bytes 6291464 | tf_op jit(solution)/shard_map/ppermute | solution.py:81
  184.4 2.7 copy-start.19
  301.0 258.7 %collective-permute-start.4 = (f32[512,1024]{1,0:T(8,128)}, f32[512,1024]{1,0:T(8,128)}, u32[]{:S(2)}, u32[]{:S(2)}) collective-permute-start(f32[512,1024]{1,0:T(8,128)} %get-tuple-element.103.reduce_any.refs_4_), channel_id=1, source_target_pairs={{0,4},{4,0},{8,12},{12,8},{16,20},{20,16},{24,28},{28,24},{1,5},{5... | collective-permute-start | bytes 6291464 | tf_op jit(solution)/shard_map/ppermute | solution.py:81
  302.5 63.2 %copy-start.5 = (f32[256,1024]{1,0:T(8,128)S(1)}, f32[256,1024]{1,0:T(8,128)}, u32[]{:S(2)}) copy-start(f32[256,1024]{1,0:T(8,128)} %refs_7_.1) | copy-start | bytes 3145732
  365.7 0.7 copy-start.12
  366.4 68.5 %copy-start.21 = (f32[512,1024]{1,0:T(8,128)S(1)}, f32[512,1024]{1,0:T(8,128)}, u32[]{:S(2)}) copy-start(f32[512,1024]{1,0:T(8,128)} %get-tuple-element.105.expand_any.refs_2_) | copy-start | bytes 6291460
  434.9 124.8 %collective-permute-start.2 = (f32[512,1024]{1,0:T(8,128)S(1)}, f32[512,1024]{1,0:T(8,128)}, u32[]{:S(2)}, u32[]{:S(2)}) collective-permute-start(f32[512,1024]{1,0:T(8,128)S(1)} %copy-done.21), channel_id=1, source_target_pairs={{0,4},{4,0},{8,12},{12,8},{16,20},{20,16},{24,28},{28,24},{1,5},{5... | collective-permute-start | bytes 6291464 | tf_op jit(solution)/shard_map/ppermute | solution.py:81
  435.9 123.7 %collective-permute-start.3 = (f32[512,1024]{1,0:T(8,128)}, f32[512,1024]{1,0:T(8,128)}, u32[]{:S(2)}, u32[]{:S(2)}) collective-permute-start(f32[512,1024]{1,0:T(8,128)} %get-tuple-element.106.attend_out_any.refs_0_), channel_id=1, source_target_pairs={{0,4},{4,0},{8,12},{12,8},{16,20},{20,16},{24,28},{28,24},{1,5},{5... | collective-permute-start | bytes 6291464 | tf_op jit(solution)/shard_map/ppermute | solution.py:81
  437.0 1.7 copy-start.3
  512.7 1.5 copy-start.2
  515.4 42.8 %copy-start.23 = (f32[32,1024]{1,0:T(8,128)S(1)}, f32[32,1024]{1,0:T(8,128)}, u32[]{:S(2)}) copy-start(f32[32,1024]{1,0:T(8,128)} %get-tuple-element.119) | copy-start | bytes 393220
  515.4 42.8 %copy-start.25 = (f32[6,1024]{1,0:T(8,128)S(1)}, f32[6,1024]{1,0:T(8,128)}, u32[]{:S(2)}) copy-start(f32[6,1024]{1,0:T(8,128)} %param.25) | copy-start | bytes 73732
  515.4 42.8 %copy-start.31 = (f32[6,1024]{1,0:T(8,128)S(1)}, f32[6,1024]{1,0:T(8,128)}, u32[]{:S(2)}) copy-start(f32[6,1024]{1,0:T(8,128)} %param.37) | copy-start | bytes 73732
  515.4 42.8 %copy-start.32 = (f32[6,1024]{1,0:T(8,128)S(1)}, f32[6,1024]{1,0:T(8,128)}, u32[]{:S(2)}) copy-start(f32[6,1024]{1,0:T(8,128)} %param.36) | copy-start | bytes 73732
  515.4 43.5 %copy-start.7 = (f32[9,1024]{1,0:T(8,128)S(1)}, f32[9,1024]{1,0:T(8,128)}, u32[]{:S(2)}) copy-start(f32[9,1024]{1,0:T(8,128)} %taps_ref.5) | copy-start | bytes 110596
  515.4 43.4 %copy-start.26 = (f32[9,1024]{1,0:T(8,128)S(1)}, f32[9,1024]{1,0:T(8,128)}, u32[]{:S(2)}) copy-start(f32[9,1024]{1,0:T(8,128)} %taps_ref.4) | copy-start | bytes 110596
  515.4 43.4 %copy-start.27 = (f32[9,1024]{1,0:T(8,128)S(1)}, f32[9,1024]{1,0:T(8,128)}, u32[]{:S(2)}) copy-start(f32[9,1024]{1,0:T(8,128)} %param.41) | copy-start | bytes 110596
  515.4 43.4 %copy-start.28 = (f32[9,1024]{1,0:T(8,128)S(1)}, f32[9,1024]{1,0:T(8,128)}, u32[]{:S(2)}) copy-start(f32[9,1024]{1,0:T(8,128)} %param.40) | copy-start | bytes 110596
  515.4 43.4 %copy-start.29 = (f32[9,1024]{1,0:T(8,128)S(1)}, f32[9,1024]{1,0:T(8,128)}, u32[]{:S(2)}) copy-start(f32[9,1024]{1,0:T(8,128)} %param.39) | copy-start | bytes 110596
  515.4 43.4 %copy-start.30 = (f32[9,1024]{1,0:T(8,128)S(1)}, f32[9,1024]{1,0:T(8,128)}, u32[]{:S(2)}) copy-start(f32[9,1024]{1,0:T(8,128)} %param.38) | copy-start | bytes 110596
  614.3 3.2 copy-start.20

commit v7 on v6

--- a/solution.py
+++ b/solution.py
@@ -85,12 +85,6 @@
     return lax.optimization_barrier(values)
 
 
-def own_half(values, axis):
-    extent = values.shape[axis] // 2
-    side = lax.axis_index("wide") % 2
-    return lax.dynamic_slice_in_dim(values, side * extent, extent, axis)
-
-
 def wide_parts():
     w = lax.axis_index("wide")
     return w % 2, w // 2
@@ -119,10 +113,11 @@
 
 
 class Scatter:
-    def __init__(self, src, held, beside, inbox, sends, arrivals, local, base):
+    def __init__(self, src, held, beside, inbox, sends, arrivals, local, base, blocks=None):
         self.src, self.held, self.beside, self.inbox = src, held, beside, inbox
+        self.blocks = blocks
         self.sends, self.arrivals, self.local, self.base = sends, arrivals, local, base
-        self.count = lax.axis_size("wide") // 2
+        self.count = lax.axis_size("wide") // 2 if blocks is None else blocks[0].shape[0]
         self.copies = {}
         self.loads = {}
 
@@ -133,15 +128,14 @@
     def load(self):
         y, z = wide_parts()
         for e in reversed(range(self.count)):
-            self.loads[e] = pltpu.make_async_copy(
-                block_of(self.src, y, line_partner(z, e)), self.held.at[e], self.local.at[e]
-            )
+            own = self.blocks[0].at[e] if self.blocks else block_of(self.src, y, line_partner(z, e))
+            self.loads[e] = pltpu.make_async_copy(own, self.held.at[e], self.local.at[e])
             self.loads[e].start()
 
     def give(self, e):
         y, z = wide_parts()
         self.copies[("y", e)] = send(
-            block_of(self.src, 1 - y, line_partner(z, e)),
+            self.blocks[1].at[e] if self.blocks else block_of(self.src, 1 - y, line_partner(z, e)),
             self.beside.at[e],
             self.sends,
             self.arrivals,
@@ -313,6 +307,7 @@
     expand_moment_any,
     reduce_moment_any,
     band_ref,
+    expand_beside,
     attend_out,
     expand,
     reduce,
@@ -323,6 +318,7 @@
     *refs,
 ):
     highs, lows, refs = refs[:MATRICES], refs[MATRICES : 2 * MATRICES], refs[2 * MATRICES :]
+    attend_turned, attend_blend, refs = refs[0], refs[1], refs[2:]
     twice, halves, inbox, block, load_sems, sends, arrivals, local = refs
     narrow_bits = bits_of(lax.axis_size("narrow"))
     wide_bits = bits_of(lax.axis_size("wide"))
@@ -337,6 +333,15 @@
         [place_at("narrow", bit) for bit in narrow_bits]
         + [place_at("wide", bit) for bit in wide_bits]
     )
+    early = expand_beside.shape[0]
+    expand_copy = send(
+        expand_any.at[pl.ds(0, early), :],
+        expand_beside,
+        sends,
+        arrivals,
+        sends.shape[0] - 1,
+        place_at("wide", 1),
+    )
     own_rows = lambda ref: ref.at[
         pl.ds(pl.multiple_of(y * (ref.shape[0] // 2), 8), ref.shape[0] // 2), :
     ]
@@ -344,15 +349,23 @@
         :, pl.ds(pl.multiple_of(y * (ref.shape[1] // 2), LANES), ref.shape[1] // 2)
     ]
     loads = []
+    own = attend_moment_any.shape[2]
+    for j in range(3):
+        pltpu.make_async_copy(
+            attend_moment_any.at[j], attend_moment.at[:, pl.ds(j * own, own)], load_sems.at[1]
+        ).start()
     for src, dst in (
         (attend_out_any, attend_out),
-        (attend_moment_any, attend_moment),
+        (None, None),
         (own_rows(output_moment_any), output_moment),
         (expand_any, expand),
         (own_columns(expand_moment_any), expand_moment),
         (reduce_any, reduce),
         (own_rows(reduce_moment_any), reduce_moment),
     ):
+        if src is None:
+            loads.append(pltpu.make_async_copy(attend_moment, attend_moment, load_sems.at[1]))
+            continue
         loads.append(pltpu.make_async_copy(src, dst, load_sems.at[len(loads)]))
         loads[-1].start()
     clip = jnp.minimum(1.0, 1.0 / (norm_ref[0:1, 0:1] + 1e-06))
@@ -393,16 +406,19 @@
     loads[0].wait()
     loads[1].wait()
     loads[2].wait()
+    for at in range(0, 3 * own, LANES):
+        attend_turned[pl.ds(at, LANES), :] = attend_moment[:, pl.ds(at, LANES)].T
+    offset = y * (3 * own // 2)
     for b in range(lines):
-        for moment, gradient_at, extent in (
-            (attend_moment, b * share, first_rows),
-            (output_moment, b * share + first_rows, second_rows),
-        ):
-            spot = pl.ds(b * extent, extent)
-            moment[spot, :] = (
-                muon_momentum * moment[spot, :]
-                + clip * attend_out[gradient_at : gradient_at + extent, :]
-            )
+        gradient = attend_out[b * share : (b + 1) * share, :]
+        spot = pl.ds(pl.multiple_of(offset + b * first_rows, 8), first_rows)
+        attend_blend[pl.ds(b * first_rows, first_rows), :] = (
+            muon_momentum * attend_turned[spot, :] + clip * gradient[:first_rows]
+        )
+        spot = pl.ds(b * second_rows, second_rows)
+        output_moment[spot, :] = (
+            muon_momentum * output_moment[spot, :] + clip * gradient[first_rows:]
+        )
 
     def cut(k, values):
         def one(i, carry):
@@ -412,7 +428,7 @@
 
         lax.fori_loop(0, highs[k].shape[0] // SLAB, one, 0, unroll=UNROLL)
 
-    cut(0, attend_moment)
+    cut(0, attend_blend)
     multiply(0)
     cut(1, output_moment)
     multiply(1)
@@ -480,6 +496,7 @@
         gather.step(item)
     keep.wait()
     gather.finish()
+    expand_copy.wait()
     for copy in copies:
         copy.wait_send()
 
@@ -496,26 +513,31 @@
     line_rows = [lines[0].shape[0] * 3 // 4, lines[0].shape[0] // 4]
     line_rows += [lines[1].shape[0], lines[2].shape[0]]
     gathers = len(bits_of(sub)) + len(wide_bits)
-    slots = parts + 2 + 2**gathers
+    slots = parts + 3 + 2**gathers
     vmem = pl.BlockSpec(memory_space=pltpu.VMEM)
     anywhere = pl.BlockSpec(memory_space=pl.ANY)
     wide = lambda *shape: pltpu.VMEM(shape, jnp.float32)
     return pl.pallas_call(
         gram_kernel,
-        out_shape=jax.ShapeDtypeStruct((size, band), jnp.float32),
+        out_shape=(
+            jax.ShapeDtypeStruct((size, band), jnp.float32),
+            jax.ShapeDtypeStruct((lines[1].shape[0] // 2, size), jnp.float32),
+        ),
         in_specs=[vmem] + [anywhere] * 7,
-        out_specs=anywhere,
+        out_specs=(anywhere, anywhere),
         scratch_shapes=[
             wide(*lines[0].shape),
             wide(*lines[1].shape),
             wide(*lines[2].shape),
-            wide(line_rows[0], size),
+            wide(size, 2 * line_rows[0]),
             wide(line_rows[1], size),
             wide(size, line_rows[2]),
             wide(line_rows[3], size),
         ]
         + [pltpu.VMEM((rows, size), jnp.bfloat16) for rows in line_rows] * 2
         + [
+            wide(2 * line_rows[0], size),
+            wide(line_rows[0], size),
             wide(count, size + band),
             wide(*halves),
             wide(*halves),
@@ -631,12 +653,72 @@
     )(gramian)
 
 
-def spread_kernel(sub, pieces, q_ref, o_ref, sends, arrivals, local):
-    half = q_ref.shape[0] // 2
+class Matrices:
+    def __init__(self, own):
+        self.own = own
+
+    def move(self, outer, inner, sem, k, inward, rows=slice(None), columns=slice(None)):
+        if k:
+            pairs = [(outer.at[rows, columns], inner.at[rows, columns])]
+        else:
+            pairs = [
+                (outer.at[j, rows], inner.at[rows, pl.ds(j * self.own, self.own)]) for j in range(3)
+            ]
+        for there, here in pairs:
+            src, dst = (there, here) if inward else (here, there)
+            pltpu.make_async_copy(src, dst, sem).start()
+
+
+def whole_of(ref, sem):
+    return pltpu.make_async_copy(ref, ref, sem)
+
+
+def assemble(band, factor_high, factor_low):
+    count = factor_high.shape[0] // LANES
+    lanes = lambda block: pl.ds((block % count) * LANES, LANES)
+    for i in range(count):
+        for j in range(count // 2 + 1):
+            part = band[lanes(i), lanes(j)]
+            spot = (lanes(i), lanes(i + j))
+            factor_high[spot], factor_low[spot] = split(part)
+            if 0 < j < count // 2:
+                spot = (lanes(i + j), lanes(i))
+                factor_high[spot], factor_low[spot] = split(part.T)
+
+
+def update(k, start, factor_high, factor_low, high, low, value):
+    spot = pl.ds(pl.multiple_of(start, BLK), BLK)
+    q_high, q_low = factor_high[spot, :], factor_low[spot, :]
+    if k in COLUMNS:
+        polar = dot_of(q_high, high[...], 1, 0) + (
+            dot_of(q_high, low[...], 1, 0) + dot_of(q_low, high[...], 1, 0)
+        )
+        where = (spot, slice(None))
+    else:
+        polar = dot_of(high[...], q_high, 1, 1) + (
+            dot_of(low[...], q_high, 1, 1) + dot_of(high[...], q_low, 1, 1)
+        )
+        where = (slice(None), spot)
+    scale = muon_rate * 0.2 * math.sqrt((3 * D, D, FF, FF)[k])
+    value[where] = value[where] * (1.0 - muon_rate * weight_decay) - scale * polar
+    return where
+
+
+def spread_kernel(sub, pieces, norm_ref, q_ref, *refs):
+    lines, others, refs = refs[:3], refs[3:7], refs[7:]
+    moments, weights, refs = refs[:4], refs[4:8], refs[8:]
+    o_ref, carried, fresh, high_outs, low_outs = refs[0], refs[1:5], refs[5:9], refs[9:13], refs[13:17]
+    refs = refs[17:]
+    pair_bands, factor_high, factor_low = refs[:3]
+    staged, values, highs, lows = refs[3:7], refs[7:11], refs[11:15], refs[15:19]
+    load_sems, value_sems, out_sems, split_sems, band_sems, sends, arrivals = refs[19:]
+    size = q_ref.shape[0]
+    half = size // 2
     step = half // pieces
     w, n = lax.axis_index("wide"), lax.axis_index("narrow")
     own = n // sub
-    across = partner(own, 2)
+    across, near = partner(own, 2), partner(own, 1)
+    far = own // 2
     near_place, far_place = place_at("narrow", sub), place_at("narrow", 2 * sub)
     side_place = place_at("wide", 1)
     greet([near_place, far_place, side_place])
@@ -652,70 +734,26 @@
         push(q_ref.at[rows(y, p)], o_ref.at[own, rows(y, p)], far_place) for p in range(pieces)
     ]
     landing = [push(q_ref, o_ref.at[own], near_place)]
-    keep = pltpu.make_async_copy(q_ref, o_ref.at[own], local.at[0])
+    keep = pltpu.make_async_copy(q_ref, o_ref.at[own], band_sems.at[0])
     keep.start()
-    aside = []
-
-    def forward(p):
-        crossing[p].wait_recv()
-        spot = o_ref.at[across, rows(y, p)]
-        aside.append(push(spot, spot, side_place))
-        landing.append(push(spot, spot, near_place))
-
-    def forward_side(p):
-        aside[p].wait_recv()
-        spot = o_ref.at[across, rows(1 - y, p)]
-        landing.append(push(spot, spot, near_place))
-
-    forward(0)
-    for p in range(1, pieces):
-        forward(p)
-        forward_side(p - 1)
-    forward_side(pieces - 1)
-    keep.wait()
-    for copy in landing:
-        copy.wait_recv()
-    for copy in copies:
-        copy.wait_send()
-
-
-def spread(band, number):
-    pieces = 4
-    slots = 1 + 4 * pieces
-    sub = lax.axis_size("narrow") // MATRICES
-    return pl.pallas_call(
-        functools.partial(spread_kernel, sub, pieces),
-        out_shape=jax.ShapeDtypeStruct((MATRICES,) + band.shape, jnp.float32),
-        in_specs=[pl.BlockSpec(memory_space=pltpu.VMEM)],
-        out_specs=pl.BlockSpec(memory_space=pl.ANY),
-        scratch_shapes=[
-            pltpu.SemaphoreType.DMA((slots,)),
-            pltpu.SemaphoreType.DMA((slots,)),
-            pltpu.SemaphoreType.DMA((1,)),
-        ],
-        compiler_params=pltpu.CompilerParams(collective_id=number, has_side_effects=True),
-    )(band)
-
-
-def finish_kernel(norm_ref, bands_any, *refs):
-    lines, others, refs = refs[0:6:2], refs[1:6:2], refs[6:]
-    moments, weights, refs = refs[:4], refs[4:8], refs[8:]
-    carried, results, refs = refs[:4], refs[4:8], refs[8:]
-    bands, factor_high, factor_low = refs[:3]
-    staged, values, highs, lows = refs[3:7], refs[7:11], refs[11:15], refs[15:19]
-    load_sems, value_sems, out_sems, band_sems = refs[19:]
-    size = factor_high.shape[0]
-    y, _ = wide_parts()
+    own_band = pltpu.make_async_copy(q_ref, pair_bands.at[own % 2], band_sems.at[1])
+    own_band.start()
+    matrices = Matrices(moments[0].shape[2])
     blocks = lax.axis_size("wide")
-    whole = []
-    fills = []
     for k in range(MATRICES):
-        sources = (lines[max(k - 1, 0)], others[max(k - 1, 0)])
         extent = staged[k].shape[0] // 2
-        for side, source in zip((y, 1 - y), sources):
+        if k >= 2:
+            pieces_of = [(y, 0, lines[k - 1])]
+            if k == 2:
+                pieces_of += [(1 - y, 0, others[1]), (1 - y, extent // 2, others[2])]
+            else:
+                pieces_of += [(1 - y, 0, others[3])]
+            for side, at, source in pieces_of:
+                to = pl.multiple_of(side * extent + at, 8)
+                spot = staged[k].at[pl.ds(to, source.shape[0]), :]
+                pltpu.make_async_copy(source, spot, load_sems.at[k]).start()
+        for side, source in ((y, lines[0]), (1 - y, others[0])):
             if k >= 2:
-                spot = staged[k].at[pl.ds(pl.multiple_of(side * extent, 8), extent), :]
-                pltpu.make_async_copy(source, spot, load_sems.at[k]).start()
                 continue
             share = (staged[0].shape[0] // blocks, staged[1].shape[0] // blocks)
             for b in range(blocks // 2):
@@ -726,13 +764,7 @@
                     staged[k].at[pl.ds(to, share[k]), :],
                     load_sems.at[k],
                 ).start()
-        whole.append(pltpu.make_async_copy(staged[k], staged[k], load_sems.at[k]))
-        fills.append(pltpu.make_async_copy(moments[k], values[k], value_sems.at[k]))
-        fills[-1].start()
-    arrivals = []
-    for k in range(MATRICES):
-        arrivals.append(pltpu.make_async_copy(bands_any.at[k], bands.at[k], band_sems.at[k]))
-        arrivals[-1].start()
+        matrices.move(moments[k], values[k], value_sems.at[k], k, True)
     clip = jnp.minimum(1.0, 1.0 / (norm_ref[0:1, 0:1] + 1e-06))
 
     def blend_rows(value, stage):
@@ -751,91 +783,220 @@
 
         lax.fori_loop(0, value.shape[1] // LANES, one, 0)
 
-    outs = []
+    aside = []
+
+    def forward(p):
+        crossing[p].wait_recv()
+        spot = o_ref.at[across, rows(y, p)]
+        aside.append(push(spot, spot, side_place))
+        landing.append(push(spot, spot, near_place))
+
+    def forward_side(p):
+        aside[p].wait_recv()
+        spot = o_ref.at[across, rows(1 - y, p)]
+        landing.append(push(spot, spot, near_place))
+
     for k in range(MATRICES):
-        whole[k].wait()
-        fills[k].wait()
+        whole_of(staged[k], load_sems.at[k]).wait()
+        whole_of(values[k], value_sems.at[k]).wait()
         blend = blend_columns if k in COLUMNS else blend_rows
         blend(values[k], staged[k])
-        outs.append(pltpu.make_async_copy(values[k], carried[k], out_sems.at[k]))
-        outs[-1].start()
+        matrices.move(carried[k], values[k], out_sems.at[k], k, False)
 
         def cut(i, carry, k=k):
             highs[k][slab_at(i), :], lows[k][slab_at(i), :] = split(values[k][slab_at(i), :])
             return carry
 
         lax.fori_loop(0, values[k].shape[0] // SLAB, cut, 0, unroll=UNROLL)
+
+        @pl.when(far != k // 2)
+        def _(k=k):
+            pltpu.make_async_copy(highs[k], high_outs[k], split_sems.at[2 * k]).start()
+            pltpu.make_async_copy(lows[k], low_outs[k], split_sems.at[2 * k + 1]).start()
+
+        if k == 1:
+            forward(0)
     for k in range(MATRICES):
-        outs[k].wait()
-        fills[k] = pltpu.make_async_copy(weights[k], values[k], value_sems.at[k])
-        fills[k].start()
-    lengths = (3 * D, D, FF, FF)
-    count = size // LANES
-    lanes = lambda block: pl.ds((block % count) * LANES, LANES)
+        whole_of(values[k], out_sems.at[k]).wait()
+
+        @pl.when(far == k // 2)
+        def _(k=k):
+            matrices.move(weights[k], values[k], value_sems.at[k], k, True)
+
+    forward(1)
+    landing[0].wait_recv()
+    near_band = pltpu.make_async_copy(o_ref.at[near], pair_bands.at[1 - own % 2], band_sems.at[2])
+    near_band.start()
+    own_band.wait()
+    near_band.wait()
+
+    def pair(index):
+        for side in range(2):
+
+            @pl.when(far == side)
+            def _(k=2 * side + index):
+                assemble(pair_bands.at[index], factor_high, factor_low)
+                whole_of(values[k], value_sems.at[k]).wait()
+
+                def one(i, carry):
+                    where = update(
+                        k, i * BLK, factor_high, factor_low, highs[k], lows[k], values[k]
+                    )
+                    matrices.move(fresh[k], values[k], out_sems.at[k], k, False, *where)
+                    return carry
+
+                lax.fori_loop(0, size // BLK, one, 0)
+
+    pair(0)
+    forward(2)
+    forward_side(0)
+    pair(1)
+    forward_side(1)
+    for p in range(3, pieces):
+        forward(p)
+        forward_side(p - 1)
+    forward_side(pieces - 1)
+    keep.wait()
     for k in range(MATRICES):
-        arrivals[k].wait()
-        for i in range(count):
-            for j in range(count // 2 + 1):
-                part = bands[k, lanes(i), lanes(j)]
-                spot = (lanes(i), lanes(i + j))
-                factor_high[spot], factor_low[spot] = split(part)
-                if 0 < j < count // 2:
-                    spot = (lanes(i + j), lanes(i))
-                    factor_high[spot], factor_low[spot] = split(part.T)
-        fills[k].wait()
-
-        def process(i, carry, k=k):
-            spot = pl.ds(pl.multiple_of(i * BLK, BLK), BLK)
-            q_high, q_low = factor_high[spot, :], factor_low[spot, :]
-            high, low = highs[k], lows[k]
-            if k in COLUMNS:
-                polar = dot_of(q_high, high[...], 1, 0) + (
-                    dot_of(q_high, low[...], 1, 0) + dot_of(q_low, high[...], 1, 0)
-                )
-                where = (spot, slice(None))
-            else:
-                polar = dot_of(high[...], q_high, 1, 1) + (
-                    dot_of(low[...], q_high, 1, 1) + dot_of(high[...], q_low, 1, 1)
-                )
-                where = (slice(None), spot)
-            scale = muon_rate * 0.2 * math.sqrt(lengths[k])
-            values[k][where] = values[k][where] * (1.0 - muon_rate * weight_decay) - scale * polar
-            pltpu.make_async_copy(
-                values[k].at[where], results[k].at[where], out_sems.at[k]
-            ).start()
-            return carry
-
-        lax.fori_loop(0, size // BLK, process, 0)
-    for k in range(MATRICES):
-        pltpu.make_async_copy(values[k], results[k], out_sems.at[k]).wait()
-
-
-def finish(norm, bands, lines, others, moments, weights):
-    size = bands.shape[1]
+
+        @pl.when(far == k // 2)
+        def _(k=k):
+            whole_of(values[k], out_sems.at[k]).wait()
+
+        @pl.when(far != k // 2)
+        def _(k=k):
+            pltpu.make_async_copy(highs[k], high_outs[k], split_sems.at[2 * k]).wait()
+            pltpu.make_async_copy(lows[k], low_outs[k], split_sems.at[2 * k + 1]).wait()
+
+    for copy in landing[1:]:
+        copy.wait_recv()
+    for copy in copies:
+        copy.wait_send()
+
+
+def spread(norm, band, lines, others, moments, weights, number):
+    pieces = 4
+    size = band.shape[0]
+    slots = 1 + 4 * pieces
+    sub = lax.axis_size("narrow") // MATRICES
+    vmem = pl.BlockSpec(memory_space=pltpu.VMEM)
     anywhere = pl.BlockSpec(memory_space=pl.ANY)
-    operands = [part for both in zip(lines, others) for part in both]
-    shapes = [jax.ShapeDtypeStruct(moment.shape, jnp.float32) for moment in moments]
+    operands = [*lines, *others]
+    f32 = [jax.ShapeDtypeStruct(moment.shape, jnp.float32) for moment in moments]
     staged = [(moment.size // size, size) for moment in moments]
+    flat = [(size, 3 * moments[0].shape[2])] + [moment.shape for moment in moments[1:]]
+    low = [jax.ShapeDtypeStruct(shape, jnp.bfloat16) for shape in flat]
     outs = pl.pallas_call(
-        finish_kernel,
-        out_shape=tuple(shapes + shapes),
-        in_specs=[pl.BlockSpec(memory_space=pltpu.VMEM)] + [anywhere] * (1 + len(operands) + 8),
-        out_specs=(anywhere,) * 8,
+        functools.partial(spread_kernel, sub, pieces),
+        out_shape=tuple(
+            [jax.ShapeDtypeStruct((MATRICES,) + band.shape, jnp.float32)] + f32 + f32 + low + low
+        ),
+        in_specs=[vmem] * 2 + [anywhere] * (len(operands) + 8),
+        out_specs=(anywhere,) * 17,
         scratch_shapes=[
-            pltpu.VMEM(bands.shape, jnp.float32),
+            pltpu.VMEM((2,) + band.shape, jnp.float32),
             pltpu.VMEM((size, size), jnp.bfloat16),
             pltpu.VMEM((size, size), jnp.bfloat16),
         ]
         + [pltpu.VMEM(shape, jnp.float32) for shape in staged]
-        + [pltpu.VMEM(moment.shape, jnp.float32) for moment in moments]
-        + [pltpu.VMEM(moment.shape, jnp.bfloat16) for moment in moments]
-        + [pltpu.VMEM(moment.shape, jnp.bfloat16) for moment in moments]
-        + [pltpu.SemaphoreType.DMA((MATRICES,))] * 4,
-        compiler_params=pltpu.CompilerParams(vmem_limit_bytes=60 * 2**20),
+        + [pltpu.VMEM(shape, jnp.float32) for shape in flat]
+        + [pltpu.VMEM(shape, jnp.bfloat16) for shape in flat] * 2
+        + [pltpu.SemaphoreType.DMA((MATRICES,))] * 3
+        + [
+            pltpu.SemaphoreType.DMA((2 * MATRICES,)),
+            pltpu.SemaphoreType.DMA((3,)),
+            pltpu.SemaphoreType.DMA((slots,)),
+            pltpu.SemaphoreType.DMA((slots,)),
+        ],
+        compiler_params=pltpu.CompilerParams(
+            collective_id=number, has_side_effects=True, vmem_limit_bytes=58 * 2**20
+        ),
         cost_estimate=pl.CostEstimate(
-            flops=18 * size * size * size, bytes_accessed=80 * size * size, transcendentals=0
+            flops=9 * size * size * size, bytes_accessed=80 * size * size, transcendentals=0
         ),
-    )(norm, bands, *operands, *moments, *weights)
+    )(norm, band, *operands, *moments, *weights)
+    return outs[0], outs[1:5], outs[5:9], outs[9:13], outs[13:17]
+
+
+def finish_kernel(sub, bands_any, *refs):
+    ready, fresh, high_ins, low_ins, weights = (refs[4 * i : 4 * i + 4] for i in range(5))
+    carried, results, refs = refs[20:24], refs[24:28], refs[28:]
+    bands, factor_high, factor_low = refs[:3]
+    news, values, highs, lows = refs[3:7], refs[7:11], refs[11:15], refs[15:19]
+    news_sems, value_sems, split_sems, band_sems, carried_sems, out_sems = refs[19:]
+    size = factor_high.shape[0]
+    far = lax.axis_index("narrow") // sub // 2
+    matrices = Matrices(weights[0].shape[2])
+    for side in range(2):
+
+        @pl.when(far == side)
+        def _(side=side):
+            for index in range(2):
+                k = 2 * (1 - side) + index
+                pltpu.make_async_copy(bands_any.at[k], bands.at[index], band_sems.at[index]).start()
+                pltpu.make_async_copy(high_ins[k], highs[k], split_sems.at[2 * index]).start()
+                pltpu.make_async_copy(low_ins[k], lows[k], split_sems.at[2 * index + 1]).start()
+                matrices.move(weights[k], values[k], value_sems.at[k], k, True)
+            for k in (2 * side, 2 * side + 1):
+                matrices.move(fresh[k], values[k], value_sems.at[k], k, True)
+
+    for k in range(MATRICES):
+        matrices.move(ready[k], news[k], news_sems.at[k], k, True)
+    for index in range(2):
+        whole_of(bands.at[index], band_sems.at[index]).wait()
+        for k in range(MATRICES):
+            if index == 0:
+                whole_of(news[k], news_sems.at[k]).wait()
+                matrices.move(carried[k], news[k], carried_sems.at[k], k, False)
+        for side in range(2):
+
+            @pl.when(far == side)
+            def _(k=2 * (1 - side) + index, done=2 * side + index):
+                whole_of(values[done], value_sems.at[done]).wait()
+                matrices.move(results[done], values[done], out_sems.at[done], done, False)
+                assemble(bands.at[index], factor_high, factor_low)
+                whole_of(highs[k], split_sems.at[2 * index]).wait()
+                whole_of(lows[k], split_sems.at[2 * index + 1]).wait()
+                whole_of(values[k], value_sems.at[k]).wait()
+
+                def one(i, carry):
+                    where = update(
+                        k, i * BLK, factor_high, factor_low, highs[k], lows[k], values[k]
+                    )
+                    matrices.move(results[k], values[k], out_sems.at[k], k, False, *where)
+                    return carry
+
+                lax.fori_loop(0, size // BLK, one, 0)
+
+    for k in range(MATRICES):
+        whole_of(news[k], carried_sems.at[k]).wait()
+        whole_of(values[k], out_sems.at[k]).wait()
+
+
+def finish(bands, ready, fresh, highs, lows, weights):
+    size = bands.shape[1]
+    sub = lax.axis_size("narrow") // MATRICES
+    anywhere = pl.BlockSpec(memory_space=pl.ANY)
+    shapes = [jax.ShapeDtypeStruct(weight.shape, jnp.float32) for weight in weights]
+    flat = [(size, 3 * weights[0].shape[2])] + [weight.shape for weight in weights[1:]]
+    outs = pl.pallas_call(
+        functools.partial(finish_kernel, sub),
+        out_shape=tuple(shapes + shapes),
+        in_specs=[anywhere] * 21,
+        out_specs=(anywhere,) * 8,
+        scratch_shapes=[
+            pltpu.VMEM((2,) + bands.shape[1:], jnp.float32),
+            pltpu.VMEM((size, size), jnp.bfloat16),
+            pltpu.VMEM((size, size), jnp.bfloat16),
+        ]
+        + [pltpu.VMEM(shape, jnp.float32) for shape in flat] * 2
+        + [pltpu.VMEM(shape, jnp.bfloat16) for shape in flat] * 2
+        + [pltpu.SemaphoreType.DMA((MATRICES,))] * 6,
+        compiler_params=pltpu.CompilerParams(vmem_limit_bytes=58 * 2**20),
+        cost_estimate=pl.CostEstimate(
+            flops=9 * size * size * size, bytes_accessed=60 * size * size, transcendentals=0
+        ),
+    )(bands, *ready, *fresh, *highs, *lows, *weights)
     return outs[:4], outs[4:]
 
 
@@ -913,7 +1074,8 @@
     ffn_half_ref,
     grad_entry_any,
     reduce_share,
-    expand_share,
+    expand_hold,
+    expand_give,
     grad_taps_ref,
     expand_full,
     reduce_full,
@@ -939,6 +1101,7 @@
     expand_beside,
     expand_inbox,
     expand_loads,
+    give_sems,
     weight_sems,
     sends,
     arrivals,
@@ -1041,7 +1204,8 @@
         ready = [(groups - 1 - step) * size + e for e in reversed(range(size))]
         for scatter in (reduce_sum, expand_sum):
             for e in ready:
-                scatter.give(e)
+                if scatter is reduce_sum or e >= count // 2:
+                    scatter.give(e)
     for step in range(groups, steps):
         for copy in fetches[step]:
             copy.wait()
@@ -1066,26 +1230,43 @@
         scatter.load()
     for p in range(pieces):
         narrow.begin(p)
-    left = [list(reversed(range(count))), list(reversed(range(count)))]
+    left = [list(reversed(range(count))), list(reversed(range(count // 2, count)))]
+    gives = []
+    for e in range(count // 2):
+        gives.append(
+            pltpu.make_async_copy(
+                block_of(grad_expand, 1 - y, line_partner(z, e)), expand_give.at[e], give_sems.at[e]
+            )
+        )
+        gives[e].start()
     scatters = (reduce_sum, expand_sum)
     scatters[0].step(left[0].pop(0))
     scatters[1].step(left[1].pop(0))
     ffn_copy.wait_recv()
     ffn_half_ref[...] = ffn[side_rows(core), :] + ffn_inbox[...]
-    turns = [0, 1, 0, 0, 1, 1]
+    turns = [0, 1, 0]
     for b in range(len(far_bits)):
         for p in range(pieces):
             narrow.step(b, p)
-            if turns and len(left[turns[0]]) > 1:
+            if turns and len(left[turns[0]]) > (turns[0] == 0):
                 which = turns.pop(0)
                 scatters[which].step(left[which].pop(0))
-    outs = []
-    for which, share in ((0, reduce_share), (1, expand_share)):
+    for which in range(2):
         while left[which]:
             scatters[which].step(left[which].pop(0))
-        out = pltpu.make_async_copy(scatters[which].held.at[0], share, scatters[which].local.at[0])
+    for e in range(count // 2):
+        expand_sum.loads[e].wait()
+    expand_sum.copies[("z", count // 2)].wait_recv()
+    expand_held[0] = expand_held[0] + expand_inbox[count // 2 - 1]
+    outs = [
+        pltpu.make_async_copy(reduce_held.at[0], reduce_share, reduce_loads.at[0]),
+        pltpu.make_async_copy(
+            expand_held.at[pl.ds(0, count // 2)], expand_hold, expand_loads.at[0]
+        ),
+    ]
+    for out in outs:
         out.start()
-        outs.append(out)
+    outs += gives
     narrow.finish()
     ffn_copy.wait_send()
     for scatter in scatters:
@@ -1116,17 +1297,19 @@
     wide = lambda *shape: pltpu.VMEM(shape, jnp.float32)
     low = lambda *shape: pltpu.VMEM(shape, jnp.bfloat16)
     share = block_shape((units, width))
+    line = lax.axis_size("wide") // 2
     return pl.pallas_call(
         functools.partial(middle_kernel, pieces),
         out_shape=(
             f32(tokens // 2, width),
             f32(tokens, width),
             f32(*share),
-            f32(*share),
+            f32(line // 2, *share),
+            f32(line // 2, *share),
             f32(9, units),
         ),
         in_specs=[vmem, vmem, vmem, vmem, anywhere, anywhere, vmem],
-        out_specs=(vmem, anywhere, anywhere, anywhere, vmem),
+        out_specs=(vmem,) + (anywhere,) * 4 + (vmem,),
         scratch_shapes=[
             wide(width, units),
             wide(units, width),
@@ -1144,6 +1327,7 @@
         + narrow_scratch((tokens, width), pieces)
         + scatter_scratch((units, width)) * 2
         + [
+            pltpu.SemaphoreType.DMA((line // 2,)),
             pltpu.SemaphoreType.DMA((2 * steps,)),
             pltpu.SemaphoreType.DMA((slots,)),
             pltpu.SemaphoreType.DMA((slots,)),
@@ -1226,9 +1410,13 @@
     normed_ref,
     back_ref,
     inverse_ref,
+    wait_tokens,
+    wait_mixed,
+    wait_hidden,
 ):
     width = tokens_ref.shape[1]
     stretch = 1.0 + scale_ref[...]
+    wait_tokens()
 
     def enter(r, carry):
         normed, inverse = norm_strip(tokens_ref[slab_at(r), :].astype(jnp.float32))
@@ -1238,6 +1426,7 @@
 
     rows = tokens_ref.shape[0]
     lax.fori_loop(0, rows // SLAB, enter, 0, unroll=UNROLL)
+    wait_mixed()
     for start in range(0, width, BLK):
         lanes = pl.ds(start, BLK)
         taps = [taps_ref[t : t + 1, lanes] for t in range(9)]
@@ -1268,6 +1457,7 @@
         out_ref[slab_at(r), :] = out.astype(jnp.bfloat16)
         return shifts + fold_rows(back), scales + fold_rows(back * normed)
 
+    wait_hidden()
     zero = jnp.zeros((8, width), jnp.float32)
     shifts, scales = lax.fori_loop(0, rows // SLAB, leave, (zero, zero), unroll=UNROLL)
     grad_shift_ref[...] = jnp.sum(shifts, axis=0, keepdims=True)
@@ -1293,10 +1483,9 @@
 ):
     tokens = mixed_ref.shape[0]
     width = context_ref.shape[1]
-    step = min(BLK, width)
-    for start in range(0, 3 * width, step):
-        columns = pl.ds(start, step)
-        low_ref[:, columns] = attend_ref[:, columns].astype(jnp.bfloat16)
+    for j in range(3):
+        columns = pl.ds(j * width, width)
+        low_ref[:, columns] = attend_ref[j].astype(jnp.bfloat16)
         triple_ref[:, columns] = dot_of(mixed_ref[...], low_ref[:, columns], 1, 0).astype(
             jnp.bfloat16
         )
@@ -1326,7 +1515,7 @@
 
 def attend(mixed, attend_weight):
     tokens, width = mixed.shape
-    own = attend_weight.shape[1] // 3
+    own = attend_weight.shape[2]
     vmem = pl.BlockSpec(memory_space=pltpu.VMEM)
     return pl.pallas_call(
         attend_kernel,
@@ -1334,7 +1523,7 @@
             jax.ShapeDtypeStruct((tokens, 3 * own), jnp.bfloat16),
             jax.ShapeDtypeStruct((tokens, own), jnp.bfloat16),
             jax.ShapeDtypeStruct((8, tokens), jnp.float32),
-            jax.ShapeDtypeStruct(attend_weight.shape, jnp.bfloat16),
+            jax.ShapeDtypeStruct((width, 3 * own), jnp.bfloat16),
         ),
         in_specs=[vmem] * 2,
         out_specs=(vmem,) * 4,
@@ -1495,7 +1684,8 @@
     context_ref,
     logsum_ref,
     reduce_share_ref,
-    expand_share_ref,
+    expand_hold,
+    expand_give,
     grad_hidden_ref,
     grad_shift_ref,
     grad_scale_ref,
@@ -1504,6 +1694,7 @@
     attend_out_share,
     reduce_line,
     expand_line,
+    expand_share,
     hidden,
     branch,
     grad_entry,
@@ -1524,6 +1715,10 @@
     scatter_beside,
     scatter_inbox,
     scatter_loads,
+    rest_held,
+    rest_beside,
+    rest_inbox,
+    rest_loads,
     load_sems,
     keep_sems,
     sends,
@@ -1551,14 +1746,20 @@
         return spot_of
 
     gathers, keeps = [], []
+    rest_base = base + 2 * (2 ** len(hops) - 1)
+    rest = Scatter(
+        None, rest_held, rest_beside, rest_inbox, sends, arrivals, rest_loads, rest_base,
+        (expand_hold, expand_give),
+    )
+    rest.start()
     for index, (share, line) in enumerate(
-        ((reduce_share_ref, reduce_line), (expand_share_ref, expand_line))
+        ((reduce_share_ref, reduce_line), (rest_held.at[0], expand_line))
     ):
         start = base + index * (2 ** len(hops) - 1)
         gathers.append(Gather(share, spot_in(line), hops, sends, arrivals, start))
-        gathers[index].step(0)
         keeps.append(pltpu.make_async_copy(share, spot_in(line)(0), keep_sems.at[index]))
-        keeps[index].start()
+    gathers[0].step(0)
+    keeps[0].start()
     step = tokens // pieces
     loads = []
     for p in range(pieces):
@@ -1609,6 +1810,8 @@
         )
     for ref, total in zip((grad_shift_ref, grad_scale_ref, grad_gate_ref), sums):
         ref[...] = jnp.sum(total, axis=0, keepdims=True)
+    for e in reversed(range(1, rest.count)):
+        rest.step(e)
     grad_context[...] = dot_of(grad_branch[...], output_low[...], 1, 1).astype(jnp.bfloat16)
     keys_t[...] = triple_ref[:, pl.ds(own, own)].T
     grad_keys[...] = jnp.zeros_like(grad_keys)
@@ -1640,6 +1843,11 @@
         lax.fori_loop(0, tokens // QUERIES, one, 0)
         if head == max(heads - 2, 0):
             gathers[0].step(1)
+            rest.step(0)
+            gathers[1].step(0)
+            keeps[1].start()
+            keeps.append(pltpu.make_async_copy(rest_held.at[0], expand_share, keep_sems.at[2]))
+            keeps[2].start()
     grad_triple[:, pl.ds(0, own)] = (grad_queries_t[...].T * scale).astype(jnp.bfloat16)
     grad_triple[:, pl.ds(own, own)] = (grad_keys[...] * scale).astype(jnp.bfloat16)
     grad_triple[:, pl.ds(2 * own, own)] = grad_values[...].astype(jnp.bfloat16)
@@ -1692,6 +1900,7 @@
     out.start()
     narrow.finish()
     scatter.finish()
+    rest.finish()
     for gather in gathers:
         gather.finish()
     for keep in keeps:
@@ -1714,7 +1923,8 @@
     context,
     logsum,
     reduce_share,
-    expand_share,
+    expand_hold,
+    expand_give,
     number,
 ):
     tokens, width = hidden.shape
@@ -1722,7 +1932,8 @@
     pieces = 4
     line = lax.axis_size("wide") // 2
     narrow_bits = bits_of(lax.axis_size("narrow"))
-    slots = (len(narrow_bits) + 1) * pieces + Scatter.slots() + 2 * (line - 1)
+    slots = (len(narrow_bits) + 1) * pieces + Scatter.slots() + 2 * (line - 1) + line - 1
+    block = reduce_share.shape
     vmem = pl.BlockSpec(memory_space=pltpu.VMEM)
     anywhere = pl.BlockSpec(memory_space=pl.ANY)
     f32 = lambda *shape: jax.ShapeDtypeStruct(shape, jnp.float32)
@@ -1738,10 +1949,11 @@
             f32(tokens, width),
             f32(4 * own // (2 * line), width),
             f32(line * reduce_share.shape[0], width),
-            f32(line * expand_share.shape[0], width),
+            f32(line * reduce_share.shape[0], width),
+            f32(*block),
         ),
-        in_specs=[anywhere] * 4 + [vmem] * 11,
-        out_specs=(vmem,) * 4 + (anywhere,) * 4,
+        in_specs=[anywhere] * 4 + [vmem] * 10 + [anywhere] * 2,
+        out_specs=(vmem,) * 4 + (anywhere,) * 5,
         scratch_shapes=[
             wide(tokens, width),
             wide(max(tokens, 4 * own), width),
@@ -1759,8 +1971,12 @@
         + narrow_scratch((tokens, width), pieces)
         + scatter_scratch((4 * own, width))
         + [
+            wide(line // 2, *block),
+            wide(line // 2, *block),
+            wide(max(line // 2 - 1, 1), *block),
+            pltpu.SemaphoreType.DMA((line // 2,)),
             pltpu.SemaphoreType.DMA((4 * pieces,)),
-            pltpu.SemaphoreType.DMA((2,)),
+            pltpu.SemaphoreType.DMA((3,)),
             pltpu.SemaphoreType.DMA((slots,)),
             pltpu.SemaphoreType.DMA((slots,)),
         ],
@@ -1787,21 +2003,22 @@
         context,
         logsum,
         reduce_share,
-        expand_share,
+        expand_hold,
+        expand_give,
     )
 
 
 def tail_kernel(
-    tokens_ref,
+    tokens_any,
     shift_ref,
     scale_ref,
     taps_ref,
-    grad_mixed_ref,
-    grad_hidden_ref,
-    hidden_ref,
-    ffn_half_ref,
-    ffn_across_ref,
-    cotangent_ref,
+    grad_mixed_any,
+    grad_hidden_any,
+    hidden_any,
+    ffn_half_any,
+    ffn_across_any,
+    cotangent_any,
     live_ref,
     gate_ref,
     rows_ref,
@@ -1814,6 +2031,12 @@
     small_ref,
     norm_ref,
     line_ref,
+    tokens_ref,
+    grad_mixed_ref,
+    grad_hidden_ref,
+    hidden_ref,
+    cotangent_ref,
+    ffn_across_ref,
     ffn,
     normed_ref,
     back_ref,
@@ -1825,10 +2048,26 @@
     spare,
     spare_in,
     keep_sems,
+    load_sems,
     sends,
     arrivals,
 ):
     width = tokens_ref.shape[1]
+    core = lax.axis_index("narrow") % 2
+    half = ffn.shape[0] // 2
+    mine = pl.ds(pl.multiple_of(core * half, SLAB), half)
+    loads = []
+    for src, dst in (
+        (ffn_half_any, ffn.at[mine, :]),
+        (ffn_across_any, ffn_across_ref),
+        (tokens_any, tokens_ref),
+        (grad_mixed_any, grad_mixed_ref),
+        (cotangent_any, cotangent_ref),
+        (grad_hidden_any, grad_hidden_ref),
+        (hidden_any, hidden_ref),
+    ):
+        loads.append(pltpu.make_async_copy(src, dst, load_sems.at[len(loads)]))
+        loads[-1].start()
     wide_bits = bits_of(lax.axis_size("wide"))
     narrow_bits = bits_of(lax.axis_size("narrow"))
     greet(
@@ -1850,10 +2089,9 @@
     gather.step(0)
     keep = pltpu.make_async_copy(attend_out_ref, spot_of(0), keep_sems.at[0])
     keep.start()
-    core = lax.axis_index("narrow") % 2
-    half = ffn.shape[0] // 2
-    mine = pl.ds(pl.multiple_of(core * half, SLAB), half)
-    ffn[mine, :] = ffn_half_ref[...] + ffn_across_ref[...]
+    loads[0].wait()
+    loads[1].wait()
+    ffn[mine, :] = ffn[mine, :] + ffn_across_ref[...]
     last = count + len(narrow_bits) + 2 ** len(hops) - 1
     ffn_copy = send(ffn.at[mine, :], ffn.at[mine, :], sends, arrivals, last, place_at("narrow", 1))
     mixer_kernel_backward(
@@ -1870,18 +2108,27 @@
         normed_ref,
         back_ref,
         inverse_ref,
+        loads[2].wait,
+        loads[3].wait,
+        loads[5].wait,
     )
     ffn_copy.wait_recv()
+    loads[4].wait()
     gate, live = gate_ref[...], live_ref[...]
 
-    def leave(r, gates):
+    def weigh(r, gates):
         spot = slab_at(r)
-        branch = ffn[spot, :]
-        block_out_ref[spot, :] = (live * (hidden_ref[spot, :] + gate * branch)).astype(jnp.bfloat16)
-        return gates + fold_rows(branch * (cotangent_ref[spot, :].astype(jnp.float32) * live))
+        return gates + fold_rows(ffn[spot, :] * (cotangent_ref[spot, :].astype(jnp.float32) * live))
+
+    def leave(r, carry):
+        spot = slab_at(r)
+        block_out_ref[spot, :] = (live * (hidden_ref[spot, :] + gate * ffn[spot, :])).astype(
+            jnp.bfloat16
+        )
+        return carry
 
     gates = lax.fori_loop(
-        0, ffn.shape[0] // SLAB, leave, jnp.zeros((8, width), jnp.float32), unroll=UNROLL
+        0, ffn.shape[0] // SLAB, weigh, jnp.zeros((8, width), jnp.float32), unroll=UNROLL
     )
     slots[0] = jnp.zeros(slots.shape[1:], jnp.float32)
     slots[0, 0:1, :] = grad_shift[...]
@@ -1905,6 +2152,8 @@
         copies.append(copy)
         if b == 0:
             gather.step(1)
+            loads[6].wait()
+            lax.fori_loop(0, ffn.shape[0] // SLAB, leave, 0, unroll=UNROLL)
         copy.wait_recv()
         slots[b + 1] = slots[b] + slots[count + 1 + b]
     total = slots[count]
@@ -1970,9 +2219,15 @@
             f32(8, LANES),
             f32(line * shares[0].shape[0], width),
         ),
-        in_specs=[vmem] * 17,
+        in_specs=[anywhere] + [vmem] * 3 + [anywhere] * 6 + [vmem] * 7,
         out_specs=(vmem,) * 4 + (anywhere,),
         scratch_shapes=[
+            pltpu.VMEM((rows, width), jnp.bfloat16),
+            wide(rows, width),
+            wide(rows, width),
+            wide(rows, width),
+            pltpu.VMEM((rows, width), jnp.bfloat16),
+            wide(rows // 2, width),
             wide(rows, width),
             wide(rows, width),
             wide(rows, width),
@@ -1984,6 +2239,7 @@
             wide(len(narrow_bits) + 1, 8, LANES),
             wide(len(narrow_bits), 8, LANES),
             pltpu.SemaphoreType.DMA((1,)),
+            pltpu.SemaphoreType.DMA((7,)),
             pltpu.SemaphoreType.DMA((total,)),
             pltpu.SemaphoreType.DMA((total,)),
         ],
@@ -2046,15 +2302,15 @@
     width = tokens.shape[2]
     flat_tokens = tokens.reshape(-1, width)
     mixed_low = mixer_forward(flat_tokens, shift_one[0], scale_one[0], mixer_kernel)
-    attend_flat = attend_weight.reshape(width, -1)
-    triple, context, logsum, attend_low = attend(mixed_low, attend_flat)
+    three = lambda matrix: jnp.transpose(matrix, (1, 0, 2))
+    triple, context, logsum, attend_low = attend(mixed_low, three(attend_weight))
     output_rows, context = together(all_rows(output_weight), context)
     branch, hidden, entry_low = enter(
         context, flat_tokens, output_rows, gate_one[0], shift_two[0], scale_two[0], 1
     )
     flat_cotangent = cotangent.reshape(-1, width)
     live_row = jnp.broadcast_to(live_mask[0], (1, width))
-    ffn_half, grad_entry, reduce_share, expand_share, grad_hidden_kernel = middle(
+    ffn_half, grad_entry, reduce_share, expand_hold, expand_give, grad_hidden_kernel = middle(
         entry_low,
         flat_cotangent,
         live_row,
@@ -2064,8 +2320,8 @@
         hidden_kernel,
         2,
     )
-    grad_entry, reduce_share, expand_share, ffn_half = together(
-        grad_entry, reduce_share, expand_share, ffn_half
+    grad_entry, reduce_share, expand_hold, ffn_half = together(
+        grad_entry, reduce_share, expand_hold, ffn_half
     )
     for bit in bits_of(lax.axis_size("narrow"))[1:-1]:
         ffn_half = ffn_half + permute(ffn_half, "narrow", bit)
@@ -2079,6 +2335,7 @@
         attend_out_share,
         reduce_line,
         expand_line,
+        expand_share,
     ) = back(
         hidden,
         branch,
@@ -2094,7 +2351,8 @@
         context,
         logsum,
         reduce_share,
-        expand_share,
+        expand_hold,
+        expand_give,
         3,
     )
     ffn_across, grad_mixed, reduce_line, attend_out_share = together(
@@ -2131,31 +2389,32 @@
     summed_hidden = summed_hidden[: hidden_kernel.size].reshape(hidden_kernel.shape)
     gradient_norm = norm[0, 0]
     clip_factor = jnp.minimum(1.0, 1.0 / (gradient_norm + 1e-06))
-    attend_moment_flat = attend_moment.reshape(width, -1)
-    attend_half = own_half(attend_moment_flat, 1).T
-    gramian = gram_whole(
+    gramian, expand_first = gram_whole(
         norm,
         [attend_out_line, expand_line, reduce_line],
-        [attend_half, output_moment, expand_moment, reduce_moment],
+        [three(attend_moment), output_moment, expand_moment, reduce_moment],
         5,
     )
     gramian, expand_line, attend_out_line = together(gramian, expand_line, attend_out_line)
-    expand_other = permute(expand_line, "wide", 1)
+    expand_other = permute(expand_line[expand_line.shape[0] // 2 :], "wide", 1)
     attend_out_other = permute(attend_out_line, "wide", 1)
-    factor = spread(polar_factor(gramian), 6)
+    factor = polar_factor(gramian)
     factor, expand_other, attend_out_other, reduce_other = together(
         factor, expand_other, attend_out_other, reduce_other
     )
-    carried, results = finish(
+    weights = [three(attend_weight), output_weight, expand_weight, reduce_weight]
+    bands, ready, fresh, highs, lows = spread(
         norm,
         factor,
         [attend_out_line, expand_line, reduce_line],
-        [attend_out_other, expand_other, reduce_other],
-        [attend_moment_flat, output_moment, expand_moment, reduce_moment],
-        [attend_flat, output_weight, expand_weight, reduce_weight],
-    )
-    attend_carried = carried[0].reshape(attend_weight.shape)
-    attend_result = results[0].reshape(attend_weight.shape)
+        [attend_out_other, expand_first, expand_other, reduce_other],
+        [three(attend_moment), output_moment, expand_moment, reduce_moment],
+        weights,
+        6,
+    )
+    carried, results = finish(bands, ready, fresh, highs, lows, weights)
+    attend_carried = jnp.transpose(carried[0], (1, 0, 2))
+    attend_result = jnp.transpose(results[0], (1, 0, 2))
     table_moment, table_square, table_result = adam_update(
         modulation_table, table_first, table_second, clip_factor * summed_table
     )

time: 627 us -> 608 us (0.970)
  local copies, waits for them, and re-layouts: 39 us -> 20.5 us
    pallas_call x1, Pallas kernels: 116 us -> 104 us  [middle(): pl.pallas_call(functools.partial(middle_kernel, pieces), out_shape=(f32(t...]
    pallas_call x1, Pallas kernels: 111 us -> 122 us  [back(): pl.pallas_call(functools.partial(back_kernel, pieces), out_shape=(f32(tok...]
    unnamed x74 -> x68, local copies, waits for them, and re-layouts: 23.9 us -> 17 us
    reshape x2 -> x0, local copies, waits for them, and re-layouts: 6.41 us -> none  [the longest x1 3.7 us: local(): attend_flat = attend_weight.reshape(width, -1)]
  transfers between devices with their start and end apart: 5 -> 5, of which waited for: 0 -> 0; matrix products, arithmetic and copies ran while one was open for 3% -> 1% of each run, Pallas kernels for 61% -> 58%
where the time goes in v7:
time: 608 us; the launch traced here: 601 us
  Pallas kernels  561 us (92%)
  local copies, waits for them, and re-layouts  20.5 us (3%)
  starting transfers between devices  8.84 us (1%)
  other arithmetic  7.88 us (1%)
    pallas_call x1, Pallas kernels, back(): pl.pallas_call(functools.partial(back_kernel, pieces), out_shape=(f32(tok...  122 us
    pallas_call x1, Pallas kernels, middle(): pl.pallas_call(functools.partial(middle_kernel, pieces), out_shape=(f32(t...  104 us
    pallas_call x1, Pallas kernels, polar_factor(): pl.pallas_call(polar_kernel, out_shape=jax.ShapeDtypeStruct(gramian.shape...  74.1 us
    pallas_call x1, Pallas kernels, gram_whole(): pl.pallas_call(gram_kernel, out_shape=(jax.ShapeDtypeStruct((size, band),...  72.1 us
    pallas_call x1, Pallas kernels, tail(): pl.pallas_call(tail_kernel, out_shape=(low(rows, width), low(rows, width)...  63.5 us
    pallas_call x1, Pallas kernels, spread(): pl.pallas_call(functools.partial(spread_kernel, sub, pieces), out_shape=t...  47.2 us
    pallas_call x1, Pallas kernels, finish(): pl.pallas_call(functools.partial(finish_kernel, sub), out_shape=tuple(sha...  31.6 us
    pallas_call x1, Pallas kernels, enter(): pl.pallas_call(functools.partial(entry_kernel, pieces), out_shape=(jax.Sh...  28.6 us
  transfers between devices with their start and end apart: 5, of which 0 were waited for; matrix products, arithmetic and copies ran while one was open for 1% of the time, Pallas kernels for 58%

profile of v7, /device:TPU:0, one launch (start us, length us, event | category | flops | bytes accessed | tf_op | source)
XLA Modules:
  0.0 600.8 jit_solution(617632484624986326)
XLA Ops:
  0.7 3.0 collective-permute-start
  4.3 0.8 bitcast_add_fusion
  5.1 0.6 slice_bitcast_fusion
  5.7 0.0 copy-start.1
  5.7 1.6 copy-done.1
  7.3 0.8 copy-done.7
  8.2 7.4 %shard_map.356.mixed_ref = bf16[1024,1024]{1,0:T(8,128)(2,1)S(1)} custom-call(bf16[1024,1024]{1,0:T(8,128)(2,1)S(1)} %bitcast.28, f32[1,1024]{1,0:T(1,128)S(1)} %get-tuple-element.179.shift_ref, f32[1,1024]{1,0:T(1,128)S(1)} %get-tuple-element.178.scale_ref, f32[9,1024]{1,0:T(8,128)S(1)} %copy-done.7), custom_call_target="tpu_custom_call" | custom-call | flops 41943040 | bytes 4194304 | tf_op jit(solution)/shard_map/pallas_call | solution.py:1386
  15.6 0.0 copy-start.5
  15.6 0.0 copy-start.22
  15.6 10.6 %shard_map.357 = (bf16[1024,768]{1,0:T(8,128)(2,1)S(1)}, bf16[1024,256]{1,0:T(8,128)(2,1)S(1)}, f32[8,1024]{1,0:T(8,128)S(1)}, bf16[1024,768]{1,0:T(8,128)(2,1)S(1)}) custom-call(bf16[1024,1024]{1,0:T(8,128)(2,1)S(1)} %shard_map.356.mixed_ref, f32[3,1024,256]{2,1,0:T(8,128)S(1)} %bitcast.26), custom_call_target="tpu_custom_call" | custom-call | flops 4294967296 | bytes 12582912 | tf_op jit(solution)/shard_map/pallas_call | solution.py:1520
  26.3 0.0 copy-start.18
  26.3 1.1 copy-done.18
  27.4 0.6 copy-done.20
  28.1 2.7 maximum_select_fusion.output_ref
  30.8 0.2 copy-done.2
  31.0 28.6 %shard_map.358 = (f32[1024,1024]{1,0:T(8,128)S(1)}, f32[1024,1024]{1,0:T(8,128)}, bf16[1024,1024]{1,0:T(8,128)(2,1)S(1)}) custom-call(bf16[1024,256]{1,0:T(8,128)(2,1)S(1)} %get-tuple-element.92.context_ref, bf16[1024,1024]{1,0:T(8,128)(2,1)S(1)} %bitcast.29, f32[512,1024]{1,0:T(8,128)S(1)} %maximum_select_fusion.output_ref, ...), custom_call_target="tpu_custom_call" | custom-call | flops 2147483648 | bytes 104857600 | tf_op jit(solution)/shard_map/pallas_call | solution.py:1634
  59.6 0.0 copy-start.15
  59.6 2.0 copy-done.15
  61.6 1.3 copy-done.16
  62.9 0.6 broadcast_in_dim.12.live_ref
  63.5 104.0 %shard_map.359 = (f32[512,1024]{1,0:T(8,128)}, f32[1024,1024]{1,0:T(8,128)}, f32[128,1024]{1,0:T(8,128)}, f32[2,128,1024]{2,1,0:T(8,128)}, f32[2,128,1024]{2,1,0:T(8,128)}, /*index=5*/f32[9,1024]{1,0:T(8,128)}) custom-call(bf16[1024,1024]{1,0:T(8,128)(2,1)} %copy-done.16, bf16[1024,1024]{1,0:T(8,128)(2,1)} %bitcast.34, f32[1,1024]{1,0:T(1,128)} %broadcast_in_dim.12.live_ref, ...), custom_call_target="tpu_custom_call" | custom-call | flops 12884901888 | bytes 209715200 | tf_op jit(solution)/shard_map/pallas_call | solution.py:1301
  167.6 1.8 collective-permute-start.1
  169.4 121.8 %shard_map.360 = (f32[1024,1024]{1,0:T(8,128)}, f32[1,1024]{1,0:T(1,128)}, f32[1,1024]{1,0:T(1,128)}, f32[1,1024]{1,0:T(1,128)}, f32[1024,1024]{1,0:T(8,128)}, /...) custom-call(f32[1024,1024]{1,0:T(8,128)} %get-tuple-element.100.hidden_any, ...), custom_call_target="tpu_custom_call" | custom-call | flops 10737418240 | bytes 157286400 | tf_op jit(solution)/shard_map/pallas_call | solution.py:1942
  291.2 1.3 pad_maximum_fusion.rows_ref
  292.6 2.0 collective-permute-start.4
  294.5 63.5 %shard_map.361 = (bf16[1024,1024]{1,0:T(8,128)(2,1)}, bf16[1024,1024]{1,0:T(8,128)(2,1)}, f32[32,1024]{1,0:T(8,128)}, f32[8,128]{1,0:T(8,128)}, f32[512,1024]{1,0:T(8,128)}) custom-call(bf16[1024,1024]{1,0:T(8,128)(2,1)} %bitcast.27, f32[1,1024]{1,0:T(1,128)} %copy-done.10, f32[1,1024]{1,0:T(1,128)} %copy-done.9, f32[9,1024]{1,0:T(8,128)} %taps_ref.5, ...), custom_call_target="tpu_custom_call" | custom-call | flops 104857600 | bytes 62914560 | tf_op jit(solution)/shard_map/pallas_call | solution.py:2213
  358.1 0.7 copy-done.11
  358.8 72.1 %shard_map.362 = (f32[1024,640]{1,0:T(8,128)}, f32[256,1024]{1,0:T(8,128)S(1)}) custom-call(f32[8,128]{1,0:T(8,128)S(1)} %copy-done.11, f32[512,1024]{1,0:T(8,128)} %get-tuple-element.130.attend_out_any.refs_0_, f32[512,1024]{1,0:T(8,128)} %get-tuple-element.129.expand_any.refs_1_, f32[512,1024]{1,0:T(8,128)} %get-tuple-element.126.reduce_any.refs_2_, ...), custom_call_target="tpu_custom_call" | custom-call | flops 3221225472 | bytes 83886080 | tf_op jit(solution)/shard_map/pallas_call | solution.py:520
  430.8 0.0 copy-start.6
  430.9 0.0 copy-start.29
  430.9 0.0 copy-start.31
  430.9 1.1 slice.40
  432.0 1.4 collective-permute-start.2
  433.4 0.6 collective-permute-start.3
  434.0 1.7 copy-done.14
  435.8 74.1 %shard_map.363.q_ref = f32[1024,640]{1,0:T(8,128)S(1)} custom-call(f32[1024,640]{1,0:T(8,128)S(1)} %copy-done.14), custom_call_target="tpu_custom_call" | custom-call | flops 109521666048 | bytes 8388608 | tf_op jit(solution)/shard_map/pallas_call | solution.py:642
  509.9 1.5 copy-done.4
  511.4 1.2 slice.39
  513.3 1.4 divide_subtract_fusion.2
  514.7 1.7 divide_subtract_fusion
  516.4 0.0 copy-start.26
  516.4 0.9 copy-done.27
  517.4 0.7 copy-done.26
  518.1 47.2 %shard_map.364 = (f32[4,1024,640]{2,1,0:T(8,128)}, f32[3,1024,256]{2,1,0:T(8,128)}, f32[256,1024]{1,0:T(8,128)}, f32[1024,1024]{1,0:T(8,128)}, f32[1024,1024]{1,...) custom-call(f32[8,128]{1,0:T(8,128)} %get-tuple-element.123.norm_ref, ...), custom_call_target="tpu_custom_call" | custom-call | flops 9663676416 | bytes 83886080 | tf_op jit(solution)/shard_map/pallas_call | solution.py:889
  565.3 31.6 %shard_map.365 = (f32[3,1024,256]{2,1,0:T(8,128)}, f32[256,1024]{1,0:T(8,128)}, f32[1024,1024]{1,0:T(8,128)}, f32[1024,1024]{1,0:T(8,128)}, f32[3,1024,256]{2,1,...) custom-call(f32[4,1024,640]{2,1,0:T(8,128)} %get-tuple-element.136.bands_any, ...), custom_call_target="tpu_custom_call" | custom-call | flops 9663676416 | bytes 62914560 | tf_op jit(solution)/shard_map/pallas_call | solution.py:982
  597.0 1.3 copy.46
  598.3 1.0 copy-done.23
  599.3 1.3 copy.47
  (49 shorter events, 0.1 us)
Async XLA Ops:
  0.7 27.4 %collective-permute-start = (f32[256,1024]{1,0:T(8,128)}, f32[256,1024]{1,0:T(8,128)}, u32[]{:S(2)}, u32[]{:S(2)}) collective-permute-start(f32[256,1024]{1,0:T(8,128)} %refs_17_.1), channel_id=1, source_target_pairs={{0,2},{1,3},{2,0},{3,1},{4,6},{5,7},{6,4},{7,5},{8,10},{9,11},{10,... | collective-permute-start | bytes 3145736 | tf_op jit(solution)/shard_map/ppermute | solution.py:81
  5.7 9.9 %copy-start.9 = (f32[1,1024]{1,0:T(1,128)}, f32[1,1024]{1,0:T(1,128)S(1)}, u32[]{:S(2)}) copy-start(f32[1,1024]{1,0:T(1,128)S(1)} %get-tuple-element.178.scale_ref) | copy-start | bytes 12292
  5.7 9.9 %copy-start.10 = (f32[1,1024]{1,0:T(1,128)}, f32[1,1024]{1,0:T(1,128)S(1)}, u32[]{:S(2)}) copy-start(f32[1,1024]{1,0:T(1,128)S(1)} %get-tuple-element.179.shift_ref) | copy-start | bytes 12292
  5.7 25.1 %copy-start.12 = (f32[1,1024]{1,0:T(1,128)}, f32[1,1024]{1,0:T(1,128)S(1)}, u32[]{:S(2)}) copy-start(f32[1,1024]{1,0:T(1,128)S(1)} %get-tuple-element.175.scale_ref) | copy-start | bytes 12292
  5.7 25.1 %copy-start.13 = (f32[1,1024]{1,0:T(1,128)}, f32[1,1024]{1,0:T(1,128)S(1)}, u32[]{:S(2)}) copy-start(f32[1,1024]{1,0:T(1,128)S(1)} %get-tuple-element.177.gate_ref) | copy-start | bytes 12292
  5.7 1.6 copy-start.1
  7.3 0.8 copy-start.7
  8.2 7.5 %copy-start = (f32[1024,3,256]{2,0,1:T(8,128)S(1)}, f32[1024,3,256]{2,0,1:T(8,128)}, u32[]{:S(2)}) copy-start(f32[1024,3,256]{2,0,1:T(8,128)} %param.28) | copy-start | bytes 9437188
  15.6 10.7 %copy-start.5 = (bf16[1024,1024]{1,0:T(8,128)(2,1)}, bf16[1024,1024]{1,0:T(8,128)(2,1)S(1)}, u32[]{:S(2)}) copy-start(bf16[1024,1024]{1,0:T(8,128)(2,1)S(1)} %shard_map.356.mixed_ref) | copy-start | bytes 6291460
  15.6 12.4 %copy-start.22 = (f32[256,1024]{1,0:T(8,128)S(1)}, f32[256,1024]{1,0:T(8,128)}, u32[]{:S(2)}) copy-start(f32[256,1024]{1,0:T(8,128)} %refs_17_.1) | copy-start | bytes 3145732
  26.3 1.1 copy-start.18
  27.4 0.6 copy-start.20
  28.1 2.7 copy-start.19
  28.1 2.7 copy-start.17
  28.1 3.0 copy-start.2
  59.6 2.0 copy-start.15
  61.6 1.3 copy-start.16
  167.6 125.0 %collective-permute-start.1 = (f32[512,1024]{1,0:T(8,128)}, f32[512,1024]{1,0:T(8,128)S(1)}, u32[]{:S(2)}, u32[]{:S(2)}) collective-permute-start(f32[512,1024]{1,0:T(8,128)} %get-tuple-element.99.ffn_half_any), channel_id=1, source_target_pairs={{0,2},{1,3},{2,0},{3,1},{4,6},{5,7},{6,4},{7,5},{8,10},{9,11},{10,... | collective-permute-start | bytes 6291464 | tf_op jit(solution)/shard_map/ppermute | solution.py:81
  292.6 2.0 copy-start.25
  292.6 223.9 %collective-permute-start.4 = (f32[512,1024]{1,0:T(8,128)}, f32[512,1024]{1,0:T(8,128)}, u32[]{:S(2)}, u32[]{:S(2)}) collective-permute-start(f32[512,1024]{1,0:T(8,128)} %get-tuple-element.126.reduce_any.refs_2_), channel_id=1, source_target_pairs={{0,4},{4,0},{8,12},{12,8},{16,20},{20,16},{24,28},{28,24},{1,5},{5... | collective-permute-start | bytes 6291464 | tf_op jit(solution)/shard_map/ppermute | solution.py:81
  294.5 63.5 %copy-start.3 = (f32[256,1024]{1,0:T(8,128)S(1)}, f32[256,1024]{1,0:T(8,128)}, u32[]{:S(2)}) copy-start(f32[256,1024]{1,0:T(8,128)} %refs_8_.1) | copy-start | bytes 3145732
  358.1 0.7 copy-start.11
  358.8 72.1 %copy-start.21 = (f32[512,1024]{1,0:T(8,128)S(1)}, f32[512,1024]{1,0:T(8,128)}, u32[]{:S(2)}) copy-start(f32[512,1024]{1,0:T(8,128)} %get-tuple-element.129.expand_any.refs_1_) | copy-start | bytes 6291460
  430.8 2.6 copy-start.6
  430.9 82.4 %copy-start.28 = (f32[32,1024]{1,0:T(8,128)S(1)}, f32[32,1024]{1,0:T(8,128)}, u32[]{:S(2)}) copy-start(f32[32,1024]{1,0:T(8,128)} %get-tuple-element.161) | copy-start | bytes 393220
  430.9 82.4 %copy-start.29 = (f32[6,1024]{1,0:T(8,128)S(1)}, f32[6,1024]{1,0:T(8,128)}, u32[]{:S(2)}) copy-start(f32[6,1024]{1,0:T(8,128)} %param.25) | copy-start | bytes 73732
  430.9 82.4 %copy-start.32 = (f32[6,1024]{1,0:T(8,128)S(1)}, f32[6,1024]{1,0:T(8,128)}, u32[]{:S(2)}) copy-start(f32[6,1024]{1,0:T(8,128)} %param.37) | copy-start | bytes 73732
  430.9 83.8 %copy-start.30 = (f32[9,1024]{1,0:T(8,128)S(1)}, f32[9,1024]{1,0:T(8,128)}, u32[]{:S(2)}) copy-start(f32[9,1024]{1,0:T(8,128)} %taps_ref.4) | copy-start | bytes 110596
  430.9 83.8 %copy-start.31 = (f32[9,1024]{1,0:T(8,128)S(1)}, f32[9,1024]{1,0:T(8,128)}, u32[]{:S(2)}) copy-start(f32[9,1024]{1,0:T(8,128)} %param.41) | copy-start | bytes 110596
  432.0 82.7 %copy-start.8 = (f32[9,1024]{1,0:T(8,128)S(1)}, f32[9,1024]{1,0:T(8,128)}, u32[]{:S(2)}) copy-start(f32[9,1024]{1,0:T(8,128)} %taps_ref.5) | copy-start | bytes 110596
  432.0 84.4 %collective-permute-start.2 = (f32[256,1024]{1,0:T(8,128)}, f32[256,1024]{1,0:T(8,128)S(1)}, u32[]{:S(2)}, u32[]{:S(2)}) collective-permute-start(f32[256,1024]{1,0:T(8,128)} %slice.40), channel_id=1, source_target_pairs={{0,4},{4,0},{8,12},{12,8},{16,20},{20,16},{24,28},{28,24},{1,5},{5... | collective-permute-start | bytes 3145736 | tf_op jit(solution)/shard_map/ppermute | solution.py:81
  433.4 83.0 %collective-permute-start.3 = (f32[512,1024]{1,0:T(8,128)}, f32[512,1024]{1,0:T(8,128)S(1)}, u32[]{:S(2)}, u32[]{:S(2)}) collective-permute-start(f32[512,1024]{1,0:T(8,128)} %get-tuple-element.130.attend_out_any.refs_0_), channel_id=1, source_target_pairs={{0,4},{4,0},{8,12},{12,8},{16,20},{20,16},{24,28},{28,24},{1,5},{5... | collective-permute-start | bytes 6291464 | tf_op jit(solution)/shard_map/ppermute | solution.py:81
  434.0 1.7 copy-start.14
  509.9 1.5 copy-start.4
  516.4 1.0 copy-start.27
  516.4 1.7 copy-start.26
  565.3 31.6 %copy-start.24 = (bf16[1024,1024]{1,0:T(8,128)(2,1)S(1)}, bf16[1024,1024]{1,0:T(8,128)(2,1)}, u32[]{:S(2)}) copy-start(bf16[1024,1024]{1,0:T(8,128)(2,1)} %get-tuple-element.121) | copy-start | bytes 6291460
  596.9 2.3 copy-start.23

commit v8 on v7

--- a/solution.py
+++ b/solution.py
@@ -189,7 +189,10 @@
         self.own, self.spot_of, self.hops = own, spot_of, hops
         self.sends, self.arrivals, self.base = sends, arrivals, base
         self.copies = {}
-        self.order = sorted(range(2 ** len(hops)), key=lambda item: (bin(item).count("1"), item))
+        last = 2 ** (len(hops) - 1)
+        self.order = sorted(
+            range(2 * last), key=lambda item: (item >= last, bin(item).count("1"), -item)
+        )
 
     def step(self, item):
         if item:
@@ -944,16 +947,18 @@
         matrices.move(ready[k], news[k], news_sems.at[k], k, True)
     for index in range(2):
         whole_of(bands.at[index], band_sems.at[index]).wait()
-        for k in range(MATRICES):
-            if index == 0:
+        if index:
+            for k in range(MATRICES):
                 whole_of(news[k], news_sems.at[k]).wait()
                 matrices.move(carried[k], news[k], carried_sems.at[k], k, False)
         for side in range(2):
 
             @pl.when(far == side)
             def _(k=2 * (1 - side) + index, done=2 * side + index):
-                whole_of(values[done], value_sems.at[done]).wait()
-                matrices.move(results[done], values[done], out_sems.at[done], done, False)
+                if index:
+                    for late in (done - 1, done):
+                        whole_of(values[late], value_sems.at[late]).wait()
+                        matrices.move(results[late], values[late], out_sems.at[late], late, False)
                 assemble(bands.at[index], factor_high, factor_low)
                 whole_of(highs[k], split_sems.at[2 * index]).wait()
                 whole_of(lows[k], split_sems.at[2 * index + 1]).wait()
@@ -1563,9 +1568,12 @@
     gate_ref,
     shift_ref,
     scale_ref,
+    branch_any,
+    hidden_any,
+    entry_ref,
     branch_ref,
     hidden_ref,
-    entry_ref,
+    out_sems,
     slots,
     output_low,
     output_inbox,
@@ -1597,6 +1605,7 @@
         jnp.bfloat16
     )
     gate, offset, stretch = gate_ref[...], shift_ref[...], 1.0 + scale_ref[...]
+    outs = []
     for p in range(pieces):
         for item in gathers[p].order[1:]:
             gathers[p].step(item)
@@ -1619,9 +1628,18 @@
             return carry
 
         lax.fori_loop(0, step // SLAB, one, 0, unroll=UNROLL)
+        for index, (src, dst) in enumerate(((branch_ref, branch_any), (hidden_ref, hidden_any))):
+            outs.append(
+                pltpu.make_async_copy(
+                    src.at[chunk(p), :], dst.at[chunk(p), :], out_sems.at[2 * p + index]
+                )
+            )
+            outs[-1].start()
     for gather in gathers:
         gather.finish()
     output_copy.wait_send()
+    for out in outs:
+        out.wait()
 
 
 def enter(context, tokens, output_rows, gate, shift, scale, number):
@@ -1639,8 +1657,11 @@
             jax.ShapeDtypeStruct((rows, width), jnp.bfloat16),
         ),
         in_specs=[vmem] * 6,
-        out_specs=(vmem,) * 3,
+        out_specs=(pl.BlockSpec(memory_space=pl.ANY),) * 2 + (vmem,),
         scratch_shapes=[
+            pltpu.VMEM((rows, width), jnp.float32),
+            pltpu.VMEM((rows, width), jnp.float32),
+            pltpu.SemaphoreType.DMA((2 * pieces,)),
             pltpu.VMEM((count, rows, own), jnp.float32),
             pltpu.VMEM((width, width), jnp.bfloat16),
             pltpu.VMEM(output_rows.shape, jnp.float32),
@@ -1715,6 +1736,10 @@
     scatter_beside,
     scatter_inbox,
     scatter_loads,
+    output_held,
+    output_beside,
+    output_inbox,
+    output_loads,
     rest_held,
     rest_beside,
     rest_inbox,
@@ -1810,6 +1835,19 @@
         )
     for ref, total in zip((grad_shift_ref, grad_scale_ref, grad_gate_ref), sums):
         ref[...] = jnp.sum(total, axis=0, keepdims=True)
+    output_grad = branch.at[pl.ds(3 * own, own), :]
+    output_grad[...] = dot_of(context_ref[...], grad_branch[...], 0, 0)
+    output_sum = Scatter(
+        output_grad,
+        output_held,
+        output_beside,
+        output_inbox,
+        sends,
+        arrivals,
+        output_loads,
+        rest_base + rest.count * 2 - 1,
+    )
+    output_sum.start()
     for e in reversed(range(1, rest.count)):
         rest.step(e)
     grad_context[...] = dot_of(grad_branch[...], output_low[...], 1, 1).astype(jnp.bfloat16)
@@ -1842,7 +1880,7 @@
 
         lax.fori_loop(0, tokens // QUERIES, one, 0)
         if head == max(heads - 2, 0):
-            gathers[0].step(1)
+            gathers[0].step(gathers[0].order[1])
             rest.step(0)
             gathers[1].step(0)
             keeps[1].start()
@@ -1851,22 +1889,16 @@
     grad_triple[:, pl.ds(0, own)] = (grad_queries_t[...].T * scale).astype(jnp.bfloat16)
     grad_triple[:, pl.ds(own, own)] = (grad_keys[...] * scale).astype(jnp.bfloat16)
     grad_triple[:, pl.ds(2 * own, own)] = grad_values[...].astype(jnp.bfloat16)
-    mixed_partial, attend_out = grad_entry, branch.at[pl.ds(0, 4 * own), :]
+    mixed_partial, attend_grad = grad_entry, branch.at[pl.ds(0, 3 * own), :]
     mixed_partial[...] = dot_of(grad_triple[...], attend_ref[...], 1, 1)
     narrow = NarrowSum(
         far_bits, pieces, mixed_partial, grad_mixed_any, near, far, held, sends, arrivals, local, 0
     )
     narrow.start()
-    grad_attend = dot_of(grad_triple[...], mixed_ref[...], 0, 0)
-    grad_output = dot_of(context_ref[...], grad_branch[...], 0, 0)
+    attend_grad[...] = dot_of(grad_triple[...], mixed_ref[...], 0, 0)
     blocks = lax.axis_size("wide")
-    first, second = 3 * own // blocks, own // blocks
-    for b in range(blocks):
-        start = b * (first + second)
-        attend_out[pl.ds(start, first), :] = grad_attend[b * first : (b + 1) * first]
-        attend_out[pl.ds(start + first, second), :] = grad_output[b * second : (b + 1) * second]
     scatter = Scatter(
-        attend_out,
+        attend_grad,
         scatter_held,
         scatter_beside,
         scatter_inbox,
@@ -1878,11 +1910,13 @@
     for p in range(pieces):
         narrow.begin(p)
     scatter.start()
+    for e in reversed(range(1, blocks // 2)):
+        output_sum.step(e)
     left = list(reversed(range(blocks // 2)))
     forwards = [(0, item) for item in gathers[0].order[2:]] + [
         (1, item) for item in gathers[1].order[1:]
     ]
-    urgent = [(1, 1)]
+    urgent = [(1, gathers[1].order[1])]
     for b in range(len(far_bits)):
         for p in range(pieces):
             narrow.step(b, p)
@@ -1892,20 +1926,34 @@
             if len(left) > 1:
                 scatter.step(left.pop(0))
     for index, item in forwards:
-        if (index, item) != (1, 1):
+        if (index, item) != (1, gathers[1].order[1]):
             gathers[index].step(item)
     while left:
         scatter.step(left.pop(0))
-    out = pltpu.make_async_copy(scatter.held.at[0], attend_out_share, scatter.local.at[0])
-    out.start()
+    output_sum.step(0)
+    first = 3 * own // blocks
+    outs = [
+        pltpu.make_async_copy(
+            scatter.held.at[0], attend_out_share.at[pl.ds(0, first), :], scatter.local.at[0]
+        ),
+        pltpu.make_async_copy(
+            output_sum.held.at[0],
+            attend_out_share.at[pl.ds(first, own // blocks), :],
+            output_sum.local.at[0],
+        ),
+    ]
+    for out in outs:
+        out.start()
     narrow.finish()
     scatter.finish()
+    output_sum.finish()
     rest.finish()
     for gather in gathers:
         gather.finish()
     for keep in keeps:
         keep.wait()
-    out.wait()
+    for out in outs:
+        out.wait()
 
 
 def back(
@@ -1932,7 +1980,7 @@
     pieces = 4
     line = lax.axis_size("wide") // 2
     narrow_bits = bits_of(lax.axis_size("narrow"))
-    slots = (len(narrow_bits) + 1) * pieces + Scatter.slots() + 2 * (line - 1) + line - 1
+    slots = (len(narrow_bits) + 1) * pieces + 2 * Scatter.slots() + 2 * (line - 1) + line - 1
     block = reduce_share.shape
     vmem = pl.BlockSpec(memory_space=pltpu.VMEM)
     anywhere = pl.BlockSpec(memory_space=pl.ANY)
@@ -1969,7 +2017,8 @@
             low(tokens, 3 * own),
         ]
         + narrow_scratch((tokens, width), pieces)
-        + scatter_scratch((4 * own, width))
+        + scatter_scratch((3 * own, width))
+        + scatter_scratch((own, width))
         + [
             wide(line // 2, *block),
             wide(line // 2, *block),
@@ -2026,11 +2075,13 @@
     attend_out_ref,
     reduce_ref,
     expand_ref,
+    reduce_line,
     tokens_grad_ref,
     block_out_ref,
     small_ref,
     norm_ref,
     line_ref,
+    reduce_other,
     tokens_ref,
     grad_mixed_ref,
     grad_hidden_ref,
@@ -2087,6 +2138,24 @@
 
     gather = Gather(attend_out_ref, spot_of, hops, sends, arrivals, count + len(narrow_bits))
     gather.step(0)
+    across = []
+
+    def cross(part):
+        extent = reduce_line.shape[0] // 2
+        spot = pl.ds(part * extent, extent)
+        slot = sends.shape[0] - 2 + part
+        across.append(
+            send(
+                reduce_line.at[spot, :],
+                reduce_other.at[spot, :],
+                sends,
+                arrivals,
+                slot,
+                place_at("wide", 1),
+            )
+        )
+
+    cross(0)
     keep = pltpu.make_async_copy(attend_out_ref, spot_of(0), keep_sems.at[0])
     keep.start()
     loads[0].wait()
@@ -2112,6 +2181,7 @@
         loads[3].wait,
         loads[5].wait,
     )
+    gather.step(gather.order[1])
     ffn_copy.wait_recv()
     loads[4].wait()
     gate, live = gate_ref[...], live_ref[...]
@@ -2151,7 +2221,7 @@
         )
         copies.append(copy)
         if b == 0:
-            gather.step(1)
+            cross(1)
             loads[6].wait()
             lax.fori_loop(0, ffn.shape[0] // SLAB, leave, 0, unroll=UNROLL)
         copy.wait_recv()
@@ -2176,6 +2246,8 @@
     keep.wait()
     gather.finish()
     ffn_copy.wait_send()
+    for copy in across:
+        copy.wait()
     for copy in copies:
         copy.wait_send()
 
@@ -2196,6 +2268,7 @@
     table_rows,
     split_rows,
     shares,
+    reduce_line,
     number,
 ):
     rows, width = tokens.shape
@@ -2203,7 +2276,7 @@
     narrow_bits = bits_of(lax.axis_size("narrow"))
     count = len(wide_bits)
     line = lax.axis_size("wide") // 2
-    total = count + len(narrow_bits) + line
+    total = count + len(narrow_bits) + line + 2
     small = -(-(6 + taps.shape[0] + split_rows.shape[0] + 1) // 8) * 8
     vmem = pl.BlockSpec(memory_space=pltpu.VMEM)
     anywhere = pl.BlockSpec(memory_space=pl.ANY)
@@ -2218,9 +2291,10 @@
             f32(small, width),
             f32(8, LANES),
             f32(line * shares[0].shape[0], width),
-        ),
-        in_specs=[anywhere] + [vmem] * 3 + [anywhere] * 6 + [vmem] * 7,
-        out_specs=(vmem,) * 4 + (anywhere,),
+            f32(*reduce_line.shape),
+        ),
+        in_specs=[anywhere] + [vmem] * 3 + [anywhere] * 6 + [vmem] * 7 + [anywhere],
+        out_specs=(vmem,) * 4 + (anywhere,) * 2,
         scratch_shapes=[
             pltpu.VMEM((rows, width), jnp.bfloat16),
             wide(rows, width),
@@ -2265,6 +2339,7 @@
         table_rows,
         split_rows,
         *shares,
+        reduce_line,
     )
 
 
@@ -2355,15 +2430,12 @@
         expand_give,
         3,
     )
-    ffn_across, grad_mixed, reduce_line, attend_out_share = together(
-        ffn_across, grad_mixed, reduce_line, attend_out_share
-    )
-    reduce_other = permute(reduce_line, "wide", 1)
+    ffn_across, grad_mixed = together(ffn_across, grad_mixed)
     shared_rows = modulation_table.shape[0] + mixer_kernel.shape[0]
     hidden_rows = -(-grad_hidden_kernel.size // width)
     padding = hidden_rows * width - grad_hidden_kernel.size
     hidden_flat = jnp.pad(grad_hidden_kernel.reshape(-1), (0, padding))
-    tokens_gradient, block_out, small, norm, attend_out_line = tail(
+    tokens_gradient, block_out, small, norm, attend_out_line, reduce_other = tail(
         flat_tokens,
         shift_one[0],
         scale_one[0],
@@ -2379,6 +2451,7 @@
         jnp.concatenate([grad_gate_one, grad_shift_two, grad_scale_two], axis=0),
         hidden_flat.reshape(hidden_rows, width),
         [attend_out_share, reduce_share, expand_share],
+        reduce_line,
         4,
     )
     tokens_gradient = tokens_gradient.reshape(tokens.shape)
@@ -2399,9 +2472,7 @@
     expand_other = permute(expand_line[expand_line.shape[0] // 2 :], "wide", 1)
     attend_out_other = permute(attend_out_line, "wide", 1)
     factor = polar_factor(gramian)
-    factor, expand_other, attend_out_other, reduce_other = together(
-        factor, expand_other, attend_out_other, reduce_other
-    )
+    factor, expand_other, attend_out_other = together(factor, expand_other, attend_out_other)
     weights = [three(attend_weight), output_weight, expand_weight, reduce_weight]
     bands, ready, fresh, highs, lows = spread(
         norm,

time: 608 us -> 594 us (0.977)
  the two profiles are of different devices: /device:TPU:0 before, /device:TPU:13 now
where the time goes in v8:
time: 594 us; the launch traced here: 586 us
  Pallas kernels  550 us (93%)
  local copies, waits for them, and re-layouts  21.8 us (4%)
  other arithmetic  7.9 us (1%)
    pallas_call x1, Pallas kernels, back(): pl.pallas_call(functools.partial(back_kernel, pieces), out_shape=(f32(tok...  127 us
    pallas_call x1, Pallas kernels, middle(): pl.pallas_call(functools.partial(middle_kernel, pieces), out_shape=(f32(t...  99 us
    pallas_call x1, Pallas kernels, polar_factor(): pl.pallas_call(polar_kernel, out_shape=jax.ShapeDtypeStruct(gramian.shape...  74.1 us
    pallas_call x1, Pallas kernels, gram_whole(): pl.pallas_call(gram_kernel, out_shape=(jax.ShapeDtypeStruct((size, band),...  72.6 us
    pallas_call x1, Pallas kernels, tail(): pl.pallas_call(tail_kernel, out_shape=(low(rows, width), low(rows, width)...  53.3 us
    pallas_call x1, Pallas kernels, spread(): pl.pallas_call(functools.partial(spread_kernel, sub, pieces), out_shape=t...  50.3 us
    pallas_call x1, Pallas kernels, enter(): pl.pallas_call(functools.partial(entry_kernel, pieces), out_shape=(jax.Sh...  29.6 us
    pallas_call x1, Pallas kernels, finish(): pl.pallas_call(functools.partial(finish_kernel, sub), out_shape=tuple(sha...  26 us
  transfers between devices with their start and end apart: 4, of which 0 were waited for; matrix products, arithmetic and copies ran while one was open for 1% of the time, Pallas kernels for 37%

profile of v8, /device:TPU:13, one launch (start us, length us, event | category | flops | bytes accessed | tf_op | source)
XLA Modules:
  0.0 586.2 jit_solution(4840928515555730579)
XLA Ops:
  0.7 1.3 collective-permute-start
  2.6 0.8 bitcast_add_fusion
  3.4 0.6 slice_bitcast_fusion
  4.0 0.0 copy-start.1
  4.0 1.6 copy-done.1
  5.6 0.8 copy-done.7
  6.4 7.4 %shard_map.356.mixed_ref = bf16[1024,1024]{1,0:T(8,128)(2,1)S(1)} custom-call(bf16[1024,1024]{1,0:T(8,128)(2,1)S(1)} %bitcast.28, f32[1,1024]{1,0:T(1,128)S(1)} %get-tuple-element.175.shift_ref, f32[1,1024]{1,0:T(1,128)S(1)} %get-tuple-element.174.scale_ref, f32[9,1024]{1,0:T(8,128)S(1)} %copy-done.7), custom_call_target="tpu_custom_call" | custom-call | flops 41943040 | bytes 4194304 | tf_op jit(solution)/shard_map/pallas_call | solution.py:1391
  13.9 0.0 copy-start.5
  13.9 0.0 copy-start.22
  13.9 10.7 %shard_map.357 = (bf16[1024,768]{1,0:T(8,128)(2,1)S(1)}, bf16[1024,256]{1,0:T(8,128)(2,1)S(1)}, f32[8,1024]{1,0:T(8,128)S(1)}, bf16[1024,768]{1,0:T(8,128)(2,1)S(1)}) custom-call(bf16[1024,1024]{1,0:T(8,128)(2,1)S(1)} %shard_map.356.mixed_ref, f32[3,1024,256]{2,1,0:T(8,128)S(1)} %bitcast.26), custom_call_target="tpu_custom_call" | custom-call | flops 4294967296 | bytes 12582912 | tf_op jit(solution)/shard_map/pallas_call | solution.py:1525
  24.6 0.0 copy-start.18
  24.6 1.1 copy-done.18
  25.8 0.6 copy-done.20
  26.4 2.7 maximum_select_fusion.output_ref
  29.1 0.2 copy-done.2
  29.4 29.6 %shard_map.358 = (f32[1024,1024]{1,0:T(8,128)S(1)}, f32[1024,1024]{1,0:T(8,128)}, bf16[1024,1024]{1,0:T(8,128)(2,1)S(1)}) custom-call(bf16[1024,256]{1,0:T(8,128)(2,1)S(1)} %get-tuple-element.90.context_ref, bf16[1024,1024]{1,0:T(8,128)(2,1)S(1)} %bitcast.29, f32[512,1024]{1,0:T(8,128)S(1)} %maximum_select_fusion.output_ref, ...), custom_call_target="tpu_custom_call" | custom-call | flops 2147483648 | bytes 104857600 | tf_op jit(solution)/shard_map/pallas_call | solution.py:1652
  59.0 0.0 copy-start.15
  59.0 2.0 copy-done.15
  61.0 1.3 copy-done.16
  62.3 0.6 broadcast_in_dim.12.live_ref
  62.9 99.0 %shard_map.359 = (f32[512,1024]{1,0:T(8,128)}, f32[1024,1024]{1,0:T(8,128)}, f32[128,1024]{1,0:T(8,128)}, f32[2,128,1024]{2,1,0:T(8,128)}, f32[2,128,1024]{2,1,0:T(8,128)}, /*index=5*/f32[9,1024]{1,0:T(8,128)}) custom-call(bf16[1024,1024]{1,0:T(8,128)(2,1)} %copy-done.16, bf16[1024,1024]{1,0:T(8,128)(2,1)} %bitcast.32, f32[1,1024]{1,0:T(1,128)} %broadcast_in_dim.12.live_ref, ...), custom_call_target="tpu_custom_call" | custom-call | flops 12884901888 | bytes 209715200 | tf_op jit(solution)/shard_map/pallas_call | solution.py:1306
  161.9 0.6 collective-permute-start.1
  162.5 126.7 %shard_map.360 = (f32[1024,1024]{1,0:T(8,128)}, f32[1,1024]{1,0:T(1,128)}, f32[1,1024]{1,0:T(1,128)}, f32[1,1024]{1,0:T(1,128)}, f32[1024,1024]{1,0:T(8,128)}, /...) custom-call(f32[1024,1024]{1,0:T(8,128)} %get-tuple-element.98.hidden_any, ...), custom_call_target="tpu_custom_call" | custom-call | flops 10737418240 | bytes 157286400 | tf_op jit(solution)/shard_map/pallas_call | solution.py:1990
  289.3 1.3 pad_maximum_fusion.rows_ref
  290.6 1.3 copy-done.23
  291.9 53.3 %shard_map.361 = (bf16[1024,1024]{1,0:T(8,128)(2,1)}, bf16[1024,1024]{1,0:T(8,128)(2,1)}, f32[32,1024]{1,0:T(8,128)}, f32[8,128]{1,0:T(8,128)}, f32[512,1024]{1,0:T(8,128)}, /*index=5*/f32[512,1024]{1,0:T(8,128)}) custom-call(bf16[1024,1024]{1,0:T(8,128)(2,1)} %bitcast.27, f32[1,1024]{1,0:T(1,128)} %copy-done.10, f32[1,1024]{1,0:T(1,128)} %copy-done.9, ...), custom_call_target="tpu_custom_call" | custom-call | flops 104857600 | bytes 62914560 | tf_op jit(solution)/shard_map/pallas_call | solution.py:2286
  345.2 0.7 copy-done.11
  345.9 72.6 %shard_map.362 = (f32[1024,640]{1,0:T(8,128)}, f32[256,1024]{1,0:T(8,128)S(1)}) custom-call(f32[8,128]{1,0:T(8,128)S(1)} %copy-done.11, f32[512,1024]{1,0:T(8,128)} %get-tuple-element.126.attend_out_any.refs_0_, f32[512,1024]{1,0:T(8,128)} %get-tuple-element.125.expand_any.refs_1_, f32[512,1024]{1,0:T(8,128)} %get-tuple-element.117.reduce_line.reduce_any.refs_2_, ...), custom_call_target="tpu_custom_call" | custom-call | flops 3221225472 | bytes 83886080 | tf_op jit(solution)/shard_map/pallas_call | solution.py:523
  418.5 0.0 copy-start.6
  418.5 0.0 copy-start.29
  418.5 0.0 copy-start.32
  418.6 1.1 slice.40
  419.6 2.2 collective-permute-start.2
  421.9 0.1 collective-permute-start.3
  422.0 1.7 copy-done.14
  423.7 74.1 %shard_map.363.q_ref = f32[1024,640]{1,0:T(8,128)S(1)} custom-call(f32[1024,640]{1,0:T(8,128)S(1)} %copy-done.14), custom_call_target="tpu_custom_call" | custom-call | flops 109521666048 | bytes 8388608 | tf_op jit(solution)/shard_map/pallas_call | solution.py:645
  497.8 0.0 copy-start.4
  497.8 1.5 copy-done.4
  499.3 1.2 slice.39
  501.2 1.4 divide_subtract_fusion.2
  502.7 1.7 divide_subtract_fusion
  504.4 1.0 copy-done.27
  505.3 0.7 copy-done.26
  506.0 50.3 %shard_map.364 = (f32[4,1024,640]{2,1,0:T(8,128)}, f32[3,1024,256]{2,1,0:T(8,128)}, f32[256,1024]{1,0:T(8,128)}, f32[1024,1024]{1,0:T(8,128)}, f32[1024,1024]{1,...) custom-call(f32[8,128]{1,0:T(8,128)} %get-tuple-element.120.norm_ref, ...), custom_call_target="tpu_custom_call" | custom-call | flops 9663676416 | bytes 83886080 | tf_op jit(solution)/shard_map/pallas_call | solution.py:892
  556.4 26.0 %shard_map.365 = (f32[3,1024,256]{2,1,0:T(8,128)}, f32[256,1024]{1,0:T(8,128)}, f32[1024,1024]{1,0:T(8,128)}, f32[1024,1024]{1,0:T(8,128)}, f32[3,1024,256]{2,1,...) custom-call(f32[4,1024,640]{2,1,0:T(8,128)} %get-tuple-element.132.bands_any, ...), custom_call_target="tpu_custom_call" | custom-call | flops 9663676416 | bytes 62914560 | tf_op jit(solution)/shard_map/pallas_call | solution.py:987
  582.4 1.3 copy.46
  583.7 1.0 copy-done.24
  584.7 1.3 copy.47
  (47 shorter events, 0.1 us)
Async XLA Ops:
  0.7 25.7 %collective-permute-start = (f32[256,1024]{1,0:T(8,128)}, f32[256,1024]{1,0:T(8,128)}, u32[]{:S(2)}, u32[]{:S(2)}) collective-permute-start(f32[256,1024]{1,0:T(8,128)} %refs_17_.1), channel_id=1, source_target_pairs={{0,2},{1,3},{2,0},{3,1},{4,6},{5,7},{6,4},{7,5},{8,10},{9,11},{10,... | collective-permute-start | bytes 3145736 | tf_op jit(solution)/shard_map/ppermute | solution.py:81
  4.0 9.9 %copy-start.9 = (f32[1,1024]{1,0:T(1,128)}, f32[1,1024]{1,0:T(1,128)S(1)}, u32[]{:S(2)}) copy-start(f32[1,1024]{1,0:T(1,128)S(1)} %get-tuple-element.174.scale_ref) | copy-start | bytes 12292
  4.0 9.9 %copy-start.10 = (f32[1,1024]{1,0:T(1,128)}, f32[1,1024]{1,0:T(1,128)S(1)}, u32[]{:S(2)}) copy-start(f32[1,1024]{1,0:T(1,128)S(1)} %get-tuple-element.175.shift_ref) | copy-start | bytes 12292
  4.0 25.1 %copy-start.12 = (f32[1,1024]{1,0:T(1,128)}, f32[1,1024]{1,0:T(1,128)S(1)}, u32[]{:S(2)}) copy-start(f32[1,1024]{1,0:T(1,128)S(1)} %get-tuple-element.171.scale_ref) | copy-start | bytes 12292
  4.0 25.1 %copy-start.13 = (f32[1,1024]{1,0:T(1,128)}, f32[1,1024]{1,0:T(1,128)S(1)}, u32[]{:S(2)}) copy-start(f32[1,1024]{1,0:T(1,128)S(1)} %get-tuple-element.173.gate_ref) | copy-start | bytes 12292
  4.0 1.6 copy-start.1
  5.6 0.8 copy-start.7
  6.4 7.5 %copy-start = (f32[1024,3,256]{2,0,1:T(8,128)S(1)}, f32[1024,3,256]{2,0,1:T(8,128)}, u32[]{:S(2)}) copy-start(f32[1024,3,256]{2,0,1:T(8,128)} %param.28) | copy-start | bytes 9437188
  13.9 10.7 %copy-start.5 = (bf16[1024,1024]{1,0:T(8,128)(2,1)}, bf16[1024,1024]{1,0:T(8,128)(2,1)S(1)}, u32[]{:S(2)}) copy-start(bf16[1024,1024]{1,0:T(8,128)(2,1)S(1)} %shard_map.356.mixed_ref) | copy-start | bytes 6291460
  13.9 12.5 %copy-start.22 = (f32[256,1024]{1,0:T(8,128)S(1)}, f32[256,1024]{1,0:T(8,128)}, u32[]{:S(2)}) copy-start(f32[256,1024]{1,0:T(8,128)} %refs_17_.1) | copy-start | bytes 3145732
  24.6 1.1 copy-start.18
  25.8 0.6 copy-start.20
  26.4 2.7 copy-start.19
  26.4 2.7 copy-start.17
  26.4 3.0 copy-start.2
  59.0 2.0 copy-start.15
  61.0 1.3 copy-start.16
  161.9 128.6 %collective-permute-start.1 = (f32[512,1024]{1,0:T(8,128)}, f32[512,1024]{1,0:T(8,128)S(1)}, u32[]{:S(2)}, u32[]{:S(2)}) collective-permute-start(f32[512,1024]{1,0:T(8,128)} %get-tuple-element.97.ffn_half_any), channel_id=1, source_target_pairs={{0,2},{1,3},{2,0},{3,1},{4,6},{5,7},{6,4},{7,5},{8,10},{9,11},{10,... | collective-permute-start | bytes 6291464 | tf_op jit(solution)/shard_map/ppermute | solution.py:81
  290.6 1.3 copy-start.23
  291.9 53.3 %copy-start.3 = (f32[256,1024]{1,0:T(8,128)S(1)}, f32[256,1024]{1,0:T(8,128)}, u32[]{:S(2)}) copy-start(f32[256,1024]{1,0:T(8,128)} %refs_8_.1) | copy-start | bytes 3145732
  345.2 0.7 copy-start.11
  345.9 72.6 %copy-start.21 = (f32[512,1024]{1,0:T(8,128)S(1)}, f32[512,1024]{1,0:T(8,128)}, u32[]{:S(2)}) copy-start(f32[512,1024]{1,0:T(8,128)} %get-tuple-element.125.expand_any.refs_1_) | copy-start | bytes 6291460
  418.5 3.4 copy-start.6
  418.5 82.7 %copy-start.28 = (f32[32,1024]{1,0:T(8,128)S(1)}, f32[32,1024]{1,0:T(8,128)}, u32[]{:S(2)}) copy-start(f32[32,1024]{1,0:T(8,128)} %get-tuple-element.157) | copy-start | bytes 393220
  418.5 82.7 %copy-start.29 = (f32[6,1024]{1,0:T(8,128)S(1)}, f32[6,1024]{1,0:T(8,128)}, u32[]{:S(2)}) copy-start(f32[6,1024]{1,0:T(8,128)} %param.25) | copy-start | bytes 73732
  418.5 82.7 %copy-start.32 = (f32[6,1024]{1,0:T(8,128)S(1)}, f32[6,1024]{1,0:T(8,128)}, u32[]{:S(2)}) copy-start(f32[6,1024]{1,0:T(8,128)} %param.37) | copy-start | bytes 73732
  418.5 84.1 %copy-start.30 = (f32[9,1024]{1,0:T(8,128)S(1)}, f32[9,1024]{1,0:T(8,128)}, u32[]{:S(2)}) copy-start(f32[9,1024]{1,0:T(8,128)} %taps_ref.4) | copy-start | bytes 110596
  418.5 84.1 %copy-start.31 = (f32[9,1024]{1,0:T(8,128)S(1)}, f32[9,1024]{1,0:T(8,128)}, u32[]{:S(2)}) copy-start(f32[9,1024]{1,0:T(8,128)} %param.41) | copy-start | bytes 110596
  419.6 83.0 %copy-start.8 = (f32[9,1024]{1,0:T(8,128)S(1)}, f32[9,1024]{1,0:T(8,128)}, u32[]{:S(2)}) copy-start(f32[9,1024]{1,0:T(8,128)} %taps_ref.5) | copy-start | bytes 110596
  419.6 84.7 %collective-permute-start.2 = (f32[256,1024]{1,0:T(8,128)}, f32[256,1024]{1,0:T(8,128)S(1)}, u32[]{:S(2)}, u32[]{:S(2)}) collective-permute-start(f32[256,1024]{1,0:T(8,128)} %slice.40), channel_id=1, source_target_pairs={{0,4},{4,0},{8,12},{12,8},{16,20},{20,16},{24,28},{28,24},{1,5},{5... | collective-permute-start | bytes 3145736 | tf_op jit(solution)/shard_map/ppermute | solution.py:81
  421.9 82.5 %collective-permute-start.3 = (f32[512,1024]{1,0:T(8,128)}, f32[512,1024]{1,0:T(8,128)S(1)}, u32[]{:S(2)}, u32[]{:S(2)}) collective-permute-start(f32[512,1024]{1,0:T(8,128)} %get-tuple-element.126.attend_out_any.refs_0_), channel_id=1, source_target_pairs={{0,4},{4,0},{8,12},{12,8},{16,20},{20,16},{24,28},{28,24},{1,5},{5... | collective-permute-start | bytes 6291464 | tf_op jit(solution)/shard_map/ppermute | solution.py:81
  422.0 1.7 copy-start.14
  497.8 1.5 copy-start.4
  504.4 1.0 copy-start.27
  504.4 1.7 copy-start.26
  556.4 26.0 %copy-start.25 = (bf16[1024,1024]{1,0:T(8,128)(2,1)S(1)}, bf16[1024,1024]{1,0:T(8,128)(2,1)}, u32[]{:S(2)}) copy-start(bf16[1024,1024]{1,0:T(8,128)(2,1)} %get-tuple-element.118) | copy-start | bytes 6291460
  582.4 2.3 copy-start.24

commit v9 on v8

--- a/solution.py
+++ b/solution.py
@@ -311,6 +311,7 @@
     reduce_moment_any,
     band_ref,
     expand_beside,
+    expand_later,
     attend_out,
     expand,
     reduce,
@@ -433,9 +434,11 @@
 
     cut(0, attend_blend)
     multiply(0)
+    loads[3].wait()
+    later_copy = pltpu.make_async_copy(expand.at[pl.ds(early, early), :], expand_later, load_sems.at[3])
+    later_copy.start()
     cut(1, output_moment)
     multiply(1)
-    loads[3].wait()
     loads[4].wait()
     for at in range(0, expand.shape[0], LANES):
         spot = pl.ds(at, LANES)
@@ -500,6 +503,7 @@
     keep.wait()
     gather.finish()
     expand_copy.wait()
+    later_copy.wait()
     for copy in copies:
         copy.wait_send()
 
@@ -525,9 +529,10 @@
         out_shape=(
             jax.ShapeDtypeStruct((size, band), jnp.float32),
             jax.ShapeDtypeStruct((lines[1].shape[0] // 2, size), jnp.float32),
+            jax.ShapeDtypeStruct((lines[1].shape[0] // 2, size), jnp.float32),
         ),
         in_specs=[vmem] + [anywhere] * 7,
-        out_specs=(anywhere, anywhere),
+        out_specs=(anywhere,) * 3,
         scratch_shapes=[
             wide(*lines[0].shape),
             wide(*lines[1].shape),
@@ -921,9 +926,13 @@
     return outs[0], outs[1:5], outs[5:9], outs[9:13], outs[13:17]
 
 
-def finish_kernel(sub, bands_any, *refs):
+def finish_kernel(sub, norm_ref, small_ref, hidden_sum_ref, *refs):
+    adam_ins, passing, refs = refs[:9], refs[9:11], refs[11:]
+    bands_any, refs = refs[0], refs[1:]
     ready, fresh, high_ins, low_ins, weights = (refs[4 * i : 4 * i + 4] for i in range(5))
     carried, results, refs = refs[20:24], refs[24:28], refs[28:]
+    adam_outs, passed, refs = refs[:9], refs[9:11], refs[11:]
+    held, pass_in, pass_out, refs = refs[:2], refs[2], refs[3], refs[4:]
     bands, factor_high, factor_low = refs[:3]
     news, values, highs, lows = refs[3:7], refs[7:11], refs[11:15], refs[15:19]
     news_sems, value_sems, split_sems, band_sems, carried_sems, out_sems = refs[19:]
@@ -945,9 +954,27 @@
 
     for k in range(MATRICES):
         matrices.move(ready[k], news[k], news_sems.at[k], k, True)
+    enters = [
+        pltpu.make_async_copy(passing[i], held[i], pass_in.at[i]) for i in range(2)
+    ]
+    leaves = [
+        pltpu.make_async_copy(held[i], passed[i], pass_out.at[i]) for i in range(2)
+    ]
+    for copy in enters:
+        copy.start()
+    clip = jnp.minimum(1.0, 1.0 / (norm_ref[0:1, 0:1] + 1e-06))
+    first, second = adam_ins[0].shape[0], adam_ins[3].shape[0]
+    sums = (small_ref[0:first, :], small_ref[first : first + second, :], hidden_sum_ref[...])
+    for i, gradient in enumerate(sums):
+        news_of = adam_update(*(ref[...] for ref in adam_ins[3 * i : 3 * i + 3]), clip * gradient)
+        for ref, value in zip(adam_outs[3 * i : 3 * i + 3], news_of):
+            ref[...] = value
     for index in range(2):
         whole_of(bands.at[index], band_sems.at[index]).wait()
         if index:
+            for enter_copy, leave_copy in zip(enters, leaves):
+                enter_copy.wait()
+                leave_copy.start()
             for k in range(MATRICES):
                 whole_of(news[k], news_sems.at[k]).wait()
                 matrices.move(carried[k], news[k], carried_sems.at[k], k, False)
@@ -973,23 +1000,30 @@
 
                 lax.fori_loop(0, size // BLK, one, 0)
 
+    for copy in leaves:
+        copy.wait()
     for k in range(MATRICES):
         whole_of(news[k], carried_sems.at[k]).wait()
         whole_of(values[k], out_sems.at[k]).wait()
 
 
-def finish(bands, ready, fresh, highs, lows, weights):
+def finish(norm, small, hidden_sum, adams, passing, bands, ready, fresh, highs, lows, weights):
     size = bands.shape[1]
     sub = lax.axis_size("narrow") // MATRICES
     anywhere = pl.BlockSpec(memory_space=pl.ANY)
     shapes = [jax.ShapeDtypeStruct(weight.shape, jnp.float32) for weight in weights]
     flat = [(size, 3 * weights[0].shape[2])] + [weight.shape for weight in weights[1:]]
+    vmem = pl.BlockSpec(memory_space=pltpu.VMEM)
+    others = [jax.ShapeDtypeStruct(array.shape, jnp.float32) for array in adams]
+    others += [jax.ShapeDtypeStruct(array.shape, array.dtype) for array in passing]
     outs = pl.pallas_call(
         functools.partial(finish_kernel, sub),
-        out_shape=tuple(shapes + shapes),
-        in_specs=[anywhere] * 21,
-        out_specs=(anywhere,) * 8,
-        scratch_shapes=[
+        out_shape=tuple(shapes + shapes + others),
+        in_specs=[vmem] * 12 + [anywhere] * 23,
+        out_specs=(anywhere,) * 8 + (vmem,) * 9 + (anywhere,) * 2,
+        scratch_shapes=[pltpu.VMEM(array.shape, array.dtype) for array in passing]
+        + [pltpu.SemaphoreType.DMA((2,)), pltpu.SemaphoreType.DMA((2,))]
+        + [
             pltpu.VMEM((2,) + bands.shape[1:], jnp.float32),
             pltpu.VMEM((size, size), jnp.bfloat16),
             pltpu.VMEM((size, size), jnp.bfloat16),
@@ -1001,8 +1035,8 @@
         cost_estimate=pl.CostEstimate(
             flops=9 * size * size * size, bytes_accessed=60 * size * size, transcendentals=0
         ),
-    )(bands, *ready, *fresh, *highs, *lows, *weights)
-    return outs[:4], outs[4:]
+    )(norm, small, hidden_sum, *adams, *passing, bands, *ready, *fresh, *highs, *lows, *weights)
+    return outs[:4], outs[4:8], outs[8:17], outs[17:]
 
 
 def adam_update(weight, moment, square, gradient):
@@ -2454,22 +2488,17 @@
         reduce_line,
         4,
     )
-    tokens_gradient = tokens_gradient.reshape(tokens.shape)
-    block_out = block_out.reshape(tokens.shape)
-    summed_table = small[: modulation_table.shape[0]]
-    summed_mixer = small[modulation_table.shape[0] : shared_rows]
     summed_hidden = small[shared_rows : shared_rows + hidden_rows].reshape(-1)
     summed_hidden = summed_hidden[: hidden_kernel.size].reshape(hidden_kernel.shape)
     gradient_norm = norm[0, 0]
-    clip_factor = jnp.minimum(1.0, 1.0 / (gradient_norm + 1e-06))
-    gramian, expand_first = gram_whole(
+    gramian, expand_first, expand_later = gram_whole(
         norm,
         [attend_out_line, expand_line, reduce_line],
         [three(attend_moment), output_moment, expand_moment, reduce_moment],
         5,
     )
     gramian, expand_line, attend_out_line = together(gramian, expand_line, attend_out_line)
-    expand_other = permute(expand_line[expand_line.shape[0] // 2 :], "wide", 1)
+    expand_other = permute(expand_later, "wide", 1)
     attend_out_other = permute(attend_out_line, "wide", 1)
     factor = polar_factor(gramian)
     factor, expand_other, attend_out_other = together(factor, expand_other, attend_out_other)
@@ -2483,18 +2512,29 @@
         weights,
         6,
     )
-    carried, results = finish(bands, ready, fresh, highs, lows, weights)
+    adams = [modulation_table, table_first, table_second]
+    adams += [mixer_kernel, mixer_first, mixer_second]
+    adams += [hidden_kernel, hidden_first, hidden_second]
+    carried, results, news, passed = finish(
+        norm,
+        small,
+        summed_hidden,
+        adams,
+        [tokens_gradient, block_out],
+        bands,
+        ready,
+        fresh,
+        highs,
+        lows,
+        weights,
+    )
+    table_moment, table_square, table_result = news[:3]
+    mixer_moment, mixer_square, mixer_result = news[3:6]
+    hidden_moment, hidden_square, hidden_result = news[6:]
+    tokens_gradient = passed[0].reshape(tokens.shape)
+    block_out = passed[1].reshape(tokens.shape)
     attend_carried = jnp.transpose(carried[0], (1, 0, 2))
     attend_result = jnp.transpose(results[0], (1, 0, 2))
-    table_moment, table_square, table_result = adam_update(
-        modulation_table, table_first, table_second, clip_factor * summed_table
-    )
-    mixer_moment, mixer_square, mixer_result = adam_update(
-        mixer_kernel, mixer_first, mixer_second, clip_factor * summed_mixer
-    )
-    hidden_moment, hidden_square, hidden_result = adam_update(
-        hidden_kernel, hidden_first, hidden_second, clip_factor * summed_hidden
-    )
     return (
         block_out,
         tokens_gradient,

time: 594 us -> 589 us (level)
    unnamed x68 -> x50, local copies, waits for them, and re-layouts: 18.4 us -> 15.6 us
  transfers between devices with their start and end apart: 4 -> 4, of which waited for: 0 -> 0; matrix products, arithmetic and copies ran while one was open for 1% -> 1% of each run, Pallas kernels for 37% -> 38%
where the time goes in v9:
time: 589 us; the launch traced here: 580 us
  Pallas kernels  551 us (94%)
  local copies, waits for them, and re-layouts  18.6 us (3%)
    pallas_call x1, Pallas kernels, back(): pl.pallas_call(functools.partial(back_kernel, pieces), out_shape=(f32(tok...  126 us
    pallas_call x1, Pallas kernels, middle(): pl.pallas_call(functools.partial(middle_kernel, pieces), out_shape=(f32(t...  98.9 us
    pallas_call x1, Pallas kernels, polar_factor(): pl.pallas_call(polar_kernel, out_shape=jax.ShapeDtypeStruct(gramian.shape...  74.1 us
    pallas_call x1, Pallas kernels, gram_whole(): pl.pallas_call(gram_kernel, out_shape=(jax.ShapeDtypeStruct((size, band),...  72 us
    pallas_call x1, Pallas kernels, tail(): pl.pallas_call(tail_kernel, out_shape=(low(rows, width), low(rows, width)...  53.7 us
    pallas_call x1, Pallas kernels, spread(): pl.pallas_call(functools.partial(spread_kernel, sub, pieces), out_shape=t...  50.7 us
    pallas_call x1, Pallas kernels, enter(): pl.pallas_call(functools.partial(entry_kernel, pieces), out_shape=(jax.Sh...  29.6 us
    pallas_call x1, Pallas kernels, finish(): pl.pallas_call(functools.partial(finish_kernel, sub), out_shape=tuple(sha...  27.9 us
  transfers between devices with their start and end apart: 4, of which 0 were waited for; matrix products, arithmetic and copies ran while one was open for 1% of the time, Pallas kernels for 38%

profile of v9, /device:TPU:13, one launch (start us, length us, event | category | flops | bytes accessed | tf_op | source)
XLA Modules:
  0.0 580.5 jit_solution(6067518989284628405)
XLA Ops:
  0.7 1.3 collective-permute-start
  2.6 0.8 bitcast_add_fusion
  3.4 0.6 slice_bitcast_fusion
  4.0 0.0 copy-start.1
  4.0 1.6 copy-done.1
  5.6 0.8 copy-done.7
  6.4 7.4 %shard_map.356.mixed_ref = bf16[1024,1024]{1,0:T(8,128)(2,1)S(1)} custom-call(bf16[1024,1024]{1,0:T(8,128)(2,1)S(1)} %bitcast.28, f32[1,1024]{1,0:T(1,128)S(1)} %get-tuple-element.187.shift_ref, f32[1,1024]{1,0:T(1,128)S(1)} %get-tuple-element.186.scale_ref, f32[9,1024]{1,0:T(8,128)S(1)} %copy-done.7), custom_call_target="tpu_custom_call" | custom-call | flops 41943040 | bytes 4194304 | tf_op jit(solution)/shard_map/pallas_call | solution.py:1425
  13.9 0.0 copy-start.5
  13.9 0.0 copy-start.20
  13.9 10.7 %shard_map.357 = (bf16[1024,768]{1,0:T(8,128)(2,1)S(1)}, bf16[1024,256]{1,0:T(8,128)(2,1)S(1)}, f32[8,1024]{1,0:T(8,128)S(1)}, bf16[1024,768]{1,0:T(8,128)(2,1)S(1)}) custom-call(bf16[1024,1024]{1,0:T(8,128)(2,1)S(1)} %shard_map.356.mixed_ref, f32[3,1024,256]{2,1,0:T(8,128)S(1)} %bitcast.26), custom_call_target="tpu_custom_call" | custom-call | flops 4294967296 | bytes 12582912 | tf_op jit(solution)/shard_map/pallas_call | solution.py:1559
  24.6 0.0 copy-start.17
  24.6 1.1 copy-done.17
  25.8 0.6 copy-done.19
  26.4 0.0 collective-permute-done
  26.4 0.0 copy-done.20
  26.4 2.7 maximum_select_fusion.output_ref
  29.2 0.2 copy-done.2
  29.4 29.6 %shard_map.358 = (f32[1024,1024]{1,0:T(8,128)S(1)}, f32[1024,1024]{1,0:T(8,128)}, bf16[1024,1024]{1,0:T(8,128)(2,1)S(1)}) custom-call(bf16[1024,256]{1,0:T(8,128)(2,1)S(1)} %get-tuple-element.102.context_ref, bf16[1024,1024]{1,0:T(8,128)(2,1)S(1)} %bitcast.29, f32[512,1024]{1,0:T(8,128)S(1)} %maximum_select_fusion.output_ref, ...), custom_call_target="tpu_custom_call" | custom-call | flops 2147483648 | bytes 104857600 | tf_op jit(solution)/shard_map/pallas_call | solution.py:1686
  59.0 0.0 copy-start.14
  59.0 2.0 copy-done.14
  61.0 1.3 copy-done.15
  62.3 0.6 broadcast_in_dim.12.live_ref
  62.9 98.9 %shard_map.359 = (f32[512,1024]{1,0:T(8,128)}, f32[1024,1024]{1,0:T(8,128)}, f32[128,1024]{1,0:T(8,128)}, f32[2,128,1024]{2,1,0:T(8,128)}, f32[2,128,1024]{2,1,0:T(8,128)}, /*index=5*/f32[9,1024]{1,0:T(8,128)}) custom-call(bf16[1024,1024]{1,0:T(8,128)(2,1)} %copy-done.15, bf16[1024,1024]{1,0:T(8,128)(2,1)} %bitcast.32, f32[1,1024]{1,0:T(1,128)} %broadcast_in_dim.12.live_ref, ...), custom_call_target="tpu_custom_call" | custom-call | flops 12884901888 | bytes 209715200 | tf_op jit(solution)/shard_map/pallas_call | solution.py:1340
  161.8 0.7 collective-permute-start.1
  162.5 126.4 %shard_map.360 = (f32[1024,1024]{1,0:T(8,128)}, f32[1,1024]{1,0:T(1,128)}, f32[1,1024]{1,0:T(1,128)}, f32[1,1024]{1,0:T(1,128)}, f32[1024,1024]{1,0:T(8,128)}, /...) custom-call(f32[1024,1024]{1,0:T(8,128)} %get-tuple-element.110.hidden_any, ...), custom_call_target="tpu_custom_call" | custom-call | flops 10737418240 | bytes 157286400 | tf_op jit(solution)/shard_map/pallas_call | solution.py:2024
  288.9 1.3 pad_maximum_fusion.rows_ref
  290.2 0.0 collective-permute-done.1.ffn_across_any
  290.2 1.3 copy-done.21
  291.5 53.7 %shard_map.361 = (bf16[1024,1024]{1,0:T(8,128)(2,1)}, bf16[1024,1024]{1,0:T(8,128)(2,1)}, f32[32,1024]{1,0:T(8,128)}, f32[8,128]{1,0:T(8,128)}, f32[512,1024]{1,0:T(8,128)}, /*index=5*/f32[512,1024]{1,0:T(8,128)}) custom-call(bf16[1024,1024]{1,0:T(8,128)(2,1)} %bitcast.27, f32[1,1024]{1,0:T(1,128)} %copy-done.9, f32[1,1024]{1,0:T(1,128)} %copy-done.8, ...), custom_call_target="tpu_custom_call" | custom-call | flops 104857600 | bytes 62914560 | tf_op jit(solution)/shard_map/pallas_call | solution.py:2320
  345.3 0.7 copy-done.10
  346.0 72.0 %shard_map.362 = (f32[1024,640]{1,0:T(8,128)}, f32[256,1024]{1,0:T(8,128)S(1)}, f32[256,1024]{1,0:T(8,128)S(1)}) custom-call(f32[8,128]{1,0:T(8,128)S(1)} %copy-done.10, f32[512,1024]{1,0:T(8,128)} %get-tuple-element.139.attend_out_any.refs_0_, f32[512,1024]{1,0:T(8,128)} %get-tuple-element.141.expand_any.refs_1_, ...), custom_call_target="tpu_custom_call" | custom-call | flops 3221225472 | bytes 83886080 | tf_op jit(solution)/shard_map/pallas_call | solution.py:527
  417.9 0.0 copy-start.6
  417.9 1.0 copy-done.6
  418.9 1.9 collective-permute-start.3
  420.8 0.0 collective-permute-start.2
  420.8 1.7 copy-done.13
  422.6 74.1 %shard_map.363.q_ref = f32[1024,640]{1,0:T(8,128)S(1)} custom-call(f32[1024,640]{1,0:T(8,128)S(1)} %copy-done.13), custom_call_target="tpu_custom_call" | custom-call | flops 109521666048 | bytes 8388608 | tf_op jit(solution)/shard_map/pallas_call | solution.py:650
  496.7 0.0 copy-start.4
  496.7 1.5 copy-done.4
  498.2 1.2 slice.31
  499.4 0.6 slice.30.hidden_sum_ref
  500.0 0.0 collective-permute-done.2.refs_5_
  500.0 0.0 collective-permute-done.3.refs_3_
  500.0 0.0 copy-start.22
  500.0 1.0 copy-done.23
  501.0 0.7 copy-done.22
  501.6 50.7 %shard_map.364 = (f32[4,1024,640]{2,1,0:T(8,128)}, f32[3,1024,256]{2,1,0:T(8,128)}, f32[256,1024]{1,0:T(8,128)}, f32[1024,1024]{1,0:T(8,128)}, f32[1024,1024]{1,...) custom-call(f32[8,128]{1,0:T(8,128)} %get-tuple-element.130.norm_ref, ...), custom_call_target="tpu_custom_call" | custom-call | flops 9663676416 | bytes 83886080 | tf_op jit(solution)/shard_map/pallas_call | solution.py:897
  552.4 27.9 %shard_map.365 = (f32[3,1024,256]{2,1,0:T(8,128)}, f32[256,1024]{1,0:T(8,128)}, f32[1024,1024]{1,0:T(8,128)}, f32[1024,1024]{1,0:T(8,128)}, f32[3,1024,256]{2,1,...) custom-call(f32[8,128]{1,0:T(8,128)} %get-tuple-element.130.norm_ref, ...), custom_call_target="tpu_custom_call" | custom-call | flops 9663676416 | bytes 62914560 | tf_op jit(solution)/shard_map/pallas_call | solution.py:1019
  (27 shorter events, 0.0 us)
Async XLA Ops:
  0.7 25.7 %collective-permute-start = (f32[256,1024]{1,0:T(8,128)}, f32[256,1024]{1,0:T(8,128)}, u32[]{:S(2)}, u32[]{:S(2)}) collective-permute-start(f32[256,1024]{1,0:T(8,128)} %refs_29_.1), channel_id=1, source_target_pairs={{0,2},{1,3},{2,0},{3,1},{4,6},{5,7},{6,4},{7,5},{8,10},{9,11},{10,... | collective-permute-start | bytes 3145736 | tf_op jit(solution)/shard_map/ppermute | solution.py:81
  4.0 9.9 %copy-start.8 = (f32[1,1024]{1,0:T(1,128)}, f32[1,1024]{1,0:T(1,128)S(1)}, u32[]{:S(2)}) copy-start(f32[1,1024]{1,0:T(1,128)S(1)} %get-tuple-element.186.scale_ref) | copy-start | bytes 12292
  4.0 9.9 %copy-start.9 = (f32[1,1024]{1,0:T(1,128)}, f32[1,1024]{1,0:T(1,128)S(1)}, u32[]{:S(2)}) copy-start(f32[1,1024]{1,0:T(1,128)S(1)} %get-tuple-element.187.shift_ref) | copy-start | bytes 12292
  4.0 25.2 %copy-start.11 = (f32[1,1024]{1,0:T(1,128)}, f32[1,1024]{1,0:T(1,128)S(1)}, u32[]{:S(2)}) copy-start(f32[1,1024]{1,0:T(1,128)S(1)} %get-tuple-element.183.scale_ref) | copy-start | bytes 12292
  4.0 25.2 %copy-start.12 = (f32[1,1024]{1,0:T(1,128)}, f32[1,1024]{1,0:T(1,128)S(1)}, u32[]{:S(2)}) copy-start(f32[1,1024]{1,0:T(1,128)S(1)} %get-tuple-element.185.gate_ref) | copy-start | bytes 12292
  4.0 1.6 copy-start.1
  5.6 0.8 copy-start.7
  6.4 7.5 %copy-start = (f32[1024,3,256]{2,0,1:T(8,128)S(1)}, f32[1024,3,256]{2,0,1:T(8,128)}, u32[]{:S(2)}) copy-start(f32[1024,3,256]{2,0,1:T(8,128)} %param.28) | copy-start | bytes 9437188
  13.9 10.7 %copy-start.5 = (bf16[1024,1024]{1,0:T(8,128)(2,1)}, bf16[1024,1024]{1,0:T(8,128)(2,1)S(1)}, u32[]{:S(2)}) copy-start(bf16[1024,1024]{1,0:T(8,128)(2,1)S(1)} %shard_map.356.mixed_ref) | copy-start | bytes 6291460
  13.9 12.5 %copy-start.20 = (f32[256,1024]{1,0:T(8,128)S(1)}, f32[256,1024]{1,0:T(8,128)}, u32[]{:S(2)}) copy-start(f32[256,1024]{1,0:T(8,128)} %refs_29_.1) | copy-start | bytes 3145732
  24.6 1.1 copy-start.17
  25.8 0.6 copy-start.19
  26.4 2.7 copy-start.18
  26.4 2.8 copy-start.16
  26.4 3.0 copy-start.2
  59.0 2.0 copy-start.14
  61.0 1.3 copy-start.15
  161.8 128.4 %collective-permute-start.1 = (f32[512,1024]{1,0:T(8,128)}, f32[512,1024]{1,0:T(8,128)S(1)}, u32[]{:S(2)}, u32[]{:S(2)}) collective-permute-start(f32[512,1024]{1,0:T(8,128)} %get-tuple-element.109.ffn_half_any), channel_id=1, source_target_pairs={{0,2},{1,3},{2,0},{3,1},{4,6},{5,7},{6,4},{7,5},{8,10},{9,11},{10,... | collective-permute-start | bytes 6291464 | tf_op jit(solution)/shard_map/ppermute | solution.py:81
  290.2 1.3 copy-start.21
  291.5 53.8 %copy-start.3 = (f32[256,1024]{1,0:T(8,128)S(1)}, f32[256,1024]{1,0:T(8,128)}, u32[]{:S(2)}) copy-start(f32[256,1024]{1,0:T(8,128)} %refs_8_.2) | copy-start | bytes 3145732
  345.3 0.7 copy-start.10
  417.9 1.0 copy-start.6
  418.9 81.1 %collective-permute-start.3 = (f32[512,1024]{1,0:T(8,128)}, f32[512,1024]{1,0:T(8,128)S(1)}, u32[]{:S(2)}, u32[]{:S(2)}) collective-permute-start(f32[512,1024]{1,0:T(8,128)} %get-tuple-element.139.attend_out_any.refs_0_), channel_id=1, source_target_pairs={{0,4},{4,0},{8,12},{12,8},{16,20},{20,16},{24,28},{28,24},{1,5},{5... | collective-permute-start | bytes 6291464 | tf_op jit(solution)/shard_map/ppermute | solution.py:81
  420.8 79.2 %collective-permute-start.2 = (f32[256,1024]{1,0:T(8,128)S(1)}, f32[256,1024]{1,0:T(8,128)S(1)}, u32[]{:S(2)}, u32[]{:S(2)}) collective-permute-start(f32[256,1024]{1,0:T(8,128)S(1)} %get-tuple-element.138), channel_id=1, source_target_pairs={{0,4},{4,0},{8,12},{12,8},{16,20},{20,16},{24,28},{28,24},{1,5},{5... | collective-permute-start | bytes 3145736 | tf_op jit(solution)/shard_map/ppermute | solution.py:81
  420.8 1.7 copy-start.13
  422.6 76.8 %copy-start.24 = (f32[32,1024]{1,0:T(8,128)S(1)}, f32[32,1024]{1,0:T(8,128)}, u32[]{:S(2)}) copy-start(f32[32,1024]{1,0:T(8,128)} %get-tuple-element.131.small_ref) | copy-start | bytes 393220
  496.7 1.5 copy-start.4
  500.0 1.0 copy-start.23
  500.0 1.7 copy-start.22

commit v10 on v9

--- a/solution.py
+++ b/solution.py
@@ -1599,6 +1599,7 @@
     context_ref,
     tokens_ref,
     output_ref,
+    other_ref,
     gate_ref,
     shift_ref,
     scale_ref,
@@ -1621,20 +1622,32 @@
     greet([place_at(axis, bit) for axis, bit in hops])
     chunk = lambda p: pl.ds(p * step, step)
     slots[narrow_position(0)] = context_ref[...].astype(jnp.float32)
-    output_copy = send(
-        output_ref, output_inbox, sends, arrivals, pieces * (count - 1), place_at("narrow", 1)
-    )
+    part = output_ref.shape[0]
+    side = (lax.axis_index("narrow") // hops[-2][1]) % 2
+    output_copies = []
+    for index, (ref, where) in enumerate(((output_ref, side), (other_ref, 1 - side))):
+        output_copies.append(
+            send(
+                ref,
+                output_inbox.at[pl.ds(pl.multiple_of(where * part, SLAB), part), :],
+                sends,
+                arrivals,
+                pieces * (count - 1) + index,
+                place_at("narrow", 1),
+            )
+        )
     gathers = []
     for p in range(pieces):
         spot_of = lambda item, p=p: slots.at[narrow_position(item), chunk(p)]
         gathers.append(Gather(spot_of(0), spot_of, hops, sends, arrivals, p * (count - 1)))
         gathers[p].step(0)
     core = lax.axis_index("narrow") % 2
-    half = output_ref.shape[0]
-    output_low[pl.ds(pl.multiple_of(core * half, SLAB), half), :] = output_ref[...].astype(
-        jnp.bfloat16
-    )
-    output_copy.wait_recv()
+    half = 2 * part
+    for ref, where in ((output_ref, side), (other_ref, 1 - side)):
+        start = pl.multiple_of(core * half + where * part, SLAB)
+        output_low[pl.ds(start, part), :] = ref[...].astype(jnp.bfloat16)
+    for copy in output_copies:
+        copy.wait_recv()
     output_low[pl.ds(pl.multiple_of((1 - core) * half, SLAB), half), :] = output_inbox[...].astype(
         jnp.bfloat16
     )
@@ -1671,18 +1684,19 @@
             outs[-1].start()
     for gather in gathers:
         gather.finish()
-    output_copy.wait_send()
+    for copy in output_copies:
+        copy.wait_send()
     for out in outs:
         out.wait()
 
 
-def enter(context, tokens, output_rows, gate, shift, scale, number):
+def enter(context, tokens, output_rows, other_rows, gate, shift, scale, number):
     pieces = 4
     rows, own = context.shape
     width = tokens.shape[1]
     count = lax.axis_size("narrow")
     vmem = pl.BlockSpec(memory_space=pltpu.VMEM)
-    slots = pieces * (count - 1) + 1
+    slots = pieces * (count - 1) + 2
     return pl.pallas_call(
         functools.partial(entry_kernel, pieces),
         out_shape=(
@@ -1690,7 +1704,7 @@
             jax.ShapeDtypeStruct((rows, width), jnp.float32),
             jax.ShapeDtypeStruct((rows, width), jnp.bfloat16),
         ),
-        in_specs=[vmem] * 6,
+        in_specs=[vmem] * 7,
         out_specs=(pl.BlockSpec(memory_space=pl.ANY),) * 2 + (vmem,),
         scratch_shapes=[
             pltpu.VMEM((rows, width), jnp.float32),
@@ -1698,7 +1712,7 @@
             pltpu.SemaphoreType.DMA((2 * pieces,)),
             pltpu.VMEM((count, rows, own), jnp.float32),
             pltpu.VMEM((width, width), jnp.bfloat16),
-            pltpu.VMEM(output_rows.shape, jnp.float32),
+            pltpu.VMEM((2 * output_rows.shape[0], width), jnp.float32),
             pltpu.SemaphoreType.DMA((slots,)),
             pltpu.SemaphoreType.DMA((slots,)),
         ],
@@ -1708,11 +1722,12 @@
         cost_estimate=pl.CostEstimate(
             flops=2 * rows * width * width, bytes_accessed=100 * rows * width, transcendentals=0
         ),
-    )(context, tokens, output_rows, gate, shift, scale)
+    )(context, tokens, output_rows, other_rows, gate, shift, scale)
 
 
 def all_rows(values):
-    for _, bit in narrow_hops()[:-1]:
+    *before, (_, last), _ = narrow_hops()
+    for _, bit in before:
         side = (lax.axis_index("narrow") // bit) % 2
         other = permute(values, "narrow", bit)
         values = jnp.where(
@@ -1720,7 +1735,7 @@
             jnp.concatenate([values, other], axis=0),
             jnp.concatenate([other, values], axis=0),
         )
-    return values
+    return values, permute(values, "narrow", last)
 
 
 def back_kernel(
@@ -2413,9 +2428,10 @@
     mixed_low = mixer_forward(flat_tokens, shift_one[0], scale_one[0], mixer_kernel)
     three = lambda matrix: jnp.transpose(matrix, (1, 0, 2))
     triple, context, logsum, attend_low = attend(mixed_low, three(attend_weight))
-    output_rows, context = together(all_rows(output_weight), context)
+    output_rows, other_rows = all_rows(output_weight)
+    other_rows, context = together(other_rows, context)
     branch, hidden, entry_low = enter(
-        context, flat_tokens, output_rows, gate_one[0], shift_two[0], scale_two[0], 1
+        context, flat_tokens, output_rows, other_rows, gate_one[0], shift_two[0], scale_two[0], 1
     )
     flat_cotangent = cotangent.reshape(-1, width)
     live_row = jnp.broadcast_to(live_mask[0], (1, width))

time: 589 us -> 587 us (level)
  no operation moved by 1% of the time
where the time goes in v10:
time: 587 us; the launch traced here: 580 us
  Pallas kernels  552 us (94%)
  local copies, waits for them, and re-layouts  18.9 us (3%)
    pallas_call x1, Pallas kernels, back(): pl.pallas_call(functools.partial(back_kernel, pieces), out_shape=(f32(tok...  127 us
    pallas_call x1, Pallas kernels, middle(): pl.pallas_call(functools.partial(middle_kernel, pieces), out_shape=(f32(t...  98.1 us
    pallas_call x1, Pallas kernels, polar_factor(): pl.pallas_call(polar_kernel, out_shape=jax.ShapeDtypeStruct(gramian.shape...  74.1 us
    pallas_call x1, Pallas kernels, gram_whole(): pl.pallas_call(gram_kernel, out_shape=(jax.ShapeDtypeStruct((size, band),...  72.2 us
    pallas_call x1, Pallas kernels, tail(): pl.pallas_call(tail_kernel, out_shape=(low(rows, width), low(rows, width)...  55 us
    pallas_call x1, Pallas kernels, spread(): pl.pallas_call(functools.partial(spread_kernel, sub, pieces), out_shape=t...  50.7 us
    pallas_call x1, Pallas kernels, enter(): pl.pallas_call(functools.partial(entry_kernel, pieces), out_shape=(jax.Sh...  29.7 us
    pallas_call x1, Pallas kernels, finish(): pl.pallas_call(functools.partial(finish_kernel, sub), out_shape=tuple(sha...  27.9 us
  transfers between devices with their start and end apart: 4, of which 0 were waited for; matrix products, arithmetic and copies ran while one was open for 1% of the time, Pallas kernels for 38%

profile of v10, /device:TPU:13, one launch (start us, length us, event | category | flops | bytes accessed | tf_op | source)
XLA Modules:
  0.0 579.5 jit_solution(6492533165230453140)
XLA Ops:
  0.7 0.0 copy-start
  0.7 1.3 collective-permute-start
  2.6 0.8 bitcast_add_fusion
  3.4 0.6 slice_bitcast_fusion
  4.0 0.0 copy-start.1
  4.0 1.6 copy-done.1
  5.6 0.8 copy-done.8
  6.4 7.4 %shard_map.356.mixed_ref = bf16[1024,1024]{1,0:T(8,128)(2,1)S(1)} custom-call(bf16[1024,1024]{1,0:T(8,128)(2,1)S(1)} %bitcast.28, f32[1,1024]{1,0:T(1,128)S(1)} %get-tuple-element.187.shift_ref, f32[1,1024]{1,0:T(1,128)S(1)} %get-tuple-element.186.scale_ref, f32[9,1024]{1,0:T(8,128)S(1)} %copy-done.8), custom_call_target="tpu_custom_call" | custom-call | flops 41943040 | bytes 4194304 | tf_op jit(solution)/shard_map/pallas_call | solution.py:1425
  13.9 0.0 copy-start.6
  13.9 0.0 copy-start.2
  13.9 0.0 copy-start.3
  13.9 10.7 %shard_map.357 = (bf16[1024,768]{1,0:T(8,128)(2,1)S(1)}, bf16[1024,256]{1,0:T(8,128)(2,1)S(1)}, f32[8,1024]{1,0:T(8,128)S(1)}, bf16[1024,768]{1,0:T(8,128)(2,1)S(1)}) custom-call(bf16[1024,1024]{1,0:T(8,128)(2,1)S(1)} %shard_map.356.mixed_ref, f32[3,1024,256]{2,1,0:T(8,128)S(1)} %bitcast.26), custom_call_target="tpu_custom_call" | custom-call | flops 4294967296 | bytes 12582912 | tf_op jit(solution)/shard_map/pallas_call | solution.py:1559
  24.6 0.0 copy-start.18
  24.7 1.1 copy-done.18
  25.8 1.1 copy-done.19
  26.9 0.0 collective-permute-done.other_ref
  26.9 0.0 copy-done.12
  27.0 29.7 %shard_map.358 = (f32[1024,1024]{1,0:T(8,128)S(1)}, f32[1024,1024]{1,0:T(8,128)}, bf16[1024,1024]{1,0:T(8,128)(2,1)S(1)}) custom-call(bf16[1024,256]{1,0:T(8,128)(2,1)S(1)} %get-tuple-element.102.context_ref, bf16[1024,1024]{1,0:T(8,128)(2,1)S(1)} %bitcast.29, f32[256,1024]{1,0:T(8,128)S(1)} %copy-done.3, f32[256,1024]{1,0:T(8,128)S(1)} %collective-permute-done.other_ref, ...), custom_call_target="tpu_custom_call" | custom-call | flops 2147483648 | bytes 104857600 | tf_op jit(solution)/shard_map/pallas_call | solution.py:1700
  56.7 0.0 copy-start.15
  56.7 2.0 copy-done.15
  58.7 1.3 copy-done.16
  60.0 0.6 broadcast_in_dim.12.live_ref
  60.6 98.1 %shard_map.359 = (f32[512,1024]{1,0:T(8,128)}, f32[1024,1024]{1,0:T(8,128)}, f32[128,1024]{1,0:T(8,128)}, f32[2,128,1024]{2,1,0:T(8,128)}, f32[2,128,1024]{2,1,0:T(8,128)}, /*index=5*/f32[9,1024]{1,0:T(8,128)}) custom-call(bf16[1024,1024]{1,0:T(8,128)(2,1)} %copy-done.16, bf16[1024,1024]{1,0:T(8,128)(2,1)} %bitcast.32, f32[1,1024]{1,0:T(1,128)} %broadcast_in_dim.12.live_ref, ...), custom_call_target="tpu_custom_call" | custom-call | flops 12884901888 | bytes 209715200 | tf_op jit(solution)/shard_map/pallas_call | solution.py:1340
  158.7 0.7 collective-permute-start.1
  159.5 126.7 %shard_map.360 = (f32[1024,1024]{1,0:T(8,128)}, f32[1,1024]{1,0:T(1,128)}, f32[1,1024]{1,0:T(1,128)}, f32[1,1024]{1,0:T(1,128)}, f32[1024,1024]{1,0:T(8,128)}, /...) custom-call(f32[1024,1024]{1,0:T(8,128)} %get-tuple-element.110.hidden_any, ...), custom_call_target="tpu_custom_call" | custom-call | flops 10737418240 | bytes 157286400 | tf_op jit(solution)/shard_map/pallas_call | solution.py:2039
  286.1 1.3 pad_maximum_fusion.rows_ref
  287.4 0.0 collective-permute-done.1.ffn_across_any
  287.4 1.3 copy-done.21
  288.8 55.0 %shard_map.361 = (bf16[1024,1024]{1,0:T(8,128)(2,1)}, bf16[1024,1024]{1,0:T(8,128)(2,1)}, f32[32,1024]{1,0:T(8,128)}, f32[8,128]{1,0:T(8,128)}, f32[512,1024]{1,0:T(8,128)}, /*index=5*/f32[512,1024]{1,0:T(8,128)}) custom-call(bf16[1024,1024]{1,0:T(8,128)(2,1)} %bitcast.27, f32[1,1024]{1,0:T(1,128)} %copy-done.10, f32[1,1024]{1,0:T(1,128)} %copy-done.9, ...), custom_call_target="tpu_custom_call" | custom-call | flops 104857600 | bytes 62914560 | tf_op jit(solution)/shard_map/pallas_call | solution.py:2335
  343.8 0.7 copy-done.11
  344.4 72.2 %shard_map.362 = (f32[1024,640]{1,0:T(8,128)}, f32[256,1024]{1,0:T(8,128)S(1)}, f32[256,1024]{1,0:T(8,128)S(1)}) custom-call(f32[8,128]{1,0:T(8,128)S(1)} %copy-done.11, f32[512,1024]{1,0:T(8,128)} %get-tuple-element.139.attend_out_any.refs_0_, f32[512,1024]{1,0:T(8,128)} %get-tuple-element.141.expand_any.refs_1_, ...), custom_call_target="tpu_custom_call" | custom-call | flops 3221225472 | bytes 83886080 | tf_op jit(solution)/shard_map/pallas_call | solution.py:527
  416.6 0.0 copy-start.7
  416.6 1.0 copy-done.7
  417.6 2.2 collective-permute-start.3
  419.8 0.0 collective-permute-start.2
  419.9 1.7 copy-done.14
  421.6 74.1 %shard_map.363.q_ref = f32[1024,640]{1,0:T(8,128)S(1)} custom-call(f32[1024,640]{1,0:T(8,128)S(1)} %copy-done.14), custom_call_target="tpu_custom_call" | custom-call | flops 109521666048 | bytes 8388608 | tf_op jit(solution)/shard_map/pallas_call | solution.py:650
  495.7 0.0 copy-start.5
  495.7 1.5 copy-done.5
  497.2 1.2 slice.31
  498.4 0.6 slice.30.hidden_sum_ref
  499.0 0.0 collective-permute-done.2.refs_5_
  499.0 0.0 collective-permute-done.3.refs_3_
  499.0 0.0 copy-start.22
  499.0 1.0 copy-done.23
  500.0 0.7 copy-done.22
  500.7 50.7 %shard_map.364 = (f32[4,1024,640]{2,1,0:T(8,128)}, f32[3,1024,256]{2,1,0:T(8,128)}, f32[256,1024]{1,0:T(8,128)}, f32[1024,1024]{1,0:T(8,128)}, f32[1024,1024]{1,...) custom-call(f32[8,128]{1,0:T(8,128)} %get-tuple-element.130.norm_ref, ...), custom_call_target="tpu_custom_call" | custom-call | flops 9663676416 | bytes 83886080 | tf_op jit(solution)/shard_map/pallas_call | solution.py:897
  551.4 27.9 %shard_map.365 = (f32[3,1024,256]{2,1,0:T(8,128)}, f32[256,1024]{1,0:T(8,128)}, f32[1024,1024]{1,0:T(8,128)}, f32[1024,1024]{1,0:T(8,128)}, f32[3,1024,256]{2,1,...) custom-call(f32[8,128]{1,0:T(8,128)} %get-tuple-element.130.norm_ref, ...), custom_call_target="tpu_custom_call" | custom-call | flops 9663676416 | bytes 62914560 | tf_op jit(solution)/shard_map/pallas_call | solution.py:1019
  (26 shorter events, 0.0 us)
Async XLA Ops:
  0.7 13.2 %copy-start = (f32[1024,3,256]{2,0,1:T(8,128)S(1)}, f32[1024,3,256]{2,0,1:T(8,128)}, u32[]{:S(2)}) copy-start(f32[1024,3,256]{2,0,1:T(8,128)} %param.28) | copy-start | bytes 9437188
  0.7 26.3 %collective-permute-start = (f32[256,1024]{1,0:T(8,128)}, f32[256,1024]{1,0:T(8,128)S(1)}, u32[]{:S(2)}, u32[]{:S(2)}) collective-permute-start(f32[256,1024]{1,0:T(8,128)} %refs_29_.1), channel_id=1, source_target_pairs={{0,2},{1,3},{2,0},{3,1},{4,6},{5,7},{6,4},{7,5},{8,10},{9,11},{10,... | collective-permute-start | bytes 3145736 | tf_op jit(solution)/shard_map/ppermute | solution.py:81
  4.0 20.6 %copy-start.9 = (f32[1,1024]{1,0:T(1,128)}, f32[1,1024]{1,0:T(1,128)S(1)}, u32[]{:S(2)}) copy-start(f32[1,1024]{1,0:T(1,128)S(1)} %get-tuple-element.186.scale_ref) | copy-start | bytes 12292
  4.0 20.6 %copy-start.10 = (f32[1,1024]{1,0:T(1,128)}, f32[1,1024]{1,0:T(1,128)S(1)}, u32[]{:S(2)}) copy-start(f32[1,1024]{1,0:T(1,128)S(1)} %get-tuple-element.187.shift_ref) | copy-start | bytes 12292
  4.0 23.0 %copy-start.12 = (f32[1,1024]{1,0:T(1,128)}, f32[1,1024]{1,0:T(1,128)S(1)}, u32[]{:S(2)}) copy-start(f32[1,1024]{1,0:T(1,128)S(1)} %get-tuple-element.183.scale_ref) | copy-start | bytes 12292
  4.0 23.0 %copy-start.13 = (f32[1,1024]{1,0:T(1,128)}, f32[1,1024]{1,0:T(1,128)S(1)}, u32[]{:S(2)}) copy-start(f32[1,1024]{1,0:T(1,128)S(1)} %get-tuple-element.185.gate_ref) | copy-start | bytes 12292
  4.0 1.6 copy-start.1
  5.6 0.8 copy-start.8
  13.9 10.8 %copy-start.6 = (bf16[1024,1024]{1,0:T(8,128)(2,1)}, bf16[1024,1024]{1,0:T(8,128)(2,1)S(1)}, u32[]{:S(2)}) copy-start(bf16[1024,1024]{1,0:T(8,128)(2,1)S(1)} %shard_map.356.mixed_ref) | copy-start | bytes 6291460
  13.9 13.1 %copy-start.2 = (bf16[1,1024,1024]{2,1,0:T(8,128)(2,1)S(1)}, bf16[1,1024,1024]{2,1,0:T(8,128)(2,1)}, u32[]{:S(2)}) copy-start(bf16[1,1024,1024]{2,1,0:T(8,128)(2,1)} %param.21) | copy-start | bytes 6291460
  13.9 13.1 %copy-start.3 = (f32[256,1024]{1,0:T(8,128)S(1)}, f32[256,1024]{1,0:T(8,128)}, u32[]{:S(2)}) copy-start(f32[256,1024]{1,0:T(8,128)} %refs_29_.1) | copy-start | bytes 3145732
  24.6 1.1 copy-start.18
  25.8 1.1 copy-start.19
  26.9 29.7 %copy-start.17 = (bf16[1024,256]{1,0:T(8,128)(2,1)}, bf16[1024,256]{1,0:T(8,128)(2,1)S(1)}, u32[]{:S(2)}) copy-start(bf16[1024,256]{1,0:T(8,128)(2,1)S(1)} %get-tuple-element.102.context_ref) | copy-start | bytes 1572868
  26.9 29.7 %copy-start.20 = (f32[8,1024]{1,0:T(8,128)}, f32[8,1024]{1,0:T(8,128)S(1)}, u32[]{:S(2)}) copy-start(f32[8,1024]{1,0:T(8,128)S(1)} %get-tuple-element.115.logsum_ref) | copy-start | bytes 98308
  56.7 2.0 copy-start.15
  58.7 1.3 copy-start.16
  158.7 128.7 %collective-permute-start.1 = (f32[512,1024]{1,0:T(8,128)}, f32[512,1024]{1,0:T(8,128)S(1)}, u32[]{:S(2)}, u32[]{:S(2)}) collective-permute-start(f32[512,1024]{1,0:T(8,128)} %get-tuple-element.109.ffn_half_any), channel_id=1, source_target_pairs={{0,2},{1,3},{2,0},{3,1},{4,6},{5,7},{6,4},{7,5},{8,10},{9,11},{10,... | collective-permute-start | bytes 6291464 | tf_op jit(solution)/shard_map/ppermute | solution.py:81
  287.4 1.3 copy-start.21
  288.8 55.0 %copy-start.4 = (f32[256,1024]{1,0:T(8,128)S(1)}, f32[256,1024]{1,0:T(8,128)}, u32[]{:S(2)}) copy-start(f32[256,1024]{1,0:T(8,128)} %refs_8_.2) | copy-start | bytes 3145732
  343.7 0.7 copy-start.11
  416.6 1.0 copy-start.7
  417.6 81.4 %collective-permute-start.3 = (f32[512,1024]{1,0:T(8,128)}, f32[512,1024]{1,0:T(8,128)S(1)}, u32[]{:S(2)}, u32[]{:S(2)}) collective-permute-start(f32[512,1024]{1,0:T(8,128)} %get-tuple-element.139.attend_out_any.refs_0_), channel_id=1, source_target_pairs={{0,4},{4,0},{8,12},{12,8},{16,20},{20,16},{24,28},{28,24},{1,5},{5... | collective-permute-start | bytes 6291464 | tf_op jit(solution)/shard_map/ppermute | solution.py:81
  419.8 79.2 %collective-permute-start.2 = (f32[256,1024]{1,0:T(8,128)S(1)}, f32[256,1024]{1,0:T(8,128)S(1)}, u32[]{:S(2)}, u32[]{:S(2)}) collective-permute-start(f32[256,1024]{1,0:T(8,128)S(1)} %get-tuple-element.138), channel_id=1, source_target_pairs={{0,4},{4,0},{8,12},{12,8},{16,20},{20,16},{24,28},{28,24},{1,5},{5... | collective-permute-start | bytes 3145736 | tf_op jit(solution)/shard_map/ppermute | solution.py:81
  419.8 1.7 copy-start.14
  421.6 76.8 %copy-start.24 = (f32[32,1024]{1,0:T(8,128)S(1)}, f32[32,1024]{1,0:T(8,128)}, u32[]{:S(2)}) copy-start(f32[32,1024]{1,0:T(8,128)} %get-tuple-element.131.small_ref) | copy-start | bytes 393220
  495.7 1.5 copy-start.5
  499.0 1.0 copy-start.23
  499.0 1.7 copy-start.22
